TPU v7x, 32 devices: a whole 2x2x4 slice. The times are simulated.
32 devices in a mesh: groups: 2 (over x), dp: 8 (over z, y), tensor: 2 (over core).
Axes of the slice: x: 2, y: 2, z: 4, core: 2. Of those that a mesh axis runs over, the one named last changes fastest.
Arguments:
- grads: bfloat16 [16, 2, 2048, 512], P(('groups', 'dp'), None, 'tensor'), parts along dimension 0, may hold values from -144 to 144
- errors: float32 [16, 2, 2048, 512], P(('groups', 'dp'), None, 'tensor'), parts along dimension 0, may hold values from -4 to 4
- seeds: int32 [2], replicated, may hold values from 0 to 999999
Outputs:
- update: bfloat16 [4, 2048, 512], P('groups', 'tensor'), parts along dimension 0
- new_errors: float32 [16, 2, 2048, 512], P(('groups', 'dp'), None, 'tensor'), parts along dimension 0
There are 2 independent parts, one for each index of `groups`. A program takes and returns all parts, laid end to end along the dimension named above; an argument that names none is the same for every part. Nothing has to cross between parts.
All inputs are finite; a program needn't handle non-finite values.
Results may differ from a plain program's by a relative error of at most 0.001.
Values sent between devices are 32-bit elements; how exact they have to be, the bound alone decides.
No kernel may reach another device: no remote copies, remote signals or barrier semaphores. Data moves between devices by JAX's collectives and lax.ppermute only.
A program may use at most 64 MiB of HBM per device.

v0:
```python
import jax
import jax.numpy as jnp
from jax import lax
from jax.sharding import PartitionSpec as P

RANK = 4


EPSILON = 1e-08


def initial_factor(seeds, rank_count, col_count):
    index = (
        jnp.arange(rank_count, dtype=jnp.int32)[:, None] * col_count
        + jnp.arange(col_count, dtype=jnp.int32)[None, :]
    )
    mixed = index[None, :, :] * 747796405 + seeds[:, None, None] * 277803737 + 12345
    mixed = mixed ^ mixed >> 15
    mixed = mixed * 1274126177
    mixed = mixed ^ mixed >> 13
    lowbits = jnp.bitwise_and(mixed, 65535)
    return (lowbits.astype(jnp.float32) - 32767.5) / 32768.0


def orthogonal(factor, reducer):
    rank_count = factor.shape[1]
    columns = [factor[:, index] for index in range(rank_count)]
    for index in range(rank_count):
        current = columns[index]
        partners = [current] + columns[index + 1 :]
        products = jnp.stack([jnp.sum(current * partner, axis=-1) for partner in partners], axis=1)
        products = reducer(products)
        length = jnp.sqrt(products[:, 0:1]) + EPSILON
        current = current / length
        columns[index] = current
        for offset in range(1, len(partners)):
            inner_value = products[:, offset : offset + 1] / length
            columns[index + offset] = columns[index + offset] - inner_value * current
    return jnp.stack(columns, axis=1)


def body(grads, errors, seeds):
    merged = grads[0].astype(jnp.float32) + errors[0]
    replicas = lax.axis_size("dp")
    start_factor = initial_factor(seeds, RANK, merged.shape[2])
    partial_value = jnp.einsum(
        "mrc,mkc->mkr", merged, start_factor, precision=lax.Precision.HIGHEST
    )
    summed = lax.psum(partial_value, "dp") / replicas
    reducer = lambda operand: lax.psum(operand, "tensor")
    left_factor = orthogonal(summed, reducer)
    right_part = jnp.einsum("mrc,mkr->mkc", merged, left_factor, precision=lax.Precision.HIGHEST)
    right_factor = lax.psum(right_part, ("dp", "tensor")) / replicas
    approx = jnp.einsum("mkr,mkc->mrc", left_factor, right_factor, precision=lax.Precision.HIGHEST)
    return (approx.astype(jnp.bfloat16), (merged - approx)[None])


def solution(mesh):
    in_specs = (
        P(("groups", "dp"), None, "tensor", None),
        P(("groups", "dp"), None, "tensor", None),
        P(),
    )
    out_specs = (P("groups", "tensor", None), P(("groups", "dp"), None, "tensor", None))
    return jax.shard_map(body, mesh=mesh, in_specs=in_specs, out_specs=out_specs, check_vma=False)
```

profile of v0, /device:TPU:0, one launch (start us, length us, event | category | flops | bytes accessed | tf_op | source)
XLA Modules:
  0.0 127.1 jit_solution(17324117520015914522)
XLA Ops:
  0.6 0.0 copy-start
  0.6 0.8 broadcast_multiply_fusion.1
  1.5 0.1 add_multiply_fusion
  1.5 6.3 %fusion.2 = f32[2,4,1024]{2,1,0:T(4,128)S(1)} fusion(f32[1,2,1024,512]{3,2,1,0:T(8,128)} %param.4, bf16[1,2,1024,512]{3,2,1,0:T(8,128)(2,1)} %param.3, s32[2]{0:T(128)S(1)} %broadcast_multiply_fusion.1, s32[4,512]{1,0:T(4,128)S(1)} %add_multiply_fusion), kind=kOutput, calls=%fused_computation.3 | convolution fusion | flops 52473856 | bytes 6332424 | tf_op jit(solution)/shard_map/mrc,mkc->mkr/dot_general | solution.py:46
  7.9 38.9 %psum.42 = f32[2,4,1024]{2,0,1:T(2,128)S(1)} all-reduce(f32[2,4,1024]{2,0,1:T(2,128)S(1)} %copy.9), channel_id=1, replica_groups=mesh['groups'=2,'dp'=8,'tensor'=2] {'dp'}, use_global_device_ids=true, to_apply=%region_0.0 | all-reduce | flops 8192 | bytes 65536 | tf_op jit(solution)/shard_map/psum | solution.py:49
  46.8 0.2 fusion.20
  46.9 2.5 %psum.43 = f32[2,4]{0,1:T(4,128)S(1)} all-reduce(f32[2,4]{0,1:T(4,128)S(1)} %pad_maximum_fusion.1), channel_id=1, replica_groups=mesh['groups'=2,'dp'=8,'tensor'=2] {'tensor'}, use_global_device_ids=true, to_apply=%region_5.0 | all-reduce | flops 8 | bytes 64 | tf_op jit(solution)/shard_map/psum | solution.py:50
  49.4 0.2 multiply_reduce_fusion.5
  49.7 2.5 %psum.44 = f32[2,3]{0,1:T(4,128)S(1)} all-reduce(f32[2,3]{0,1:T(4,128)S(1)} %pad_maximum_fusion.2), channel_id=1, replica_groups=mesh['groups'=2,'dp'=8,'tensor'=2] {'tensor'}, use_global_device_ids=true, to_apply=%region_9.0 | all-reduce | flops 6 | bytes 48 | tf_op jit(solution)/shard_map/psum | solution.py:50
  52.2 0.2 multiply_reduce_fusion.2
  52.4 2.5 %psum.45 = f32[2,2]{0,1:T(2,128)S(1)} all-reduce(f32[2,2]{0,1:T(2,128)S(1)} %pad_maximum_fusion.3), channel_id=1, replica_groups=mesh['groups'=2,'dp'=8,'tensor'=2] {'tensor'}, use_global_device_ids=true, to_apply=%region_12.0 | all-reduce | flops 4 | bytes 32 | tf_op jit(solution)/shard_map/psum | solution.py:50
  54.9 0.2 multiply_reduce_fusion
  55.1 2.5 %psum.46 = f32[2,1]{0,1:T(1,128)S(1)} all-reduce(f32[2,1]{0,1:T(1,128)S(1)} %bitcast.75), channel_id=1, replica_groups=mesh['groups'=2,'dp'=8,'tensor'=2] {'tensor'}, use_global_device_ids=true, to_apply=%region_14.0 | all-reduce | flops 2 | bytes 16 | tf_op jit(solution)/shard_map/psum | solution.py:50
  57.6 0.1 subtract_divide_fusion
  57.7 0.0 copy-done
  57.7 4.5 %fusion = f32[2,4,512]{2,1,0:T(4,128)S(1)} fusion(f32[1,2,1024,512]{3,2,1,0:T(8,128)} %param.4, bf16[1,2,1024,512]{3,2,1,0:T(8,128)(2,1)S(1)} %copy-done, f32[2,4,1024]{2,0,1:T(2,128)S(1)} %pad_maximum_fusion), kind=kOutput, calls=%fused_computation.1 | convolution fusion | flops 52428800 | bytes 6340608 | tf_op jit(solution)/shard_map/mrc,mkr->mkc/dot_general | solution.py:52
  62.2 57.7 %psum.47 = f32[2,4,512]{2,1,0:T(4,128)S(1)} all-reduce(f32[2,4,512]{2,1,0:T(4,128)S(1)} %fusion), channel_id=1, replica_groups=mesh['groups'=2,'dp'=8,'tensor'=2] {'dp','tensor'}, use_global_device_ids=true, to_apply=%region_15.0 | all-reduce | flops 4096 | bytes 32768 | tf_op jit(solution)/shard_map/psum | solution.py:53
  119.9 7.2 %fusion.4 = (f32[1,2,1024,512]{3,2,1,0:T(8,128)}, bf16[2,1024,512]{2,1,0:T(8,128)(2,1)}) fusion(f32[1,2,1024,512]{3,2,1,0:T(8,128)} %param.4, bf16[1,2,1024,512]{3,2,1,0:T(8,128)(2,1)S(1)} %copy-done, f32[2,4,512]{2,1,0:T(4,128)S(1)} %psum.47, f32[2,4,1024]{2,0,1:T(2,128)S(1)} %pad_maximum_fusion), kind=kOutput, calls=%fused_computation.5 | convolution fusion | flops 54530048 | bytes 12632064 | tf_op jit(solution)/shard_map/mkr,mkc->mrc/dot_general | solution.py:54
  (11 shorter events, 0.2 us)
Async XLA Ops:
  0.6 57.1 %copy-start = (bf16[1,2,1024,512]{3,2,1,0:T(8,128)(2,1)S(1)}, bf16[1,2,1024,512]{3,2,1,0:T(8,128)(2,1)}, u32[]{:S(2)}) copy-start(bf16[1,2,1024,512]{3,2,1,0:T(8,128)(2,1)} %param.3) | copy-start | bytes 6291460
where the time goes:
time: 127 us
  blocking collectives  106 us (83%)
  matrix products  18 us (14%)
  other arithmetic  1.91 us (2%)
    psum x1, blocking collectives, body(): right_factor = lax.psum(right_part, ('dp', 'tensor')) / replicas  57.7 us
    psum x1, blocking collectives, body(): summed = lax.psum(partial_value, 'dp') / replicas  38.9 us
    psum x4, blocking collectives, body(): reducer = lambda operand: lax.psum(operand, 'tensor')  9.88 us
    dot_general x1, matrix products, body(): jnp.einsum('mkr,mkc->mrc', left_factor, right_factor, precision=lax.Preci...  7.2 us
    dot_general x1, matrix products, body(): jnp.einsum('mrc,mkc->mkr', merged, start_factor, precision=lax.Precision....  6.32 us
    dot_general x1, matrix products, body(): jnp.einsum('mrc,mkr->mkc', merged, left_factor, precision=lax.Precision.H...  4.5 us

commit v1 on v0

--- a/solution.py
+++ b/solution.py
@@ -22,35 +22,47 @@
     return (lowbits.astype(jnp.float32) - 32767.5) / 32768.0
 
 
-def orthogonal(factor, reducer):
+def orthogonal(factor):
     rank_count = factor.shape[1]
     columns = [factor[:, index] for index in range(rank_count)]
     for index in range(rank_count):
         current = columns[index]
-        partners = [current] + columns[index + 1 :]
-        products = jnp.stack([jnp.sum(current * partner, axis=-1) for partner in partners], axis=1)
-        products = reducer(products)
-        length = jnp.sqrt(products[:, 0:1]) + EPSILON
+        length = jnp.sqrt(jnp.sum(current * current, axis=-1, keepdims=True)) + EPSILON
         current = current / length
         columns[index] = current
-        for offset in range(1, len(partners)):
-            inner_value = products[:, offset : offset + 1] / length
-            columns[index + offset] = columns[index + offset] - inner_value * current
+        for other in range(index + 1, rank_count):
+            inner = jnp.sum(current * columns[other], axis=-1, keepdims=True)
+            columns[other] = columns[other] - inner * current
     return jnp.stack(columns, axis=1)
+
+
+def swap_sum(value, axis):
+    count = lax.axis_size(axis)
+    step = 1
+    while step < count:
+        pairs = [(index, index ^ step) for index in range(count)]
+        value = value + lax.ppermute(value, axis, pairs)
+        step *= 2
+    return value
 
 
 def body(grads, errors, seeds):
     merged = grads[0].astype(jnp.float32) + errors[0]
     replicas = lax.axis_size("dp")
+    half = lax.axis_index("tensor")
+    rows = merged.shape[1]
     start_factor = initial_factor(seeds, RANK, merged.shape[2])
     partial_value = jnp.einsum(
         "mrc,mkc->mkr", merged, start_factor, precision=lax.Precision.HIGHEST
     )
-    summed = lax.psum(partial_value, "dp") / replicas
-    reducer = lambda operand: lax.psum(operand, "tensor")
-    left_factor = orthogonal(summed, reducer)
+    summed = swap_sum(partial_value, "dp") / replicas
+    other = lax.ppermute(summed, "tensor", [(0, 1), (1, 0)])
+    first = jnp.where(half == 0, summed, other)
+    second = jnp.where(half == 0, other, summed)
+    whole = orthogonal(jnp.concatenate([first, second], axis=-1))
+    left_factor = lax.dynamic_slice_in_dim(whole, half * rows, rows, axis=2)
     right_part = jnp.einsum("mrc,mkr->mkc", merged, left_factor, precision=lax.Precision.HIGHEST)
-    right_factor = lax.psum(right_part, ("dp", "tensor")) / replicas
+    right_factor = swap_sum(swap_sum(right_part, "tensor"), "dp") / replicas
     approx = jnp.einsum("mkr,mkc->mrc", left_factor, right_factor, precision=lax.Precision.HIGHEST)
     return (approx.astype(jnp.bfloat16), (merged - approx)[None])
 

time: 127 us -> 48.6 us (0.38)
  blocking collectives: 106 us -> 0 us
  starting transfers between devices: 0 us -> 15.2 us
  waiting for transfers between devices: 0 us -> 13.3 us
  matrix products: 18 us -> 16.5 us
    psum x6 -> x0, blocking collectives: 106 us -> none  [the longest x1 57.7 us: body(): right_factor = lax.psum(right_part, ('dp', 'tensor')) / replicas]
    ppermute x0 -> x8, starting transfers between devices: none -> 15.2 us  [the longest x7 15.1 us: swap_sum(): value = value + lax.ppermute(value, axis, pairs)]
    ppermute x0 -> x8, waiting for transfers between devices: none -> 13.3 us  [the longest x7 12.1 us: swap_sum(): value = value + lax.ppermute(value, axis, pairs)]
    dot_general x1, matrix products: 7.2 us -> 5.73 us  [body(): jnp.einsum('mkr,mkc->mrc', left_factor, right_factor, precision=lax.Preci...]
  transfers between devices with their start and end apart: 0 -> 8, of which waited for: 0 -> 8; matrix products, arithmetic and copies ran while one was open for 0% -> 0% of each run, Pallas kernels for 0% -> 0%
where the time goes in v1:
time: 48.6 us; the launch traced here: 48.4 us
  matrix products  16.5 us (34%)
  starting transfers between devices  15.2 us (31%)
  waiting for transfers between devices  13.3 us (27%)
  other arithmetic  2.59 us (5%)
  between operations  0.73 us (2%)
    ppermute x7, starting transfers between devices, swap_sum(): value = value + lax.ppermute(value, axis, pairs)  15.1 us
    ppermute x7, waiting for transfers between devices, swap_sum(): value = value + lax.ppermute(value, axis, pairs)  12.1 us
    dot_general x1, matrix products, body(): jnp.einsum('mrc,mkc->mkr', merged, start_factor, precision=lax.Precision....  6.32 us
    dot_general x1, matrix products, body(): jnp.einsum('mkr,mkc->mrc', left_factor, right_factor, precision=lax.Preci...  5.73 us
    dot_general x1, matrix products, body(): jnp.einsum('mrc,mkr->mkc', merged, left_factor, precision=lax.Precision.H...  4.5 us
    ppermute x1, waiting for transfers between devices, body(): other = lax.ppermute(summed, 'tensor', [(0, 1), (1, 0)])  1.18 us
  transfers between devices with their start and end apart: 8, of which 8 were waited for; matrix products, arithmetic and copies ran while one was open for 0% of the time, Pallas kernels for 0%

profile of v1, /device:TPU:0, one launch (start us, length us, event | category | flops | bytes accessed | tf_op | source)
XLA Modules:
  0.0 48.4 jit_solution(3018063317347775017)
XLA Ops:
  0.6 0.0 copy-start.1
  0.7 0.8 %broadcast_multiply_fusion = s32[2]{0:T(128)S(1)} fusion(s32[2]{0:T(128)} %param.5), kind=kLoop, calls=%fused_computation.83 | loop fusion | flops 2 | bytes 16 | tf_op jit(solution)/shard_map/mul | solution.py:17
  1.5 0.1 add_multiply_fusion.1
  1.5 6.3 %fusion.2 = f32[2,4,1024]{2,1,0:T(4,128)S(1)} fusion(f32[1,2,1024,512]{3,2,1,0:T(8,128)} %param.4, bf16[1,2,1024,512]{3,2,1,0:T(8,128)(2,1)} %param.3, s32[2]{0:T(128)S(1)} %broadcast_multiply_fusion, s32[4,512]{1,0:T(4,128)S(1)} %add_multiply_fusion.1), kind=kOutput, calls=%fused_computation.3 | convolution fusion | flops 52473856 | bytes 6332424 | tf_op jit(solution)/shard_map/mrc,mkc->mkr/dot_general | solution.py:55
  7.9 3.0 %collective-permute-start = (f32[2,4,1024]{2,0,1:T(2,128)S(1)}, f32[2,4,1024]{2,0,1:T(2,128)S(1)}, u32[]{:S(2)}, u32[]{:S(2)}) collective-permute-start(f32[2,4,1024]{2,0,1:T(2,128)S(1)} %copy.10), channel_id=1, source_target_pairs={{0,2},{2,0},{4,6},{6,4},{8,10},{10,8},{12,14},{14,12},{1,3},{3,1},... | collective-permute-start | bytes 98312 | tf_op jit(solution)/shard_map/ppermute | solution.py:44
  10.9 1.9 %collective-permute-done = f32[2,4,1024]{2,0,1:T(2,128)S(1)} collective-permute-done((f32[2,4,1024]{2,0,1:T(2,128)S(1)}, f32[2,4,1024]{2,0,1:T(2,128)S(1)}, u32[]{:S(2)}, u32[]{:S(2)}) %collective-permute-start) | collective-permute-done | bytes 32800 | tf_op jit(solution)/shard_map/ppermute | solution.py:44
  12.9 2.1 %collective-permute-start.1 = (f32[2,4,1024]{2,0,1:T(2,128)S(1)}, f32[2,4,1024]{2,0,1:T(2,128)S(1)}, u32[]{:S(2)}, u32[]{:S(2)}) collective-permute-start(f32[2,4,1024]{2,0,1:T(2,128)S(1)} %copy_add_fusion), channel_id=1, source_target_pairs={{0,4},{2,6},{4,0},{6,2},{8,12},{10,14},{12,8},{14,10},{1,5},{3,7},... | collective-permute-start | bytes 98312 | tf_op jit(solution)/shard_map/ppermute | solution.py:44
  15.0 1.9 %collective-permute-done.1 = f32[2,4,1024]{2,0,1:T(2,128)S(1)} collective-permute-done((f32[2,4,1024]{2,0,1:T(2,128)S(1)}, f32[2,4,1024]{2,0,1:T(2,128)S(1)}, u32[]{:S(2)}, u32[]{:S(2)}) %collective-permute-start.1) | collective-permute-done | bytes 32800 | tf_op jit(solution)/shard_map/ppermute | solution.py:44
  16.9 3.1 %collective-permute-start.2 = (f32[2,4,1024]{2,0,1:T(2,128)S(1)}, f32[2,4,1024]{2,0,1:T(2,128)S(1)}, u32[]{:S(2)}, u32[]{:S(2)}) collective-permute-start(f32[2,4,1024]{2,0,1:T(2,128)S(1)} %add.110), channel_id=1, source_target_pairs={{0,8},{2,10},{4,12},{6,14},{8,0},{10,2},{12,4},{14,6},{1,9},{3,11}... | collective-permute-start | bytes 98312 | tf_op jit(solution)/shard_map/ppermute | solution.py:44
  20.0 1.9 %collective-permute-done.2 = f32[2,4,1024]{2,0,1:T(2,128)S(1)} collective-permute-done((f32[2,4,1024]{2,0,1:T(2,128)S(1)}, f32[2,4,1024]{2,0,1:T(2,128)S(1)}, u32[]{:S(2)}, u32[]{:S(2)}) %collective-permute-start.2) | collective-permute-done | bytes 32800 | tf_op jit(solution)/shard_map/ppermute | solution.py:44
  21.9 0.1 collective-permute-start.3
  22.0 0.0 copy-start
  22.0 1.2 %collective-permute-done.3 = f32[2,4,1024]{2,0,1:T(2,128)S(1)} collective-permute-done((f32[2,4,1024]{2,0,1:T(2,128)S(1)}, f32[2,4,1024]{2,0,1:T(2,128)S(1)}, u32[]{:S(2)}, u32[]{:S(2)}) %collective-permute-start.3) | collective-permute-done | bytes 32800 | tf_op jit(solution)/shard_map/ppermute | solution.py:59
  23.2 0.1 fusion.23
  23.4 0.2 fusion.20
  23.6 0.2 multiply_reduce_fusion.5
  23.8 0.2 multiply_reduce_fusion.2
  24.0 0.2 multiply_reduce_fusion.3
  24.3 0.2 multiply_reduce_fusion.1
  24.5 0.2 multiply_reduce_fusion
  24.7 0.1 subtract_divide_fusion
  24.9 0.0 copy-done.1
  24.9 4.5 %fusion = f32[2,4,512]{2,1,0:T(4,128)S(1)} fusion(f32[1,2,1024,512]{3,2,1,0:T(8,128)} %param.4, bf16[1,2,1024,512]{3,2,1,0:T(8,128)(2,1)S(1)} %copy-done.1, f32[2,4,1024]{2,0,1:T(2,128)S(1)} %fusion.7), kind=kOutput, calls=%fused_computation.1 | convolution fusion | flops 52428800 | bytes 6340608 | tf_op jit(solution)/shard_map/mrc,mkr->mkc/dot_general | solution.py:64
  29.4 0.2 collective-permute-start.4
  29.5 1.0 %collective-permute-done.4 = f32[2,4,512]{2,1,0:T(4,128)S(1)} collective-permute-done((f32[2,4,512]{2,1,0:T(4,128)S(1)}, f32[2,4,512]{2,1,0:T(4,128)S(1)}, u32[]{:S(2)}, u32[]{:S(2)}) %collective-permute-start.4) | collective-permute-done | bytes 16416 | tf_op jit(solution)/shard_map/ppermute | solution.py:44
  30.6 1.8 %collective-permute-start.5 = (f32[2,4,512]{2,1,0:T(4,128)S(1)}, f32[2,4,512]{2,1,0:T(4,128)S(1)}, u32[]{:S(2)}, u32[]{:S(2)}) collective-permute-start(f32[2,4,512]{2,1,0:T(4,128)S(1)} %add.117), channel_id=1, source_target_pairs={{0,2},{2,0},{4,6},{6,4},{8,10},{10,8},{12,14},{14,12},{1,3},{3,1},... | collective-permute-start | bytes 49160 | tf_op jit(solution)/shard_map/ppermute | solution.py:44
  32.4 1.9 %collective-permute-done.5 = f32[2,4,512]{2,1,0:T(4,128)S(1)} collective-permute-done((f32[2,4,512]{2,1,0:T(4,128)S(1)}, f32[2,4,512]{2,1,0:T(4,128)S(1)}, u32[]{:S(2)}, u32[]{:S(2)}) %collective-permute-start.5) | collective-permute-done | bytes 16416 | tf_op jit(solution)/shard_map/ppermute | solution.py:44
  34.3 1.9 %collective-permute-start.6 = (f32[2,4,512]{2,1,0:T(4,128)S(1)}, f32[2,4,512]{2,1,0:T(4,128)S(1)}, u32[]{:S(2)}, u32[]{:S(2)}) collective-permute-start(f32[2,4,512]{2,1,0:T(4,128)S(1)} %add.118), channel_id=1, source_target_pairs={{0,4},{2,6},{4,0},{6,2},{8,12},{10,14},{12,8},{14,10},{1,5},{3,7},... | collective-permute-start | bytes 49160 | tf_op jit(solution)/shard_map/ppermute | solution.py:44
  36.2 1.8 %collective-permute-done.6 = f32[2,4,512]{2,1,0:T(4,128)S(1)} collective-permute-done((f32[2,4,512]{2,1,0:T(4,128)S(1)}, f32[2,4,512]{2,1,0:T(4,128)S(1)}, u32[]{:S(2)}, u32[]{:S(2)}) %collective-permute-start.6) | collective-permute-done | bytes 16416 | tf_op jit(solution)/shard_map/ppermute | solution.py:44
  38.0 2.9 %collective-permute-start.7 = (f32[2,4,512]{2,1,0:T(4,128)S(1)}, f32[2,4,512]{2,1,0:T(4,128)S(1)}, u32[]{:S(2)}, u32[]{:S(2)}) collective-permute-start(f32[2,4,512]{2,1,0:T(4,128)S(1)} %add.119), channel_id=1, source_target_pairs={{0,8},{2,10},{4,12},{6,14},{8,0},{10,2},{12,4},{14,6},{1,9},{3,11}... | collective-permute-start | bytes 49160 | tf_op jit(solution)/shard_map/ppermute | solution.py:44
  41.0 1.7 %collective-permute-done.7 = f32[2,4,512]{2,1,0:T(4,128)S(1)} collective-permute-done((f32[2,4,512]{2,1,0:T(4,128)S(1)}, f32[2,4,512]{2,1,0:T(4,128)S(1)}, u32[]{:S(2)}, u32[]{:S(2)}) %collective-permute-start.7) | collective-permute-done | bytes 16416 | tf_op jit(solution)/shard_map/ppermute | solution.py:44
  42.7 5.7 %fusion.4 = (f32[1,2,1024,512]{3,2,1,0:T(8,128)}, bf16[2,1024,512]{2,1,0:T(8,128)(2,1)}) fusion(f32[1,2,1024,512]{3,2,1,0:T(8,128)S(1)} %copy-done, bf16[1,2,1024,512]{3,2,1,0:T(8,128)(2,1)S(1)} %copy-done.1, f32[2,4,512]{2,1,0:T(4,128)S(1)} %add.119, f32[2,4,512]{2,1,0:T(4,128)S(1)} %collective-permute-done.7, f32[2,4,1024]{2,0,1:T(2,128)S(1)} %fusion.7), kind=kOutput, calls=%fused_computation.5 | convolution fusion | flops 54534144 | bytes 12648448 | tf_op jit(solution)/shard_map/mkr,mkc->mrc/dot_general | solution.py:66
  (15 shorter events, 0.2 us)
Async XLA Ops:
  0.6 24.2 %copy-start.1 = (bf16[1,2,1024,512]{3,2,1,0:T(8,128)(2,1)S(1)}, bf16[1,2,1024,512]{3,2,1,0:T(8,128)(2,1)}, u32[]{:S(2)}) copy-start(bf16[1,2,1024,512]{3,2,1,0:T(8,128)(2,1)} %param.3) | copy-start | bytes 6291460
  7.9 4.9 %collective-permute-start = (f32[2,4,1024]{2,0,1:T(2,128)S(1)}, f32[2,4,1024]{2,0,1:T(2,128)S(1)}, u32[]{:S(2)}, u32[]{:S(2)}) collective-permute-start(f32[2,4,1024]{2,0,1:T(2,128)S(1)} %copy.10), channel_id=1, source_target_pairs={{0,2},{2,0},{4,6},{6,4},{8,10},{10,8},{12,14},{14,12},{1,3},{3,1},... | collective-permute-start | bytes 98312 | tf_op jit(solution)/shard_map/ppermute | solution.py:44
  12.9 4.0 %collective-permute-start.1 = (f32[2,4,1024]{2,0,1:T(2,128)S(1)}, f32[2,4,1024]{2,0,1:T(2,128)S(1)}, u32[]{:S(2)}, u32[]{:S(2)}) collective-permute-start(f32[2,4,1024]{2,0,1:T(2,128)S(1)} %copy_add_fusion), channel_id=1, source_target_pairs={{0,4},{2,6},{4,0},{6,2},{8,12},{10,14},{12,8},{14,10},{1,5},{3,7},... | collective-permute-start | bytes 98312 | tf_op jit(solution)/shard_map/ppermute | solution.py:44
  16.9 5.0 %collective-permute-start.2 = (f32[2,4,1024]{2,0,1:T(2,128)S(1)}, f32[2,4,1024]{2,0,1:T(2,128)S(1)}, u32[]{:S(2)}, u32[]{:S(2)}) collective-permute-start(f32[2,4,1024]{2,0,1:T(2,128)S(1)} %add.110), channel_id=1, source_target_pairs={{0,8},{2,10},{4,12},{6,14},{8,0},{10,2},{12,4},{14,6},{1,9},{3,11}... | collective-permute-start | bytes 98312 | tf_op jit(solution)/shard_map/ppermute | solution.py:44
  21.9 1.3 %collective-permute-start.3 = (f32[2,4,1024]{2,0,1:T(2,128)S(1)}, f32[2,4,1024]{2,0,1:T(2,128)S(1)}, u32[]{:S(2)}, u32[]{:S(2)}) collective-permute-start(f32[2,4,1024]{2,0,1:T(2,128)S(1)} %add_multiply_fusion), channel_id=1, source_target_pairs={{0,1},{1,0},{2,3},{3,2},{4,5},{5,4},{6,7},{7,6},{8,9},{9,8},{10,11... | collective-permute-start | bytes 98312 | tf_op jit(solution)/shard_map/ppermute | solution.py:59
  22.0 20.7 %copy-start = (f32[1,2,1024,512]{3,2,1,0:T(8,128)S(1)}, f32[1,2,1024,512]{3,2,1,0:T(8,128)}, u32[]{:S(2)}) copy-start(f32[1,2,1024,512]{3,2,1,0:T(8,128)} %param.4) | copy-start | bytes 12582916
  29.4 1.2 %collective-permute-start.4 = (f32[2,4,512]{2,1,0:T(4,128)S(1)}, f32[2,4,512]{2,1,0:T(4,128)S(1)}, u32[]{:S(2)}, u32[]{:S(2)}) collective-permute-start(f32[2,4,512]{2,1,0:T(4,128)S(1)} %fusion), channel_id=1, source_target_pairs={{0,1},{1,0},{2,3},{3,2},{4,5},{5,4},{6,7},{7,6},{8,9},{9,8},{10,11... | collective-permute-start | bytes 49160 | tf_op jit(solution)/shard_map/ppermute | solution.py:44
  30.6 3.7 %collective-permute-start.5 = (f32[2,4,512]{2,1,0:T(4,128)S(1)}, f32[2,4,512]{2,1,0:T(4,128)S(1)}, u32[]{:S(2)}, u32[]{:S(2)}) collective-permute-start(f32[2,4,512]{2,1,0:T(4,128)S(1)} %add.117), channel_id=1, source_target_pairs={{0,2},{2,0},{4,6},{6,4},{8,10},{10,8},{12,14},{14,12},{1,3},{3,1},... | collective-permute-start | bytes 49160 | tf_op jit(solution)/shard_map/ppermute | solution.py:44
  34.3 3.7 %collective-permute-start.6 = (f32[2,4,512]{2,1,0:T(4,128)S(1)}, f32[2,4,512]{2,1,0:T(4,128)S(1)}, u32[]{:S(2)}, u32[]{:S(2)}) collective-permute-start(f32[2,4,512]{2,1,0:T(4,128)S(1)} %add.118), channel_id=1, source_target_pairs={{0,4},{2,6},{4,0},{6,2},{8,12},{10,14},{12,8},{14,10},{1,5},{3,7},... | collective-permute-start | bytes 49160 | tf_op jit(solution)/shard_map/ppermute | solution.py:44
  38.0 4.7 %collective-permute-start.7 = (f32[2,4,512]{2,1,0:T(4,128)S(1)}, f32[2,4,512]{2,1,0:T(4,128)S(1)}, u32[]{:S(2)}, u32[]{:S(2)}) collective-permute-start(f32[2,4,512]{2,1,0:T(4,128)S(1)} %add.119), channel_id=1, source_target_pairs={{0,8},{2,10},{4,12},{6,14},{8,0},{10,2},{12,4},{14,6},{1,9},{3,11}... | collective-permute-start | bytes 49160 | tf_op jit(solution)/shard_map/ppermute | solution.py:44

commit v2 on v1

--- a/solution.py
+++ b/solution.py
@@ -36,16 +36,6 @@
     return jnp.stack(columns, axis=1)
 
 
-def swap_sum(value, axis):
-    count = lax.axis_size(axis)
-    step = 1
-    while step < count:
-        pairs = [(index, index ^ step) for index in range(count)]
-        value = value + lax.ppermute(value, axis, pairs)
-        step *= 2
-    return value
-
-
 def body(grads, errors, seeds):
     merged = grads[0].astype(jnp.float32) + errors[0]
     replicas = lax.axis_size("dp")
@@ -55,14 +45,15 @@
     partial_value = jnp.einsum(
         "mrc,mkc->mkr", merged, start_factor, precision=lax.Precision.HIGHEST
     )
-    summed = swap_sum(partial_value, "dp") / replicas
-    other = lax.ppermute(summed, "tensor", [(0, 1), (1, 0)])
-    first = jnp.where(half == 0, summed, other)
-    second = jnp.where(half == 0, other, summed)
-    whole = orthogonal(jnp.concatenate([first, second], axis=-1))
+    mats, ranks = partial_value.shape[:2]
+    pieces = partial_value.reshape(mats, ranks, replicas, rows // replicas)
+    pieces = lax.all_to_all(pieces.transpose(2, 0, 1, 3), "dp", 0, 0)
+    summed = jnp.sum(pieces, axis=0) / replicas
+    parts = lax.all_gather(summed, ("tensor", "dp"))
+    whole = orthogonal(parts.transpose(1, 2, 0, 3).reshape(mats, ranks, 2 * rows))
     left_factor = lax.dynamic_slice_in_dim(whole, half * rows, rows, axis=2)
     right_part = jnp.einsum("mrc,mkr->mkc", merged, left_factor, precision=lax.Precision.HIGHEST)
-    right_factor = swap_sum(swap_sum(right_part, "tensor"), "dp") / replicas
+    right_factor = jnp.sum(lax.all_gather(right_part, ("dp", "tensor")), axis=0) / replicas
     approx = jnp.einsum("mkr,mkc->mrc", left_factor, right_factor, precision=lax.Precision.HIGHEST)
     return (approx.astype(jnp.bfloat16), (merged - approx)[None])
 

time: 48.6 us -> 84.9 us (1.75)
  blocking collectives: 0 us -> 48.8 us
  starting transfers between devices: 15.2 us -> 7.28 us
  waiting for transfers between devices: 13.3 us -> 6.69 us
  matrix products: 16.5 us -> 18 us
    all_gather x0 -> x2, blocking collectives: none -> 48.8 us  [the longest x1 29.2 us: body(): parts = lax.all_gather(summed, ('tensor', 'dp'))]
    ppermute x8 -> x0, starting transfers between devices: 15.2 us -> none  [the longest x7 15.1 us: swap_sum(): value = value + lax.ppermute(value, axis, pairs)]
    ppermute x8 -> x0, waiting for transfers between devices: 13.3 us -> none  [the longest x7 12.1 us: swap_sum(): value = value + lax.ppermute(value, axis, pairs)]
    all_to_all x0 -> x1, starting transfers between devices: none -> 7.28 us  [body(): pieces = lax.all_to_all(pieces.transpose(2, 0, 1, 3), 'dp', 0, 0)]
    all_to_all x0 -> x1, waiting for transfers between devices: none -> 6.69 us  [body(): pieces = lax.all_to_all(pieces.transpose(2, 0, 1, 3), 'dp', 0, 0)]
    dot_general x1, matrix products: 5.73 us -> 7.2 us  [body(): jnp.einsum('mkr,mkc->mrc', left_factor, right_factor, precision=lax.Preci...]
  transfers between devices with their start and end apart: 8 -> 1, of which waited for: 8 -> 1; matrix products, arithmetic and copies ran while one was open for 0% -> 0% of each run, Pallas kernels for 0% -> 0%
where the time goes in v2:
time: 84.9 us; the launch traced here: 84.7 us
  blocking collectives  48.8 us (57%)
  matrix products  18 us (21%)
  starting transfers between devices  7.28 us (9%)
  waiting for transfers between devices  6.69 us (8%)
  other arithmetic  2.57 us (3%)
    all_gather x1, blocking collectives, body(): parts = lax.all_gather(summed, ('tensor', 'dp'))  29.2 us
    all_gather x1, blocking collectives, body(): lax.all_gather(right_part, ('dp', 'tensor'))  19.6 us
    all_to_all x1, starting transfers between devices, body(): pieces = lax.all_to_all(pieces.transpose(2, 0, 1, 3), 'dp', 0, 0)  7.28 us
    dot_general x1, matrix products, body(): jnp.einsum('mkr,mkc->mrc', left_factor, right_factor, precision=lax.Preci...  7.2 us
    all_to_all x1, waiting for transfers between devices, body(): pieces = lax.all_to_all(pieces.transpose(2, 0, 1, 3), 'dp', 0, 0)  6.69 us
    dot_general x1, matrix products, body(): jnp.einsum('mrc,mkc->mkr', merged, start_factor, precision=lax.Precision....  6.32 us
    dot_general x1, matrix products, body(): jnp.einsum('mrc,mkr->mkc', merged, left_factor, precision=lax.Precision.H...  4.5 us
  transfers between devices with their start and end apart: 1, of which 1 were waited for; matrix products, arithmetic and copies ran while one was open for 0% of the time, Pallas kernels for 0%

profile of v2, /device:TPU:0, one launch (start us, length us, event | category | flops | bytes accessed | tf_op | source)
XLA Modules:
  0.0 84.7 jit_solution(7215195582386718204)
XLA Ops:
  0.6 0.0 copy-start
  0.7 0.8 broadcast_multiply_fusion.1
  1.5 0.1 add_multiply_fusion
  1.5 6.3 %fusion.5 = f32[2,1,8,4,128]{4,3,2,1,0:T(4,128)S(1)} fusion(f32[1,2,1024,512]{3,2,1,0:T(8,128)} %param.4, bf16[1,2,1024,512]{3,2,1,0:T(8,128)(2,1)} %param.3, s32[2]{0:T(128)S(1)} %broadcast_multiply_fusion.1, s32[4,512]{1,0:T(4,128)S(1)} %add_multiply_fusion), kind=kOutput, calls=%fused_computation.7 | convolution fusion | flops 52473856 | bytes 6332424 | tf_op jit(solution)/shard_map/mrc,mkc->mkr/dot_general | solution.py:45
  7.8 0.6 copy.37
  8.5 7.3 %all-to-all-start = ((f32[8,2,4,128]{3,2,1,0:T(4,128)}), f32[8,2,4,128]{3,2,1,0:T(4,128)S(1)}, u32[]{:S(2)}, u32[]{:S(2)}) async-start(f32[8,2,4,128]{3,2,1,0:T(4,128)} %bitcast.49), calls=%async_computation | async-start | bytes 65536 | tf_op jit(solution)/shard_map/all_to_all | solution.py:50
  15.8 6.7 %all-to-all-done = f32[8,2,4,128]{3,2,1,0:T(4,128)S(1)} async-done(((f32[8,2,4,128]{3,2,1,0:T(4,128)}), f32[8,2,4,128]{3,2,1,0:T(4,128)S(1)}, u32[]{:S(2)}, u32[]{:S(2)}) %all-to-all-start) | async-done | bytes 32800 | tf_op jit(solution)/shard_map/all_to_all | solution.py:50
  22.5 29.2 %all-gather = f32[32,4,128]{2,1,0:T(4,128)S(1)} all-gather(f32[2,4,128]{2,1,0:T(4,128)S(1)} %broadcast_multiply_fusion), channel_id=2, replica_groups=mesh['groups'=2,'dp'=8,'tensor'=2] {'tensor','dp'}, dimensions={0}, use_global_device_ids=true | all-gather | bytes 69632 | tf_op jit(solution)/shard_map/all_gather | solution.py:52
  51.7 0.1 fusion.23
  51.8 0.2 fusion.20
  52.1 0.2 multiply_reduce_fusion.5
  52.3 0.2 multiply_reduce_fusion.2
  52.5 0.2 multiply_reduce_fusion.3
  52.7 0.2 multiply_reduce_fusion.1
  52.9 0.2 multiply_reduce_fusion
  53.1 0.1 subtract_divide_fusion
  53.3 0.0 copy-done
  53.3 4.5 %fusion = f32[2,4,512]{2,1,0:T(4,128)S(1)} fusion(f32[1,2,1024,512]{3,2,1,0:T(8,128)} %param.4, bf16[1,2,1024,512]{3,2,1,0:T(8,128)(2,1)S(1)} %copy-done, f32[2,4,1024]{2,0,1:T(2,128)S(1)} %fusion.10), kind=kOutput, calls=%fused_computation.1 | convolution fusion | flops 52428800 | bytes 6340608 | tf_op jit(solution)/shard_map/mrc,mkr->mkc/dot_general | solution.py:55
  57.8 19.6 %all-gather.1 = f32[32,4,512]{2,1,0:T(4,128)S(1)} all-gather(f32[2,4,512]{2,1,0:T(4,128)S(1)} %fusion), channel_id=3, replica_groups=mesh['groups'=2,'dp'=8,'tensor'=2] {'dp','tensor'}, dimensions={0}, use_global_device_ids=true | all-gather | bytes 278528 | tf_op jit(solution)/shard_map/all_gather | solution.py:56
  77.4 0.1 reduce_sum.119
  77.5 7.2 %fusion.4 = (f32[1,2,1024,512]{3,2,1,0:T(8,128)}, bf16[2,1024,512]{2,1,0:T(8,128)(2,1)}) fusion(f32[1,2,1024,512]{3,2,1,0:T(8,128)} %param.4, bf16[1,2,1024,512]{3,2,1,0:T(8,128)(2,1)S(1)} %copy-done, f32[2,4,512]{2,1,0:T(4,128)S(1)} %reduce_sum.119, f32[2,4,1024]{2,0,1:T(2,128)S(1)} %fusion.10), kind=kOutput, calls=%fused_computation.5 | convolution fusion | flops 54530048 | bytes 12632064 | tf_op jit(solution)/shard_map/mkr,mkc->mrc/dot_general | solution.py:57
  (9 shorter events, 0.1 us)
Async XLA Ops:
  0.6 52.7 %copy-start = (bf16[1,2,1024,512]{3,2,1,0:T(8,128)(2,1)S(1)}, bf16[1,2,1024,512]{3,2,1,0:T(8,128)(2,1)}, u32[]{:S(2)}) copy-start(bf16[1,2,1024,512]{3,2,1,0:T(8,128)(2,1)} %param.3) | copy-start | bytes 6291460
  8.5 14.0 %all-to-all-start = ((f32[8,2,4,128]{3,2,1,0:T(4,128)}), f32[8,2,4,128]{3,2,1,0:T(4,128)S(1)}, u32[]{:S(2)}, u32[]{:S(2)}) async-start(f32[8,2,4,128]{3,2,1,0:T(4,128)} %bitcast.49), calls=%async_computation | async-start | bytes 65536 | tf_op jit(solution)/shard_map/all_to_all | solution.py:50

commit v3 on v1

v3 whole, which is shorter than its diff:
```python
import functools

import jax
import jax.numpy as jnp
from jax import lax
from jax.experimental import pallas as pl
from jax.experimental.pallas import tpu as pltpu
from jax.sharding import PartitionSpec as P

RANK = 4
EPSILON = 1e-08
CHUNKS = 4
BF16 = jnp.bfloat16
F32 = jnp.float32


def halves(value):
    high = value.astype(BF16).astype(F32)
    return high, value - high


def start_rows(seeds_ref, mats, cols):
    shape = (mats * RANK, cols)
    row = lax.broadcasted_iota(jnp.int32, shape, 0)
    col = lax.broadcasted_iota(jnp.int32, shape, 1)
    mat = row // RANK
    seed = jnp.full(shape, seeds_ref[0], jnp.int32)
    for index in range(1, mats):
        seed = jnp.where(mat == index, seeds_ref[index], seed)
    mixed = ((row - mat * RANK) * cols + col) * 747796405 + seed * 277803737 + 12345
    mixed = mixed ^ (mixed >> 15)
    mixed = mixed * 1274126177
    mixed = mixed ^ (mixed >> 13)
    lowbits = jnp.bitwise_and(mixed, 65535)
    return (lowbits.astype(F32) - 32767.5) / 32768.0


def fold(mat, value, product):
    part = product[: value.shape[0]] + product[value.shape[0] :]
    row = lax.broadcasted_iota(jnp.int32, value.shape, 0)
    return jnp.where(row // RANK == mat, part, value)


def project_body(seeds_ref, grads_ref, errors_ref, left_ref, merged_ref, high_ref, low_ref, seed, gbuf, ebuf, seed_sem, sems):
    _, mats, rows, cols = grads_ref.shape
    size = rows // CHUNKS
    seed_copy = pltpu.make_async_copy(seeds_ref, seed, seed_sem)
    seed_copy.start()
    copies = []
    for mat in range(mats):
        for chunk in range(CHUNKS):
            at = pl.ds(chunk * size, size)
            slot = mat * CHUNKS + chunk
            pair = (
                pltpu.make_async_copy(grads_ref.at[0, mat, at], gbuf.at[mat, at], sems.at[0, slot]),
                pltpu.make_async_copy(errors_ref.at[0, mat, at], ebuf.at[mat, at], sems.at[1, slot]),
            )
            for copy in pair:
                copy.start()
            copies.append(pair)
    seed_copy.wait()
    start = start_rows(seed, mats, cols)
    weights = jnp.concatenate(halves(start), axis=0).astype(BF16)
    dims = (((1,), (1,)), ((), ()))
    for chunk in range(CHUNKS):
        at = pl.ds(chunk * size, size)
        left = jnp.zeros((mats * RANK, size), F32)
        for mat in range(mats):
            for copy in copies[mat * CHUNKS + chunk]:
                copy.wait()
            value = gbuf[mat, at].astype(F32) + ebuf[mat, at]
            high = value.astype(BF16)
            low = (value - high.astype(F32)).astype(BF16)
            merged_ref[mat, at] = value
            high_ref[mat, at] = high
            low_ref[mat, at] = low
            product = lax.dot_general(weights, high, dims, preferred_element_type=F32)
            product = product + lax.dot_general(weights, low, dims, preferred_element_type=F32)
            left = fold(mat, left, product)
        left_ref[:, at] = left


def project(seeds, grads, errors):
    _, mats, rows, cols = grads.shape
    return pl.pallas_call(
        project_body,
        out_shape=(
            jax.ShapeDtypeStruct((mats * RANK, rows), F32),
            pltpu.VMEM((mats, rows, cols), F32),
            pltpu.VMEM((mats, rows, cols), BF16),
            pltpu.VMEM((mats, rows, cols), BF16),
        ),
        in_specs=[pl.BlockSpec(memory_space=pltpu.HBM)] * 3,
        out_specs=[pl.BlockSpec(memory_space=pltpu.VMEM)] * 4,
        scratch_shapes=[
            pltpu.SMEM(seeds.shape, seeds.dtype),
            pltpu.VMEM((mats, rows, cols), BF16),
            pltpu.VMEM((mats, rows, cols), F32),
            pltpu.SemaphoreType.DMA,
            pltpu.SemaphoreType.DMA((2, mats * CHUNKS)),
        ],
        compiler_params=pltpu.CompilerParams(vmem_limit_bytes=24 * 2**20),
        name="project",
    )(*[pltpu.with_memory_space_constraint(value, pltpu.HBM) for value in (seeds, grads, errors)])


def spread(column, count):
    picked = jnp.concatenate(
        [jnp.broadcast_to(column[row : row + 1], (RANK, column.shape[1])) for row in range(0, count, RANK)],
        axis=0,
    )
    return picked


def orthogonal(mine, other):
    count = mine.shape[0]
    lane = lax.broadcasted_iota(jnp.int32, (count, 1), 0) % RANK
    for index in range(RANK):
        current = spread(mine[index : count - RANK + index + 1], count - RANK + 1)
        partner = spread(other[index : count - RANK + index + 1], count - RANK + 1)
        products = jnp.sum(mine * current, axis=1, keepdims=True) + jnp.sum(
            other * partner, axis=1, keepdims=True
        )
        square = spread(products[index : count - RANK + index + 1], count - RANK + 1)
        length = jnp.sqrt(square) + EPSILON
        current = current / length
        partner = partner / length
        inner = products / length
        mine = jnp.where(lane == index, current, jnp.where(lane > index, mine - inner * current, mine))
        other = jnp.where(lane == index, partner, jnp.where(lane > index, other - inner * partner, other))
    return mine


def reflect_body(mine_ref, other_ref, high_ref, low_ref, left_ref, right_ref):
    mats, rows, cols = high_ref.shape
    left = orthogonal(mine_ref[...], other_ref[...])
    left_ref[...] = left
    weights = jnp.concatenate(halves(left), axis=0).astype(BF16)
    right = jnp.zeros((mats * RANK, cols), F32)
    for mat in range(mats):
        product = jnp.dot(weights, high_ref[mat], preferred_element_type=F32)
        product = product + jnp.dot(weights, low_ref[mat], preferred_element_type=F32)
        right = fold(mat, right, product)
    right_ref[...] = right


def reflect(mine, other, high, low):
    mats, rows, cols = high.shape
    return pl.pallas_call(
        reflect_body,
        out_shape=(
            jax.ShapeDtypeStruct((mats * RANK, rows), F32),
            jax.ShapeDtypeStruct((mats * RANK, cols), F32),
        ),
        in_specs=[pl.BlockSpec(memory_space=pltpu.VMEM)] * 4,
        out_specs=[pl.BlockSpec(memory_space=pltpu.VMEM)] * 2,
        compiler_params=pltpu.CompilerParams(vmem_limit_bytes=24 * 2**20),
        name="reflect",
    )(mine, other, pltpu.with_memory_space_constraint(high, pltpu.VMEM), pltpu.with_memory_space_constraint(low, pltpu.VMEM))


def finish_body(scale, left_ref, right_ref, merged_ref, update_ref, errors_ref, ubuf, ebuf, sems):
    mats, rows, cols = merged_ref.shape
    size = rows // CHUNKS
    left_high, left_low = halves(left_ref[...])
    right_high, right_low = halves(right_ref[...] * scale)
    left = jnp.concatenate([left_high, left_low, left_high, left_low], axis=0).T.astype(BF16)
    right = jnp.concatenate([right_high, right_high, right_low, right_low], axis=0)
    row = lax.broadcasted_iota(jnp.int32, right.shape, 0) % (mats * RANK)
    copies = []
    for mat in range(mats):
        weights = jnp.where(row // RANK == mat, right, 0.0).astype(BF16)
        for chunk in range(CHUNKS):
            at = pl.ds(chunk * size, size)
            slot = mat * CHUNKS + chunk
            approx = jnp.dot(left[chunk * size : (chunk + 1) * size], weights, preferred_element_type=F32)
            ubuf[mat, at] = approx.astype(BF16)
            ebuf[mat, at] = merged_ref[mat, at] - approx
            for copy in (
                pltpu.make_async_copy(ubuf.at[mat, at], update_ref.at[mat, at], sems.at[0, slot]),
                pltpu.make_async_copy(ebuf.at[mat, at], errors_ref.at[0, mat, at], sems.at[1, slot]),
            ):
                copy.start()
                copies.append(copy)
    for copy in copies:
        copy.wait()


def finish(left, right, merged, scale):
    mats, rows, cols = merged.shape
    return pl.pallas_call(
        functools.partial(finish_body, scale),
        out_shape=(
            jax.ShapeDtypeStruct((mats, rows, cols), BF16),
            jax.ShapeDtypeStruct((1, mats, rows, cols), F32),
        ),
        in_specs=[pl.BlockSpec(memory_space=pltpu.VMEM)] * 3,
        out_specs=[pl.BlockSpec(memory_space=pltpu.HBM)] * 2,
        scratch_shapes=[
            pltpu.VMEM((mats, rows, cols), BF16),
            pltpu.VMEM((mats, rows, cols), F32),
            pltpu.SemaphoreType.DMA((2, mats * CHUNKS)),
        ],
        compiler_params=pltpu.CompilerParams(vmem_limit_bytes=24 * 2**20),
        name="finish",
    )(left, right, pltpu.with_memory_space_constraint(merged, pltpu.VMEM))


def swap_sum(value, axis):
    count = lax.axis_size(axis)
    step = 1
    while step < count:
        pairs = [(index, index ^ step) for index in range(count)]
        value = value + lax.ppermute(value, axis, pairs)
        step *= 2
    return value


def body(grads, errors, seeds):
    replicas = lax.axis_size("dp")
    left_part, merged, high, low = project(seeds, grads, errors)
    mine = swap_sum(left_part, "dp") / replicas
    other = lax.ppermute(mine, "tensor", [(0, 1), (1, 0)])
    left, right_part = reflect(mine, other, high, low)
    right = swap_sum(swap_sum(right_part, "tensor"), "dp")
    return finish(left, right, merged, 1.0 / replicas)


def solution(mesh):
    in_specs = (
        P(("groups", "dp"), None, "tensor", None),
        P(("groups", "dp"), None, "tensor", None),
        P(),
    )
    out_specs = (P("groups", "tensor", None), P(("groups", "dp"), None, "tensor", None))
    return jax.shard_map(body, mesh=mesh, in_specs=in_specs, out_specs=out_specs, check_vma=False)
```

time: 48.6 us -> 38.7 us (0.80)
  matrix products: 16.5 us -> 0 us
  Pallas kernels: 0 us -> 9.48 us
  other arithmetic: 2.59 us -> 0.03 us
    dot_general x3 -> x0, matrix products: 16.5 us -> none  [the longest x1 6.32 us: body(): jnp.einsum('mrc,mkc->mkr', merged, start_factor, precision=lax.Precision....]
    pallas_call x0 -> x3, Pallas kernels: none -> 9.48 us  [the longest x1 5.04 us: project(): pl.pallas_call(project_body, out_shape=(jax.ShapeDtypeStruct((mats * RANK...]
    reduce_sum x7 -> x0, other arithmetic: 1.43 us -> none  [the longest x4 0.75 us: orthogonal(): jnp.sum(current * current, axis=-1, keepdims=True)]
    mul x3 -> x0, other arithmetic: 0.88 us -> none  [the longest x1 0.81 us: initial_factor(): seeds[:, None, None] * 277803737]
where the time goes in v3:
time: 38.7 us; the launch traced here: 38.5 us
  starting transfers between devices  15 us (39%)
  waiting for transfers between devices  13.3 us (34%)
  Pallas kernels  9.48 us (24%)
  between operations  0.66 us (2%)
    ppermute x7, starting transfers between devices, swap_sum(): value = value + lax.ppermute(value, axis, pairs)  15 us
    ppermute x7, waiting for transfers between devices, swap_sum(): value = value + lax.ppermute(value, axis, pairs)  12.1 us
    pallas_call x1, Pallas kernels, project(): pl.pallas_call(project_body, out_shape=(jax.ShapeDtypeStruct((mats * RANK...  5.04 us
    pallas_call x1, Pallas kernels, finish(): pl.pallas_call(functools.partial(finish_body, scale), out_shape=(jax.Shap...  3.07 us
    pallas_call x1, Pallas kernels, reflect(): pl.pallas_call(reflect_body, out_shape=(jax.ShapeDtypeStruct((mats * RANK...  1.37 us
    ppermute x1, waiting for transfers between devices, body(): other = lax.ppermute(mine, 'tensor', [(0, 1), (1, 0)])  1.2 us
  transfers between devices with their start and end apart: 8, of which 8 were waited for; matrix products, arithmetic and copies ran while one was open for 0% of the time, Pallas kernels for 0%

profile of v3, /device:TPU:0, one launch (start us, length us, event | category | flops | bytes accessed | tf_op | source)
XLA Modules:
  0.0 38.5 jit_solution(13643240027094274547)
XLA Ops:
  0.6 5.0 %project.1 = (f32[8,1024]{1,0:T(8,128)S(1)}, f32[2,1024,512]{2,1,0:T(8,128)S(1)}, bf16[2,1024,512]{2,1,0:T(8,128)(2,1)S(1)}, bf16[2,1024,512]{2,1,0:T(8,128)(2,1)S(1)}) custom-call(s32[2]{0:T(128)} %seeds_ref.1, bf16[1,2,1024,512]{3,2,1,0:T(8,128)(2,1)} %grads_ref.1, f32[1,2,1024,512]{3,2,1,0:T(8,128)} %errors_ref.1), custom_call_target="tpu_custom_call" | custom-call | tf_op jit(solution)/shard_map/project/pallas_call | solution.py:85
  5.7 3.0 %collective-permute-start = (f32[8,1024]{1,0:T(8,128)S(1)}, f32[8,1024]{1,0:T(8,128)S(1)}, u32[]{:S(2)}, u32[]{:S(2)}) collective-permute-start(f32[8,1024]{1,0:T(8,128)S(1)} %get-tuple-element.8), channel_id=1, source_target_pairs={{0,2},{2,0},{4,6},{6,4},{8,10},{10,8},{12,14},{14,12},{1,3},{3,1},... | collective-permute-start | bytes 98312 | tf_op jit(solution)/shard_map/ppermute | solution.py:214
  8.7 1.9 %collective-permute-done = f32[8,1024]{1,0:T(8,128)S(1)} collective-permute-done((f32[8,1024]{1,0:T(8,128)S(1)}, f32[8,1024]{1,0:T(8,128)S(1)}, u32[]{:S(2)}, u32[]{:S(2)}) %collective-permute-start) | collective-permute-done | bytes 32800 | tf_op jit(solution)/shard_map/ppermute | solution.py:214
  10.6 2.1 %collective-permute-start.1 = (f32[8,1024]{1,0:T(8,128)S(1)}, f32[8,1024]{1,0:T(8,128)S(1)}, u32[]{:S(2)}, u32[]{:S(2)}) collective-permute-start(f32[8,1024]{1,0:T(8,128)S(1)} %add.21), channel_id=1, source_target_pairs={{0,4},{2,6},{4,0},{6,2},{8,12},{10,14},{12,8},{14,10},{1,5},{3,7},... | collective-permute-start | bytes 98312 | tf_op jit(solution)/shard_map/ppermute | solution.py:214
  12.7 1.9 %collective-permute-done.1 = f32[8,1024]{1,0:T(8,128)S(1)} collective-permute-done((f32[8,1024]{1,0:T(8,128)S(1)}, f32[8,1024]{1,0:T(8,128)S(1)}, u32[]{:S(2)}, u32[]{:S(2)}) %collective-permute-start.1) | collective-permute-done | bytes 32800 | tf_op jit(solution)/shard_map/ppermute | solution.py:214
  14.6 3.0 %collective-permute-start.2 = (f32[8,1024]{1,0:T(8,128)S(1)}, f32[8,1024]{1,0:T(8,128)S(1)}, u32[]{:S(2)}, u32[]{:S(2)}) collective-permute-start(f32[8,1024]{1,0:T(8,128)S(1)} %add.22), channel_id=1, source_target_pairs={{0,8},{2,10},{4,12},{6,14},{8,0},{10,2},{12,4},{14,6},{1,9},{3,11}... | collective-permute-start | bytes 98312 | tf_op jit(solution)/shard_map/ppermute | solution.py:214
  17.6 1.9 %collective-permute-done.2 = f32[8,1024]{1,0:T(8,128)S(1)} collective-permute-done((f32[8,1024]{1,0:T(8,128)S(1)}, f32[8,1024]{1,0:T(8,128)S(1)}, u32[]{:S(2)}, u32[]{:S(2)}) %collective-permute-start.2) | collective-permute-done | bytes 32800 | tf_op jit(solution)/shard_map/ppermute | solution.py:214
  19.5 0.0 collective-permute-start.3
  19.5 1.2 %collective-permute-done.3.other_ref = f32[8,1024]{1,0:T(8,128)S(1)} collective-permute-done((f32[8,1024]{1,0:T(8,128)S(1)}, f32[8,1024]{1,0:T(8,128)S(1)}, u32[]{:S(2)}, u32[]{:S(2)}) %collective-permute-start.3) | collective-permute-done | bytes 32800 | tf_op jit(solution)/shard_map/ppermute | solution.py:223
  20.7 1.4 %reflect.1 = (f32[8,1024]{1,0:T(8,128)S(1)}, f32[8,512]{1,0:T(8,128)S(1)}) custom-call(f32[8,1024]{1,0:T(8,128)S(1)} %add_multiply_fusion.mine_ref, f32[8,1024]{1,0:T(8,128)S(1)} %collective-permute-done.3.other_ref, bf16[2,1024,512]{2,1,0:T(8,128)(2,1)S(1)} %get-tuple-element.9.high_ref, bf16[2,1024,512]{2,1,0:T(8,128)(2,1)S(1)} %get-tuple-element.10.low_ref), custom_call_target="tpu_custom_call" | custom-call | tf_op jit(solution)/shard_map/reflect/pallas_call | solution.py:149
  22.1 0.2 collective-permute-start.4
  22.3 1.0 %collective-permute-done.4 = f32[8,512]{1,0:T(8,128)S(1)} collective-permute-done((f32[8,512]{1,0:T(8,128)S(1)}, f32[8,512]{1,0:T(8,128)S(1)}, u32[]{:S(2)}, u32[]{:S(2)}) %collective-permute-start.4) | collective-permute-done | bytes 16416 | tf_op jit(solution)/shard_map/ppermute | solution.py:214
  23.3 1.9 %collective-permute-start.5 = (f32[8,512]{1,0:T(8,128)S(1)}, f32[8,512]{1,0:T(8,128)S(1)}, u32[]{:S(2)}, u32[]{:S(2)}) collective-permute-start(f32[8,512]{1,0:T(8,128)S(1)} %add.24), channel_id=1, source_target_pairs={{0,2},{2,0},{4,6},{6,4},{8,10},{10,8},{12,14},{14,12},{1,3},{3,1},... | collective-permute-start | bytes 49160 | tf_op jit(solution)/shard_map/ppermute | solution.py:214
  25.1 1.9 %collective-permute-done.5 = f32[8,512]{1,0:T(8,128)S(1)} collective-permute-done((f32[8,512]{1,0:T(8,128)S(1)}, f32[8,512]{1,0:T(8,128)S(1)}, u32[]{:S(2)}, u32[]{:S(2)}) %collective-permute-start.5) | collective-permute-done | bytes 16416 | tf_op jit(solution)/shard_map/ppermute | solution.py:214
  27.0 1.9 %collective-permute-start.6 = (f32[8,512]{1,0:T(8,128)S(1)}, f32[8,512]{1,0:T(8,128)S(1)}, u32[]{:S(2)}, u32[]{:S(2)}) collective-permute-start(f32[8,512]{1,0:T(8,128)S(1)} %add.25), channel_id=1, source_target_pairs={{0,4},{2,6},{4,0},{6,2},{8,12},{10,14},{12,8},{14,10},{1,5},{3,7},... | collective-permute-start | bytes 49160 | tf_op jit(solution)/shard_map/ppermute | solution.py:214
  28.9 1.8 %collective-permute-done.6 = f32[8,512]{1,0:T(8,128)S(1)} collective-permute-done((f32[8,512]{1,0:T(8,128)S(1)}, f32[8,512]{1,0:T(8,128)S(1)}, u32[]{:S(2)}, u32[]{:S(2)}) %collective-permute-start.6) | collective-permute-done | bytes 16416 | tf_op jit(solution)/shard_map/ppermute | solution.py:214
  30.8 2.9 %collective-permute-start.7 = (f32[8,512]{1,0:T(8,128)S(1)}, f32[8,512]{1,0:T(8,128)S(1)}, u32[]{:S(2)}, u32[]{:S(2)}) collective-permute-start(f32[8,512]{1,0:T(8,128)S(1)} %add.26), channel_id=1, source_target_pairs={{0,8},{2,10},{4,12},{6,14},{8,0},{10,2},{12,4},{14,6},{1,9},{3,11}... | collective-permute-start | bytes 49160 | tf_op jit(solution)/shard_map/ppermute | solution.py:214
  33.7 1.7 %collective-permute-done.7 = f32[8,512]{1,0:T(8,128)S(1)} collective-permute-done((f32[8,512]{1,0:T(8,128)S(1)}, f32[8,512]{1,0:T(8,128)S(1)}, u32[]{:S(2)}, u32[]{:S(2)}) %collective-permute-start.7) | collective-permute-done | bytes 16416 | tf_op jit(solution)/shard_map/ppermute | solution.py:214
  35.4 3.1 %finish.1 = (bf16[2,1024,512]{2,1,0:T(8,128)(2,1)}, f32[1,2,1024,512]{3,2,1,0:T(8,128)}) custom-call(f32[8,1024]{1,0:T(8,128)S(1)} %get-tuple-element.11.left_ref, f32[8,512]{1,0:T(8,128)S(1)} %add.27.right_ref, f32[2,1024,512]{2,1,0:T(8,128)S(1)} %get-tuple-element.13.merged_ref), custom_call_target="tpu_custom_call" | custom-call | tf_op jit(solution)/shard_map/finish/pallas_call | solution.py:191
  (7 shorter events, 0.0 us)
Async XLA Ops:
  5.7 4.9 %collective-permute-start = (f32[8,1024]{1,0:T(8,128)S(1)}, f32[8,1024]{1,0:T(8,128)S(1)}, u32[]{:S(2)}, u32[]{:S(2)}) collective-permute-start(f32[8,1024]{1,0:T(8,128)S(1)} %get-tuple-element.8), channel_id=1, source_target_pairs={{0,2},{2,0},{4,6},{6,4},{8,10},{10,8},{12,14},{14,12},{1,3},{3,1},... | collective-permute-start | bytes 98312 | tf_op jit(solution)/shard_map/ppermute | solution.py:214
  10.6 4.0 %collective-permute-start.1 = (f32[8,1024]{1,0:T(8,128)S(1)}, f32[8,1024]{1,0:T(8,128)S(1)}, u32[]{:S(2)}, u32[]{:S(2)}) collective-permute-start(f32[8,1024]{1,0:T(8,128)S(1)} %add.21), channel_id=1, source_target_pairs={{0,4},{2,6},{4,0},{6,2},{8,12},{10,14},{12,8},{14,10},{1,5},{3,7},... | collective-permute-start | bytes 98312 | tf_op jit(solution)/shard_map/ppermute | solution.py:214
  14.6 4.9 %collective-permute-start.2 = (f32[8,1024]{1,0:T(8,128)S(1)}, f32[8,1024]{1,0:T(8,128)S(1)}, u32[]{:S(2)}, u32[]{:S(2)}) collective-permute-start(f32[8,1024]{1,0:T(8,128)S(1)} %add.22), channel_id=1, source_target_pairs={{0,8},{2,10},{4,12},{6,14},{8,0},{10,2},{12,4},{14,6},{1,9},{3,11}... | collective-permute-start | bytes 98312 | tf_op jit(solution)/shard_map/ppermute | solution.py:214
  19.5 1.2 %collective-permute-start.3 = (f32[8,1024]{1,0:T(8,128)S(1)}, f32[8,1024]{1,0:T(8,128)S(1)}, u32[]{:S(2)}, u32[]{:S(2)}) collective-permute-start(f32[8,1024]{1,0:T(8,128)S(1)} %add_multiply_fusion.mine_ref), channel_id=1, source_target_pairs={{0,1},{1,0},{2,3},{3,2},{4,5},{5,4},{6,7},{7,6},{8,9},{9,8},{10,11... | collective-permute-start | bytes 98312 | tf_op jit(solution)/shard_map/ppermute | solution.py:223
  22.1 1.2 %collective-permute-start.4 = (f32[8,512]{1,0:T(8,128)S(1)}, f32[8,512]{1,0:T(8,128)S(1)}, u32[]{:S(2)}, u32[]{:S(2)}) collective-permute-start(f32[8,512]{1,0:T(8,128)S(1)} %get-tuple-element.12), channel_id=1, source_target_pairs={{0,1},{1,0},{2,3},{3,2},{4,5},{5,4},{6,7},{7,6},{8,9},{9,8},{10,11... | collective-permute-start | bytes 49160 | tf_op jit(solution)/shard_map/ppermute | solution.py:214
  23.3 3.7 %collective-permute-start.5 = (f32[8,512]{1,0:T(8,128)S(1)}, f32[8,512]{1,0:T(8,128)S(1)}, u32[]{:S(2)}, u32[]{:S(2)}) collective-permute-start(f32[8,512]{1,0:T(8,128)S(1)} %add.24), channel_id=1, source_target_pairs={{0,2},{2,0},{4,6},{6,4},{8,10},{10,8},{12,14},{14,12},{1,3},{3,1},... | collective-permute-start | bytes 49160 | tf_op jit(solution)/shard_map/ppermute | solution.py:214
  27.0 3.7 %collective-permute-start.6 = (f32[8,512]{1,0:T(8,128)S(1)}, f32[8,512]{1,0:T(8,128)S(1)}, u32[]{:S(2)}, u32[]{:S(2)}) collective-permute-start(f32[8,512]{1,0:T(8,128)S(1)} %add.25), channel_id=1, source_target_pairs={{0,4},{2,6},{4,0},{6,2},{8,12},{10,14},{12,8},{14,10},{1,5},{3,7},... | collective-permute-start | bytes 49160 | tf_op jit(solution)/shard_map/ppermute | solution.py:214
  30.8 4.7 %collective-permute-start.7 = (f32[8,512]{1,0:T(8,128)S(1)}, f32[8,512]{1,0:T(8,128)S(1)}, u32[]{:S(2)}, u32[]{:S(2)}) collective-permute-start(f32[8,512]{1,0:T(8,128)S(1)} %add.26), channel_id=1, source_target_pairs={{0,8},{2,10},{4,12},{6,14},{8,0},{10,2},{12,4},{14,6},{1,9},{3,11}... | collective-permute-start | bytes 49160 | tf_op jit(solution)/shard_map/ppermute | solution.py:214

commit v4 on v3

--- a/solution.py
+++ b/solution.py
@@ -131,9 +131,12 @@
     return mine
 
 
-def reflect_body(mine_ref, other_ref, high_ref, low_ref, left_ref, right_ref):
+def reflect_body(scale, core_ref, whole_ref, high_ref, low_ref, left_ref, right_ref):
     mats, rows, cols = high_ref.shape
-    left = orthogonal(mine_ref[...], other_ref[...])
+    upper = whole_ref[: mats * RANK] * scale
+    lower = whole_ref[mats * RANK :] * scale
+    first = core_ref[0] == 0
+    left = orthogonal(jnp.where(first, lower, upper), jnp.where(first, upper, lower))
     left_ref[...] = left
     weights = jnp.concatenate(halves(left), axis=0).astype(BF16)
     right = jnp.zeros((mats * RANK, cols), F32)
@@ -144,19 +147,19 @@
     right_ref[...] = right
 
 
-def reflect(mine, other, high, low):
+def reflect(core, whole, high, low, scale):
     mats, rows, cols = high.shape
     return pl.pallas_call(
-        reflect_body,
+        functools.partial(reflect_body, scale),
         out_shape=(
             jax.ShapeDtypeStruct((mats * RANK, rows), F32),
             jax.ShapeDtypeStruct((mats * RANK, cols), F32),
         ),
-        in_specs=[pl.BlockSpec(memory_space=pltpu.VMEM)] * 4,
+        in_specs=[pl.BlockSpec(memory_space=pltpu.SMEM)] + [pl.BlockSpec(memory_space=pltpu.VMEM)] * 3,
         out_specs=[pl.BlockSpec(memory_space=pltpu.VMEM)] * 2,
         compiler_params=pltpu.CompilerParams(vmem_limit_bytes=24 * 2**20),
         name="reflect",
-    )(mine, other, pltpu.with_memory_space_constraint(high, pltpu.VMEM), pltpu.with_memory_space_constraint(low, pltpu.VMEM))
+    )(core, whole, pltpu.with_memory_space_constraint(high, pltpu.VMEM), pltpu.with_memory_space_constraint(low, pltpu.VMEM))
 
 
 def finish_body(scale, left_ref, right_ref, merged_ref, update_ref, errors_ref, ubuf, ebuf, sems):
@@ -206,23 +209,25 @@
     )(left, right, pltpu.with_memory_space_constraint(merged, pltpu.VMEM))
 
 
-def swap_sum(value, axis):
-    count = lax.axis_size(axis)
-    step = 1
-    while step < count:
-        pairs = [(index, index ^ step) for index in range(count)]
-        value = value + lax.ppermute(value, axis, pairs)
-        step *= 2
-    return value
+def spread_sum(value):
+    count = lax.axis_size("dp")
+    axes = ("dp", "tensor")
+    terms = [
+        lax.ppermute(value, axes, [(2 * at + 1, 2 * (at ^ step)) for at in range(count)])
+        for step in range(count)
+    ]
+    while len(terms) > 1:
+        terms = [terms[at] + terms[at + 1] for at in range(0, len(terms), 2)]
+    return terms[0] + lax.ppermute(terms[0], "tensor", [(0, 1)])
 
 
 def body(grads, errors, seeds):
     replicas = lax.axis_size("dp")
     left_part, merged, high, low = project(seeds, grads, errors)
-    mine = swap_sum(left_part, "dp") / replicas
-    other = lax.ppermute(mine, "tensor", [(0, 1), (1, 0)])
-    left, right_part = reflect(mine, other, high, low)
-    right = swap_sum(swap_sum(right_part, "tensor"), "dp")
+    partner = lax.ppermute(left_part, "tensor", [(0, 1)])
+    whole = spread_sum(jnp.concatenate([left_part, partner], axis=0))
+    left, right_part = reflect(lax.axis_index("tensor").reshape(1), whole, high, low, 1.0 / replicas)
+    right = spread_sum(right_part + lax.ppermute(right_part, "tensor", [(0, 1)]))
     return finish(left, right, merged, 1.0 / replicas)
 
 

time: 38.7 us -> 59.4 us (1.53)
  starting transfers between devices: 15 us -> 29 us
  local copies, waits for them, and re-layouts: 0 us -> 4.92 us
  waiting for transfers between devices: 13.3 us -> 14.6 us
    ppermute x8 -> x20, starting transfers between devices: 15 us -> 29 us  [the longest x16 20.6 us: spread_sum(): lax.ppermute(value, axes, [(2 * at + 1, 2 * (at ^ step)) for at in range(...]
    unnamed x0 -> x9, local copies, waits for them, and re-layouts: none -> 4.92 us
    ppermute x8 -> x20, waiting for transfers between devices: 13.3 us -> 14.6 us  [the longest x16 11.3 us: spread_sum(): lax.ppermute(value, axes, [(2 * at + 1, 2 * (at ^ step)) for at in range(...]
  transfers between devices with their start and end apart: 8 -> 20, of which waited for: 8 -> 14; matrix products, arithmetic and copies ran while one was open for 0% -> 0% of each run, Pallas kernels for 0% -> 0%
where the time goes in v4:
time: 59.4 us; the launch traced here: 58.9 us
  starting transfers between devices  29 us (49%)
  waiting for transfers between devices  14.6 us (25%)
  Pallas kernels  9.49 us (16%)
  local copies, waits for them, and re-layouts  4.92 us (8%)
  between operations  0.88 us (1%)
    ppermute x16, starting transfers between devices, spread_sum(): lax.ppermute(value, axes, [(2 * at + 1, 2 * (at ^ step)) for at in range(...  20.6 us
    ppermute x16, waiting for transfers between devices, spread_sum(): lax.ppermute(value, axes, [(2 * at + 1, 2 * (at ^ step)) for at in range(...  11.3 us
    pallas_call x1, Pallas kernels, project(): pl.pallas_call(project_body, out_shape=(jax.ShapeDtypeStruct((mats * RANK...  5.05 us
    unnamed x9, local copies, waits for them, and re-layouts  4.92 us
    ppermute x2, starting transfers between devices, spread_sum(): return terms[0] + lax.ppermute(terms[0], 'tensor', [(0, 1)])  3.76 us
    pallas_call x1, Pallas kernels, finish(): pl.pallas_call(functools.partial(finish_body, scale), out_shape=(jax.Shap...  3.07 us
    ppermute x1, starting transfers between devices, body(): partner = lax.ppermute(left_part, 'tensor', [(0, 1)])  2.35 us
    ppermute x1, starting transfers between devices, body(): lax.ppermute(right_part, 'tensor', [(0, 1)])  2.26 us
  transfers between devices with their start and end apart: 20, of which 14 were waited for; matrix products, arithmetic and copies ran while one was open for 0% of the time, Pallas kernels for 0%

profile of v4, /device:TPU:0, one launch (start us, length us, event | category | flops | bytes accessed | tf_op | source)
XLA Modules:
  0.0 58.9 jit_solution(10339808431820590077)
XLA Ops:
  0.6 5.1 %project.1 = (f32[8,1024]{1,0:T(8,128)S(1)}, f32[2,1024,512]{2,1,0:T(8,128)S(1)}, bf16[2,1024,512]{2,1,0:T(8,128)(2,1)S(1)}, bf16[2,1024,512]{2,1,0:T(8,128)(2,1)S(1)}) custom-call(s32[2]{0:T(128)} %seeds_ref.1, bf16[1,2,1024,512]{3,2,1,0:T(8,128)(2,1)} %grads_ref.1, f32[1,2,1024,512]{3,2,1,0:T(8,128)} %errors_ref.1), custom_call_target="tpu_custom_call" | custom-call | tf_op jit(solution)/shard_map/project/pallas_call | solution.py:85
  5.7 2.0 %copy-done = f32[2,1024,512]{2,1,0:T(8,128)} copy-done((f32[2,1024,512]{2,1,0:T(8,128)}, f32[2,1024,512]{2,1,0:T(8,128)S(1)}, u32[]{:S(2)}) %copy-start) | copy-done | bytes 4194328
  7.7 1.3 %copy-done.2 = bf16[2,1024,512]{2,1,0:T(8,128)(2,1)} copy-done((bf16[2,1024,512]{2,1,0:T(8,128)(2,1)}, bf16[2,1024,512]{2,1,0:T(8,128)(2,1)S(1)}, u32[]{:S(2)}) %copy-start.2) | copy-done | bytes 2097176
  9.0 2.3 %collective-permute-start = (f32[8,1024]{1,0:T(8,128)S(1)}, f32[8,1024]{1,0:T(8,128)S(1)}, u32[]{:S(2)}, u32[]{:S(2)}) collective-permute-start(f32[8,1024]{1,0:T(8,128)S(1)} %get-tuple-element.8), channel_id=1, source_target_pairs={{0,1},{2,3},{4,5},{6,7},{8,9},{10,11},{12,13},{14,15},{16,17},{18,... | collective-permute-start | bytes 98312 | tf_op jit(solution)/shard_map/ppermute | solution.py:227
  12.2 1.3 %collective-permute-start.8 = (f32[16,1024]{1,0:T(8,128)S(1)}, f32[16,1024]{1,0:T(8,128)S(1)}, u32[]{:S(2)}, u32[]{:S(2)}) collective-permute-start(f32[16,1024]{1,0:T(8,128)S(1)} %constant_dynamic-update-slice_fusion), channel_id=1, source_target_pairs={{1,14},{3,12},{5,10},{7,8},{9,6},{11,4},{13,2},{15,0},{17,30},{19,... | collective-permute-start | bytes 196616 | tf_op jit(solution)/shard_map/ppermute | solution.py:216
  13.5 1.3 %collective-permute-start.7 = (f32[16,1024]{1,0:T(8,128)S(1)}, f32[16,1024]{1,0:T(8,128)S(1)}, u32[]{:S(2)}, u32[]{:S(2)}) collective-permute-start(f32[16,1024]{1,0:T(8,128)S(1)} %constant_dynamic-update-slice_fusion), channel_id=1, source_target_pairs={{1,12},{3,14},{5,8},{7,10},{9,4},{11,6},{13,0},{15,2},{17,28},{19,... | collective-permute-start | bytes 196616 | tf_op jit(solution)/shard_map/ppermute | solution.py:216
  14.8 1.3 %collective-permute-start.6 = (f32[16,1024]{1,0:T(8,128)S(1)}, f32[16,1024]{1,0:T(8,128)S(1)}, u32[]{:S(2)}, u32[]{:S(2)}) collective-permute-start(f32[16,1024]{1,0:T(8,128)S(1)} %constant_dynamic-update-slice_fusion), channel_id=1, source_target_pairs={{1,10},{3,8},{5,14},{7,12},{9,2},{11,0},{13,6},{15,4},{17,26},{19,... | collective-permute-start | bytes 196616 | tf_op jit(solution)/shard_map/ppermute | solution.py:216
  16.1 1.3 %collective-permute-start.5 = (f32[16,1024]{1,0:T(8,128)S(1)}, f32[16,1024]{1,0:T(8,128)S(1)}, u32[]{:S(2)}, u32[]{:S(2)}) collective-permute-start(f32[16,1024]{1,0:T(8,128)S(1)} %constant_dynamic-update-slice_fusion), channel_id=1, source_target_pairs={{1,8},{3,10},{5,12},{7,14},{9,0},{11,2},{13,4},{15,6},{17,24},{19,... | collective-permute-start | bytes 196616 | tf_op jit(solution)/shard_map/ppermute | solution.py:216
  17.4 1.3 %collective-permute-start.4 = (f32[16,1024]{1,0:T(8,128)S(1)}, f32[16,1024]{1,0:T(8,128)S(1)}, u32[]{:S(2)}, u32[]{:S(2)}) collective-permute-start(f32[16,1024]{1,0:T(8,128)S(1)} %constant_dynamic-update-slice_fusion), channel_id=1, source_target_pairs={{1,6},{3,4},{5,2},{7,0},{9,14},{11,12},{13,10},{15,8},{17,22},{19,... | collective-permute-start | bytes 196616 | tf_op jit(solution)/shard_map/ppermute | solution.py:216
  18.7 2.2 %collective-permute-done.8 = f32[16,1024]{1,0:T(8,128)S(1)} collective-permute-done((f32[16,1024]{1,0:T(8,128)S(1)}, f32[16,1024]{1,0:T(8,128)S(1)}, u32[]{:S(2)}, u32[]{:S(2)}) %collective-permute-start.8) | collective-permute-done | bytes 65568 | tf_op jit(solution)/shard_map/ppermute | solution.py:216
  20.9 1.3 %collective-permute-start.3 = (f32[16,1024]{1,0:T(8,128)S(1)}, f32[16,1024]{1,0:T(8,128)S(1)}, u32[]{:S(2)}, u32[]{:S(2)}) collective-permute-start(f32[16,1024]{1,0:T(8,128)S(1)} %constant_dynamic-update-slice_fusion), channel_id=1, source_target_pairs={{1,4},{3,6},{5,0},{7,2},{9,12},{11,14},{13,8},{15,10},{17,20},{19,... | collective-permute-start | bytes 196616 | tf_op jit(solution)/shard_map/ppermute | solution.py:216
  22.8 1.3 %collective-permute-start.2 = (f32[16,1024]{1,0:T(8,128)S(1)}, f32[16,1024]{1,0:T(8,128)S(1)}, u32[]{:S(2)}, u32[]{:S(2)}) collective-permute-start(f32[16,1024]{1,0:T(8,128)S(1)} %constant_dynamic-update-slice_fusion), channel_id=1, source_target_pairs={{1,2},{3,0},{5,6},{7,4},{9,10},{11,8},{13,14},{15,12},{17,18},{19,... | collective-permute-start | bytes 196616 | tf_op jit(solution)/shard_map/ppermute | solution.py:216
  24.1 1.3 %collective-permute-start.1 = (f32[16,1024]{1,0:T(8,128)S(1)}, f32[16,1024]{1,0:T(8,128)S(1)}, u32[]{:S(2)}, u32[]{:S(2)}) collective-permute-start(f32[16,1024]{1,0:T(8,128)S(1)} %constant_dynamic-update-slice_fusion), channel_id=1, source_target_pairs={{1,0},{3,2},{5,4},{7,6},{9,8},{11,10},{13,12},{15,14},{17,16},{19,... | collective-permute-start | bytes 196616 | tf_op jit(solution)/shard_map/ppermute | solution.py:216
  25.6 1.3 %collective-permute-done.4 = f32[16,1024]{1,0:T(8,128)S(1)} collective-permute-done((f32[16,1024]{1,0:T(8,128)S(1)}, f32[16,1024]{1,0:T(8,128)S(1)}, u32[]{:S(2)}, u32[]{:S(2)}) %collective-permute-start.4) | collective-permute-done | bytes 65568 | tf_op jit(solution)/shard_map/ppermute | solution.py:216
  26.9 1.3 %collective-permute-done.3 = f32[16,1024]{1,0:T(8,128)S(1)} collective-permute-done((f32[16,1024]{1,0:T(8,128)S(1)}, f32[16,1024]{1,0:T(8,128)S(1)}, u32[]{:S(2)}, u32[]{:S(2)}) %collective-permute-start.3) | collective-permute-done | bytes 65568 | tf_op jit(solution)/shard_map/ppermute | solution.py:216
  28.2 1.3 %collective-permute-done.2 = f32[16,1024]{1,0:T(8,128)S(1)} collective-permute-done((f32[16,1024]{1,0:T(8,128)S(1)}, f32[16,1024]{1,0:T(8,128)S(1)}, u32[]{:S(2)}, u32[]{:S(2)}) %collective-permute-start.2) | collective-permute-done | bytes 65568 | tf_op jit(solution)/shard_map/ppermute | solution.py:216
  29.6 2.0 %collective-permute-start.9 = (f32[16,1024]{1,0:T(8,128)S(1)}, f32[16,1024]{1,0:T(8,128)S(1)}, u32[]{:S(2)}, u32[]{:S(2)}) collective-permute-start(f32[16,1024]{1,0:T(8,128)S(1)} %add_add_fusion), channel_id=1, source_target_pairs={{0,1},{2,3},{4,5},{6,7},{8,9},{10,11},{12,13},{14,15},{16,17},{18,... | collective-permute-start | bytes 196616 | tf_op jit(solution)/shard_map/ppermute | solution.py:221
  32.5 1.6 %copy-done.3 = bf16[2,1024,512]{2,1,0:T(8,128)(2,1)S(1)} copy-done((bf16[2,1024,512]{2,1,0:T(8,128)(2,1)S(1)}, bf16[2,1024,512]{2,1,0:T(8,128)(2,1)}, u32[]{:S(2)}) %copy-start.3) | copy-done | bytes 2097176
  34.1 1.4 %reflect.1 = (f32[8,1024]{1,0:T(8,128)S(1)}, f32[8,512]{1,0:T(8,128)S(1)}) custom-call(s32[1]{0:T(128)} %bitcast.core_ref, f32[16,1024]{1,0:T(8,128)S(1)} %add.58.whole_ref, bf16[2,1024,512]{2,1,0:T(8,128)(2,1)S(1)} %get-tuple-element.9.high_ref, bf16[2,1024,512]{2,1,0:T(8,128)(2,1)S(1)} %copy-done.3), custom_call_target="tpu_custom_call" | custom-call | tf_op jit(solution)/shard_map/reflect/pallas_call | solution.py:152
  35.5 2.3 %collective-permute-start.10 = (f32[8,512]{1,0:T(8,128)S(1)}, f32[8,512]{1,0:T(8,128)S(1)}, u32[]{:S(2)}, u32[]{:S(2)}) collective-permute-start(f32[8,512]{1,0:T(8,128)S(1)} %get-tuple-element.12), channel_id=1, source_target_pairs={{0,1},{2,3},{4,5},{6,7},{8,9},{10,11},{12,13},{14,15},{16,17},{18,... | collective-permute-start | bytes 49160 | tf_op jit(solution)/shard_map/ppermute | solution.py:230
  38.5 1.3 %collective-permute-start.18 = (f32[8,512]{1,0:T(8,128)S(1)}, f32[8,512]{1,0:T(8,128)S(1)}, u32[]{:S(2)}, u32[]{:S(2)}) collective-permute-start(f32[8,512]{1,0:T(8,128)S(1)} %add.59), channel_id=1, source_target_pairs={{1,14},{3,12},{5,10},{7,8},{9,6},{11,4},{13,2},{15,0},{17,30},{19,... | collective-permute-start | bytes 49160 | tf_op jit(solution)/shard_map/ppermute | solution.py:216
  39.8 1.3 %collective-permute-start.17 = (f32[8,512]{1,0:T(8,128)S(1)}, f32[8,512]{1,0:T(8,128)S(1)}, u32[]{:S(2)}, u32[]{:S(2)}) collective-permute-start(f32[8,512]{1,0:T(8,128)S(1)} %add.59), channel_id=1, source_target_pairs={{1,12},{3,14},{5,8},{7,10},{9,4},{11,6},{13,0},{15,2},{17,28},{19,... | collective-permute-start | bytes 49160 | tf_op jit(solution)/shard_map/ppermute | solution.py:216
  41.1 1.3 %collective-permute-start.16 = (f32[8,512]{1,0:T(8,128)S(1)}, f32[8,512]{1,0:T(8,128)S(1)}, u32[]{:S(2)}, u32[]{:S(2)}) collective-permute-start(f32[8,512]{1,0:T(8,128)S(1)} %add.59), channel_id=1, source_target_pairs={{1,10},{3,8},{5,14},{7,12},{9,2},{11,0},{13,6},{15,4},{17,26},{19,... | collective-permute-start | bytes 49160 | tf_op jit(solution)/shard_map/ppermute | solution.py:216
  42.4 1.3 %collective-permute-start.15 = (f32[8,512]{1,0:T(8,128)S(1)}, f32[8,512]{1,0:T(8,128)S(1)}, u32[]{:S(2)}, u32[]{:S(2)}) collective-permute-start(f32[8,512]{1,0:T(8,128)S(1)} %add.59), channel_id=1, source_target_pairs={{1,8},{3,10},{5,12},{7,14},{9,0},{11,2},{13,4},{15,6},{17,24},{19,... | collective-permute-start | bytes 49160 | tf_op jit(solution)/shard_map/ppermute | solution.py:216
  43.7 1.3 %collective-permute-start.14 = (f32[8,512]{1,0:T(8,128)S(1)}, f32[8,512]{1,0:T(8,128)S(1)}, u32[]{:S(2)}, u32[]{:S(2)}) collective-permute-start(f32[8,512]{1,0:T(8,128)S(1)} %add.59), channel_id=1, source_target_pairs={{1,6},{3,4},{5,2},{7,0},{9,14},{11,12},{13,10},{15,8},{17,22},{19,... | collective-permute-start | bytes 49160 | tf_op jit(solution)/shard_map/ppermute | solution.py:216
  45.0 1.3 %collective-permute-done.18 = f32[8,512]{1,0:T(8,128)S(1)} collective-permute-done((f32[8,512]{1,0:T(8,128)S(1)}, f32[8,512]{1,0:T(8,128)S(1)}, u32[]{:S(2)}, u32[]{:S(2)}) %collective-permute-start.18) | collective-permute-done | bytes 16416 | tf_op jit(solution)/shard_map/ppermute | solution.py:216
  46.3 1.3 %collective-permute-start.13 = (f32[8,512]{1,0:T(8,128)S(1)}, f32[8,512]{1,0:T(8,128)S(1)}, u32[]{:S(2)}, u32[]{:S(2)}) collective-permute-start(f32[8,512]{1,0:T(8,128)S(1)} %add.59), channel_id=1, source_target_pairs={{1,4},{3,6},{5,0},{7,2},{9,12},{11,14},{13,8},{15,10},{17,20},{19,... | collective-permute-start | bytes 49160 | tf_op jit(solution)/shard_map/ppermute | solution.py:216
  47.6 1.3 %collective-permute-start.12 = (f32[8,512]{1,0:T(8,128)S(1)}, f32[8,512]{1,0:T(8,128)S(1)}, u32[]{:S(2)}, u32[]{:S(2)}) collective-permute-start(f32[8,512]{1,0:T(8,128)S(1)} %add.59), channel_id=1, source_target_pairs={{1,2},{3,0},{5,6},{7,4},{9,10},{11,8},{13,14},{15,12},{17,18},{19,... | collective-permute-start | bytes 49160 | tf_op jit(solution)/shard_map/ppermute | solution.py:216
  48.9 1.3 %collective-permute-start.11 = (f32[8,512]{1,0:T(8,128)S(1)}, f32[8,512]{1,0:T(8,128)S(1)}, u32[]{:S(2)}, u32[]{:S(2)}) collective-permute-start(f32[8,512]{1,0:T(8,128)S(1)} %add.59), channel_id=1, source_target_pairs={{1,0},{3,2},{5,4},{7,6},{9,8},{11,10},{13,12},{15,14},{17,16},{19,... | collective-permute-start | bytes 49160 | tf_op jit(solution)/shard_map/ppermute | solution.py:216
  51.3 1.9 %collective-permute-done.12 = f32[8,512]{1,0:T(8,128)S(1)} collective-permute-done((f32[8,512]{1,0:T(8,128)S(1)}, f32[8,512]{1,0:T(8,128)S(1)}, u32[]{:S(2)}, u32[]{:S(2)}) %collective-permute-start.12) | collective-permute-done | bytes 16416 | tf_op jit(solution)/shard_map/ppermute | solution.py:216
  53.3 1.8 %collective-permute-start.19 = (f32[8,512]{1,0:T(8,128)S(1)}, f32[8,512]{1,0:T(8,128)S(1)}, u32[]{:S(2)}, u32[]{:S(2)}) collective-permute-start(f32[8,512]{1,0:T(8,128)S(1)} %add_add_fusion.1), channel_id=1, source_target_pairs={{0,1},{2,3},{4,5},{6,7},{8,9},{10,11},{12,13},{14,15},{16,17},{18,... | collective-permute-start | bytes 49160 | tf_op jit(solution)/shard_map/ppermute | solution.py:221
  55.9 3.1 %finish.1 = (bf16[2,1024,512]{2,1,0:T(8,128)(2,1)}, f32[1,2,1024,512]{3,2,1,0:T(8,128)}) custom-call(f32[8,1024]{1,0:T(8,128)S(1)} %get-tuple-element.11.left_ref, f32[8,512]{1,0:T(8,128)S(1)} %add.67.right_ref, f32[2,1024,512]{2,1,0:T(8,128)S(1)} %copy-done.1), custom_call_target="tpu_custom_call" | custom-call | tf_op jit(solution)/shard_map/finish/pallas_call | solution.py:194
  (26 shorter events, 5.4 us)
Async XLA Ops:
  5.7 2.0 %copy-start = (f32[2,1024,512]{2,1,0:T(8,128)}, f32[2,1024,512]{2,1,0:T(8,128)S(1)}, u32[]{:S(2)}) copy-start(f32[2,1024,512]{2,1,0:T(8,128)S(1)} %get-tuple-element.13.merged_ref) | copy-start | bytes 12582916
  7.7 1.3 %copy-start.2 = (bf16[2,1024,512]{2,1,0:T(8,128)(2,1)}, bf16[2,1024,512]{2,1,0:T(8,128)(2,1)S(1)}, u32[]{:S(2)}) copy-start(bf16[2,1024,512]{2,1,0:T(8,128)(2,1)S(1)} %get-tuple-element.10.low_ref) | copy-start | bytes 6291460
  9.0 3.2 %collective-permute-start = (f32[8,1024]{1,0:T(8,128)S(1)}, f32[8,1024]{1,0:T(8,128)S(1)}, u32[]{:S(2)}, u32[]{:S(2)}) collective-permute-start(f32[8,1024]{1,0:T(8,128)S(1)} %get-tuple-element.8), channel_id=1, source_target_pairs={{0,1},{2,3},{4,5},{6,7},{8,9},{10,11},{12,13},{14,15},{16,17},{18,... | collective-permute-start | bytes 98312 | tf_op jit(solution)/shard_map/ppermute | solution.py:227
  12.2 8.7 %collective-permute-start.8 = (f32[16,1024]{1,0:T(8,128)S(1)}, f32[16,1024]{1,0:T(8,128)S(1)}, u32[]{:S(2)}, u32[]{:S(2)}) collective-permute-start(f32[16,1024]{1,0:T(8,128)S(1)} %constant_dynamic-update-slice_fusion), channel_id=1, source_target_pairs={{1,14},{3,12},{5,10},{7,8},{9,6},{11,4},{13,2},{15,0},{17,30},{19,... | collective-permute-start | bytes 196616 | tf_op jit(solution)/shard_map/ppermute | solution.py:216
  13.5 9.3 %collective-permute-start.7 = (f32[16,1024]{1,0:T(8,128)S(1)}, f32[16,1024]{1,0:T(8,128)S(1)}, u32[]{:S(2)}, u32[]{:S(2)}) collective-permute-start(f32[16,1024]{1,0:T(8,128)S(1)} %constant_dynamic-update-slice_fusion), channel_id=1, source_target_pairs={{1,12},{3,14},{5,8},{7,10},{9,4},{11,6},{13,0},{15,2},{17,28},{19,... | collective-permute-start | bytes 196616 | tf_op jit(solution)/shard_map/ppermute | solution.py:216
  14.8 9.3 %collective-permute-start.6 = (f32[16,1024]{1,0:T(8,128)S(1)}, f32[16,1024]{1,0:T(8,128)S(1)}, u32[]{:S(2)}, u32[]{:S(2)}) collective-permute-start(f32[16,1024]{1,0:T(8,128)S(1)} %constant_dynamic-update-slice_fusion), channel_id=1, source_target_pairs={{1,10},{3,8},{5,14},{7,12},{9,2},{11,0},{13,6},{15,4},{17,26},{19,... | collective-permute-start | bytes 196616 | tf_op jit(solution)/shard_map/ppermute | solution.py:216
  16.1 9.5 %collective-permute-start.5 = (f32[16,1024]{1,0:T(8,128)S(1)}, f32[16,1024]{1,0:T(8,128)S(1)}, u32[]{:S(2)}, u32[]{:S(2)}) collective-permute-start(f32[16,1024]{1,0:T(8,128)S(1)} %constant_dynamic-update-slice_fusion), channel_id=1, source_target_pairs={{1,8},{3,10},{5,12},{7,14},{9,0},{11,2},{13,4},{15,6},{17,24},{19,... | collective-permute-start | bytes 196616 | tf_op jit(solution)/shard_map/ppermute | solution.py:216
  17.4 9.5 %collective-permute-start.4 = (f32[16,1024]{1,0:T(8,128)S(1)}, f32[16,1024]{1,0:T(8,128)S(1)}, u32[]{:S(2)}, u32[]{:S(2)}) collective-permute-start(f32[16,1024]{1,0:T(8,128)S(1)} %constant_dynamic-update-slice_fusion), channel_id=1, source_target_pairs={{1,6},{3,4},{5,2},{7,0},{9,14},{11,12},{13,10},{15,8},{17,22},{19,... | collective-permute-start | bytes 196616 | tf_op jit(solution)/shard_map/ppermute | solution.py:216
  20.9 7.4 %collective-permute-start.3 = (f32[16,1024]{1,0:T(8,128)S(1)}, f32[16,1024]{1,0:T(8,128)S(1)}, u32[]{:S(2)}, u32[]{:S(2)}) collective-permute-start(f32[16,1024]{1,0:T(8,128)S(1)} %constant_dynamic-update-slice_fusion), channel_id=1, source_target_pairs={{1,4},{3,6},{5,0},{7,2},{9,12},{11,14},{13,8},{15,10},{17,20},{19,... | collective-permute-start | bytes 196616 | tf_op jit(solution)/shard_map/ppermute | solution.py:216
  22.8 6.8 %collective-permute-start.2 = (f32[16,1024]{1,0:T(8,128)S(1)}, f32[16,1024]{1,0:T(8,128)S(1)}, u32[]{:S(2)}, u32[]{:S(2)}) collective-permute-start(f32[16,1024]{1,0:T(8,128)S(1)} %constant_dynamic-update-slice_fusion), channel_id=1, source_target_pairs={{1,2},{3,0},{5,6},{7,4},{9,10},{11,8},{13,14},{15,12},{17,18},{19,... | collective-permute-start | bytes 196616 | tf_op jit(solution)/shard_map/ppermute | solution.py:216
  24.1 5.5 %collective-permute-start.1 = (f32[16,1024]{1,0:T(8,128)S(1)}, f32[16,1024]{1,0:T(8,128)S(1)}, u32[]{:S(2)}, u32[]{:S(2)}) collective-permute-start(f32[16,1024]{1,0:T(8,128)S(1)} %constant_dynamic-update-slice_fusion), channel_id=1, source_target_pairs={{1,0},{3,2},{5,4},{7,6},{9,8},{11,10},{13,12},{15,14},{17,16},{19,... | collective-permute-start | bytes 196616 | tf_op jit(solution)/shard_map/ppermute | solution.py:216
  29.6 2.9 %collective-permute-start.9 = (f32[16,1024]{1,0:T(8,128)S(1)}, f32[16,1024]{1,0:T(8,128)S(1)}, u32[]{:S(2)}, u32[]{:S(2)}) collective-permute-start(f32[16,1024]{1,0:T(8,128)S(1)} %add_add_fusion), channel_id=1, source_target_pairs={{0,1},{2,3},{4,5},{6,7},{8,9},{10,11},{12,13},{14,15},{16,17},{18,... | collective-permute-start | bytes 196616 | tf_op jit(solution)/shard_map/ppermute | solution.py:221
  32.5 1.6 %copy-start.3 = (bf16[2,1024,512]{2,1,0:T(8,128)(2,1)S(1)}, bf16[2,1024,512]{2,1,0:T(8,128)(2,1)}, u32[]{:S(2)}) copy-start(bf16[2,1024,512]{2,1,0:T(8,128)(2,1)} %copy-done.2) | copy-start | bytes 6291460
  34.1 21.8 %copy-start.1 = (f32[2,1024,512]{2,1,0:T(8,128)S(1)}, f32[2,1024,512]{2,1,0:T(8,128)}, u32[]{:S(2)}) copy-start(f32[2,1024,512]{2,1,0:T(8,128)} %copy-done) | copy-start | bytes 12582916
  35.5 3.1 %collective-permute-start.10 = (f32[8,512]{1,0:T(8,128)S(1)}, f32[8,512]{1,0:T(8,128)S(1)}, u32[]{:S(2)}, u32[]{:S(2)}) collective-permute-start(f32[8,512]{1,0:T(8,128)S(1)} %get-tuple-element.12), channel_id=1, source_target_pairs={{0,1},{2,3},{4,5},{6,7},{8,9},{10,11},{12,13},{14,15},{16,17},{18,... | collective-permute-start | bytes 49160 | tf_op jit(solution)/shard_map/ppermute | solution.py:230
  38.5 7.7 %collective-permute-start.18 = (f32[8,512]{1,0:T(8,128)S(1)}, f32[8,512]{1,0:T(8,128)S(1)}, u32[]{:S(2)}, u32[]{:S(2)}) collective-permute-start(f32[8,512]{1,0:T(8,128)S(1)} %add.59), channel_id=1, source_target_pairs={{1,14},{3,12},{5,10},{7,8},{9,6},{11,4},{13,2},{15,0},{17,30},{19,... | collective-permute-start | bytes 49160 | tf_op jit(solution)/shard_map/ppermute | solution.py:216
  39.8 7.7 %collective-permute-start.17 = (f32[8,512]{1,0:T(8,128)S(1)}, f32[8,512]{1,0:T(8,128)S(1)}, u32[]{:S(2)}, u32[]{:S(2)}) collective-permute-start(f32[8,512]{1,0:T(8,128)S(1)} %add.59), channel_id=1, source_target_pairs={{1,12},{3,14},{5,8},{7,10},{9,4},{11,6},{13,0},{15,2},{17,28},{19,... | collective-permute-start | bytes 49160 | tf_op jit(solution)/shard_map/ppermute | solution.py:216
  41.1 7.8 %collective-permute-start.16 = (f32[8,512]{1,0:T(8,128)S(1)}, f32[8,512]{1,0:T(8,128)S(1)}, u32[]{:S(2)}, u32[]{:S(2)}) collective-permute-start(f32[8,512]{1,0:T(8,128)S(1)} %add.59), channel_id=1, source_target_pairs={{1,10},{3,8},{5,14},{7,12},{9,2},{11,0},{13,6},{15,4},{17,26},{19,... | collective-permute-start | bytes 49160 | tf_op jit(solution)/shard_map/ppermute | solution.py:216
  42.4 7.8 %collective-permute-start.15 = (f32[8,512]{1,0:T(8,128)S(1)}, f32[8,512]{1,0:T(8,128)S(1)}, u32[]{:S(2)}, u32[]{:S(2)}) collective-permute-start(f32[8,512]{1,0:T(8,128)S(1)} %add.59), channel_id=1, source_target_pairs={{1,8},{3,10},{5,12},{7,14},{9,0},{11,2},{13,4},{15,6},{17,24},{19,... | collective-permute-start | bytes 49160 | tf_op jit(solution)/shard_map/ppermute | solution.py:216
  43.7 6.9 %collective-permute-start.14 = (f32[8,512]{1,0:T(8,128)S(1)}, f32[8,512]{1,0:T(8,128)S(1)}, u32[]{:S(2)}, u32[]{:S(2)}) collective-permute-start(f32[8,512]{1,0:T(8,128)S(1)} %add.59), channel_id=1, source_target_pairs={{1,6},{3,4},{5,2},{7,0},{9,14},{11,12},{13,10},{15,8},{17,22},{19,... | collective-permute-start | bytes 49160 | tf_op jit(solution)/shard_map/ppermute | solution.py:216
  46.3 5.0 %collective-permute-start.13 = (f32[8,512]{1,0:T(8,128)S(1)}, f32[8,512]{1,0:T(8,128)S(1)}, u32[]{:S(2)}, u32[]{:S(2)}) collective-permute-start(f32[8,512]{1,0:T(8,128)S(1)} %add.59), channel_id=1, source_target_pairs={{1,4},{3,6},{5,0},{7,2},{9,12},{11,14},{13,8},{15,10},{17,20},{19,... | collective-permute-start | bytes 49160 | tf_op jit(solution)/shard_map/ppermute | solution.py:216
  47.6 5.7 %collective-permute-start.12 = (f32[8,512]{1,0:T(8,128)S(1)}, f32[8,512]{1,0:T(8,128)S(1)}, u32[]{:S(2)}, u32[]{:S(2)}) collective-permute-start(f32[8,512]{1,0:T(8,128)S(1)} %add.59), channel_id=1, source_target_pairs={{1,2},{3,0},{5,6},{7,4},{9,10},{11,8},{13,14},{15,12},{17,18},{19,... | collective-permute-start | bytes 49160 | tf_op jit(solution)/shard_map/ppermute | solution.py:216
  48.9 4.4 %collective-permute-start.11 = (f32[8,512]{1,0:T(8,128)S(1)}, f32[8,512]{1,0:T(8,128)S(1)}, u32[]{:S(2)}, u32[]{:S(2)}) collective-permute-start(f32[8,512]{1,0:T(8,128)S(1)} %add.59), channel_id=1, source_target_pairs={{1,0},{3,2},{5,4},{7,6},{9,8},{11,10},{13,12},{15,14},{17,16},{19,... | collective-permute-start | bytes 49160 | tf_op jit(solution)/shard_map/ppermute | solution.py:216
  53.3 2.6 %collective-permute-start.19 = (f32[8,512]{1,0:T(8,128)S(1)}, f32[8,512]{1,0:T(8,128)S(1)}, u32[]{:S(2)}, u32[]{:S(2)}) collective-permute-start(f32[8,512]{1,0:T(8,128)S(1)} %add_add_fusion.1), channel_id=1, source_target_pairs={{0,1},{2,3},{4,5},{6,7},{8,9},{10,11},{12,13},{14,15},{16,17},{18,... | collective-permute-start | bytes 49160 | tf_op jit(solution)/shard_map/ppermute | solution.py:221

commit v5 on v4

--- a/solution.py
+++ b/solution.py
@@ -131,12 +131,13 @@
     return mine
 
 
-def reflect_body(scale, core_ref, whole_ref, high_ref, low_ref, left_ref, right_ref):
+def reflect_body(scale, core_ref, kept_ref, given_ref, high_ref, low_ref, left_ref, right_ref):
     mats, rows, cols = high_ref.shape
-    upper = whole_ref[: mats * RANK] * scale
-    lower = whole_ref[mats * RANK :] * scale
+    half = mats * RANK
     first = core_ref[0] == 0
-    left = orthogonal(jnp.where(first, lower, upper), jnp.where(first, upper, lower))
+    mine = jnp.where(first, kept_ref[half:], given_ref[:half]) * scale
+    other = jnp.where(first, kept_ref[:half], given_ref[half:]) * scale
+    left = orthogonal(mine, other)
     left_ref[...] = left
     weights = jnp.concatenate(halves(left), axis=0).astype(BF16)
     right = jnp.zeros((mats * RANK, cols), F32)
@@ -147,7 +148,7 @@
     right_ref[...] = right
 
 
-def reflect(core, whole, high, low, scale):
+def reflect(core, kept, given, high, low, scale):
     mats, rows, cols = high.shape
     return pl.pallas_call(
         functools.partial(reflect_body, scale),
@@ -155,18 +156,19 @@
             jax.ShapeDtypeStruct((mats * RANK, rows), F32),
             jax.ShapeDtypeStruct((mats * RANK, cols), F32),
         ),
-        in_specs=[pl.BlockSpec(memory_space=pltpu.SMEM)] + [pl.BlockSpec(memory_space=pltpu.VMEM)] * 3,
+        in_specs=[pl.BlockSpec(memory_space=pltpu.SMEM)] + [pl.BlockSpec(memory_space=pltpu.VMEM)] * 4,
         out_specs=[pl.BlockSpec(memory_space=pltpu.VMEM)] * 2,
         compiler_params=pltpu.CompilerParams(vmem_limit_bytes=24 * 2**20),
         name="reflect",
-    )(core, whole, pltpu.with_memory_space_constraint(high, pltpu.VMEM), pltpu.with_memory_space_constraint(low, pltpu.VMEM))
-
-
-def finish_body(scale, left_ref, right_ref, merged_ref, update_ref, errors_ref, ubuf, ebuf, sems):
+    )(core, kept, given, pltpu.with_memory_space_constraint(high, pltpu.VMEM), pltpu.with_memory_space_constraint(low, pltpu.VMEM))
+
+
+def finish_body(scale, core_ref, left_ref, kept_ref, given_ref, merged_ref, update_ref, errors_ref, ubuf, ebuf, sems):
     mats, rows, cols = merged_ref.shape
     size = rows // CHUNKS
     left_high, left_low = halves(left_ref[...])
-    right_high, right_low = halves(right_ref[...] * scale)
+    right = jnp.where(core_ref[0] == 0, kept_ref[...], given_ref[...])
+    right_high, right_low = halves(right * scale)
     left = jnp.concatenate([left_high, left_low, left_high, left_low], axis=0).T.astype(BF16)
     right = jnp.concatenate([right_high, right_high, right_low, right_low], axis=0)
     row = lax.broadcasted_iota(jnp.int32, right.shape, 0) % (mats * RANK)
@@ -189,7 +191,7 @@
         copy.wait()
 
 
-def finish(left, right, merged, scale):
+def finish(core, left, kept, given, merged, scale):
     mats, rows, cols = merged.shape
     return pl.pallas_call(
         functools.partial(finish_body, scale),
@@ -197,7 +199,7 @@
             jax.ShapeDtypeStruct((mats, rows, cols), BF16),
             jax.ShapeDtypeStruct((1, mats, rows, cols), F32),
         ),
-        in_specs=[pl.BlockSpec(memory_space=pltpu.VMEM)] * 3,
+        in_specs=[pl.BlockSpec(memory_space=pltpu.SMEM)] + [pl.BlockSpec(memory_space=pltpu.VMEM)] * 4,
         out_specs=[pl.BlockSpec(memory_space=pltpu.HBM)] * 2,
         scratch_shapes=[
             pltpu.VMEM((mats, rows, cols), BF16),
@@ -206,29 +208,43 @@
         ],
         compiler_params=pltpu.CompilerParams(vmem_limit_bytes=24 * 2**20),
         name="finish",
-    )(left, right, pltpu.with_memory_space_constraint(merged, pltpu.VMEM))
+    )(core, left, kept, given, pltpu.with_memory_space_constraint(merged, pltpu.VMEM))
+
+
+def swap(value):
+    return lax.ppermute(value, "tensor", [(0, 1), (1, 0)])
 
 
 def spread_sum(value):
     count = lax.axis_size("dp")
     axes = ("dp", "tensor")
-    terms = [
-        lax.ppermute(value, axes, [(2 * at + 1, 2 * (at ^ step)) for at in range(count)])
-        for step in range(count)
-    ]
+    last = max(count // 4, 1)
+    step = 1
+    while step < last:
+        pairs = []
+        for at in range(count):
+            pairs += [(2 * at, 2 * at), (2 * at + 1, 2 * (at ^ step) + 1)]
+        value = value + lax.ppermute(value, axes, pairs)
+        step *= 2
+    terms = []
+    for offset in range(0, count, last):
+        pairs = []
+        for at in range(count):
+            pairs += [(2 * at, 2 * at + 1), (2 * at + 1, 2 * (at ^ offset))]
+        terms.append(lax.ppermute(value, axes, pairs))
     while len(terms) > 1:
         terms = [terms[at] + terms[at + 1] for at in range(0, len(terms), 2)]
-    return terms[0] + lax.ppermute(terms[0], "tensor", [(0, 1)])
+    return terms[0], swap(terms[0])
 
 
 def body(grads, errors, seeds):
     replicas = lax.axis_size("dp")
+    core = lax.axis_index("tensor").reshape(1)
     left_part, merged, high, low = project(seeds, grads, errors)
-    partner = lax.ppermute(left_part, "tensor", [(0, 1)])
-    whole = spread_sum(jnp.concatenate([left_part, partner], axis=0))
-    left, right_part = reflect(lax.axis_index("tensor").reshape(1), whole, high, low, 1.0 / replicas)
-    right = spread_sum(right_part + lax.ppermute(right_part, "tensor", [(0, 1)]))
-    return finish(left, right, merged, 1.0 / replicas)
+    kept, given = spread_sum(jnp.concatenate([left_part, swap(left_part)], axis=0))
+    left, right_part = reflect(core, kept, given, high, low, 1.0 / replicas)
+    kept, given = spread_sum(right_part + swap(right_part))
+    return finish(core, left, kept, given, merged, 1.0 / replicas)
 
 
 def solution(mesh):

time: 59.4 us -> 42.1 us (0.71)
  starting transfers between devices: 29 us -> 15.7 us
  waiting for transfers between devices: 14.6 us -> 11 us
    ppermute x20 -> x14, starting transfers between devices: 29 us -> 15.7 us  [the longest x8 13.7 us: spread_sum(): terms.append(lax.ppermute(value, axes, pairs))]
    ppermute x20 -> x14, waiting for transfers between devices: 14.6 us -> 11 us  [the longest x8 6.69 us: spread_sum(): terms.append(lax.ppermute(value, axes, pairs))]
  transfers between devices with their start and end apart: 20 -> 14, of which waited for: 14 -> 9; matrix products, arithmetic and copies ran while one was open for 0% -> 0% of each run, Pallas kernels for 0% -> 0%
where the time goes in v5:
time: 42.1 us; the launch traced here: 41.9 us
  starting transfers between devices  15.7 us (37%)
  waiting for transfers between devices  11 us (26%)
  Pallas kernels  9.5 us (23%)
  local copies, waits for them, and re-layouts  4.93 us (12%)
  between operations  0.74 us (2%)
    ppermute x8, starting transfers between devices, spread_sum(): terms.append(lax.ppermute(value, axes, pairs))  13.7 us
    ppermute x8, waiting for transfers between devices, spread_sum(): terms.append(lax.ppermute(value, axes, pairs))  6.69 us
    pallas_call x1, Pallas kernels, project(): pl.pallas_call(project_body, out_shape=(jax.ShapeDtypeStruct((mats * RANK...  5.05 us
    unnamed x9, local copies, waits for them, and re-layouts  4.92 us
    ppermute x4, waiting for transfers between devices, swap(): return lax.ppermute(value, 'tensor', [(0, 1), (1, 0)])  4.29 us
    pallas_call x1, Pallas kernels, finish(): pl.pallas_call(functools.partial(finish_body, scale), out_shape=(jax.Shap...  3.07 us
    pallas_call x1, Pallas kernels, reflect(): pl.pallas_call(functools.partial(reflect_body, scale), out_shape=(jax.Sha...  1.38 us
    ppermute x2, starting transfers between devices, spread_sum(): value = value + lax.ppermute(value, axes, pairs)  1.3 us
  transfers between devices with their start and end apart: 14, of which 9 were waited for; matrix products, arithmetic and copies ran while one was open for 0% of the time, Pallas kernels for 0%

profile of v5, /device:TPU:0, one launch (start us, length us, event | category | flops | bytes accessed | tf_op | source)
XLA Modules:
  0.0 41.9 jit_solution(16797281362393526451)
XLA Ops:
  0.6 5.1 %project.1 = (f32[8,1024]{1,0:T(8,128)S(1)}, f32[2,1024,512]{2,1,0:T(8,128)S(1)}, bf16[2,1024,512]{2,1,0:T(8,128)(2,1)S(1)}, bf16[2,1024,512]{2,1,0:T(8,128)(2,1)S(1)}) custom-call(s32[2]{0:T(128)} %seeds_ref.1, bf16[1,2,1024,512]{3,2,1,0:T(8,128)(2,1)} %grads_ref.1, f32[1,2,1024,512]{3,2,1,0:T(8,128)} %errors_ref.1), custom_call_target="tpu_custom_call" | custom-call | tf_op jit(solution)/shard_map/project/pallas_call | solution.py:85
  5.7 0.0 copy-start
  5.7 2.0 %copy-done = f32[2,1024,512]{2,1,0:T(8,128)} copy-done((f32[2,1024,512]{2,1,0:T(8,128)}, f32[2,1024,512]{2,1,0:T(8,128)S(1)}, u32[]{:S(2)}) %copy-start) | copy-done | bytes 4194328
  7.7 1.3 %copy-done.2 = bf16[2,1024,512]{2,1,0:T(8,128)(2,1)} copy-done((bf16[2,1024,512]{2,1,0:T(8,128)(2,1)}, bf16[2,1024,512]{2,1,0:T(8,128)(2,1)S(1)}, u32[]{:S(2)}) %copy-start.2) | copy-done | bytes 2097176
  9.0 0.5 %collective-permute-start = (f32[8,1024]{1,0:T(8,128)S(1)}, f32[8,1024]{1,0:T(8,128)S(1)}, u32[]{:S(2)}, u32[]{:S(2)}) collective-permute-start(f32[8,1024]{1,0:T(8,128)S(1)} %get-tuple-element.8), channel_id=1, source_target_pairs={{0,1},{1,0},{2,3},{3,2},{4,5},{5,4},{6,7},{7,6},{8,9},{9,8},{10,11... | collective-permute-start | bytes 98312 | tf_op jit(solution)/shard_map/ppermute | solution.py:215
  9.5 0.9 %collective-permute-done = f32[8,1024]{1,0:T(8,128)S(1)} collective-permute-done((f32[8,1024]{1,0:T(8,128)S(1)}, f32[8,1024]{1,0:T(8,128)S(1)}, u32[]{:S(2)}, u32[]{:S(2)}) %collective-permute-start) | collective-permute-done | bytes 32800 | tf_op jit(solution)/shard_map/ppermute | solution.py:215
  10.3 0.7 %collective-permute-start.1 = (f32[16,1024]{1,0:T(8,128)S(1)}, f32[16,1024]{1,0:T(8,128)S(1)}, u32[]{:S(2)}, u32[]{:S(2)}) collective-permute-start(f32[16,1024]{1,0:T(8,128)S(1)} %constant_dynamic-update-slice_fusion), channel_id=1, source_target_pairs={{0,0},{1,3},{2,2},{3,1},{4,4},{5,7},{6,6},{7,5},{8,8},{9,11},{10,1... | collective-permute-start | bytes 196616 | tf_op jit(solution)/shard_map/ppermute | solution.py:227
  11.0 0.0 collective-permute-done.1
  11.0 5.7 %collective-permute-start.5 = (f32[16,1024]{1,0:T(8,128)S(1)}, f32[16,1024]{1,0:T(8,128)S(1)}, u32[]{:S(2)}, u32[]{:S(2)}) collective-permute-start(f32[16,1024]{1,0:T(8,128)S(1)} %add.27), channel_id=1, source_target_pairs={{0,1},{1,12},{2,3},{3,14},{4,5},{5,8},{6,7},{7,10},{8,9},{9,4},{10... | collective-permute-start | bytes 196616 | tf_op jit(solution)/shard_map/ppermute | solution.py:234
  16.7 0.1 collective-permute-start.4
  16.8 2.9 %collective-permute-start.3 = (f32[16,1024]{1,0:T(8,128)S(1)}, f32[16,1024]{1,0:T(8,128)S(1)}, u32[]{:S(2)}, u32[]{:S(2)}) collective-permute-start(f32[16,1024]{1,0:T(8,128)S(1)} %add.27), channel_id=1, source_target_pairs={{0,1},{1,4},{2,3},{3,6},{4,5},{5,0},{6,7},{7,2},{8,9},{9,12},{10,1... | collective-permute-start | bytes 196616 | tf_op jit(solution)/shard_map/ppermute | solution.py:234
  19.6 0.0 collective-permute-start.2
  19.6 2.6 %collective-permute-done.5 = f32[16,1024]{1,0:T(8,128)S(1)} collective-permute-done((f32[16,1024]{1,0:T(8,128)S(1)}, f32[16,1024]{1,0:T(8,128)S(1)}, u32[]{:S(2)}, u32[]{:S(2)}) %collective-permute-start.5) | collective-permute-done | bytes 65568 | tf_op jit(solution)/shard_map/ppermute | solution.py:234
  22.2 1.0 %collective-permute-done.4 = f32[16,1024]{1,0:T(8,128)S(1)} collective-permute-done((f32[16,1024]{1,0:T(8,128)S(1)}, f32[16,1024]{1,0:T(8,128)S(1)}, u32[]{:S(2)}, u32[]{:S(2)}) %collective-permute-start.4) | collective-permute-done | bytes 65568 | tf_op jit(solution)/shard_map/ppermute | solution.py:234
  23.2 0.1 collective-permute-start.6
  23.3 1.2 %collective-permute-done.6.given_ref = f32[16,1024]{1,0:T(8,128)S(1)} collective-permute-done((f32[16,1024]{1,0:T(8,128)S(1)}, f32[16,1024]{1,0:T(8,128)S(1)}, u32[]{:S(2)}, u32[]{:S(2)}) %collective-permute-start.6) | collective-permute-done | bytes 65568 | tf_op jit(solution)/shard_map/ppermute | solution.py:215
  24.5 1.6 %copy-done.3 = bf16[2,1024,512]{2,1,0:T(8,128)(2,1)S(1)} copy-done((bf16[2,1024,512]{2,1,0:T(8,128)(2,1)S(1)}, bf16[2,1024,512]{2,1,0:T(8,128)(2,1)}, u32[]{:S(2)}) %copy-start.3) | copy-done | bytes 2097176
  26.1 1.4 %reflect.1 = (f32[8,1024]{1,0:T(8,128)S(1)}, f32[8,512]{1,0:T(8,128)S(1)}) custom-call(s32[1]{0:T(128)} %bitcast.core_ref, f32[16,1024]{1,0:T(8,128)S(1)} %add_add_fusion.kept_ref, f32[16,1024]{1,0:T(8,128)S(1)} %collective-permute-done.6.given_ref, bf16[2,1024,512]{2,1,0:T(8,128)(2,1)S(1)} %get-tuple-element.9.high_ref, bf16[2,1024,512]{2,1,0:T(8,128)(2,1)S(1)} %copy-done.3), custom_call_target="tpu_custom_call" | custom-call | tf_op jit(solution)/shard_map/reflect/pallas_call | solution.py:153
  27.5 0.2 collective-permute-start.7
  27.7 1.0 %collective-permute-done.7 = f32[8,512]{1,0:T(8,128)S(1)} collective-permute-done((f32[8,512]{1,0:T(8,128)S(1)}, f32[8,512]{1,0:T(8,128)S(1)}, u32[]{:S(2)}, u32[]{:S(2)}) %collective-permute-start.7) | collective-permute-done | bytes 16416 | tf_op jit(solution)/shard_map/ppermute | solution.py:215
  28.7 0.7 %collective-permute-start.8 = (f32[8,512]{1,0:T(8,128)S(1)}, f32[8,512]{1,0:T(8,128)S(1)}, u32[]{:S(2)}, u32[]{:S(2)}) collective-permute-start(f32[8,512]{1,0:T(8,128)S(1)} %add.31), channel_id=1, source_target_pairs={{0,0},{1,3},{2,2},{3,1},{4,4},{5,7},{6,6},{7,5},{8,8},{9,11},{10,1... | collective-permute-start | bytes 49160 | tf_op jit(solution)/shard_map/ppermute | solution.py:227
  29.3 0.0 collective-permute-done.8
  29.4 4.0 %collective-permute-start.12 = (f32[8,512]{1,0:T(8,128)S(1)}, f32[8,512]{1,0:T(8,128)S(1)}, u32[]{:S(2)}, u32[]{:S(2)}) collective-permute-start(f32[8,512]{1,0:T(8,128)S(1)} %add.32), channel_id=1, source_target_pairs={{0,1},{1,12},{2,3},{3,14},{4,5},{5,8},{6,7},{7,10},{8,9},{9,4},{10... | collective-permute-start | bytes 49160 | tf_op jit(solution)/shard_map/ppermute | solution.py:234
  33.3 0.1 collective-permute-start.11
  33.4 1.0 %collective-permute-start.10 = (f32[8,512]{1,0:T(8,128)S(1)}, f32[8,512]{1,0:T(8,128)S(1)}, u32[]{:S(2)}, u32[]{:S(2)}) collective-permute-start(f32[8,512]{1,0:T(8,128)S(1)} %add.32), channel_id=1, source_target_pairs={{0,1},{1,4},{2,3},{3,6},{4,5},{5,0},{6,7},{7,2},{8,9},{9,12},{10,1... | collective-permute-start | bytes 49160 | tf_op jit(solution)/shard_map/ppermute | solution.py:234
  34.4 0.0 collective-permute-start.9
  34.4 2.4 %collective-permute-done.12 = f32[8,512]{1,0:T(8,128)S(1)} collective-permute-done((f32[8,512]{1,0:T(8,128)S(1)}, f32[8,512]{1,0:T(8,128)S(1)}, u32[]{:S(2)}, u32[]{:S(2)}) %collective-permute-start.12) | collective-permute-done | bytes 16416 | tf_op jit(solution)/shard_map/ppermute | solution.py:234
  36.9 0.5 %collective-permute-done.11 = f32[8,512]{1,0:T(8,128)S(1)} collective-permute-done((f32[8,512]{1,0:T(8,128)S(1)}, f32[8,512]{1,0:T(8,128)S(1)}, u32[]{:S(2)}, u32[]{:S(2)}) %collective-permute-start.11) | collective-permute-done | bytes 16416 | tf_op jit(solution)/shard_map/ppermute | solution.py:234
  37.4 0.2 collective-permute-done.10
  37.6 0.1 collective-permute-start.13
  37.7 1.2 %collective-permute-done.13.given_ref = f32[8,512]{1,0:T(8,128)S(1)} collective-permute-done((f32[8,512]{1,0:T(8,128)S(1)}, f32[8,512]{1,0:T(8,128)S(1)}, u32[]{:S(2)}, u32[]{:S(2)}) %collective-permute-start.13) | collective-permute-done | bytes 16416 | tf_op jit(solution)/shard_map/ppermute | solution.py:215
  38.8 3.1 %finish.1 = (bf16[2,1024,512]{2,1,0:T(8,128)(2,1)}, f32[1,2,1024,512]{3,2,1,0:T(8,128)}) custom-call(s32[1]{0:T(128)} %bitcast.core_ref, f32[8,1024]{1,0:T(8,128)S(1)} %get-tuple-element.11.left_ref, f32[8,512]{1,0:T(8,128)S(1)} %add_add_fusion.1.kept_ref, f32[8,512]{1,0:T(8,128)S(1)} %collective-permute-done.13.given_ref, f32[2,1024,512]{2,1,0:T(8,128)S(1)} %copy-done.1), custom_call_target="tpu_custom_call" | custom-call | tf_op jit(solution)/shard_map/finish/pallas_call | solution.py:196
  (14 shorter events, 0.1 us)
Async XLA Ops:
  5.7 2.0 %copy-start = (f32[2,1024,512]{2,1,0:T(8,128)}, f32[2,1024,512]{2,1,0:T(8,128)S(1)}, u32[]{:S(2)}) copy-start(f32[2,1024,512]{2,1,0:T(8,128)S(1)} %get-tuple-element.13.merged_ref) | copy-start | bytes 12582916
  7.7 1.3 %copy-start.2 = (bf16[2,1024,512]{2,1,0:T(8,128)(2,1)}, bf16[2,1024,512]{2,1,0:T(8,128)(2,1)S(1)}, u32[]{:S(2)}) copy-start(bf16[2,1024,512]{2,1,0:T(8,128)(2,1)S(1)} %get-tuple-element.10.low_ref) | copy-start | bytes 6291460
  9.0 1.3 %collective-permute-start = (f32[8,1024]{1,0:T(8,128)S(1)}, f32[8,1024]{1,0:T(8,128)S(1)}, u32[]{:S(2)}, u32[]{:S(2)}) collective-permute-start(f32[8,1024]{1,0:T(8,128)S(1)} %get-tuple-element.8), channel_id=1, source_target_pairs={{0,1},{1,0},{2,3},{3,2},{4,5},{5,4},{6,7},{7,6},{8,9},{9,8},{10,11... | collective-permute-start | bytes 98312 | tf_op jit(solution)/shard_map/ppermute | solution.py:215
  10.3 0.7 %collective-permute-start.1 = (f32[16,1024]{1,0:T(8,128)S(1)}, f32[16,1024]{1,0:T(8,128)S(1)}, u32[]{:S(2)}, u32[]{:S(2)}) collective-permute-start(f32[16,1024]{1,0:T(8,128)S(1)} %constant_dynamic-update-slice_fusion), channel_id=1, source_target_pairs={{0,0},{1,3},{2,2},{3,1},{4,4},{5,7},{6,6},{7,5},{8,8},{9,11},{10,1... | collective-permute-start | bytes 196616 | tf_op jit(solution)/shard_map/ppermute | solution.py:227
  11.0 11.1 %collective-permute-start.5 = (f32[16,1024]{1,0:T(8,128)S(1)}, f32[16,1024]{1,0:T(8,128)S(1)}, u32[]{:S(2)}, u32[]{:S(2)}) collective-permute-start(f32[16,1024]{1,0:T(8,128)S(1)} %add.27), channel_id=1, source_target_pairs={{0,1},{1,12},{2,3},{3,14},{4,5},{5,8},{6,7},{7,10},{8,9},{9,4},{10... | collective-permute-start | bytes 196616 | tf_op jit(solution)/shard_map/ppermute | solution.py:234
  16.7 6.5 %collective-permute-start.4 = (f32[16,1024]{1,0:T(8,128)S(1)}, f32[16,1024]{1,0:T(8,128)S(1)}, u32[]{:S(2)}, u32[]{:S(2)}) collective-permute-start(f32[16,1024]{1,0:T(8,128)S(1)} %add.27), channel_id=1, source_target_pairs={{0,1},{1,8},{2,3},{3,10},{4,5},{5,12},{6,7},{7,14},{8,9},{9,0},{10... | collective-permute-start | bytes 196616 | tf_op jit(solution)/shard_map/ppermute | solution.py:234
  16.8 6.4 %collective-permute-start.3 = (f32[16,1024]{1,0:T(8,128)S(1)}, f32[16,1024]{1,0:T(8,128)S(1)}, u32[]{:S(2)}, u32[]{:S(2)}) collective-permute-start(f32[16,1024]{1,0:T(8,128)S(1)} %add.27), channel_id=1, source_target_pairs={{0,1},{1,4},{2,3},{3,6},{4,5},{5,0},{6,7},{7,2},{8,9},{9,12},{10,1... | collective-permute-start | bytes 196616 | tf_op jit(solution)/shard_map/ppermute | solution.py:234
  19.6 3.6 %collective-permute-start.2 = (f32[16,1024]{1,0:T(8,128)S(1)}, f32[16,1024]{1,0:T(8,128)S(1)}, u32[]{:S(2)}, u32[]{:S(2)}) collective-permute-start(f32[16,1024]{1,0:T(8,128)S(1)} %add.27), channel_id=1, source_target_pairs={{0,1},{1,0},{2,3},{3,2},{4,5},{5,4},{6,7},{7,6},{8,9},{9,8},{10,11... | collective-permute-start | bytes 196616 | tf_op jit(solution)/shard_map/ppermute | solution.py:234
  23.2 1.3 %collective-permute-start.6 = (f32[16,1024]{1,0:T(8,128)S(1)}, f32[16,1024]{1,0:T(8,128)S(1)}, u32[]{:S(2)}, u32[]{:S(2)}) collective-permute-start(f32[16,1024]{1,0:T(8,128)S(1)} %add_add_fusion.kept_ref), channel_id=1, source_target_pairs={{0,1},{1,0},{2,3},{3,2},{4,5},{5,4},{6,7},{7,6},{8,9},{9,8},{10,11... | collective-permute-start | bytes 196616 | tf_op jit(solution)/shard_map/ppermute | solution.py:215
  24.5 1.6 %copy-start.3 = (bf16[2,1024,512]{2,1,0:T(8,128)(2,1)S(1)}, bf16[2,1024,512]{2,1,0:T(8,128)(2,1)}, u32[]{:S(2)}) copy-start(bf16[2,1024,512]{2,1,0:T(8,128)(2,1)} %copy-done.2) | copy-start | bytes 6291460
  26.1 12.7 %copy-start.1 = (f32[2,1024,512]{2,1,0:T(8,128)S(1)}, f32[2,1024,512]{2,1,0:T(8,128)}, u32[]{:S(2)}) copy-start(f32[2,1024,512]{2,1,0:T(8,128)} %copy-done) | copy-start | bytes 12582916
  27.5 1.2 %collective-permute-start.7 = (f32[8,512]{1,0:T(8,128)S(1)}, f32[8,512]{1,0:T(8,128)S(1)}, u32[]{:S(2)}, u32[]{:S(2)}) collective-permute-start(f32[8,512]{1,0:T(8,128)S(1)} %get-tuple-element.12), channel_id=1, source_target_pairs={{0,1},{1,0},{2,3},{3,2},{4,5},{5,4},{6,7},{7,6},{8,9},{9,8},{10,11... | collective-permute-start | bytes 49160 | tf_op jit(solution)/shard_map/ppermute | solution.py:215
  28.7 0.7 %collective-permute-start.8 = (f32[8,512]{1,0:T(8,128)S(1)}, f32[8,512]{1,0:T(8,128)S(1)}, u32[]{:S(2)}, u32[]{:S(2)}) collective-permute-start(f32[8,512]{1,0:T(8,128)S(1)} %add.31), channel_id=1, source_target_pairs={{0,0},{1,3},{2,2},{3,1},{4,4},{5,7},{6,6},{7,5},{8,8},{9,11},{10,1... | collective-permute-start | bytes 49160 | tf_op jit(solution)/shard_map/ppermute | solution.py:227
  29.4 7.5 %collective-permute-start.12 = (f32[8,512]{1,0:T(8,128)S(1)}, f32[8,512]{1,0:T(8,128)S(1)}, u32[]{:S(2)}, u32[]{:S(2)}) collective-permute-start(f32[8,512]{1,0:T(8,128)S(1)} %add.32), channel_id=1, source_target_pairs={{0,1},{1,12},{2,3},{3,14},{4,5},{5,8},{6,7},{7,10},{8,9},{9,4},{10... | collective-permute-start | bytes 49160 | tf_op jit(solution)/shard_map/ppermute | solution.py:234
  33.3 4.1 %collective-permute-start.11 = (f32[8,512]{1,0:T(8,128)S(1)}, f32[8,512]{1,0:T(8,128)S(1)}, u32[]{:S(2)}, u32[]{:S(2)}) collective-permute-start(f32[8,512]{1,0:T(8,128)S(1)} %add.32), channel_id=1, source_target_pairs={{0,1},{1,8},{2,3},{3,10},{4,5},{5,12},{6,7},{7,14},{8,9},{9,0},{10... | collective-permute-start | bytes 49160 | tf_op jit(solution)/shard_map/ppermute | solution.py:234
  33.4 4.2 %collective-permute-start.10 = (f32[8,512]{1,0:T(8,128)S(1)}, f32[8,512]{1,0:T(8,128)S(1)}, u32[]{:S(2)}, u32[]{:S(2)}) collective-permute-start(f32[8,512]{1,0:T(8,128)S(1)} %add.32), channel_id=1, source_target_pairs={{0,1},{1,4},{2,3},{3,6},{4,5},{5,0},{6,7},{7,2},{8,9},{9,12},{10,1... | collective-permute-start | bytes 49160 | tf_op jit(solution)/shard_map/ppermute | solution.py:234
  34.4 3.1 %collective-permute-start.9 = (f32[8,512]{1,0:T(8,128)S(1)}, f32[8,512]{1,0:T(8,128)S(1)}, u32[]{:S(2)}, u32[]{:S(2)}) collective-permute-start(f32[8,512]{1,0:T(8,128)S(1)} %add.32), channel_id=1, source_target_pairs={{0,1},{1,0},{2,3},{3,2},{4,5},{5,4},{6,7},{7,6},{8,9},{9,8},{10,11... | collective-permute-start | bytes 49160 | tf_op jit(solution)/shard_map/ppermute | solution.py:234
  37.6 1.2 %collective-permute-start.13 = (f32[8,512]{1,0:T(8,128)S(1)}, f32[8,512]{1,0:T(8,128)S(1)}, u32[]{:S(2)}, u32[]{:S(2)}) collective-permute-start(f32[8,512]{1,0:T(8,128)S(1)} %add_add_fusion.1.kept_ref), channel_id=1, source_target_pairs={{0,1},{1,0},{2,3},{3,2},{4,5},{5,4},{6,7},{7,6},{8,9},{9,8},{10,11... | collective-permute-start | bytes 49160 | tf_op jit(solution)/shard_map/ppermute | solution.py:215

commit v6 on v3

--- a/solution.py
+++ b/solution.py
@@ -131,9 +131,9 @@
     return mine
 
 
-def reflect_body(mine_ref, other_ref, high_ref, low_ref, left_ref, right_ref):
+def reflect_body(scale, both_ref, high_ref, low_ref, left_ref, right_ref):
     mats, rows, cols = high_ref.shape
-    left = orthogonal(mine_ref[...], other_ref[...])
+    left = orthogonal(both_ref[0] * scale, both_ref[1] * scale)
     left_ref[...] = left
     weights = jnp.concatenate(halves(left), axis=0).astype(BF16)
     right = jnp.zeros((mats * RANK, cols), F32)
@@ -144,19 +144,19 @@
     right_ref[...] = right
 
 
-def reflect(mine, other, high, low):
+def reflect(both, high, low, scale):
     mats, rows, cols = high.shape
     return pl.pallas_call(
-        reflect_body,
+        functools.partial(reflect_body, scale),
         out_shape=(
             jax.ShapeDtypeStruct((mats * RANK, rows), F32),
             jax.ShapeDtypeStruct((mats * RANK, cols), F32),
         ),
-        in_specs=[pl.BlockSpec(memory_space=pltpu.VMEM)] * 4,
+        in_specs=[pl.BlockSpec(memory_space=pltpu.VMEM)] * 3,
         out_specs=[pl.BlockSpec(memory_space=pltpu.VMEM)] * 2,
         compiler_params=pltpu.CompilerParams(vmem_limit_bytes=24 * 2**20),
         name="reflect",
-    )(mine, other, pltpu.with_memory_space_constraint(high, pltpu.VMEM), pltpu.with_memory_space_constraint(low, pltpu.VMEM))
+    )(both, pltpu.with_memory_space_constraint(high, pltpu.VMEM), pltpu.with_memory_space_constraint(low, pltpu.VMEM))
 
 
 def finish_body(scale, left_ref, right_ref, merged_ref, update_ref, errors_ref, ubuf, ebuf, sems):
@@ -206,12 +206,16 @@
     )(left, right, pltpu.with_memory_space_constraint(merged, pltpu.VMEM))
 
 
-def swap_sum(value, axis):
-    count = lax.axis_size(axis)
+def swap(value):
+    return lax.ppermute(value, "tensor", [(0, 1), (1, 0)])
+
+
+def cross_sum(value, turn):
+    count = lax.axis_size("dp")
     step = 1
     while step < count:
-        pairs = [(index, index ^ step) for index in range(count)]
-        value = value + lax.ppermute(value, axis, pairs)
+        pairs = [(2 * at + core, 2 * (at ^ step) + 1 - core) for at in range(count) for core in range(2)]
+        value = value + turn(lax.ppermute(value, ("dp", "tensor"), pairs))
         step *= 2
     return value
 
@@ -219,10 +223,10 @@
 def body(grads, errors, seeds):
     replicas = lax.axis_size("dp")
     left_part, merged, high, low = project(seeds, grads, errors)
-    mine = swap_sum(left_part, "dp") / replicas
-    other = lax.ppermute(mine, "tensor", [(0, 1), (1, 0)])
-    left, right_part = reflect(mine, other, high, low)
-    right = swap_sum(swap_sum(right_part, "tensor"), "dp")
+    both = jnp.stack([left_part, swap(left_part)], axis=0)
+    both = cross_sum(both, lambda taken: lax.rev(taken, (0,)))
+    left, right_part = reflect(both, high, low, 1.0 / replicas)
+    right = cross_sum(right_part + swap(right_part), lambda taken: taken)
     return finish(left, right, merged, 1.0 / replicas)
 
 

time: 38.7 us -> 39 us (level)
  starting transfers between devices: 15 us -> 15.6 us
    ppermute x8, starting transfers between devices: 15 us -> 15.6 us  [the longest x6 14.7 us: cross_sum(): value = value + turn(lax.ppermute(value, ('dp', 'tensor'), pairs))]
where the time goes in v6:
time: 39 us; the launch traced here: 38.9 us
  starting transfers between devices  15.6 us (40%)
  waiting for transfers between devices  13.1 us (34%)
  Pallas kernels  9.49 us (24%)
  between operations  0.66 us (2%)
    ppermute x6, starting transfers between devices, cross_sum(): value = value + turn(lax.ppermute(value, ('dp', 'tensor'), pairs))  14.7 us
    ppermute x6, waiting for transfers between devices, cross_sum(): value = value + turn(lax.ppermute(value, ('dp', 'tensor'), pairs))  11.4 us
    pallas_call x1, Pallas kernels, project(): pl.pallas_call(project_body, out_shape=(jax.ShapeDtypeStruct((mats * RANK...  5.04 us
    pallas_call x1, Pallas kernels, finish(): pl.pallas_call(functools.partial(finish_body, scale), out_shape=(jax.Shap...  3.07 us
    ppermute x2, waiting for transfers between devices, swap(): return lax.ppermute(value, 'tensor', [(0, 1), (1, 0)])  1.75 us
    pallas_call x1, Pallas kernels, reflect(): pl.pallas_call(functools.partial(reflect_body, scale), out_shape=(jax.Sha...  1.38 us
    ppermute x2, starting transfers between devices, swap(): return lax.ppermute(value, 'tensor', [(0, 1), (1, 0)])  0.82 us
  transfers between devices with their start and end apart: 8, of which 8 were waited for; matrix products, arithmetic and copies ran while one was open for 0% of the time, Pallas kernels for 0%

profile of v6, /device:TPU:0, one launch (start us, length us, event | category | flops | bytes accessed | tf_op | source)
XLA Modules:
  0.0 38.9 jit_solution(17237507442579525536)
XLA Ops:
  0.6 5.0 %project.1 = (f32[8,1024]{1,0:T(8,128)S(1)}, f32[2,1024,512]{2,1,0:T(8,128)S(1)}, bf16[2,1024,512]{2,1,0:T(8,128)(2,1)S(1)}, bf16[2,1024,512]{2,1,0:T(8,128)(2,1)S(1)}) custom-call(s32[2]{0:T(128)} %seeds_ref.1, bf16[1,2,1024,512]{3,2,1,0:T(8,128)(2,1)} %grads_ref.1, f32[1,2,1024,512]{3,2,1,0:T(8,128)} %errors_ref.1), custom_call_target="tpu_custom_call" | custom-call | tf_op jit(solution)/shard_map/project/pallas_call | solution.py:85
  5.7 0.5 %collective-permute-start = (f32[8,1024]{1,0:T(8,128)S(1)}, f32[8,1024]{1,0:T(8,128)S(1)}, u32[]{:S(2)}, u32[]{:S(2)}) collective-permute-start(f32[8,1024]{1,0:T(8,128)S(1)} %get-tuple-element.8), channel_id=1, source_target_pairs={{0,1},{1,0},{2,3},{3,2},{4,5},{5,4},{6,7},{7,6},{8,9},{9,8},{10,11... | collective-permute-start | bytes 98312 | tf_op jit(solution)/shard_map/ppermute | solution.py:210
  6.2 0.9 %collective-permute-done = f32[8,1024]{1,0:T(8,128)S(1)} collective-permute-done((f32[8,1024]{1,0:T(8,128)S(1)}, f32[8,1024]{1,0:T(8,128)S(1)}, u32[]{:S(2)}, u32[]{:S(2)}) %collective-permute-start) | collective-permute-done | bytes 32800 | tf_op jit(solution)/shard_map/ppermute | solution.py:210
  7.1 2.6 %collective-permute-start.1 = (f32[2,8,1024]{2,1,0:T(8,128)S(1)}, f32[2,8,1024]{2,1,0:T(8,128)S(1)}, u32[]{:S(2)}, u32[]{:S(2)}) collective-permute-start(f32[2,8,1024]{2,1,0:T(8,128)S(1)} %pad_maximum_fusion), channel_id=1, source_target_pairs={{0,3},{1,2},{2,1},{3,0},{4,7},{5,6},{6,5},{7,4},{8,11},{9,10},{10,... | collective-permute-start | bytes 196616 | tf_op jit(solution)/shard_map/ppermute | solution.py:218
  9.7 2.2 %collective-permute-done.1 = f32[2,8,1024]{2,1,0:T(8,128)S(1)} collective-permute-done((f32[2,8,1024]{2,1,0:T(8,128)S(1)}, f32[2,8,1024]{2,1,0:T(8,128)S(1)}, u32[]{:S(2)}, u32[]{:S(2)}) %collective-permute-start.1) | collective-permute-done | bytes 65568 | tf_op jit(solution)/shard_map/ppermute | solution.py:218
  11.9 2.0 %collective-permute-start.2 = (f32[2,8,1024]{2,1,0:T(8,128)S(1)}, f32[2,8,1024]{2,1,0:T(8,128)S(1)}, u32[]{:S(2)}, u32[]{:S(2)}) collective-permute-start(f32[2,8,1024]{2,1,0:T(8,128)S(1)} %reverse_add_fusion.2), channel_id=1, source_target_pairs={{0,5},{1,4},{2,7},{3,6},{4,1},{5,0},{6,3},{7,2},{8,13},{9,12},{10,... | collective-permute-start | bytes 196616 | tf_op jit(solution)/shard_map/ppermute | solution.py:218
  13.9 2.2 %collective-permute-done.2 = f32[2,8,1024]{2,1,0:T(8,128)S(1)} collective-permute-done((f32[2,8,1024]{2,1,0:T(8,128)S(1)}, f32[2,8,1024]{2,1,0:T(8,128)S(1)}, u32[]{:S(2)}, u32[]{:S(2)}) %collective-permute-start.2) | collective-permute-done | bytes 65568 | tf_op jit(solution)/shard_map/ppermute | solution.py:218
  16.1 3.0 %collective-permute-start.3 = (f32[2,8,1024]{2,1,0:T(8,128)S(1)}, f32[2,8,1024]{2,1,0:T(8,128)S(1)}, u32[]{:S(2)}, u32[]{:S(2)}) collective-permute-start(f32[2,8,1024]{2,1,0:T(8,128)S(1)} %reverse_add_fusion.1), channel_id=1, source_target_pairs={{0,9},{1,8},{2,11},{3,10},{4,13},{5,12},{6,15},{7,14},{8,1},{9,0},... | collective-permute-start | bytes 196616 | tf_op jit(solution)/shard_map/ppermute | solution.py:218
  19.1 2.2 %collective-permute-done.3 = f32[2,8,1024]{2,1,0:T(8,128)S(1)} collective-permute-done((f32[2,8,1024]{2,1,0:T(8,128)S(1)}, f32[2,8,1024]{2,1,0:T(8,128)S(1)}, u32[]{:S(2)}, u32[]{:S(2)}) %collective-permute-start.3) | collective-permute-done | bytes 65568 | tf_op jit(solution)/shard_map/ppermute | solution.py:218
  21.3 1.4 %reflect.1 = (f32[8,1024]{1,0:T(8,128)S(1)}, f32[8,512]{1,0:T(8,128)S(1)}) custom-call(f32[2,8,1024]{2,1,0:T(8,128)S(1)} %reverse_add_fusion.both_ref, bf16[2,1024,512]{2,1,0:T(8,128)(2,1)S(1)} %get-tuple-element.9.high_ref, bf16[2,1024,512]{2,1,0:T(8,128)(2,1)S(1)} %get-tuple-element.10.low_ref), custom_call_target="tpu_custom_call" | custom-call | tf_op jit(solution)/shard_map/reflect/pallas_call | solution.py:149
  22.6 0.3 collective-permute-start.4
  22.9 0.9 %collective-permute-done.4 = f32[8,512]{1,0:T(8,128)S(1)} collective-permute-done((f32[8,512]{1,0:T(8,128)S(1)}, f32[8,512]{1,0:T(8,128)S(1)}, u32[]{:S(2)}, u32[]{:S(2)}) %collective-permute-start.4) | collective-permute-done | bytes 16416 | tf_op jit(solution)/shard_map/ppermute | solution.py:210
  23.8 3.1 %collective-permute-start.5 = (f32[8,512]{1,0:T(8,128)S(1)}, f32[8,512]{1,0:T(8,128)S(1)}, u32[]{:S(2)}, u32[]{:S(2)}) collective-permute-start(f32[8,512]{1,0:T(8,128)S(1)} %add.24), channel_id=1, source_target_pairs={{0,3},{1,2},{2,1},{3,0},{4,7},{5,6},{6,5},{7,4},{8,11},{9,10},{10,... | collective-permute-start | bytes 49160 | tf_op jit(solution)/shard_map/ppermute | solution.py:218
  27.0 1.4 %collective-permute-done.5 = f32[8,512]{1,0:T(8,128)S(1)} collective-permute-done((f32[8,512]{1,0:T(8,128)S(1)}, f32[8,512]{1,0:T(8,128)S(1)}, u32[]{:S(2)}, u32[]{:S(2)}) %collective-permute-start.5) | collective-permute-done | bytes 16416 | tf_op jit(solution)/shard_map/ppermute | solution.py:218
  28.4 1.2 %collective-permute-start.6 = (f32[8,512]{1,0:T(8,128)S(1)}, f32[8,512]{1,0:T(8,128)S(1)}, u32[]{:S(2)}, u32[]{:S(2)}) collective-permute-start(f32[8,512]{1,0:T(8,128)S(1)} %add.25), channel_id=1, source_target_pairs={{0,5},{1,4},{2,7},{3,6},{4,1},{5,0},{6,3},{7,2},{8,13},{9,12},{10,... | collective-permute-start | bytes 49160 | tf_op jit(solution)/shard_map/ppermute | solution.py:218
  29.7 1.9 %collective-permute-done.6 = f32[8,512]{1,0:T(8,128)S(1)} collective-permute-done((f32[8,512]{1,0:T(8,128)S(1)}, f32[8,512]{1,0:T(8,128)S(1)}, u32[]{:S(2)}, u32[]{:S(2)}) %collective-permute-start.6) | collective-permute-done | bytes 16416 | tf_op jit(solution)/shard_map/ppermute | solution.py:218
  31.6 2.8 %collective-permute-start.7 = (f32[8,512]{1,0:T(8,128)S(1)}, f32[8,512]{1,0:T(8,128)S(1)}, u32[]{:S(2)}, u32[]{:S(2)}) collective-permute-start(f32[8,512]{1,0:T(8,128)S(1)} %add.26), channel_id=1, source_target_pairs={{0,9},{1,8},{2,11},{3,10},{4,13},{5,12},{6,15},{7,14},{8,1},{9,0},... | collective-permute-start | bytes 49160 | tf_op jit(solution)/shard_map/ppermute | solution.py:218
  34.4 1.4 %collective-permute-done.7 = f32[8,512]{1,0:T(8,128)S(1)} collective-permute-done((f32[8,512]{1,0:T(8,128)S(1)}, f32[8,512]{1,0:T(8,128)S(1)}, u32[]{:S(2)}, u32[]{:S(2)}) %collective-permute-start.7) | collective-permute-done | bytes 16416 | tf_op jit(solution)/shard_map/ppermute | solution.py:218
  35.8 3.1 %finish.1 = (bf16[2,1024,512]{2,1,0:T(8,128)(2,1)}, f32[1,2,1024,512]{3,2,1,0:T(8,128)}) custom-call(f32[8,1024]{1,0:T(8,128)S(1)} %get-tuple-element.11.left_ref, f32[8,512]{1,0:T(8,128)S(1)} %add.27.right_ref, f32[2,1024,512]{2,1,0:T(8,128)S(1)} %get-tuple-element.13.merged_ref), custom_call_target="tpu_custom_call" | custom-call | tf_op jit(solution)/shard_map/finish/pallas_call | solution.py:191
  (8 shorter events, 0.1 us)
Async XLA Ops:
  5.7 1.4 %collective-permute-start = (f32[8,1024]{1,0:T(8,128)S(1)}, f32[8,1024]{1,0:T(8,128)S(1)}, u32[]{:S(2)}, u32[]{:S(2)}) collective-permute-start(f32[8,1024]{1,0:T(8,128)S(1)} %get-tuple-element.8), channel_id=1, source_target_pairs={{0,1},{1,0},{2,3},{3,2},{4,5},{5,4},{6,7},{7,6},{8,9},{9,8},{10,11... | collective-permute-start | bytes 98312 | tf_op jit(solution)/shard_map/ppermute | solution.py:210
  7.1 4.8 %collective-permute-start.1 = (f32[2,8,1024]{2,1,0:T(8,128)S(1)}, f32[2,8,1024]{2,1,0:T(8,128)S(1)}, u32[]{:S(2)}, u32[]{:S(2)}) collective-permute-start(f32[2,8,1024]{2,1,0:T(8,128)S(1)} %pad_maximum_fusion), channel_id=1, source_target_pairs={{0,3},{1,2},{2,1},{3,0},{4,7},{5,6},{6,5},{7,4},{8,11},{9,10},{10,... | collective-permute-start | bytes 196616 | tf_op jit(solution)/shard_map/ppermute | solution.py:218
  11.9 4.2 %collective-permute-start.2 = (f32[2,8,1024]{2,1,0:T(8,128)S(1)}, f32[2,8,1024]{2,1,0:T(8,128)S(1)}, u32[]{:S(2)}, u32[]{:S(2)}) collective-permute-start(f32[2,8,1024]{2,1,0:T(8,128)S(1)} %reverse_add_fusion.2), channel_id=1, source_target_pairs={{0,5},{1,4},{2,7},{3,6},{4,1},{5,0},{6,3},{7,2},{8,13},{9,12},{10,... | collective-permute-start | bytes 196616 | tf_op jit(solution)/shard_map/ppermute | solution.py:218
  16.1 5.2 %collective-permute-start.3 = (f32[2,8,1024]{2,1,0:T(8,128)S(1)}, f32[2,8,1024]{2,1,0:T(8,128)S(1)}, u32[]{:S(2)}, u32[]{:S(2)}) collective-permute-start(f32[2,8,1024]{2,1,0:T(8,128)S(1)} %reverse_add_fusion.1), channel_id=1, source_target_pairs={{0,9},{1,8},{2,11},{3,10},{4,13},{5,12},{6,15},{7,14},{8,1},{9,0},... | collective-permute-start | bytes 196616 | tf_op jit(solution)/shard_map/ppermute | solution.py:218
  22.6 1.2 %collective-permute-start.4 = (f32[8,512]{1,0:T(8,128)S(1)}, f32[8,512]{1,0:T(8,128)S(1)}, u32[]{:S(2)}, u32[]{:S(2)}) collective-permute-start(f32[8,512]{1,0:T(8,128)S(1)} %get-tuple-element.12), channel_id=1, source_target_pairs={{0,1},{1,0},{2,3},{3,2},{4,5},{5,4},{6,7},{7,6},{8,9},{9,8},{10,11... | collective-permute-start | bytes 49160 | tf_op jit(solution)/shard_map/ppermute | solution.py:210
  23.8 4.6 %collective-permute-start.5 = (f32[8,512]{1,0:T(8,128)S(1)}, f32[8,512]{1,0:T(8,128)S(1)}, u32[]{:S(2)}, u32[]{:S(2)}) collective-permute-start(f32[8,512]{1,0:T(8,128)S(1)} %add.24), channel_id=1, source_target_pairs={{0,3},{1,2},{2,1},{3,0},{4,7},{5,6},{6,5},{7,4},{8,11},{9,10},{10,... | collective-permute-start | bytes 49160 | tf_op jit(solution)/shard_map/ppermute | solution.py:218
  28.4 3.2 %collective-permute-start.6 = (f32[8,512]{1,0:T(8,128)S(1)}, f32[8,512]{1,0:T(8,128)S(1)}, u32[]{:S(2)}, u32[]{:S(2)}) collective-permute-start(f32[8,512]{1,0:T(8,128)S(1)} %add.25), channel_id=1, source_target_pairs={{0,5},{1,4},{2,7},{3,6},{4,1},{5,0},{6,3},{7,2},{8,13},{9,12},{10,... | collective-permute-start | bytes 49160 | tf_op jit(solution)/shard_map/ppermute | solution.py:218
  31.6 4.2 %collective-permute-start.7 = (f32[8,512]{1,0:T(8,128)S(1)}, f32[8,512]{1,0:T(8,128)S(1)}, u32[]{:S(2)}, u32[]{:S(2)}) collective-permute-start(f32[8,512]{1,0:T(8,128)S(1)} %add.26), channel_id=1, source_target_pairs={{0,9},{1,8},{2,11},{3,10},{4,13},{5,12},{6,15},{7,14},{8,1},{9,0},... | collective-permute-start | bytes 49160 | tf_op jit(solution)/shard_map/ppermute | solution.py:218

commit v7 on v3

--- a/solution.py
+++ b/solution.py
@@ -41,23 +41,20 @@
     return jnp.where(row // RANK == mat, part, value)
 
 
-def project_body(seeds_ref, grads_ref, errors_ref, left_ref, merged_ref, high_ref, low_ref, seed, gbuf, ebuf, seed_sem, sems):
+def project_body(seeds_ref, grads_ref, errors_ref, left_ref, gbuf, ebuf, seed, seed_sem, sems):
     _, mats, rows, cols = grads_ref.shape
     size = rows // CHUNKS
     seed_copy = pltpu.make_async_copy(seeds_ref, seed, seed_sem)
     seed_copy.start()
     copies = []
-    for mat in range(mats):
-        for chunk in range(CHUNKS):
-            at = pl.ds(chunk * size, size)
-            slot = mat * CHUNKS + chunk
-            pair = (
-                pltpu.make_async_copy(grads_ref.at[0, mat, at], gbuf.at[mat, at], sems.at[0, slot]),
-                pltpu.make_async_copy(errors_ref.at[0, mat, at], ebuf.at[mat, at], sems.at[1, slot]),
-            )
-            for copy in pair:
-                copy.start()
-            copies.append(pair)
+    for chunk in range(CHUNKS):
+        at = pl.ds(chunk * size, size)
+        for mat in range(mats):
+            slot = chunk * mats + mat
+            copies.append(pltpu.make_async_copy(grads_ref.at[0, mat, at], gbuf.at[mat, at], sems.at[0, slot]))
+            copies.append(pltpu.make_async_copy(errors_ref.at[0, mat, at], ebuf.at[mat, at], sems.at[1, slot]))
+    for copy in copies:
+        copy.start()
     seed_copy.wait()
     start = start_rows(seed, mats, cols)
     weights = jnp.concatenate(halves(start), axis=0).astype(BF16)
@@ -65,15 +62,12 @@
     for chunk in range(CHUNKS):
         at = pl.ds(chunk * size, size)
         left = jnp.zeros((mats * RANK, size), F32)
+        for copy in copies[2 * mats * chunk : 2 * mats * (chunk + 1)]:
+            copy.wait()
         for mat in range(mats):
-            for copy in copies[mat * CHUNKS + chunk]:
-                copy.wait()
             value = gbuf[mat, at].astype(F32) + ebuf[mat, at]
             high = value.astype(BF16)
             low = (value - high.astype(F32)).astype(BF16)
-            merged_ref[mat, at] = value
-            high_ref[mat, at] = high
-            low_ref[mat, at] = low
             product = lax.dot_general(weights, high, dims, preferred_element_type=F32)
             product = product + lax.dot_general(weights, low, dims, preferred_element_type=F32)
             left = fold(mat, left, product)
@@ -86,22 +80,47 @@
         project_body,
         out_shape=(
             jax.ShapeDtypeStruct((mats * RANK, rows), F32),
+            pltpu.VMEM((mats, rows, cols), BF16),
             pltpu.VMEM((mats, rows, cols), F32),
-            pltpu.VMEM((mats, rows, cols), BF16),
-            pltpu.VMEM((mats, rows, cols), BF16),
         ),
         in_specs=[pl.BlockSpec(memory_space=pltpu.HBM)] * 3,
-        out_specs=[pl.BlockSpec(memory_space=pltpu.VMEM)] * 4,
+        out_specs=[pl.BlockSpec(memory_space=pltpu.VMEM)] * 3,
         scratch_shapes=[
             pltpu.SMEM(seeds.shape, seeds.dtype),
-            pltpu.VMEM((mats, rows, cols), BF16),
-            pltpu.VMEM((mats, rows, cols), F32),
             pltpu.SemaphoreType.DMA,
             pltpu.SemaphoreType.DMA((2, mats * CHUNKS)),
         ],
-        compiler_params=pltpu.CompilerParams(vmem_limit_bytes=24 * 2**20),
+        compiler_params=pltpu.CompilerParams(vmem_limit_bytes=16 * 2**20),
         name="project",
     )(*[pltpu.with_memory_space_constraint(value, pltpu.HBM) for value in (seeds, grads, errors)])
+
+
+def merge_body(grads_ref, errors_ref, merged_ref, high_ref, low_ref):
+    mats, rows, cols = grads_ref.shape
+    size = 64
+
+    @pl.loop(0, rows // size)
+    def _(step):
+        at = pl.ds(pl.multiple_of(step * size, size), size)
+        for mat in range(mats):
+            value = grads_ref[mat, at].astype(F32) + errors_ref[mat, at]
+            high = value.astype(BF16)
+            merged_ref[mat, at] = value
+            high_ref[mat, at] = high
+            low_ref[mat, at] = (value - high.astype(F32)).astype(BF16)
+
+
+def merge(grads, errors):
+    shape = grads.shape
+    return pl.pallas_call(
+        merge_body,
+        out_shape=(pltpu.VMEM(shape, F32), pltpu.VMEM(shape, BF16), pltpu.VMEM(shape, BF16)),
+        in_specs=[pl.BlockSpec(memory_space=pltpu.VMEM)] * 2,
+        out_specs=[pl.BlockSpec(memory_space=pltpu.VMEM)] * 3,
+        compiler_params=pltpu.CompilerParams(vmem_limit_bytes=16 * 2**20),
+        cost_estimate=pl.CostEstimate(flops=3 * grads.size, bytes_accessed=14 * grads.size, transcendentals=0),
+        name="merge",
+    )(*[pltpu.with_memory_space_constraint(value, pltpu.VMEM) for value in (grads, errors)])
 
 
 def spread(column, count):
@@ -131,9 +150,9 @@
     return mine
 
 
-def reflect_body(mine_ref, other_ref, high_ref, low_ref, left_ref, right_ref):
+def reflect_body(scale, mine_ref, other_ref, high_ref, low_ref, left_ref, right_ref):
     mats, rows, cols = high_ref.shape
-    left = orthogonal(mine_ref[...], other_ref[...])
+    left = orthogonal(mine_ref[...] * scale, other_ref[...] * scale)
     left_ref[...] = left
     weights = jnp.concatenate(halves(left), axis=0).astype(BF16)
     right = jnp.zeros((mats * RANK, cols), F32)
@@ -144,10 +163,10 @@
     right_ref[...] = right
 
 
-def reflect(mine, other, high, low):
+def reflect(mine, other, high, low, scale):
     mats, rows, cols = high.shape
     return pl.pallas_call(
-        reflect_body,
+        functools.partial(reflect_body, scale),
         out_shape=(
             jax.ShapeDtypeStruct((mats * RANK, rows), F32),
             jax.ShapeDtypeStruct((mats * RANK, cols), F32),
@@ -206,23 +225,31 @@
     )(left, right, pltpu.with_memory_space_constraint(merged, pltpu.VMEM))
 
 
+def swap(value, axis, step):
+    pairs = [(index, index ^ step) for index in range(lax.axis_size(axis))]
+    return lax.ppermute(value, axis, pairs)
+
+
 def swap_sum(value, axis):
     count = lax.axis_size(axis)
+    last = max(count // 4, 1)
     step = 1
-    while step < count:
-        pairs = [(index, index ^ step) for index in range(count)]
-        value = value + lax.ppermute(value, axis, pairs)
+    while step < last:
+        value = value + swap(value, axis, step)
         step *= 2
-    return value
+    terms = [value] + [swap(value, axis, offset) for offset in range(last, count, last)]
+    while len(terms) > 1:
+        terms = [terms[at] + terms[at + 1] for at in range(0, len(terms), 2)]
+    return terms[0]
 
 
 def body(grads, errors, seeds):
     replicas = lax.axis_size("dp")
-    left_part, merged, high, low = project(seeds, grads, errors)
-    mine = swap_sum(left_part, "dp") / replicas
-    other = lax.ppermute(mine, "tensor", [(0, 1), (1, 0)])
-    left, right_part = reflect(mine, other, high, low)
-    right = swap_sum(swap_sum(right_part, "tensor"), "dp")
+    left_part, grads, errors = project(seeds, grads, errors)
+    merged, high, low = merge(grads, errors)
+    mine = swap_sum(left_part, "dp")
+    left, right_part = reflect(mine, swap(mine, "tensor", 1), high, low, 1.0 / replicas)
+    right = swap_sum(right_part + swap(right_part, "tensor", 1), "dp")
     return finish(left, right, merged, 1.0 / replicas)
 
 

time: 38.7 us -> 35 us (0.904)
  waiting for transfers between devices: 13.3 us -> 11.5 us
  starting transfers between devices: 15 us -> 13.9 us
  Pallas kernels: 9.48 us -> 8.67 us
    ppermute x8 -> x10, waiting for transfers between devices: 13.3 us -> 11.5 us  [swap(): return lax.ppermute(value, axis, pairs)]
    pallas_call x1, Pallas kernels: 5.04 us -> 3.35 us  [project(): pl.pallas_call(project_body, out_shape=(jax.ShapeDtypeStruct((mats * RANK...]
    ppermute x8 -> x10, starting transfers between devices: 15 us -> 13.9 us  [swap(): return lax.ppermute(value, axis, pairs)]
    pallas_call x1 -> x2, Pallas kernels: 1.37 us -> 2.25 us  [the longest x1 1.38 us: reflect(): pl.pallas_call(functools.partial(reflect_body, scale), out_shape=(jax.Sha...]
  transfers between devices with their start and end apart: 8 -> 10, of which waited for: 8 -> 9; matrix products, arithmetic and copies ran while one was open for 0% -> 0% of each run, Pallas kernels for 0% -> 3%
where the time goes in v7:
time: 35 us; the launch traced here: 34.8 us
  starting transfers between devices  13.9 us (40%)
  waiting for transfers between devices  11.5 us (33%)
  Pallas kernels  8.67 us (25%)
  between operations  0.67 us (2%)
    ppermute x10, starting transfers between devices, swap(): return lax.ppermute(value, axis, pairs)  13.9 us
    ppermute x10, waiting for transfers between devices, swap(): return lax.ppermute(value, axis, pairs)  11.5 us
    pallas_call x1, Pallas kernels, project(): pl.pallas_call(project_body, out_shape=(jax.ShapeDtypeStruct((mats * RANK...  3.35 us
    pallas_call x1, Pallas kernels, finish(): pl.pallas_call(functools.partial(finish_body, scale), out_shape=(jax.Shap...  3.07 us
    pallas_call x1, Pallas kernels, reflect(): pl.pallas_call(functools.partial(reflect_body, scale), out_shape=(jax.Sha...  1.38 us
    pallas_call x1, Pallas kernels, merge(): pl.pallas_call(merge_body, out_shape=(pltpu.VMEM(shape, F32), pltpu.VMEM(...  0.87 us
  transfers between devices with their start and end apart: 10, of which 9 were waited for; matrix products, arithmetic and copies ran while one was open for 0% of the time, Pallas kernels for 3%

profile of v7, /device:TPU:0, one launch (start us, length us, event | category | flops | bytes accessed | tf_op | source)
XLA Modules:
  0.0 34.8 jit_solution(6753186940586176477)
XLA Ops:
  0.6 3.4 %project.1 = (f32[8,1024]{1,0:T(8,128)S(1)}, bf16[2,1024,512]{2,1,0:T(8,128)(2,1)S(1)}, f32[2,1024,512]{2,1,0:T(8,128)S(1)}) custom-call(s32[2]{0:T(128)} %seeds_ref.1, bf16[1,2,1024,512]{3,2,1,0:T(8,128)(2,1)} %grads_ref.1, f32[1,2,1024,512]{3,2,1,0:T(8,128)} %errors_ref.1), custom_call_target="tpu_custom_call" | custom-call | tf_op jit(solution)/shard_map/project/pallas_call | solution.py:79
  4.0 3.0 %collective-permute-start = (f32[8,1024]{1,0:T(8,128)S(1)}, f32[8,1024]{1,0:T(8,128)S(1)}, u32[]{:S(2)}, u32[]{:S(2)}) collective-permute-start(f32[8,1024]{1,0:T(8,128)S(1)} %get-tuple-element.10), channel_id=1, source_target_pairs={{0,2},{2,0},{4,6},{6,4},{8,10},{10,8},{12,14},{14,12},{1,3},{3,1},... | collective-permute-start | bytes 98312 | tf_op jit(solution)/shard_map/ppermute | solution.py:230
  7.0 1.9 %collective-permute-done = f32[8,1024]{1,0:T(8,128)S(1)} collective-permute-done((f32[8,1024]{1,0:T(8,128)S(1)}, f32[8,1024]{1,0:T(8,128)S(1)}, u32[]{:S(2)}, u32[]{:S(2)}) %collective-permute-start) | collective-permute-done | bytes 32800 | tf_op jit(solution)/shard_map/ppermute | solution.py:230
  8.9 4.1 %collective-permute-start.3 = (f32[8,1024]{1,0:T(8,128)S(1)}, f32[8,1024]{1,0:T(8,128)S(1)}, u32[]{:S(2)}, u32[]{:S(2)}) collective-permute-start(f32[8,1024]{1,0:T(8,128)S(1)} %add.27), channel_id=1, source_target_pairs={{0,12},{2,14},{4,8},{6,10},{8,4},{10,6},{12,0},{14,2},{1,13},{3,15... | collective-permute-start | bytes 98312 | tf_op jit(solution)/shard_map/ppermute | solution.py:230
  13.0 0.0 collective-permute-start.2
  13.0 0.6 %collective-permute-start.1 = (f32[8,1024]{1,0:T(8,128)S(1)}, f32[8,1024]{1,0:T(8,128)S(1)}, u32[]{:S(2)}, u32[]{:S(2)}) collective-permute-start(f32[8,1024]{1,0:T(8,128)S(1)} %add.27), channel_id=1, source_target_pairs={{0,4},{2,6},{4,0},{6,2},{8,12},{10,14},{12,8},{14,10},{1,5},{3,7},... | collective-permute-start | bytes 98312 | tf_op jit(solution)/shard_map/ppermute | solution.py:230
  13.7 1.3 %collective-permute-done.3 = f32[8,1024]{1,0:T(8,128)S(1)} collective-permute-done((f32[8,1024]{1,0:T(8,128)S(1)}, f32[8,1024]{1,0:T(8,128)S(1)}, u32[]{:S(2)}, u32[]{:S(2)}) %collective-permute-start.3) | collective-permute-done | bytes 32800 | tf_op jit(solution)/shard_map/ppermute | solution.py:230
  15.0 2.9 %collective-permute-done.2 = f32[8,1024]{1,0:T(8,128)S(1)} collective-permute-done((f32[8,1024]{1,0:T(8,128)S(1)}, f32[8,1024]{1,0:T(8,128)S(1)}, u32[]{:S(2)}, u32[]{:S(2)}) %collective-permute-start.2) | collective-permute-done | bytes 32800 | tf_op jit(solution)/shard_map/ppermute | solution.py:230
  17.8 0.0 collective-permute-done.1
  17.9 0.1 collective-permute-start.4
  17.9 0.9 %merge.1 = (f32[2,1024,512]{2,1,0:T(8,128)S(1)}, bf16[2,1024,512]{2,1,0:T(8,128)(2,1)S(1)}, bf16[2,1024,512]{2,1,0:T(8,128)(2,1)S(1)}) custom-call(bf16[2,1024,512]{2,1,0:T(8,128)(2,1)S(1)} %get-tuple-element.11.grads_ref, f32[2,1024,512]{2,1,0:T(8,128)S(1)} %get-tuple-element.12.errors_ref), custom_call_target="tpu_custom_call" | custom-call | flops 3145728 | bytes 14680064 | tf_op jit(solution)/shard_map/merge/pallas_call | solution.py:115
  18.8 0.3 collective-permute-done.4.other_ref
  19.1 1.4 %reflect.1 = (f32[8,1024]{1,0:T(8,128)S(1)}, f32[8,512]{1,0:T(8,128)S(1)}) custom-call(f32[8,1024]{1,0:T(8,128)S(1)} %add_add_fusion.mine_ref, f32[8,1024]{1,0:T(8,128)S(1)} %collective-permute-done.4.other_ref, bf16[2,1024,512]{2,1,0:T(8,128)(2,1)S(1)} %get-tuple-element.13.high_ref, bf16[2,1024,512]{2,1,0:T(8,128)(2,1)S(1)} %get-tuple-element.14.low_ref), custom_call_target="tpu_custom_call" | custom-call | tf_op jit(solution)/shard_map/reflect/pallas_call | solution.py:168
  20.5 0.2 collective-permute-start.5
  20.7 1.0 %collective-permute-done.5 = f32[8,512]{1,0:T(8,128)S(1)} collective-permute-done((f32[8,512]{1,0:T(8,128)S(1)}, f32[8,512]{1,0:T(8,128)S(1)}, u32[]{:S(2)}, u32[]{:S(2)}) %collective-permute-start.5) | collective-permute-done | bytes 16416 | tf_op jit(solution)/shard_map/ppermute | solution.py:230
  21.7 1.5 %collective-permute-start.6 = (f32[8,512]{1,0:T(8,128)S(1)}, f32[8,512]{1,0:T(8,128)S(1)}, u32[]{:S(2)}, u32[]{:S(2)}) collective-permute-start(f32[8,512]{1,0:T(8,128)S(1)} %add.31), channel_id=1, source_target_pairs={{0,2},{2,0},{4,6},{6,4},{8,10},{10,8},{12,14},{14,12},{1,3},{3,1},... | collective-permute-start | bytes 49160 | tf_op jit(solution)/shard_map/ppermute | solution.py:230
  23.2 2.2 %collective-permute-done.6 = f32[8,512]{1,0:T(8,128)S(1)} collective-permute-done((f32[8,512]{1,0:T(8,128)S(1)}, f32[8,512]{1,0:T(8,128)S(1)}, u32[]{:S(2)}, u32[]{:S(2)}) %collective-permute-start.6) | collective-permute-done | bytes 16416 | tf_op jit(solution)/shard_map/ppermute | solution.py:230
  25.5 1.5 %collective-permute-start.9 = (f32[8,512]{1,0:T(8,128)S(1)}, f32[8,512]{1,0:T(8,128)S(1)}, u32[]{:S(2)}, u32[]{:S(2)}) collective-permute-start(f32[8,512]{1,0:T(8,128)S(1)} %add.32), channel_id=1, source_target_pairs={{0,12},{2,14},{4,8},{6,10},{8,4},{10,6},{12,0},{14,2},{1,13},{3,15... | collective-permute-start | bytes 49160 | tf_op jit(solution)/shard_map/ppermute | solution.py:230
  26.9 0.6 %collective-permute-start.8 = (f32[8,512]{1,0:T(8,128)S(1)}, f32[8,512]{1,0:T(8,128)S(1)}, u32[]{:S(2)}, u32[]{:S(2)}) collective-permute-start(f32[8,512]{1,0:T(8,128)S(1)} %add.32), channel_id=1, source_target_pairs={{0,8},{2,10},{4,12},{6,14},{8,0},{10,2},{12,4},{14,6},{1,9},{3,11}... | collective-permute-start | bytes 49160 | tf_op jit(solution)/shard_map/ppermute | solution.py:230
  27.5 2.3 %collective-permute-start.7 = (f32[8,512]{1,0:T(8,128)S(1)}, f32[8,512]{1,0:T(8,128)S(1)}, u32[]{:S(2)}, u32[]{:S(2)}) collective-permute-start(f32[8,512]{1,0:T(8,128)S(1)} %add.32), channel_id=1, source_target_pairs={{0,4},{2,6},{4,0},{6,2},{8,12},{10,14},{12,8},{14,10},{1,5},{3,7},... | collective-permute-start | bytes 49160 | tf_op jit(solution)/shard_map/ppermute | solution.py:230
  29.8 1.1 %collective-permute-done.9 = f32[8,512]{1,0:T(8,128)S(1)} collective-permute-done((f32[8,512]{1,0:T(8,128)S(1)}, f32[8,512]{1,0:T(8,128)S(1)}, u32[]{:S(2)}, u32[]{:S(2)}) %collective-permute-start.9) | collective-permute-done | bytes 16416 | tf_op jit(solution)/shard_map/ppermute | solution.py:230
  31.0 0.6 %collective-permute-done.8 = f32[8,512]{1,0:T(8,128)S(1)} collective-permute-done((f32[8,512]{1,0:T(8,128)S(1)}, f32[8,512]{1,0:T(8,128)S(1)}, u32[]{:S(2)}, u32[]{:S(2)}) %collective-permute-start.8) | collective-permute-done | bytes 16416 | tf_op jit(solution)/shard_map/ppermute | solution.py:230
  31.6 0.2 collective-permute-done.7
  31.7 3.1 %finish.1 = (bf16[2,1024,512]{2,1,0:T(8,128)(2,1)}, f32[1,2,1024,512]{3,2,1,0:T(8,128)}) custom-call(f32[8,1024]{1,0:T(8,128)S(1)} %get-tuple-element.15.left_ref, f32[8,512]{1,0:T(8,128)S(1)} %add_add_fusion.1.right_ref, f32[2,1024,512]{2,1,0:T(8,128)S(1)} %get-tuple-element.17.merged_ref), custom_call_target="tpu_custom_call" | custom-call | tf_op jit(solution)/shard_map/finish/pallas_call | solution.py:210
  (5 shorter events, 0.0 us)
Async XLA Ops:
  4.0 4.9 %collective-permute-start = (f32[8,1024]{1,0:T(8,128)S(1)}, f32[8,1024]{1,0:T(8,128)S(1)}, u32[]{:S(2)}, u32[]{:S(2)}) collective-permute-start(f32[8,1024]{1,0:T(8,128)S(1)} %get-tuple-element.10), channel_id=1, source_target_pairs={{0,2},{2,0},{4,6},{6,4},{8,10},{10,8},{12,14},{14,12},{1,3},{3,1},... | collective-permute-start | bytes 98312 | tf_op jit(solution)/shard_map/ppermute | solution.py:230
  8.9 6.0 %collective-permute-start.3 = (f32[8,1024]{1,0:T(8,128)S(1)}, f32[8,1024]{1,0:T(8,128)S(1)}, u32[]{:S(2)}, u32[]{:S(2)}) collective-permute-start(f32[8,1024]{1,0:T(8,128)S(1)} %add.27), channel_id=1, source_target_pairs={{0,12},{2,14},{4,8},{6,10},{8,4},{10,6},{12,0},{14,2},{1,13},{3,15... | collective-permute-start | bytes 98312 | tf_op jit(solution)/shard_map/ppermute | solution.py:230
  13.0 4.8 %collective-permute-start.2 = (f32[8,1024]{1,0:T(8,128)S(1)}, f32[8,1024]{1,0:T(8,128)S(1)}, u32[]{:S(2)}, u32[]{:S(2)}) collective-permute-start(f32[8,1024]{1,0:T(8,128)S(1)} %add.27), channel_id=1, source_target_pairs={{0,8},{2,10},{4,12},{6,14},{8,0},{10,2},{12,4},{14,6},{1,9},{3,11}... | collective-permute-start | bytes 98312 | tf_op jit(solution)/shard_map/ppermute | solution.py:230
  13.0 4.8 %collective-permute-start.1 = (f32[8,1024]{1,0:T(8,128)S(1)}, f32[8,1024]{1,0:T(8,128)S(1)}, u32[]{:S(2)}, u32[]{:S(2)}) collective-permute-start(f32[8,1024]{1,0:T(8,128)S(1)} %add.27), channel_id=1, source_target_pairs={{0,4},{2,6},{4,0},{6,2},{8,12},{10,14},{12,8},{14,10},{1,5},{3,7},... | collective-permute-start | bytes 98312 | tf_op jit(solution)/shard_map/ppermute | solution.py:230
  17.9 1.3 %collective-permute-start.4 = (f32[8,1024]{1,0:T(8,128)S(1)}, f32[8,1024]{1,0:T(8,128)S(1)}, u32[]{:S(2)}, u32[]{:S(2)}) collective-permute-start(f32[8,1024]{1,0:T(8,128)S(1)} %add_add_fusion.mine_ref), channel_id=1, source_target_pairs={{0,1},{1,0},{2,3},{3,2},{4,5},{5,4},{6,7},{7,6},{8,9},{9,8},{10,11... | collective-permute-start | bytes 98312 | tf_op jit(solution)/shard_map/ppermute | solution.py:230
  20.5 1.2 %collective-permute-start.5 = (f32[8,512]{1,0:T(8,128)S(1)}, f32[8,512]{1,0:T(8,128)S(1)}, u32[]{:S(2)}, u32[]{:S(2)}) collective-permute-start(f32[8,512]{1,0:T(8,128)S(1)} %get-tuple-element.16), channel_id=1, source_target_pairs={{0,1},{1,0},{2,3},{3,2},{4,5},{5,4},{6,7},{7,6},{8,9},{9,8},{10,11... | collective-permute-start | bytes 49160 | tf_op jit(solution)/shard_map/ppermute | solution.py:230
  21.7 3.7 %collective-permute-start.6 = (f32[8,512]{1,0:T(8,128)S(1)}, f32[8,512]{1,0:T(8,128)S(1)}, u32[]{:S(2)}, u32[]{:S(2)}) collective-permute-start(f32[8,512]{1,0:T(8,128)S(1)} %add.31), channel_id=1, source_target_pairs={{0,2},{2,0},{4,6},{6,4},{8,10},{10,8},{12,14},{14,12},{1,3},{3,1},... | collective-permute-start | bytes 49160 | tf_op jit(solution)/shard_map/ppermute | solution.py:230
  25.5 5.5 %collective-permute-start.9 = (f32[8,512]{1,0:T(8,128)S(1)}, f32[8,512]{1,0:T(8,128)S(1)}, u32[]{:S(2)}, u32[]{:S(2)}) collective-permute-start(f32[8,512]{1,0:T(8,128)S(1)} %add.32), channel_id=1, source_target_pairs={{0,12},{2,14},{4,8},{6,10},{8,4},{10,6},{12,0},{14,2},{1,13},{3,15... | collective-permute-start | bytes 49160 | tf_op jit(solution)/shard_map/ppermute | solution.py:230
  26.9 4.7 %collective-permute-start.8 = (f32[8,512]{1,0:T(8,128)S(1)}, f32[8,512]{1,0:T(8,128)S(1)}, u32[]{:S(2)}, u32[]{:S(2)}) collective-permute-start(f32[8,512]{1,0:T(8,128)S(1)} %add.32), channel_id=1, source_target_pairs={{0,8},{2,10},{4,12},{6,14},{8,0},{10,2},{12,4},{14,6},{1,9},{3,11}... | collective-permute-start | bytes 49160 | tf_op jit(solution)/shard_map/ppermute | solution.py:230
  27.5 4.2 %collective-permute-start.7 = (f32[8,512]{1,0:T(8,128)S(1)}, f32[8,512]{1,0:T(8,128)S(1)}, u32[]{:S(2)}, u32[]{:S(2)}) collective-permute-start(f32[8,512]{1,0:T(8,128)S(1)} %add.32), channel_id=1, source_target_pairs={{0,4},{2,6},{4,0},{6,2},{8,12},{10,14},{12,8},{14,10},{1,5},{3,7},... | collective-permute-start | bytes 49160 | tf_op jit(solution)/shard_map/ppermute | solution.py:230

commit v8 on v7

--- a/solution.py
+++ b/solution.py
@@ -9,7 +9,7 @@
 
 RANK = 4
 EPSILON = 1e-08
-CHUNKS = 4
+CHUNKS = 8
 BF16 = jnp.bfloat16
 F32 = jnp.float32
 
@@ -123,30 +123,30 @@
     )(*[pltpu.with_memory_space_constraint(value, pltpu.VMEM) for value in (grads, errors)])
 
 
-def spread(column, count):
-    picked = jnp.concatenate(
-        [jnp.broadcast_to(column[row : row + 1], (RANK, column.shape[1])) for row in range(0, count, RANK)],
+def pick(rows, index, count):
+    return jnp.concatenate(
+        [
+            jnp.broadcast_to(rows[start + index : start + index + 1], (RANK, rows.shape[1]))
+            for start in range(0, count, RANK)
+        ],
         axis=0,
     )
-    return picked
 
 
 def orthogonal(mine, other):
     count = mine.shape[0]
-    lane = lax.broadcasted_iota(jnp.int32, (count, 1), 0) % RANK
+    rank = lax.broadcasted_iota(jnp.int32, (count, 1), 0) % RANK
     for index in range(RANK):
-        current = spread(mine[index : count - RANK + index + 1], count - RANK + 1)
-        partner = spread(other[index : count - RANK + index + 1], count - RANK + 1)
-        products = jnp.sum(mine * current, axis=1, keepdims=True) + jnp.sum(
-            other * partner, axis=1, keepdims=True
-        )
-        square = spread(products[index : count - RANK + index + 1], count - RANK + 1)
-        length = jnp.sqrt(square) + EPSILON
-        current = current / length
-        partner = partner / length
-        inner = products / length
-        mine = jnp.where(lane == index, current, jnp.where(lane > index, mine - inner * current, mine))
-        other = jnp.where(lane == index, partner, jnp.where(lane > index, other - inner * partner, other))
+        current = pick(mine, index, count)
+        partner = pick(other, index, count)
+        products = jnp.sum(mine * current + other * partner, axis=1, keepdims=True)
+        inverse = 1.0 / (jnp.sqrt(pick(products, index, count)) + EPSILON)
+        inner = products * inverse
+        weight = jnp.where(rank > index, inner * inverse, 0.0)
+        here = rank == index
+        mine = jnp.where(here, mine * inverse, mine - weight * current)
+        if index < RANK - 1:
+            other = jnp.where(here, other * inverse, other - weight * partner)
     return mine
 
 
@@ -178,13 +178,29 @@
     )(mine, other, pltpu.with_memory_space_constraint(high, pltpu.VMEM), pltpu.with_memory_space_constraint(low, pltpu.VMEM))
 
 
+def turn_body(left_ref, turned_ref):
+    high, low = halves(left_ref[...])
+    turned_ref[...] = jnp.concatenate([high, low, high, low], axis=0).T.astype(BF16)
+
+
+def turn(left):
+    count, rows = left.shape
+    return pl.pallas_call(
+        turn_body,
+        out_shape=pltpu.VMEM((rows, 4 * count), BF16),
+        in_specs=[pl.BlockSpec(memory_space=pltpu.VMEM)],
+        out_specs=pl.BlockSpec(memory_space=pltpu.VMEM),
+        compiler_params=pltpu.CompilerParams(vmem_limit_bytes=16 * 2**20),
+        cost_estimate=pl.CostEstimate(flops=16 * left.size, bytes_accessed=64 * left.size, transcendentals=0),
+        name="turn",
+    )(left)
+
+
 def finish_body(scale, left_ref, right_ref, merged_ref, update_ref, errors_ref, ubuf, ebuf, sems):
     mats, rows, cols = merged_ref.shape
     size = rows // CHUNKS
-    left_high, left_low = halves(left_ref[...])
-    right_high, right_low = halves(right_ref[...] * scale)
-    left = jnp.concatenate([left_high, left_low, left_high, left_low], axis=0).T.astype(BF16)
-    right = jnp.concatenate([right_high, right_high, right_low, right_low], axis=0)
+    high, low = halves(right_ref[...] * scale)
+    right = jnp.concatenate([high, high, low, low], axis=0)
     row = lax.broadcasted_iota(jnp.int32, right.shape, 0) % (mats * RANK)
     copies = []
     for mat in range(mats):
@@ -192,7 +208,7 @@
         for chunk in range(CHUNKS):
             at = pl.ds(chunk * size, size)
             slot = mat * CHUNKS + chunk
-            approx = jnp.dot(left[chunk * size : (chunk + 1) * size], weights, preferred_element_type=F32)
+            approx = jnp.dot(left_ref[at], weights, preferred_element_type=F32)
             ubuf[mat, at] = approx.astype(BF16)
             ebuf[mat, at] = merged_ref[mat, at] - approx
             for copy in (
@@ -220,24 +236,37 @@
             pltpu.VMEM((mats, rows, cols), F32),
             pltpu.SemaphoreType.DMA((2, mats * CHUNKS)),
         ],
-        compiler_params=pltpu.CompilerParams(vmem_limit_bytes=24 * 2**20),
+        compiler_params=pltpu.CompilerParams(vmem_limit_bytes=16 * 2**20),
         name="finish",
-    )(left, right, pltpu.with_memory_space_constraint(merged, pltpu.VMEM))
-
-
-def swap(value, axis, step):
-    pairs = [(index, index ^ step) for index in range(lax.axis_size(axis))]
-    return lax.ppermute(value, axis, pairs)
-
-
-def swap_sum(value, axis):
-    count = lax.axis_size(axis)
+    )(
+        pltpu.with_memory_space_constraint(left, pltpu.VMEM),
+        right,
+        pltpu.with_memory_space_constraint(merged, pltpu.VMEM),
+    )
+
+
+def swap(value, axes, pairs):
+    return lax.ppermute(value, axes, pairs + [(target, source) for source, target in pairs])
+
+
+def swap_cores(value):
+    return swap(value, "tensor", [(0, 1)])
+
+
+def swap_chips(value, step, cross):
+    lower = [at for at in range(lax.axis_size("dp")) if at < at ^ step]
+    pairs = [(2 * at + core, 2 * (at ^ step) + (core ^ cross)) for at in lower for core in range(2)]
+    return swap(value, ("dp", "tensor"), pairs)
+
+
+def chips_sum(value, cross):
+    count = lax.axis_size("dp")
     last = max(count // 4, 1)
     step = 1
     while step < last:
-        value = value + swap(value, axis, step)
+        value = value + swap_chips(value, step, cross)
         step *= 2
-    terms = [value] + [swap(value, axis, offset) for offset in range(last, count, last)]
+    terms = [value] + [swap_chips(value, offset, cross) for offset in range(last, count, last)]
     while len(terms) > 1:
         terms = [terms[at] + terms[at + 1] for at in range(0, len(terms), 2)]
     return terms[0]
@@ -247,10 +276,10 @@
     replicas = lax.axis_size("dp")
     left_part, grads, errors = project(seeds, grads, errors)
     merged, high, low = merge(grads, errors)
-    mine = swap_sum(left_part, "dp")
-    left, right_part = reflect(mine, swap(mine, "tensor", 1), high, low, 1.0 / replicas)
-    right = swap_sum(right_part + swap(right_part, "tensor", 1), "dp")
-    return finish(left, right, merged, 1.0 / replicas)
+    mine = chips_sum(left_part, 0)
+    left, right_part = reflect(mine, swap_cores(mine), high, low, 1.0 / replicas)
+    right = chips_sum(right_part + swap_cores(right_part), 1)
+    return finish(turn(left), right, merged, 1.0 / replicas)
 
 
 def solution(mesh):

time: 35 us -> 34.2 us (0.977)
  starting transfers between devices: 13.9 us -> 13.2 us
  waiting for transfers between devices: 11.5 us -> 10.9 us
  Pallas kernels: 8.67 us -> 9.17 us
    ppermute x10, starting transfers between devices: 13.9 us -> 13.2 us  [swap(): lax.ppermute(value, axes, pairs + [(target, source) for source, target in...]
    ppermute x10, waiting for transfers between devices: 11.5 us -> 10.9 us  [swap(): lax.ppermute(value, axes, pairs + [(target, source) for source, target in...]
    pallas_call x1, Pallas kernels: 3.35 us -> 3.71 us  [project(): pl.pallas_call(project_body, out_shape=(jax.ShapeDtypeStruct((mats * RANK...]
where the time goes in v8:
time: 34.2 us; the launch traced here: 34.1 us
  starting transfers between devices  13.2 us (39%)
  waiting for transfers between devices  10.9 us (32%)
  Pallas kernels  9.17 us (27%)
  between operations  0.68 us (2%)
    ppermute x10, starting transfers between devices, swap(): lax.ppermute(value, axes, pairs + [(target, source) for source, target in...  13.2 us
    ppermute x10, waiting for transfers between devices, swap(): lax.ppermute(value, axes, pairs + [(target, source) for source, target in...  10.9 us
    pallas_call x1, Pallas kernels, project(): pl.pallas_call(project_body, out_shape=(jax.ShapeDtypeStruct((mats * RANK...  3.71 us
    pallas_call x1, Pallas kernels, finish(): pl.pallas_call(functools.partial(finish_body, scale), out_shape=(jax.Shap...  3.09 us
    pallas_call x1, Pallas kernels, reflect(): pl.pallas_call(functools.partial(reflect_body, scale), out_shape=(jax.Sha...  1.36 us
    pallas_call x1, Pallas kernels, merge(): pl.pallas_call(merge_body, out_shape=(pltpu.VMEM(shape, F32), pltpu.VMEM(...  0.87 us
  transfers between devices with their start and end apart: 10, of which 9 were waited for; matrix products, arithmetic and copies ran while one was open for 0% of the time, Pallas kernels for 3%

profile of v8, /device:TPU:0, one launch (start us, length us, event | category | flops | bytes accessed | tf_op | source)
XLA Modules:
  0.0 34.1 jit_solution(493437317509622030)
XLA Ops:
  0.6 3.7 %project.1 = (f32[8,1024]{1,0:T(8,128)S(1)}, bf16[2,1024,512]{2,1,0:T(8,128)(2,1)S(1)}, f32[2,1024,512]{2,1,0:T(8,128)S(1)}) custom-call(s32[2]{0:T(128)} %seeds_ref.1, bf16[1,2,1024,512]{3,2,1,0:T(8,128)(2,1)} %grads_ref.1, f32[1,2,1024,512]{3,2,1,0:T(8,128)} %errors_ref.1), custom_call_target="tpu_custom_call" | custom-call | tf_op jit(solution)/shard_map/project/pallas_call | solution.py:79
  4.3 3.0 %collective-permute-start = (f32[8,1024]{1,0:T(8,128)S(1)}, f32[8,1024]{1,0:T(8,128)S(1)}, u32[]{:S(2)}, u32[]{:S(2)}) collective-permute-start(f32[8,1024]{1,0:T(8,128)S(1)} %get-tuple-element.10), channel_id=1, source_target_pairs={{0,2},{1,3},{4,6},{5,7},{8,10},{9,11},{12,14},{13,15},{2,0},{3,1},... | collective-permute-start | bytes 98312 | tf_op jit(solution)/shard_map/ppermute | solution.py:249
  7.4 1.9 %collective-permute-done = f32[8,1024]{1,0:T(8,128)S(1)} collective-permute-done((f32[8,1024]{1,0:T(8,128)S(1)}, f32[8,1024]{1,0:T(8,128)S(1)}, u32[]{:S(2)}, u32[]{:S(2)}) %collective-permute-start) | collective-permute-done | bytes 32800 | tf_op jit(solution)/shard_map/ppermute | solution.py:249
  9.3 4.1 %collective-permute-start.3 = (f32[8,1024]{1,0:T(8,128)S(1)}, f32[8,1024]{1,0:T(8,128)S(1)}, u32[]{:S(2)}, u32[]{:S(2)}) collective-permute-start(f32[8,1024]{1,0:T(8,128)S(1)} %add.27), channel_id=1, source_target_pairs={{0,12},{1,13},{2,14},{3,15},{4,8},{5,9},{6,10},{7,11},{12,0},{13,1... | collective-permute-start | bytes 98312 | tf_op jit(solution)/shard_map/ppermute | solution.py:249
  13.4 0.0 collective-permute-start.2
  13.4 0.6 %collective-permute-start.1 = (f32[8,1024]{1,0:T(8,128)S(1)}, f32[8,1024]{1,0:T(8,128)S(1)}, u32[]{:S(2)}, u32[]{:S(2)}) collective-permute-start(f32[8,1024]{1,0:T(8,128)S(1)} %add.27), channel_id=1, source_target_pairs={{0,4},{1,5},{2,6},{3,7},{8,12},{9,13},{10,14},{11,15},{4,0},{5,1},... | collective-permute-start | bytes 98312 | tf_op jit(solution)/shard_map/ppermute | solution.py:249
  14.0 1.3 %collective-permute-done.3 = f32[8,1024]{1,0:T(8,128)S(1)} collective-permute-done((f32[8,1024]{1,0:T(8,128)S(1)}, f32[8,1024]{1,0:T(8,128)S(1)}, u32[]{:S(2)}, u32[]{:S(2)}) %collective-permute-start.3) | collective-permute-done | bytes 32800 | tf_op jit(solution)/shard_map/ppermute | solution.py:249
  15.3 2.9 %collective-permute-done.2 = f32[8,1024]{1,0:T(8,128)S(1)} collective-permute-done((f32[8,1024]{1,0:T(8,128)S(1)}, f32[8,1024]{1,0:T(8,128)S(1)}, u32[]{:S(2)}, u32[]{:S(2)}) %collective-permute-start.2) | collective-permute-done | bytes 32800 | tf_op jit(solution)/shard_map/ppermute | solution.py:249
  18.2 0.0 collective-permute-done.1
  18.2 0.1 collective-permute-start.4
  18.3 0.9 %merge.1 = (f32[2,1024,512]{2,1,0:T(8,128)S(1)}, bf16[2,1024,512]{2,1,0:T(8,128)(2,1)S(1)}, bf16[2,1024,512]{2,1,0:T(8,128)(2,1)S(1)}) custom-call(bf16[2,1024,512]{2,1,0:T(8,128)(2,1)S(1)} %get-tuple-element.11.grads_ref, f32[2,1024,512]{2,1,0:T(8,128)S(1)} %get-tuple-element.12.errors_ref), custom_call_target="tpu_custom_call" | custom-call | flops 3145728 | bytes 14680064 | tf_op jit(solution)/shard_map/merge/pallas_call | solution.py:115
  19.2 0.3 collective-permute-done.4.other_ref
  19.5 1.4 %reflect.1 = (f32[8,1024]{1,0:T(8,128)S(1)}, f32[8,512]{1,0:T(8,128)S(1)}) custom-call(f32[8,1024]{1,0:T(8,128)S(1)} %add_add_fusion.mine_ref, f32[8,1024]{1,0:T(8,128)S(1)} %collective-permute-done.4.other_ref, bf16[2,1024,512]{2,1,0:T(8,128)(2,1)S(1)} %get-tuple-element.13.high_ref, bf16[2,1024,512]{2,1,0:T(8,128)(2,1)S(1)} %get-tuple-element.14.low_ref), custom_call_target="tpu_custom_call" | custom-call | tf_op jit(solution)/shard_map/reflect/pallas_call | solution.py:168
  20.8 0.2 collective-permute-start.5
  21.0 1.0 %collective-permute-done.5 = f32[8,512]{1,0:T(8,128)S(1)} collective-permute-done((f32[8,512]{1,0:T(8,128)S(1)}, f32[8,512]{1,0:T(8,128)S(1)}, u32[]{:S(2)}, u32[]{:S(2)}) %collective-permute-start.5) | collective-permute-done | bytes 16416 | tf_op jit(solution)/shard_map/ppermute | solution.py:249
  22.0 1.3 %collective-permute-start.6 = (f32[8,512]{1,0:T(8,128)S(1)}, f32[8,512]{1,0:T(8,128)S(1)}, u32[]{:S(2)}, u32[]{:S(2)}) collective-permute-start(f32[8,512]{1,0:T(8,128)S(1)} %add.31), channel_id=1, source_target_pairs={{0,3},{1,2},{4,7},{5,6},{8,11},{9,10},{12,15},{13,14},{3,0},{2,1},... | collective-permute-start | bytes 49160 | tf_op jit(solution)/shard_map/ppermute | solution.py:249
  23.4 1.9 %collective-permute-done.6 = f32[8,512]{1,0:T(8,128)S(1)} collective-permute-done((f32[8,512]{1,0:T(8,128)S(1)}, f32[8,512]{1,0:T(8,128)S(1)}, u32[]{:S(2)}, u32[]{:S(2)}) %collective-permute-start.6) | collective-permute-done | bytes 16416 | tf_op jit(solution)/shard_map/ppermute | solution.py:249
  25.2 1.2 %collective-permute-start.9 = (f32[8,512]{1,0:T(8,128)S(1)}, f32[8,512]{1,0:T(8,128)S(1)}, u32[]{:S(2)}, u32[]{:S(2)}) collective-permute-start(f32[8,512]{1,0:T(8,128)S(1)} %add.32), channel_id=1, source_target_pairs={{0,13},{1,12},{2,15},{3,14},{4,9},{5,8},{6,11},{7,10},{13,0},{12,1... | collective-permute-start | bytes 49160 | tf_op jit(solution)/shard_map/ppermute | solution.py:249
  26.5 0.6 %collective-permute-start.8 = (f32[8,512]{1,0:T(8,128)S(1)}, f32[8,512]{1,0:T(8,128)S(1)}, u32[]{:S(2)}, u32[]{:S(2)}) collective-permute-start(f32[8,512]{1,0:T(8,128)S(1)} %add.32), channel_id=1, source_target_pairs={{0,9},{1,8},{2,11},{3,10},{4,13},{5,12},{6,15},{7,14},{9,0},{8,1},... | collective-permute-start | bytes 49160 | tf_op jit(solution)/shard_map/ppermute | solution.py:249
  27.1 2.0 %collective-permute-start.7 = (f32[8,512]{1,0:T(8,128)S(1)}, f32[8,512]{1,0:T(8,128)S(1)}, u32[]{:S(2)}, u32[]{:S(2)}) collective-permute-start(f32[8,512]{1,0:T(8,128)S(1)} %add.32), channel_id=1, source_target_pairs={{0,5},{1,4},{2,7},{3,6},{8,13},{9,12},{10,15},{11,14},{5,0},{4,1},... | collective-permute-start | bytes 49160 | tf_op jit(solution)/shard_map/ppermute | solution.py:249
  29.1 0.1 turn.1.left_ref
  29.3 0.9 %collective-permute-done.9 = f32[8,512]{1,0:T(8,128)S(1)} collective-permute-done((f32[8,512]{1,0:T(8,128)S(1)}, f32[8,512]{1,0:T(8,128)S(1)}, u32[]{:S(2)}, u32[]{:S(2)}) %collective-permute-start.9) | collective-permute-done | bytes 16416 | tf_op jit(solution)/shard_map/ppermute | solution.py:249
  30.2 0.6 %collective-permute-done.8 = f32[8,512]{1,0:T(8,128)S(1)} collective-permute-done((f32[8,512]{1,0:T(8,128)S(1)}, f32[8,512]{1,0:T(8,128)S(1)}, u32[]{:S(2)}, u32[]{:S(2)}) %collective-permute-start.8) | collective-permute-done | bytes 16416 | tf_op jit(solution)/shard_map/ppermute | solution.py:249
  30.7 0.2 collective-permute-done.7
  31.0 3.1 %finish.1 = (bf16[2,1024,512]{2,1,0:T(8,128)(2,1)}, f32[1,2,1024,512]{3,2,1,0:T(8,128)}) custom-call(bf16[1024,32]{1,0:T(8,128)(2,1)S(1)} %turn.1.left_ref, f32[8,512]{1,0:T(8,128)S(1)} %add_add_fusion.1.right_ref, f32[2,1024,512]{2,1,0:T(8,128)S(1)} %get-tuple-element.17.merged_ref), custom_call_target="tpu_custom_call" | custom-call | tf_op jit(solution)/shard_map/finish/pallas_call | solution.py:226
  (5 shorter events, 0.0 us)
Async XLA Ops:
  4.3 4.9 %collective-permute-start = (f32[8,1024]{1,0:T(8,128)S(1)}, f32[8,1024]{1,0:T(8,128)S(1)}, u32[]{:S(2)}, u32[]{:S(2)}) collective-permute-start(f32[8,1024]{1,0:T(8,128)S(1)} %get-tuple-element.10), channel_id=1, source_target_pairs={{0,2},{1,3},{4,6},{5,7},{8,10},{9,11},{12,14},{13,15},{2,0},{3,1},... | collective-permute-start | bytes 98312 | tf_op jit(solution)/shard_map/ppermute | solution.py:249
  9.3 6.0 %collective-permute-start.3 = (f32[8,1024]{1,0:T(8,128)S(1)}, f32[8,1024]{1,0:T(8,128)S(1)}, u32[]{:S(2)}, u32[]{:S(2)}) collective-permute-start(f32[8,1024]{1,0:T(8,128)S(1)} %add.27), channel_id=1, source_target_pairs={{0,12},{1,13},{2,14},{3,15},{4,8},{5,9},{6,10},{7,11},{12,0},{13,1... | collective-permute-start | bytes 98312 | tf_op jit(solution)/shard_map/ppermute | solution.py:249
  13.4 4.8 %collective-permute-start.2 = (f32[8,1024]{1,0:T(8,128)S(1)}, f32[8,1024]{1,0:T(8,128)S(1)}, u32[]{:S(2)}, u32[]{:S(2)}) collective-permute-start(f32[8,1024]{1,0:T(8,128)S(1)} %add.27), channel_id=1, source_target_pairs={{0,8},{1,9},{2,10},{3,11},{4,12},{5,13},{6,14},{7,15},{8,0},{9,1},... | collective-permute-start | bytes 98312 | tf_op jit(solution)/shard_map/ppermute | solution.py:249
  13.4 4.8 %collective-permute-start.1 = (f32[8,1024]{1,0:T(8,128)S(1)}, f32[8,1024]{1,0:T(8,128)S(1)}, u32[]{:S(2)}, u32[]{:S(2)}) collective-permute-start(f32[8,1024]{1,0:T(8,128)S(1)} %add.27), channel_id=1, source_target_pairs={{0,4},{1,5},{2,6},{3,7},{8,12},{9,13},{10,14},{11,15},{4,0},{5,1},... | collective-permute-start | bytes 98312 | tf_op jit(solution)/shard_map/ppermute | solution.py:249
  18.2 1.3 %collective-permute-start.4 = (f32[8,1024]{1,0:T(8,128)S(1)}, f32[8,1024]{1,0:T(8,128)S(1)}, u32[]{:S(2)}, u32[]{:S(2)}) collective-permute-start(f32[8,1024]{1,0:T(8,128)S(1)} %add_add_fusion.mine_ref), channel_id=1, source_target_pairs={{0,1},{1,0},{2,3},{3,2},{4,5},{5,4},{6,7},{7,6},{8,9},{9,8},{10,11... | collective-permute-start | bytes 98312 | tf_op jit(solution)/shard_map/ppermute | solution.py:249
  20.8 1.2 %collective-permute-start.5 = (f32[8,512]{1,0:T(8,128)S(1)}, f32[8,512]{1,0:T(8,128)S(1)}, u32[]{:S(2)}, u32[]{:S(2)}) collective-permute-start(f32[8,512]{1,0:T(8,128)S(1)} %get-tuple-element.16), channel_id=1, source_target_pairs={{0,1},{1,0},{2,3},{3,2},{4,5},{5,4},{6,7},{7,6},{8,9},{9,8},{10,11... | collective-permute-start | bytes 49160 | tf_op jit(solution)/shard_map/ppermute | solution.py:249
  22.0 3.2 %collective-permute-start.6 = (f32[8,512]{1,0:T(8,128)S(1)}, f32[8,512]{1,0:T(8,128)S(1)}, u32[]{:S(2)}, u32[]{:S(2)}) collective-permute-start(f32[8,512]{1,0:T(8,128)S(1)} %add.31), channel_id=1, source_target_pairs={{0,3},{1,2},{4,7},{5,6},{8,11},{9,10},{12,15},{13,14},{3,0},{2,1},... | collective-permute-start | bytes 49160 | tf_op jit(solution)/shard_map/ppermute | solution.py:249
  25.2 5.0 %collective-permute-start.9 = (f32[8,512]{1,0:T(8,128)S(1)}, f32[8,512]{1,0:T(8,128)S(1)}, u32[]{:S(2)}, u32[]{:S(2)}) collective-permute-start(f32[8,512]{1,0:T(8,128)S(1)} %add.32), channel_id=1, source_target_pairs={{0,13},{1,12},{2,15},{3,14},{4,9},{5,8},{6,11},{7,10},{13,0},{12,1... | collective-permute-start | bytes 49160 | tf_op jit(solution)/shard_map/ppermute | solution.py:249
  26.5 4.3 %collective-permute-start.8 = (f32[8,512]{1,0:T(8,128)S(1)}, f32[8,512]{1,0:T(8,128)S(1)}, u32[]{:S(2)}, u32[]{:S(2)}) collective-permute-start(f32[8,512]{1,0:T(8,128)S(1)} %add.32), channel_id=1, source_target_pairs={{0,9},{1,8},{2,11},{3,10},{4,13},{5,12},{6,15},{7,14},{9,0},{8,1},... | collective-permute-start | bytes 49160 | tf_op jit(solution)/shard_map/ppermute | solution.py:249
  27.1 3.9 %collective-permute-start.7 = (f32[8,512]{1,0:T(8,128)S(1)}, f32[8,512]{1,0:T(8,128)S(1)}, u32[]{:S(2)}, u32[]{:S(2)}) collective-permute-start(f32[8,512]{1,0:T(8,128)S(1)} %add.32), channel_id=1, source_target_pairs={{0,5},{1,4},{2,7},{3,6},{8,13},{9,12},{10,15},{11,14},{5,0},{4,1},... | collective-permute-start | bytes 49160 | tf_op jit(solution)/shard_map/ppermute | solution.py:249

commit v9 on v8

--- a/solution.py
+++ b/solution.py
@@ -9,7 +9,9 @@
 
 RANK = 4
 EPSILON = 1e-08
-CHUNKS = 8
+CHUNKS = 4
+SPLIT = ((3, 6), (5, 4), (1, 7))
+SHARED = 2
 BF16 = jnp.bfloat16
 F32 = jnp.float32
 
@@ -57,8 +59,7 @@
         copy.start()
     seed_copy.wait()
     start = start_rows(seed, mats, cols)
-    weights = jnp.concatenate(halves(start), axis=0).astype(BF16)
-    dims = (((1,), (1,)), ((), ()))
+    weights = jnp.concatenate(halves(start), axis=0).T.astype(BF16)
     for chunk in range(CHUNKS):
         at = pl.ds(chunk * size, size)
         left = jnp.zeros((mats * RANK, size), F32)
@@ -68,9 +69,9 @@
             value = gbuf[mat, at].astype(F32) + ebuf[mat, at]
             high = value.astype(BF16)
             low = (value - high.astype(F32)).astype(BF16)
-            product = lax.dot_general(weights, high, dims, preferred_element_type=F32)
-            product = product + lax.dot_general(weights, low, dims, preferred_element_type=F32)
-            left = fold(mat, left, product)
+            product = jnp.dot(high, weights, preferred_element_type=F32)
+            product = product + jnp.dot(low, weights, preferred_element_type=F32)
+            left = fold(mat, left, product.T)
         left_ref[:, at] = left
 
 
@@ -196,10 +197,30 @@
     )(left)
 
 
-def finish_body(scale, left_ref, right_ref, merged_ref, update_ref, errors_ref, ubuf, ebuf, sems):
+def total(own_ref, both_ref, taken_refs, given_refs):
+    first = lax.axis_index("tensor") == 0
+    terms = {0: own_ref[...], SHARED: both_ref[...]}
+    for masks, taken_ref, given_ref in zip(SPLIT, taken_refs, given_refs):
+        taken, given = taken_ref[...], given_ref[...]
+        terms[masks[0]] = jnp.where(first, taken, given)
+        terms[masks[1]] = jnp.where(first, given, taken)
+    sums = [terms[index] for index in range(len(terms))]
+    while len(sums) > 1:
+        sums = [sums[at] + sums[at + 1] for at in range(0, len(sums), 2)]
+    return sums[0]
+
+
+def finish_body(scale, count, left_ref, merged_ref, own_ref, both_ref, *refs):
+    taken_refs, given_refs = refs[:count], refs[count : 2 * count]
+    update_ref, errors_ref, ubuf, ebuf, sems = refs[2 * count :]
+    right = total(own_ref, both_ref, taken_refs, given_refs) * scale
+    finish_rows(right, left_ref, merged_ref, update_ref, errors_ref, ubuf, ebuf, sems)
+
+
+def finish_rows(right, left_ref, merged_ref, update_ref, errors_ref, ubuf, ebuf, sems):
     mats, rows, cols = merged_ref.shape
     size = rows // CHUNKS
-    high, low = halves(right_ref[...] * scale)
+    high, low = halves(right)
     right = jnp.concatenate([high, high, low, low], axis=0)
     row = lax.broadcasted_iota(jnp.int32, right.shape, 0) % (mats * RANK)
     copies = []
@@ -221,15 +242,15 @@
         copy.wait()
 
 
-def finish(left, right, merged, scale):
+def finish(left, merged, own, both, taken, given, scale):
     mats, rows, cols = merged.shape
     return pl.pallas_call(
-        functools.partial(finish_body, scale),
+        functools.partial(finish_body, scale, len(taken)),
         out_shape=(
             jax.ShapeDtypeStruct((mats, rows, cols), BF16),
             jax.ShapeDtypeStruct((1, mats, rows, cols), F32),
         ),
-        in_specs=[pl.BlockSpec(memory_space=pltpu.VMEM)] * 3,
+        in_specs=[pl.BlockSpec(memory_space=pltpu.VMEM)] * (4 + 2 * len(taken)),
         out_specs=[pl.BlockSpec(memory_space=pltpu.HBM)] * 2,
         scratch_shapes=[
             pltpu.VMEM((mats, rows, cols), BF16),
@@ -240,8 +261,11 @@
         name="finish",
     )(
         pltpu.with_memory_space_constraint(left, pltpu.VMEM),
-        right,
         pltpu.with_memory_space_constraint(merged, pltpu.VMEM),
+        own,
+        both,
+        *taken,
+        *given,
     )
 
 
@@ -253,33 +277,49 @@
     return swap(value, "tensor", [(0, 1)])
 
 
-def swap_chips(value, step, cross):
-    lower = [at for at in range(lax.axis_size("dp")) if at < at ^ step]
-    pairs = [(2 * at + core, 2 * (at ^ step) + (core ^ cross)) for at in lower for core in range(2)]
+def swap_chips(value, masks, cross=0):
+    pairs = []
+    for core in range(2):
+        for at in range(lax.axis_size("dp")):
+            partner = at ^ masks[core]
+            if at < partner:
+                pairs.append((2 * at + core, 2 * partner + (core ^ cross)))
     return swap(value, ("dp", "tensor"), pairs)
 
 
-def chips_sum(value, cross):
+def chips_sum(value):
     count = lax.axis_size("dp")
     last = max(count // 4, 1)
     step = 1
     while step < last:
-        value = value + swap_chips(value, step, cross)
+        value = value + swap_chips(value, (step, step))
         step *= 2
-    terms = [value] + [swap_chips(value, offset, cross) for offset in range(last, count, last)]
+    terms = [value] + [swap_chips(value, (offset, offset)) for offset in range(last, count, last)]
     while len(terms) > 1:
         terms = [terms[at] + terms[at + 1] for at in range(0, len(terms), 2)]
     return terms[0]
+
+
+def chips_terms(value):
+    count = lax.axis_size("dp")
+    last = count // 8
+    step = 1
+    while step < last:
+        value = value + swap_chips(value, (step, step), 1)
+        step *= 2
+    both = swap_chips(value, (SHARED * last, SHARED * last), 1)
+    taken = [swap_chips(value, (lower * last, upper * last)) for lower, upper in SPLIT[::-1]][::-1]
+    return value, both, taken, [swap_cores(term) for term in taken]
 
 
 def body(grads, errors, seeds):
     replicas = lax.axis_size("dp")
     left_part, grads, errors = project(seeds, grads, errors)
     merged, high, low = merge(grads, errors)
-    mine = chips_sum(left_part, 0)
+    mine = chips_sum(left_part)
     left, right_part = reflect(mine, swap_cores(mine), high, low, 1.0 / replicas)
-    right = chips_sum(right_part + swap_cores(right_part), 1)
-    return finish(turn(left), right, merged, 1.0 / replicas)
+    terms = chips_terms(right_part + swap_cores(right_part))
+    return finish(turn(left), merged, *terms, 1.0 / replicas)
 
 
 def solution(mesh):

time: 34.2 us -> 34.2 us (level)
  starting transfers between devices: 13.2 us -> 14.6 us
  waiting for transfers between devices: 10.9 us -> 9.93 us
  Pallas kernels: 9.17 us -> 8.82 us
    ppermute x10 -> x13, starting transfers between devices: 13.2 us -> 14.6 us  [swap(): lax.ppermute(value, axes, pairs + [(target, source) for source, target in...]
    ppermute x10 -> x13, waiting for transfers between devices: 10.9 us -> 9.93 us  [swap(): lax.ppermute(value, axes, pairs + [(target, source) for source, target in...]
  transfers between devices with their start and end apart: 10 -> 13, of which waited for: 9 -> 9; matrix products, arithmetic and copies ran while one was open for 0% -> 0% of each run, Pallas kernels for 3% -> 3%
where the time goes in v9:
time: 34.2 us; the launch traced here: 34.1 us
  starting transfers between devices  14.6 us (43%)
  waiting for transfers between devices  9.93 us (29%)
  Pallas kernels  8.82 us (26%)
  between operations  0.7 us (2%)
    ppermute x13, starting transfers between devices, swap(): lax.ppermute(value, axes, pairs + [(target, source) for source, target in...  14.6 us
    ppermute x13, waiting for transfers between devices, swap(): lax.ppermute(value, axes, pairs + [(target, source) for source, target in...  9.93 us
    pallas_call x1, Pallas kernels, project(): pl.pallas_call(project_body, out_shape=(jax.ShapeDtypeStruct((mats * RANK...  3.45 us
    pallas_call x1, Pallas kernels, finish(): pl.pallas_call(functools.partial(finish_body, scale, len(taken)), out_sha...  3 us
    pallas_call x1, Pallas kernels, reflect(): pl.pallas_call(functools.partial(reflect_body, scale), out_shape=(jax.Sha...  1.36 us
    pallas_call x1, Pallas kernels, merge(): pl.pallas_call(merge_body, out_shape=(pltpu.VMEM(shape, F32), pltpu.VMEM(...  0.87 us
  transfers between devices with their start and end apart: 13, of which 9 were waited for; matrix products, arithmetic and copies ran while one was open for 0% of the time, Pallas kernels for 3%

profile of v9, /device:TPU:0, one launch (start us, length us, event | category | flops | bytes accessed | tf_op | source)
XLA Modules:
  0.0 34.1 jit_solution(5720084267972754700)
XLA Ops:
  0.6 3.5 %project.1 = (f32[8,1024]{1,0:T(8,128)S(1)}, bf16[2,1024,512]{2,1,0:T(8,128)(2,1)S(1)}, f32[2,1024,512]{2,1,0:T(8,128)S(1)}) custom-call(s32[2]{0:T(128)} %seeds_ref.1, bf16[1,2,1024,512]{3,2,1,0:T(8,128)(2,1)} %grads_ref.1, f32[1,2,1024,512]{3,2,1,0:T(8,128)} %errors_ref.1), custom_call_target="tpu_custom_call" | custom-call | tf_op jit(solution)/shard_map/project/pallas_call | solution.py:80
  4.1 3.0 %collective-permute-start = (f32[8,1024]{1,0:T(8,128)S(1)}, f32[8,1024]{1,0:T(8,128)S(1)}, u32[]{:S(2)}, u32[]{:S(2)}) collective-permute-start(f32[8,1024]{1,0:T(8,128)S(1)} %get-tuple-element.10), channel_id=1, source_target_pairs={{0,2},{4,6},{8,10},{12,14},{1,3},{5,7},{9,11},{13,15},{2,0},{6,4},... | collective-permute-start | bytes 98312 | tf_op jit(solution)/shard_map/ppermute | solution.py:273
  7.1 1.9 %collective-permute-done = f32[8,1024]{1,0:T(8,128)S(1)} collective-permute-done((f32[8,1024]{1,0:T(8,128)S(1)}, f32[8,1024]{1,0:T(8,128)S(1)}, u32[]{:S(2)}, u32[]{:S(2)}) %collective-permute-start) | collective-permute-done | bytes 32800 | tf_op jit(solution)/shard_map/ppermute | solution.py:273
  9.0 4.1 %collective-permute-start.3 = (f32[8,1024]{1,0:T(8,128)S(1)}, f32[8,1024]{1,0:T(8,128)S(1)}, u32[]{:S(2)}, u32[]{:S(2)}) collective-permute-start(f32[8,1024]{1,0:T(8,128)S(1)} %add.15), channel_id=1, source_target_pairs={{0,12},{2,14},{4,8},{6,10},{1,13},{3,15},{5,9},{7,11},{12,0},{14,2... | collective-permute-start | bytes 98312 | tf_op jit(solution)/shard_map/ppermute | solution.py:273
  13.1 0.0 collective-permute-start.2
  13.1 0.6 %collective-permute-start.1 = (f32[8,1024]{1,0:T(8,128)S(1)}, f32[8,1024]{1,0:T(8,128)S(1)}, u32[]{:S(2)}, u32[]{:S(2)}) collective-permute-start(f32[8,1024]{1,0:T(8,128)S(1)} %add.15), channel_id=1, source_target_pairs={{0,4},{2,6},{8,12},{10,14},{1,5},{3,7},{9,13},{11,15},{4,0},{6,2},... | collective-permute-start | bytes 98312 | tf_op jit(solution)/shard_map/ppermute | solution.py:273
  13.8 1.3 %collective-permute-done.3 = f32[8,1024]{1,0:T(8,128)S(1)} collective-permute-done((f32[8,1024]{1,0:T(8,128)S(1)}, f32[8,1024]{1,0:T(8,128)S(1)}, u32[]{:S(2)}, u32[]{:S(2)}) %collective-permute-start.3) | collective-permute-done | bytes 32800 | tf_op jit(solution)/shard_map/ppermute | solution.py:273
  15.0 2.9 %collective-permute-done.2 = f32[8,1024]{1,0:T(8,128)S(1)} collective-permute-done((f32[8,1024]{1,0:T(8,128)S(1)}, f32[8,1024]{1,0:T(8,128)S(1)}, u32[]{:S(2)}, u32[]{:S(2)}) %collective-permute-start.2) | collective-permute-done | bytes 32800 | tf_op jit(solution)/shard_map/ppermute | solution.py:273
  17.9 0.0 collective-permute-done.1
  17.9 0.1 collective-permute-start.4
  18.0 0.9 %merge.1 = (f32[2,1024,512]{2,1,0:T(8,128)S(1)}, bf16[2,1024,512]{2,1,0:T(8,128)(2,1)S(1)}, bf16[2,1024,512]{2,1,0:T(8,128)(2,1)S(1)}) custom-call(bf16[2,1024,512]{2,1,0:T(8,128)(2,1)S(1)} %get-tuple-element.11.grads_ref, f32[2,1024,512]{2,1,0:T(8,128)S(1)} %get-tuple-element.12.errors_ref), custom_call_target="tpu_custom_call" | custom-call | flops 3145728 | bytes 14680064 | tf_op jit(solution)/shard_map/merge/pallas_call | solution.py:116
  18.9 0.3 collective-permute-done.4.other_ref
  19.2 1.4 %reflect.1 = (f32[8,1024]{1,0:T(8,128)S(1)}, f32[8,512]{1,0:T(8,128)S(1)}) custom-call(f32[8,1024]{1,0:T(8,128)S(1)} %add_add_fusion.mine_ref, f32[8,1024]{1,0:T(8,128)S(1)} %collective-permute-done.4.other_ref, bf16[2,1024,512]{2,1,0:T(8,128)(2,1)S(1)} %get-tuple-element.13.high_ref, bf16[2,1024,512]{2,1,0:T(8,128)(2,1)S(1)} %get-tuple-element.14.low_ref), custom_call_target="tpu_custom_call" | custom-call | tf_op jit(solution)/shard_map/reflect/pallas_call | solution.py:169
  20.6 0.2 collective-permute-start.5
  20.8 1.0 %collective-permute-done.5 = f32[8,512]{1,0:T(8,128)S(1)} collective-permute-done((f32[8,512]{1,0:T(8,128)S(1)}, f32[8,512]{1,0:T(8,128)S(1)}, u32[]{:S(2)}, u32[]{:S(2)}) %collective-permute-start.5) | collective-permute-done | bytes 16416 | tf_op jit(solution)/shard_map/ppermute | solution.py:273
  21.8 1.5 %collective-permute-start.9 = (f32[8,512]{1,0:T(8,128)S(1)}, f32[8,512]{1,0:T(8,128)S(1)}, u32[]{:S(2)}, u32[]{:S(2)}) collective-permute-start(f32[8,512]{1,0:T(8,128)S(1)} %add.19.own_ref), channel_id=1, source_target_pairs={{0,2},{4,6},{8,10},{12,14},{1,15},{3,13},{5,11},{7,9},{2,0},{6,4},... | collective-permute-start | bytes 49160 | tf_op jit(solution)/shard_map/ppermute | solution.py:273
  23.3 2.0 %collective-permute-start.8 = (f32[8,512]{1,0:T(8,128)S(1)}, f32[8,512]{1,0:T(8,128)S(1)}, u32[]{:S(2)}, u32[]{:S(2)}) collective-permute-start(f32[8,512]{1,0:T(8,128)S(1)} %add.19.own_ref), channel_id=1, source_target_pairs={{0,10},{2,8},{4,14},{6,12},{1,9},{3,11},{5,13},{7,15},{10,0},{8,2}... | collective-permute-start | bytes 49160 | tf_op jit(solution)/shard_map/ppermute | solution.py:273
  25.3 1.0 %collective-permute-start.7 = (f32[8,512]{1,0:T(8,128)S(1)}, f32[8,512]{1,0:T(8,128)S(1)}, u32[]{:S(2)}, u32[]{:S(2)}) collective-permute-start(f32[8,512]{1,0:T(8,128)S(1)} %add.19.own_ref), channel_id=1, source_target_pairs={{0,6},{2,4},{8,14},{10,12},{1,13},{3,15},{5,9},{7,11},{6,0},{4,2},... | collective-permute-start | bytes 49160 | tf_op jit(solution)/shard_map/ppermute | solution.py:273
  26.2 0.4 %collective-permute-start.6 = (f32[8,512]{1,0:T(8,128)S(1)}, f32[8,512]{1,0:T(8,128)S(1)}, u32[]{:S(2)}, u32[]{:S(2)}) collective-permute-start(f32[8,512]{1,0:T(8,128)S(1)} %add.19.own_ref), channel_id=1, source_target_pairs={{0,5},{2,7},{8,13},{10,15},{1,4},{3,6},{9,12},{11,14},{5,0},{7,2},... | collective-permute-start | bytes 49160 | tf_op jit(solution)/shard_map/ppermute | solution.py:273
  26.6 0.0 collective-permute-done.9.refs_2_
  26.7 1.7 %collective-permute-start.12 = (f32[8,512]{1,0:T(8,128)S(1)}, f32[8,512]{1,0:T(8,128)S(1)}, u32[]{:S(2)}, u32[]{:S(2)}) collective-permute-start(f32[8,512]{1,0:T(8,128)S(1)} %collective-permute-done.9.refs_2_), channel_id=1, source_target_pairs={{0,1},{1,0},{2,3},{3,2},{4,5},{5,4},{6,7},{7,6},{8,9},{9,8},{10,11... | collective-permute-start | bytes 49160 | tf_op jit(solution)/shard_map/ppermute | solution.py:273
  28.4 0.6 %collective-permute-done.8.refs_1_ = f32[8,512]{1,0:T(8,128)S(1)} collective-permute-done((f32[8,512]{1,0:T(8,128)S(1)}, f32[8,512]{1,0:T(8,128)S(1)}, u32[]{:S(2)}, u32[]{:S(2)}) %collective-permute-start.8) | collective-permute-done | bytes 16416 | tf_op jit(solution)/shard_map/ppermute | solution.py:273
  29.0 0.0 collective-permute-start.11
  29.0 0.9 %collective-permute-done.7.refs_0_ = f32[8,512]{1,0:T(8,128)S(1)} collective-permute-done((f32[8,512]{1,0:T(8,128)S(1)}, f32[8,512]{1,0:T(8,128)S(1)}, u32[]{:S(2)}, u32[]{:S(2)}) %collective-permute-start.7) | collective-permute-done | bytes 16416 | tf_op jit(solution)/shard_map/ppermute | solution.py:273
  29.9 0.0 collective-permute-start.10
  29.9 0.1 turn.1.left_ref
  30.1 0.0 collective-permute-done.6.both_ref
  30.1 0.0 collective-permute-done.12.refs_5_
  30.1 0.1 collective-permute-done.11.refs_4_
  30.2 0.9 %collective-permute-done.10.refs_3_ = f32[8,512]{1,0:T(8,128)S(1)} collective-permute-done((f32[8,512]{1,0:T(8,128)S(1)}, f32[8,512]{1,0:T(8,128)S(1)}, u32[]{:S(2)}, u32[]{:S(2)}) %collective-permute-start.10) | collective-permute-done | bytes 16416 | tf_op jit(solution)/shard_map/ppermute | solution.py:273
  31.1 3.0 %finish.1 = (bf16[2,1024,512]{2,1,0:T(8,128)(2,1)}, f32[1,2,1024,512]{3,2,1,0:T(8,128)}) custom-call(bf16[1024,32]{1,0:T(8,128)(2,1)S(1)} %turn.1.left_ref, f32[2,1024,512]{2,1,0:T(8,128)S(1)} %get-tuple-element.16.merged_ref, f32[8,512]{1,0:T(8,128)S(1)} %add.19.own_ref, f32[8,512]{1,0:T(8,128)S(1)} %collective-permute-done.6.both_ref, ...), custom_call_target="tpu_custom_call" | custom-call | tf_op jit(solution)/shard_map/finish/pallas_call | solution.py:247
  (3 shorter events, 0.0 us)
Async XLA Ops:
  4.1 4.9 %collective-permute-start = (f32[8,1024]{1,0:T(8,128)S(1)}, f32[8,1024]{1,0:T(8,128)S(1)}, u32[]{:S(2)}, u32[]{:S(2)}) collective-permute-start(f32[8,1024]{1,0:T(8,128)S(1)} %get-tuple-element.10), channel_id=1, source_target_pairs={{0,2},{4,6},{8,10},{12,14},{1,3},{5,7},{9,11},{13,15},{2,0},{6,4},... | collective-permute-start | bytes 98312 | tf_op jit(solution)/shard_map/ppermute | solution.py:273
  9.0 6.0 %collective-permute-start.3 = (f32[8,1024]{1,0:T(8,128)S(1)}, f32[8,1024]{1,0:T(8,128)S(1)}, u32[]{:S(2)}, u32[]{:S(2)}) collective-permute-start(f32[8,1024]{1,0:T(8,128)S(1)} %add.15), channel_id=1, source_target_pairs={{0,12},{2,14},{4,8},{6,10},{1,13},{3,15},{5,9},{7,11},{12,0},{14,2... | collective-permute-start | bytes 98312 | tf_op jit(solution)/shard_map/ppermute | solution.py:273
  13.1 4.8 %collective-permute-start.2 = (f32[8,1024]{1,0:T(8,128)S(1)}, f32[8,1024]{1,0:T(8,128)S(1)}, u32[]{:S(2)}, u32[]{:S(2)}) collective-permute-start(f32[8,1024]{1,0:T(8,128)S(1)} %add.15), channel_id=1, source_target_pairs={{0,8},{2,10},{4,12},{6,14},{1,9},{3,11},{5,13},{7,15},{8,0},{10,2}... | collective-permute-start | bytes 98312 | tf_op jit(solution)/shard_map/ppermute | solution.py:273
  13.1 4.8 %collective-permute-start.1 = (f32[8,1024]{1,0:T(8,128)S(1)}, f32[8,1024]{1,0:T(8,128)S(1)}, u32[]{:S(2)}, u32[]{:S(2)}) collective-permute-start(f32[8,1024]{1,0:T(8,128)S(1)} %add.15), channel_id=1, source_target_pairs={{0,4},{2,6},{8,12},{10,14},{1,5},{3,7},{9,13},{11,15},{4,0},{6,2},... | collective-permute-start | bytes 98312 | tf_op jit(solution)/shard_map/ppermute | solution.py:273
  17.9 1.3 %collective-permute-start.4 = (f32[8,1024]{1,0:T(8,128)S(1)}, f32[8,1024]{1,0:T(8,128)S(1)}, u32[]{:S(2)}, u32[]{:S(2)}) collective-permute-start(f32[8,1024]{1,0:T(8,128)S(1)} %add_add_fusion.mine_ref), channel_id=1, source_target_pairs={{0,1},{1,0},{2,3},{3,2},{4,5},{5,4},{6,7},{7,6},{8,9},{9,8},{10,11... | collective-permute-start | bytes 98312 | tf_op jit(solution)/shard_map/ppermute | solution.py:273
  20.6 1.2 %collective-permute-start.5 = (f32[8,512]{1,0:T(8,128)S(1)}, f32[8,512]{1,0:T(8,128)S(1)}, u32[]{:S(2)}, u32[]{:S(2)}) collective-permute-start(f32[8,512]{1,0:T(8,128)S(1)} %get-tuple-element.17), channel_id=1, source_target_pairs={{0,1},{1,0},{2,3},{3,2},{4,5},{5,4},{6,7},{7,6},{8,9},{9,8},{10,11... | collective-permute-start | bytes 49160 | tf_op jit(solution)/shard_map/ppermute | solution.py:273
  21.8 4.9 %collective-permute-start.9 = (f32[8,512]{1,0:T(8,128)S(1)}, f32[8,512]{1,0:T(8,128)S(1)}, u32[]{:S(2)}, u32[]{:S(2)}) collective-permute-start(f32[8,512]{1,0:T(8,128)S(1)} %add.19.own_ref), channel_id=1, source_target_pairs={{0,2},{4,6},{8,10},{12,14},{1,15},{3,13},{5,11},{7,9},{2,0},{6,4},... | collective-permute-start | bytes 49160 | tf_op jit(solution)/shard_map/ppermute | solution.py:273
  23.3 5.7 %collective-permute-start.8 = (f32[8,512]{1,0:T(8,128)S(1)}, f32[8,512]{1,0:T(8,128)S(1)}, u32[]{:S(2)}, u32[]{:S(2)}) collective-permute-start(f32[8,512]{1,0:T(8,128)S(1)} %add.19.own_ref), channel_id=1, source_target_pairs={{0,10},{2,8},{4,14},{6,12},{1,9},{3,11},{5,13},{7,15},{10,0},{8,2}... | collective-permute-start | bytes 49160 | tf_op jit(solution)/shard_map/ppermute | solution.py:273
  25.3 4.6 %collective-permute-start.7 = (f32[8,512]{1,0:T(8,128)S(1)}, f32[8,512]{1,0:T(8,128)S(1)}, u32[]{:S(2)}, u32[]{:S(2)}) collective-permute-start(f32[8,512]{1,0:T(8,128)S(1)} %add.19.own_ref), channel_id=1, source_target_pairs={{0,6},{2,4},{8,14},{10,12},{1,13},{3,15},{5,9},{7,11},{6,0},{4,2},... | collective-permute-start | bytes 49160 | tf_op jit(solution)/shard_map/ppermute | solution.py:273
  26.2 3.8 %collective-permute-start.6 = (f32[8,512]{1,0:T(8,128)S(1)}, f32[8,512]{1,0:T(8,128)S(1)}, u32[]{:S(2)}, u32[]{:S(2)}) collective-permute-start(f32[8,512]{1,0:T(8,128)S(1)} %add.19.own_ref), channel_id=1, source_target_pairs={{0,5},{2,7},{8,13},{10,15},{1,4},{3,6},{9,12},{11,14},{5,0},{7,2},... | collective-permute-start | bytes 49160 | tf_op jit(solution)/shard_map/ppermute | solution.py:273
  26.7 3.4 %collective-permute-start.12 = (f32[8,512]{1,0:T(8,128)S(1)}, f32[8,512]{1,0:T(8,128)S(1)}, u32[]{:S(2)}, u32[]{:S(2)}) collective-permute-start(f32[8,512]{1,0:T(8,128)S(1)} %collective-permute-done.9.refs_2_), channel_id=1, source_target_pairs={{0,1},{1,0},{2,3},{3,2},{4,5},{5,4},{6,7},{7,6},{8,9},{9,8},{10,11... | collective-permute-start | bytes 49160 | tf_op jit(solution)/shard_map/ppermute | solution.py:273
  29.0 1.2 %collective-permute-start.11 = (f32[8,512]{1,0:T(8,128)S(1)}, f32[8,512]{1,0:T(8,128)S(1)}, u32[]{:S(2)}, u32[]{:S(2)}) collective-permute-start(f32[8,512]{1,0:T(8,128)S(1)} %collective-permute-done.8.refs_1_), channel_id=1, source_target_pairs={{0,1},{1,0},{2,3},{3,2},{4,5},{5,4},{6,7},{7,6},{8,9},{9,8},{10,11... | collective-permute-start | bytes 49160 | tf_op jit(solution)/shard_map/ppermute | solution.py:273
  29.9 1.2 %collective-permute-start.10 = (f32[8,512]{1,0:T(8,128)S(1)}, f32[8,512]{1,0:T(8,128)S(1)}, u32[]{:S(2)}, u32[]{:S(2)}) collective-permute-start(f32[8,512]{1,0:T(8,128)S(1)} %collective-permute-done.7.refs_0_), channel_id=1, source_target_pairs={{0,1},{1,0},{2,3},{3,2},{4,5},{5,4},{6,7},{7,6},{8,9},{9,8},{10,11... | collective-permute-start | bytes 49160 | tf_op jit(solution)/shard_map/ppermute | solution.py:273

commit v10 on v8

--- a/solution.py
+++ b/solution.py
@@ -9,7 +9,7 @@
 
 RANK = 4
 EPSILON = 1e-08
-CHUNKS = 8
+CHUNKS = 4
 BF16 = jnp.bfloat16
 F32 = jnp.float32
 
@@ -95,9 +95,10 @@
     )(*[pltpu.with_memory_space_constraint(value, pltpu.HBM) for value in (seeds, grads, errors)])
 
 
-def merge_body(grads_ref, errors_ref, merged_ref, high_ref, low_ref):
+def merge_body(grads_ref, errors_ref, merged_ref, high_ref, low_ref, zero_ref):
     mats, rows, cols = grads_ref.shape
     size = 64
+    zero_ref[...] = jnp.zeros_like(zero_ref)
 
     @pl.loop(0, rows // size)
     def _(step):
@@ -114,9 +115,14 @@
     shape = grads.shape
     return pl.pallas_call(
         merge_body,
-        out_shape=(pltpu.VMEM(shape, F32), pltpu.VMEM(shape, BF16), pltpu.VMEM(shape, BF16)),
+        out_shape=(
+            pltpu.VMEM(shape, F32),
+            pltpu.VMEM(shape, BF16),
+            pltpu.VMEM(shape, BF16),
+            jax.ShapeDtypeStruct((shape[0] * RANK, shape[1]), F32),
+        ),
         in_specs=[pl.BlockSpec(memory_space=pltpu.VMEM)] * 2,
-        out_specs=[pl.BlockSpec(memory_space=pltpu.VMEM)] * 3,
+        out_specs=[pl.BlockSpec(memory_space=pltpu.VMEM)] * 4,
         compiler_params=pltpu.CompilerParams(vmem_limit_bytes=16 * 2**20),
         cost_estimate=pl.CostEstimate(flops=3 * grads.size, bytes_accessed=14 * grads.size, transcendentals=0),
         name="merge",
@@ -259,12 +265,13 @@
     return swap(value, ("dp", "tensor"), pairs)
 
 
-def chips_sum(value, cross):
+def chips_sum(value, cross, zero=0.0):
     count = lax.axis_size("dp")
     last = max(count // 4, 1)
     step = 1
     while step < last:
-        value = value + swap_chips(value, step, cross)
+        value = value + (swap_chips(value, step, cross) + zero)
+        zero = 0.0
         step *= 2
     terms = [value] + [swap_chips(value, offset, cross) for offset in range(last, count, last)]
     while len(terms) > 1:
@@ -275,8 +282,8 @@
 def body(grads, errors, seeds):
     replicas = lax.axis_size("dp")
     left_part, grads, errors = project(seeds, grads, errors)
-    merged, high, low = merge(grads, errors)
-    mine = chips_sum(left_part, 0)
+    merged, high, low, zero = merge(grads, errors)
+    mine = chips_sum(left_part, 0, zero)
     left, right_part = reflect(mine, swap_cores(mine), high, low, 1.0 / replicas)
     right = chips_sum(right_part + swap_cores(right_part), 1)
     return finish(turn(left), right, merged, 1.0 / replicas)

time: 34.2 us -> 35.1 us (1.026)
  waiting for transfers between devices: 10.9 us -> 12.4 us
  Pallas kernels: 9.17 us -> 8.71 us
    ppermute x10, waiting for transfers between devices: 10.9 us -> 12.4 us  [swap(): lax.ppermute(value, axes, pairs + [(target, source) for source, target in...]
    pallas_call x1, Pallas kernels: 3.71 us -> 3.35 us  [project(): pl.pallas_call(project_body, out_shape=(jax.ShapeDtypeStruct((mats * RANK...]
  transfers between devices with their start and end apart: 10 -> 10, of which waited for: 9 -> 8; matrix products, arithmetic and copies ran while one was open for 0% -> 0% of each run, Pallas kernels for 3% -> 3%
where the time goes in v10:
time: 35.1 us; the launch traced here: 35 us
  starting transfers between devices  13.2 us (38%)
  waiting for transfers between devices  12.4 us (35%)
  Pallas kernels  8.71 us (25%)
  between operations  0.69 us (2%)
    ppermute x10, starting transfers between devices, swap(): lax.ppermute(value, axes, pairs + [(target, source) for source, target in...  13.2 us
    ppermute x10, waiting for transfers between devices, swap(): lax.ppermute(value, axes, pairs + [(target, source) for source, target in...  12.4 us
    pallas_call x1, Pallas kernels, project(): pl.pallas_call(project_body, out_shape=(jax.ShapeDtypeStruct((mats * RANK...  3.35 us
    pallas_call x1, Pallas kernels, finish(): pl.pallas_call(functools.partial(finish_body, scale), out_shape=(jax.Shap...  3 us
    pallas_call x1, Pallas kernels, reflect(): pl.pallas_call(functools.partial(reflect_body, scale), out_shape=(jax.Sha...  1.36 us
    pallas_call x1, Pallas kernels, merge(): pl.pallas_call(merge_body, out_shape=(pltpu.VMEM(shape, F32), pltpu.VMEM(...  0.86 us
  transfers between devices with their start and end apart: 10, of which 8 were waited for; matrix products, arithmetic and copies ran while one was open for 0% of the time, Pallas kernels for 3%

profile of v10, /device:TPU:0, one launch (start us, length us, event | category | flops | bytes accessed | tf_op | source)
XLA Modules:
  0.0 35.0 jit_solution(13910725682851582162)
XLA Ops:
  0.6 3.4 %project.1 = (f32[8,1024]{1,0:T(8,128)S(1)}, bf16[2,1024,512]{2,1,0:T(8,128)(2,1)S(1)}, f32[2,1024,512]{2,1,0:T(8,128)S(1)}) custom-call(s32[2]{0:T(128)} %seeds_ref.1, bf16[1,2,1024,512]{3,2,1,0:T(8,128)(2,1)} %grads_ref.1, f32[1,2,1024,512]{3,2,1,0:T(8,128)} %errors_ref.1), custom_call_target="tpu_custom_call" | custom-call | tf_op jit(solution)/shard_map/project/pallas_call | solution.py:79
  4.0 3.0 %collective-permute-start = (f32[8,1024]{1,0:T(8,128)S(1)}, f32[8,1024]{1,0:T(8,128)S(1)}, u32[]{:S(2)}, u32[]{:S(2)}) collective-permute-start(f32[8,1024]{1,0:T(8,128)S(1)} %get-tuple-element.11), channel_id=1, source_target_pairs={{0,2},{1,3},{4,6},{5,7},{8,10},{9,11},{12,14},{13,15},{2,0},{3,1},... | collective-permute-start | bytes 98312 | tf_op jit(solution)/shard_map/ppermute | solution.py:255
  7.0 0.9 %merge.1 = (f32[2,1024,512]{2,1,0:T(8,128)S(1)}, bf16[2,1024,512]{2,1,0:T(8,128)(2,1)S(1)}, bf16[2,1024,512]{2,1,0:T(8,128)(2,1)S(1)}, f32[8,1024]{1,0:T(8,128)S(1)}) custom-call(bf16[2,1024,512]{2,1,0:T(8,128)(2,1)S(1)} %get-tuple-element.12.grads_ref, f32[2,1024,512]{2,1,0:T(8,128)S(1)} %get-tuple-element.13.errors_ref), custom_call_target="tpu_custom_call" | custom-call | flops 3145728 | bytes 14680064 | tf_op jit(solution)/shard_map/merge/pallas_call | solution.py:116
  7.9 1.0 %collective-permute-done = f32[8,1024]{1,0:T(8,128)S(1)} collective-permute-done((f32[8,1024]{1,0:T(8,128)S(1)}, f32[8,1024]{1,0:T(8,128)S(1)}, u32[]{:S(2)}, u32[]{:S(2)}) %collective-permute-start) | collective-permute-done | bytes 32800 | tf_op jit(solution)/shard_map/ppermute | solution.py:255
  8.9 2.1 %collective-permute-start.1 = (f32[8,1024]{1,0:T(8,128)S(1)}, f32[8,1024]{1,0:T(8,128)S(1)}, u32[]{:S(2)}, u32[]{:S(2)}) collective-permute-start(f32[8,1024]{1,0:T(8,128)S(1)} %add_add_fusion.1), channel_id=1, source_target_pairs={{0,4},{1,5},{2,6},{3,7},{8,12},{9,13},{10,14},{11,15},{4,0},{5,1},... | collective-permute-start | bytes 98312 | tf_op jit(solution)/shard_map/ppermute | solution.py:255
  11.1 2.6 %collective-permute-start.2 = (f32[8,1024]{1,0:T(8,128)S(1)}, f32[8,1024]{1,0:T(8,128)S(1)}, u32[]{:S(2)}, u32[]{:S(2)}) collective-permute-start(f32[8,1024]{1,0:T(8,128)S(1)} %add_add_fusion.1), channel_id=1, source_target_pairs={{0,8},{1,9},{2,10},{3,11},{4,12},{5,13},{6,14},{7,15},{8,0},{9,1},... | collective-permute-start | bytes 98312 | tf_op jit(solution)/shard_map/ppermute | solution.py:255
  13.7 0.0 collective-permute-start.3
  13.7 0.0 collective-permute-done.1
  13.7 2.5 %collective-permute-done.2 = f32[8,1024]{1,0:T(8,128)S(1)} collective-permute-done((f32[8,1024]{1,0:T(8,128)S(1)}, f32[8,1024]{1,0:T(8,128)S(1)}, u32[]{:S(2)}, u32[]{:S(2)}) %collective-permute-start.2) | collective-permute-done | bytes 32800 | tf_op jit(solution)/shard_map/ppermute | solution.py:255
  16.1 3.2 %collective-permute-done.3 = f32[8,1024]{1,0:T(8,128)S(1)} collective-permute-done((f32[8,1024]{1,0:T(8,128)S(1)}, f32[8,1024]{1,0:T(8,128)S(1)}, u32[]{:S(2)}, u32[]{:S(2)}) %collective-permute-start.3) | collective-permute-done | bytes 32800 | tf_op jit(solution)/shard_map/ppermute | solution.py:255
  19.4 0.1 collective-permute-start.4
  19.5 1.2 %collective-permute-done.4.other_ref = f32[8,1024]{1,0:T(8,128)S(1)} collective-permute-done((f32[8,1024]{1,0:T(8,128)S(1)}, f32[8,1024]{1,0:T(8,128)S(1)}, u32[]{:S(2)}, u32[]{:S(2)}) %collective-permute-start.4) | collective-permute-done | bytes 32800 | tf_op jit(solution)/shard_map/ppermute | solution.py:255
  20.7 1.4 %reflect.1 = (f32[8,1024]{1,0:T(8,128)S(1)}, f32[8,512]{1,0:T(8,128)S(1)}) custom-call(f32[8,1024]{1,0:T(8,128)S(1)} %add_add_fusion.mine_ref, f32[8,1024]{1,0:T(8,128)S(1)} %collective-permute-done.4.other_ref, bf16[2,1024,512]{2,1,0:T(8,128)(2,1)S(1)} %get-tuple-element.15.high_ref, bf16[2,1024,512]{2,1,0:T(8,128)(2,1)S(1)} %get-tuple-element.16.low_ref), custom_call_target="tpu_custom_call" | custom-call | tf_op jit(solution)/shard_map/reflect/pallas_call | solution.py:174
  22.0 0.2 collective-permute-start.5
  22.2 1.0 %collective-permute-done.5 = f32[8,512]{1,0:T(8,128)S(1)} collective-permute-done((f32[8,512]{1,0:T(8,128)S(1)}, f32[8,512]{1,0:T(8,128)S(1)}, u32[]{:S(2)}, u32[]{:S(2)}) %collective-permute-start.5) | collective-permute-done | bytes 16416 | tf_op jit(solution)/shard_map/ppermute | solution.py:255
  23.2 1.3 %collective-permute-start.6 = (f32[8,512]{1,0:T(8,128)S(1)}, f32[8,512]{1,0:T(8,128)S(1)}, u32[]{:S(2)}, u32[]{:S(2)}) collective-permute-start(f32[8,512]{1,0:T(8,128)S(1)} %add.35), channel_id=1, source_target_pairs={{0,3},{1,2},{4,7},{5,6},{8,11},{9,10},{12,15},{13,14},{3,0},{2,1},... | collective-permute-start | bytes 49160 | tf_op jit(solution)/shard_map/ppermute | solution.py:255
  24.5 1.9 %collective-permute-done.6 = f32[8,512]{1,0:T(8,128)S(1)} collective-permute-done((f32[8,512]{1,0:T(8,128)S(1)}, f32[8,512]{1,0:T(8,128)S(1)}, u32[]{:S(2)}, u32[]{:S(2)}) %collective-permute-start.6) | collective-permute-done | bytes 16416 | tf_op jit(solution)/shard_map/ppermute | solution.py:255
  26.4 0.0 collective-permute-start.7
  26.4 0.6 %collective-permute-start.8 = (f32[8,512]{1,0:T(8,128)S(1)}, f32[8,512]{1,0:T(8,128)S(1)}, u32[]{:S(2)}, u32[]{:S(2)}) collective-permute-start(f32[8,512]{1,0:T(8,128)S(1)} %add.36), channel_id=1, source_target_pairs={{0,9},{1,8},{2,11},{3,10},{4,13},{5,12},{6,15},{7,14},{9,0},{8,1},... | collective-permute-start | bytes 49160 | tf_op jit(solution)/shard_map/ppermute | solution.py:255
  27.0 3.2 %collective-permute-start.9 = (f32[8,512]{1,0:T(8,128)S(1)}, f32[8,512]{1,0:T(8,128)S(1)}, u32[]{:S(2)}, u32[]{:S(2)}) collective-permute-start(f32[8,512]{1,0:T(8,128)S(1)} %add.36), channel_id=1, source_target_pairs={{0,13},{1,12},{2,15},{3,14},{4,9},{5,8},{6,11},{7,10},{13,0},{12,1... | collective-permute-start | bytes 49160 | tf_op jit(solution)/shard_map/ppermute | solution.py:255
  30.3 0.1 turn.1.left_ref
  30.4 0.0 collective-permute-done.7
  30.4 0.1 collective-permute-done.8
  30.5 1.5 %collective-permute-done.9 = f32[8,512]{1,0:T(8,128)S(1)} collective-permute-done((f32[8,512]{1,0:T(8,128)S(1)}, f32[8,512]{1,0:T(8,128)S(1)}, u32[]{:S(2)}, u32[]{:S(2)}) %collective-permute-start.9) | collective-permute-done | bytes 16416 | tf_op jit(solution)/shard_map/ppermute | solution.py:255
  32.0 3.0 %finish.1 = (bf16[2,1024,512]{2,1,0:T(8,128)(2,1)}, f32[1,2,1024,512]{3,2,1,0:T(8,128)}) custom-call(bf16[1024,32]{1,0:T(8,128)(2,1)S(1)} %turn.1.left_ref, f32[8,512]{1,0:T(8,128)S(1)} %add_add_fusion.2.right_ref, f32[2,1024,512]{2,1,0:T(8,128)S(1)} %get-tuple-element.19.merged_ref), custom_call_target="tpu_custom_call" | custom-call | tf_op jit(solution)/shard_map/finish/pallas_call | solution.py:232
  (5 shorter events, 0.0 us)
Async XLA Ops:
  4.0 4.9 %collective-permute-start = (f32[8,1024]{1,0:T(8,128)S(1)}, f32[8,1024]{1,0:T(8,128)S(1)}, u32[]{:S(2)}, u32[]{:S(2)}) collective-permute-start(f32[8,1024]{1,0:T(8,128)S(1)} %get-tuple-element.11), channel_id=1, source_target_pairs={{0,2},{1,3},{4,6},{5,7},{8,10},{9,11},{12,14},{13,15},{2,0},{3,1},... | collective-permute-start | bytes 98312 | tf_op jit(solution)/shard_map/ppermute | solution.py:255
  8.9 4.7 %collective-permute-start.1 = (f32[8,1024]{1,0:T(8,128)S(1)}, f32[8,1024]{1,0:T(8,128)S(1)}, u32[]{:S(2)}, u32[]{:S(2)}) collective-permute-start(f32[8,1024]{1,0:T(8,128)S(1)} %add_add_fusion.1), channel_id=1, source_target_pairs={{0,4},{1,5},{2,6},{3,7},{8,12},{9,13},{10,14},{11,15},{4,0},{5,1},... | collective-permute-start | bytes 98312 | tf_op jit(solution)/shard_map/ppermute | solution.py:255
  11.1 5.1 %collective-permute-start.2 = (f32[8,1024]{1,0:T(8,128)S(1)}, f32[8,1024]{1,0:T(8,128)S(1)}, u32[]{:S(2)}, u32[]{:S(2)}) collective-permute-start(f32[8,1024]{1,0:T(8,128)S(1)} %add_add_fusion.1), channel_id=1, source_target_pairs={{0,8},{1,9},{2,10},{3,11},{4,12},{5,13},{6,14},{7,15},{8,0},{9,1},... | collective-permute-start | bytes 98312 | tf_op jit(solution)/shard_map/ppermute | solution.py:255
  13.7 5.7 %collective-permute-start.3 = (f32[8,1024]{1,0:T(8,128)S(1)}, f32[8,1024]{1,0:T(8,128)S(1)}, u32[]{:S(2)}, u32[]{:S(2)}) collective-permute-start(f32[8,1024]{1,0:T(8,128)S(1)} %add_add_fusion.1), channel_id=1, source_target_pairs={{0,12},{1,13},{2,14},{3,15},{4,8},{5,9},{6,10},{7,11},{12,0},{13,1... | collective-permute-start | bytes 98312 | tf_op jit(solution)/shard_map/ppermute | solution.py:255
  19.4 1.3 %collective-permute-start.4 = (f32[8,1024]{1,0:T(8,128)S(1)}, f32[8,1024]{1,0:T(8,128)S(1)}, u32[]{:S(2)}, u32[]{:S(2)}) collective-permute-start(f32[8,1024]{1,0:T(8,128)S(1)} %add_add_fusion.mine_ref), channel_id=1, source_target_pairs={{0,1},{1,0},{2,3},{3,2},{4,5},{5,4},{6,7},{7,6},{8,9},{9,8},{10,11... | collective-permute-start | bytes 98312 | tf_op jit(solution)/shard_map/ppermute | solution.py:255
  22.0 1.2 %collective-permute-start.5 = (f32[8,512]{1,0:T(8,128)S(1)}, f32[8,512]{1,0:T(8,128)S(1)}, u32[]{:S(2)}, u32[]{:S(2)}) collective-permute-start(f32[8,512]{1,0:T(8,128)S(1)} %get-tuple-element.18), channel_id=1, source_target_pairs={{0,1},{1,0},{2,3},{3,2},{4,5},{5,4},{6,7},{7,6},{8,9},{9,8},{10,11... | collective-permute-start | bytes 49160 | tf_op jit(solution)/shard_map/ppermute | solution.py:255
  23.2 3.2 %collective-permute-start.6 = (f32[8,512]{1,0:T(8,128)S(1)}, f32[8,512]{1,0:T(8,128)S(1)}, u32[]{:S(2)}, u32[]{:S(2)}) collective-permute-start(f32[8,512]{1,0:T(8,128)S(1)} %add.35), channel_id=1, source_target_pairs={{0,3},{1,2},{4,7},{5,6},{8,11},{9,10},{12,15},{13,14},{3,0},{2,1},... | collective-permute-start | bytes 49160 | tf_op jit(solution)/shard_map/ppermute | solution.py:255
  26.4 4.0 %collective-permute-start.7 = (f32[8,512]{1,0:T(8,128)S(1)}, f32[8,512]{1,0:T(8,128)S(1)}, u32[]{:S(2)}, u32[]{:S(2)}) collective-permute-start(f32[8,512]{1,0:T(8,128)S(1)} %add.36), channel_id=1, source_target_pairs={{0,5},{1,4},{2,7},{3,6},{8,13},{9,12},{10,15},{11,14},{5,0},{4,1},... | collective-permute-start | bytes 49160 | tf_op jit(solution)/shard_map/ppermute | solution.py:255
  26.4 4.1 %collective-permute-start.8 = (f32[8,512]{1,0:T(8,128)S(1)}, f32[8,512]{1,0:T(8,128)S(1)}, u32[]{:S(2)}, u32[]{:S(2)}) collective-permute-start(f32[8,512]{1,0:T(8,128)S(1)} %add.36), channel_id=1, source_target_pairs={{0,9},{1,8},{2,11},{3,10},{4,13},{5,12},{6,15},{7,14},{9,0},{8,1},... | collective-permute-start | bytes 49160 | tf_op jit(solution)/shard_map/ppermute | solution.py:255
  27.0 5.0 %collective-permute-start.9 = (f32[8,512]{1,0:T(8,128)S(1)}, f32[8,512]{1,0:T(8,128)S(1)}, u32[]{:S(2)}, u32[]{:S(2)}) collective-permute-start(f32[8,512]{1,0:T(8,128)S(1)} %add.36), channel_id=1, source_target_pairs={{0,13},{1,12},{2,15},{3,14},{4,9},{5,8},{6,11},{7,10},{13,0},{12,1... | collective-permute-start | bytes 49160 | tf_op jit(solution)/shard_map/ppermute | solution.py:255

commit v11 on v10

--- a/solution.py
+++ b/solution.py
@@ -273,9 +273,10 @@
         value = value + (swap_chips(value, step, cross) + zero)
         zero = 0.0
         step *= 2
-    terms = [value] + [swap_chips(value, offset, cross) for offset in range(last, count, last)]
+    terms = [swap_chips(value, offset, cross) for offset in range(count - last, 0, -last)]
+    terms = [value] + terms[::-1]
     while len(terms) > 1:
-        terms = [terms[at] + terms[at + 1] for at in range(0, len(terms), 2)]
+        terms = [terms[at + 1] + terms[at] for at in range(0, len(terms), 2)]
     return terms[0]
 
 

time: 35.1 us -> 33.7 us (0.960)
  waiting for transfers between devices: 12.4 us -> 10.9 us
    ppermute x10, waiting for transfers between devices: 12.4 us -> 10.9 us  [swap(): lax.ppermute(value, axes, pairs + [(target, source) for source, target in...]
  transfers between devices with their start and end apart: 10 -> 10, of which waited for: 8 -> 9; matrix products, arithmetic and copies ran while one was open for 0% -> 0% of each run, Pallas kernels for 3% -> 3%
where the time goes in v11:
time: 33.7 us; the launch traced here: 33.6 us
  starting transfers between devices  13.2 us (39%)
  waiting for transfers between devices  10.9 us (32%)
  Pallas kernels  8.7 us (26%)
  between operations  0.68 us (2%)
    ppermute x10, starting transfers between devices, swap(): lax.ppermute(value, axes, pairs + [(target, source) for source, target in...  13.2 us
    ppermute x10, waiting for transfers between devices, swap(): lax.ppermute(value, axes, pairs + [(target, source) for source, target in...  10.9 us
    pallas_call x1, Pallas kernels, project(): pl.pallas_call(project_body, out_shape=(jax.ShapeDtypeStruct((mats * RANK...  3.35 us
    pallas_call x1, Pallas kernels, finish(): pl.pallas_call(functools.partial(finish_body, scale), out_shape=(jax.Shap...  2.99 us
    pallas_call x1, Pallas kernels, reflect(): pl.pallas_call(functools.partial(reflect_body, scale), out_shape=(jax.Sha...  1.36 us
    pallas_call x1, Pallas kernels, merge(): pl.pallas_call(merge_body, out_shape=(pltpu.VMEM(shape, F32), pltpu.VMEM(...  0.86 us
  transfers between devices with their start and end apart: 10, of which 9 were waited for; matrix products, arithmetic and copies ran while one was open for 0% of the time, Pallas kernels for 3%

profile of v11, /device:TPU:0, one launch (start us, length us, event | category | flops | bytes accessed | tf_op | source)
XLA Modules:
  0.0 33.6 jit_solution(14851527134177169292)
XLA Ops:
  0.6 3.4 %project.1 = (f32[8,1024]{1,0:T(8,128)S(1)}, bf16[2,1024,512]{2,1,0:T(8,128)(2,1)S(1)}, f32[2,1024,512]{2,1,0:T(8,128)S(1)}) custom-call(s32[2]{0:T(128)} %seeds_ref.1, bf16[1,2,1024,512]{3,2,1,0:T(8,128)(2,1)} %grads_ref.1, f32[1,2,1024,512]{3,2,1,0:T(8,128)} %errors_ref.1), custom_call_target="tpu_custom_call" | custom-call | tf_op jit(solution)/shard_map/project/pallas_call | solution.py:79
  4.0 3.0 %collective-permute-start = (f32[8,1024]{1,0:T(8,128)S(1)}, f32[8,1024]{1,0:T(8,128)S(1)}, u32[]{:S(2)}, u32[]{:S(2)}) collective-permute-start(f32[8,1024]{1,0:T(8,128)S(1)} %get-tuple-element.11), channel_id=1, source_target_pairs={{0,2},{1,3},{4,6},{5,7},{8,10},{9,11},{12,14},{13,15},{2,0},{3,1},... | collective-permute-start | bytes 98312 | tf_op jit(solution)/shard_map/ppermute | solution.py:255
  7.0 0.9 %merge.1 = (f32[2,1024,512]{2,1,0:T(8,128)S(1)}, bf16[2,1024,512]{2,1,0:T(8,128)(2,1)S(1)}, bf16[2,1024,512]{2,1,0:T(8,128)(2,1)S(1)}, f32[8,1024]{1,0:T(8,128)S(1)}) custom-call(bf16[2,1024,512]{2,1,0:T(8,128)(2,1)S(1)} %get-tuple-element.12.grads_ref, f32[2,1024,512]{2,1,0:T(8,128)S(1)} %get-tuple-element.13.errors_ref), custom_call_target="tpu_custom_call" | custom-call | flops 3145728 | bytes 14680064 | tf_op jit(solution)/shard_map/merge/pallas_call | solution.py:116
  7.9 1.0 %collective-permute-done = f32[8,1024]{1,0:T(8,128)S(1)} collective-permute-done((f32[8,1024]{1,0:T(8,128)S(1)}, f32[8,1024]{1,0:T(8,128)S(1)}, u32[]{:S(2)}, u32[]{:S(2)}) %collective-permute-start) | collective-permute-done | bytes 32800 | tf_op jit(solution)/shard_map/ppermute | solution.py:255
  8.9 4.2 %collective-permute-start.1 = (f32[8,1024]{1,0:T(8,128)S(1)}, f32[8,1024]{1,0:T(8,128)S(1)}, u32[]{:S(2)}, u32[]{:S(2)}) collective-permute-start(f32[8,1024]{1,0:T(8,128)S(1)} %add_add_fusion.1), channel_id=1, source_target_pairs={{0,12},{1,13},{2,14},{3,15},{4,8},{5,9},{6,10},{7,11},{12,0},{13,1... | collective-permute-start | bytes 98312 | tf_op jit(solution)/shard_map/ppermute | solution.py:255
  13.1 0.0 collective-permute-start.2
  13.1 0.6 %collective-permute-start.3 = (f32[8,1024]{1,0:T(8,128)S(1)}, f32[8,1024]{1,0:T(8,128)S(1)}, u32[]{:S(2)}, u32[]{:S(2)}) collective-permute-start(f32[8,1024]{1,0:T(8,128)S(1)} %add_add_fusion.1), channel_id=1, source_target_pairs={{0,4},{1,5},{2,6},{3,7},{8,12},{9,13},{10,14},{11,15},{4,0},{5,1},... | collective-permute-start | bytes 98312 | tf_op jit(solution)/shard_map/ppermute | solution.py:255
  13.7 1.3 %collective-permute-done.1 = f32[8,1024]{1,0:T(8,128)S(1)} collective-permute-done((f32[8,1024]{1,0:T(8,128)S(1)}, f32[8,1024]{1,0:T(8,128)S(1)}, u32[]{:S(2)}, u32[]{:S(2)}) %collective-permute-start.1) | collective-permute-done | bytes 32800 | tf_op jit(solution)/shard_map/ppermute | solution.py:255
  15.0 2.9 %collective-permute-done.2 = f32[8,1024]{1,0:T(8,128)S(1)} collective-permute-done((f32[8,1024]{1,0:T(8,128)S(1)}, f32[8,1024]{1,0:T(8,128)S(1)}, u32[]{:S(2)}, u32[]{:S(2)}) %collective-permute-start.2) | collective-permute-done | bytes 32800 | tf_op jit(solution)/shard_map/ppermute | solution.py:255
  17.9 0.0 collective-permute-done.3
  17.9 0.1 collective-permute-start.4
  18.0 1.2 %collective-permute-done.4.other_ref = f32[8,1024]{1,0:T(8,128)S(1)} collective-permute-done((f32[8,1024]{1,0:T(8,128)S(1)}, f32[8,1024]{1,0:T(8,128)S(1)}, u32[]{:S(2)}, u32[]{:S(2)}) %collective-permute-start.4) | collective-permute-done | bytes 32800 | tf_op jit(solution)/shard_map/ppermute | solution.py:255
  19.2 1.4 %reflect.1 = (f32[8,1024]{1,0:T(8,128)S(1)}, f32[8,512]{1,0:T(8,128)S(1)}) custom-call(f32[8,1024]{1,0:T(8,128)S(1)} %add_add_fusion.mine_ref, f32[8,1024]{1,0:T(8,128)S(1)} %collective-permute-done.4.other_ref, bf16[2,1024,512]{2,1,0:T(8,128)(2,1)S(1)} %get-tuple-element.15.high_ref, bf16[2,1024,512]{2,1,0:T(8,128)(2,1)S(1)} %get-tuple-element.16.low_ref), custom_call_target="tpu_custom_call" | custom-call | tf_op jit(solution)/shard_map/reflect/pallas_call | solution.py:174
  20.6 0.2 collective-permute-start.5
  20.7 1.0 %collective-permute-done.5 = f32[8,512]{1,0:T(8,128)S(1)} collective-permute-done((f32[8,512]{1,0:T(8,128)S(1)}, f32[8,512]{1,0:T(8,128)S(1)}, u32[]{:S(2)}, u32[]{:S(2)}) %collective-permute-start.5) | collective-permute-done | bytes 16416 | tf_op jit(solution)/shard_map/ppermute | solution.py:255
  21.8 1.3 %collective-permute-start.6 = (f32[8,512]{1,0:T(8,128)S(1)}, f32[8,512]{1,0:T(8,128)S(1)}, u32[]{:S(2)}, u32[]{:S(2)}) collective-permute-start(f32[8,512]{1,0:T(8,128)S(1)} %add.35), channel_id=1, source_target_pairs={{0,3},{1,2},{4,7},{5,6},{8,11},{9,10},{12,15},{13,14},{3,0},{2,1},... | collective-permute-start | bytes 49160 | tf_op jit(solution)/shard_map/ppermute | solution.py:255
  23.0 1.9 %collective-permute-done.6 = f32[8,512]{1,0:T(8,128)S(1)} collective-permute-done((f32[8,512]{1,0:T(8,128)S(1)}, f32[8,512]{1,0:T(8,128)S(1)}, u32[]{:S(2)}, u32[]{:S(2)}) %collective-permute-start.6) | collective-permute-done | bytes 16416 | tf_op jit(solution)/shard_map/ppermute | solution.py:255
  24.9 1.2 %collective-permute-start.7 = (f32[8,512]{1,0:T(8,128)S(1)}, f32[8,512]{1,0:T(8,128)S(1)}, u32[]{:S(2)}, u32[]{:S(2)}) collective-permute-start(f32[8,512]{1,0:T(8,128)S(1)} %add.36), channel_id=1, source_target_pairs={{0,13},{1,12},{2,15},{3,14},{4,9},{5,8},{6,11},{7,10},{13,0},{12,1... | collective-permute-start | bytes 49160 | tf_op jit(solution)/shard_map/ppermute | solution.py:255
  26.2 0.6 %collective-permute-start.8 = (f32[8,512]{1,0:T(8,128)S(1)}, f32[8,512]{1,0:T(8,128)S(1)}, u32[]{:S(2)}, u32[]{:S(2)}) collective-permute-start(f32[8,512]{1,0:T(8,128)S(1)} %add.36), channel_id=1, source_target_pairs={{0,9},{1,8},{2,11},{3,10},{4,13},{5,12},{6,15},{7,14},{9,0},{8,1},... | collective-permute-start | bytes 49160 | tf_op jit(solution)/shard_map/ppermute | solution.py:255
  26.8 2.0 %collective-permute-start.9 = (f32[8,512]{1,0:T(8,128)S(1)}, f32[8,512]{1,0:T(8,128)S(1)}, u32[]{:S(2)}, u32[]{:S(2)}) collective-permute-start(f32[8,512]{1,0:T(8,128)S(1)} %add.36), channel_id=1, source_target_pairs={{0,5},{1,4},{2,7},{3,6},{8,13},{9,12},{10,15},{11,14},{5,0},{4,1},... | collective-permute-start | bytes 49160 | tf_op jit(solution)/shard_map/ppermute | solution.py:255
  28.8 0.1 turn.1.left_ref
  28.9 0.9 %collective-permute-done.7 = f32[8,512]{1,0:T(8,128)S(1)} collective-permute-done((f32[8,512]{1,0:T(8,128)S(1)}, f32[8,512]{1,0:T(8,128)S(1)}, u32[]{:S(2)}, u32[]{:S(2)}) %collective-permute-start.7) | collective-permute-done | bytes 16416 | tf_op jit(solution)/shard_map/ppermute | solution.py:255
  29.9 0.5 %collective-permute-done.8 = f32[8,512]{1,0:T(8,128)S(1)} collective-permute-done((f32[8,512]{1,0:T(8,128)S(1)}, f32[8,512]{1,0:T(8,128)S(1)}, u32[]{:S(2)}, u32[]{:S(2)}) %collective-permute-start.8) | collective-permute-done | bytes 16416 | tf_op jit(solution)/shard_map/ppermute | solution.py:255
  30.4 0.1 collective-permute-done.9
  30.6 3.0 %finish.1 = (bf16[2,1024,512]{2,1,0:T(8,128)(2,1)}, f32[1,2,1024,512]{3,2,1,0:T(8,128)}) custom-call(bf16[1024,32]{1,0:T(8,128)(2,1)S(1)} %turn.1.left_ref, f32[8,512]{1,0:T(8,128)S(1)} %add_add_fusion.2.right_ref, f32[2,1024,512]{2,1,0:T(8,128)S(1)} %get-tuple-element.19.merged_ref), custom_call_target="tpu_custom_call" | custom-call | tf_op jit(solution)/shard_map/finish/pallas_call | solution.py:232
  (5 shorter events, 0.0 us)
Async XLA Ops:
  4.0 4.9 %collective-permute-start = (f32[8,1024]{1,0:T(8,128)S(1)}, f32[8,1024]{1,0:T(8,128)S(1)}, u32[]{:S(2)}, u32[]{:S(2)}) collective-permute-start(f32[8,1024]{1,0:T(8,128)S(1)} %get-tuple-element.11), channel_id=1, source_target_pairs={{0,2},{1,3},{4,6},{5,7},{8,10},{9,11},{12,14},{13,15},{2,0},{3,1},... | collective-permute-start | bytes 98312 | tf_op jit(solution)/shard_map/ppermute | solution.py:255
  8.9 6.1 %collective-permute-start.1 = (f32[8,1024]{1,0:T(8,128)S(1)}, f32[8,1024]{1,0:T(8,128)S(1)}, u32[]{:S(2)}, u32[]{:S(2)}) collective-permute-start(f32[8,1024]{1,0:T(8,128)S(1)} %add_add_fusion.1), channel_id=1, source_target_pairs={{0,12},{1,13},{2,14},{3,15},{4,8},{5,9},{6,10},{7,11},{12,0},{13,1... | collective-permute-start | bytes 98312 | tf_op jit(solution)/shard_map/ppermute | solution.py:255
  13.1 4.8 %collective-permute-start.2 = (f32[8,1024]{1,0:T(8,128)S(1)}, f32[8,1024]{1,0:T(8,128)S(1)}, u32[]{:S(2)}, u32[]{:S(2)}) collective-permute-start(f32[8,1024]{1,0:T(8,128)S(1)} %add_add_fusion.1), channel_id=1, source_target_pairs={{0,8},{1,9},{2,10},{3,11},{4,12},{5,13},{6,14},{7,15},{8,0},{9,1},... | collective-permute-start | bytes 98312 | tf_op jit(solution)/shard_map/ppermute | solution.py:255
  13.1 4.8 %collective-permute-start.3 = (f32[8,1024]{1,0:T(8,128)S(1)}, f32[8,1024]{1,0:T(8,128)S(1)}, u32[]{:S(2)}, u32[]{:S(2)}) collective-permute-start(f32[8,1024]{1,0:T(8,128)S(1)} %add_add_fusion.1), channel_id=1, source_target_pairs={{0,4},{1,5},{2,6},{3,7},{8,12},{9,13},{10,14},{11,15},{4,0},{5,1},... | collective-permute-start | bytes 98312 | tf_op jit(solution)/shard_map/ppermute | solution.py:255
  17.9 1.3 %collective-permute-start.4 = (f32[8,1024]{1,0:T(8,128)S(1)}, f32[8,1024]{1,0:T(8,128)S(1)}, u32[]{:S(2)}, u32[]{:S(2)}) collective-permute-start(f32[8,1024]{1,0:T(8,128)S(1)} %add_add_fusion.mine_ref), channel_id=1, source_target_pairs={{0,1},{1,0},{2,3},{3,2},{4,5},{5,4},{6,7},{7,6},{8,9},{9,8},{10,11... | collective-permute-start | bytes 98312 | tf_op jit(solution)/shard_map/ppermute | solution.py:255
  20.6 1.2 %collective-permute-start.5 = (f32[8,512]{1,0:T(8,128)S(1)}, f32[8,512]{1,0:T(8,128)S(1)}, u32[]{:S(2)}, u32[]{:S(2)}) collective-permute-start(f32[8,512]{1,0:T(8,128)S(1)} %get-tuple-element.18), channel_id=1, source_target_pairs={{0,1},{1,0},{2,3},{3,2},{4,5},{5,4},{6,7},{7,6},{8,9},{9,8},{10,11... | collective-permute-start | bytes 49160 | tf_op jit(solution)/shard_map/ppermute | solution.py:255
  21.8 3.2 %collective-permute-start.6 = (f32[8,512]{1,0:T(8,128)S(1)}, f32[8,512]{1,0:T(8,128)S(1)}, u32[]{:S(2)}, u32[]{:S(2)}) collective-permute-start(f32[8,512]{1,0:T(8,128)S(1)} %add.35), channel_id=1, source_target_pairs={{0,3},{1,2},{4,7},{5,6},{8,11},{9,10},{12,15},{13,14},{3,0},{2,1},... | collective-permute-start | bytes 49160 | tf_op jit(solution)/shard_map/ppermute | solution.py:255
  24.9 5.0 %collective-permute-start.7 = (f32[8,512]{1,0:T(8,128)S(1)}, f32[8,512]{1,0:T(8,128)S(1)}, u32[]{:S(2)}, u32[]{:S(2)}) collective-permute-start(f32[8,512]{1,0:T(8,128)S(1)} %add.36), channel_id=1, source_target_pairs={{0,13},{1,12},{2,15},{3,14},{4,9},{5,8},{6,11},{7,10},{13,0},{12,1... | collective-permute-start | bytes 49160 | tf_op jit(solution)/shard_map/ppermute | solution.py:255
  26.2 4.3 %collective-permute-start.8 = (f32[8,512]{1,0:T(8,128)S(1)}, f32[8,512]{1,0:T(8,128)S(1)}, u32[]{:S(2)}, u32[]{:S(2)}) collective-permute-start(f32[8,512]{1,0:T(8,128)S(1)} %add.36), channel_id=1, source_target_pairs={{0,9},{1,8},{2,11},{3,10},{4,13},{5,12},{6,15},{7,14},{9,0},{8,1},... | collective-permute-start | bytes 49160 | tf_op jit(solution)/shard_map/ppermute | solution.py:255
  26.8 3.8 %collective-permute-start.9 = (f32[8,512]{1,0:T(8,128)S(1)}, f32[8,512]{1,0:T(8,128)S(1)}, u32[]{:S(2)}, u32[]{:S(2)}) collective-permute-start(f32[8,512]{1,0:T(8,128)S(1)} %add.36), channel_id=1, source_target_pairs={{0,5},{1,4},{2,7},{3,6},{8,13},{9,12},{10,15},{11,14},{5,0},{4,1},... | collective-permute-start | bytes 49160 | tf_op jit(solution)/shard_map/ppermute | solution.py:255

commit v12 on v11

--- a/solution.py
+++ b/solution.py
@@ -65,10 +65,11 @@
         for copy in copies[2 * mats * chunk : 2 * mats * (chunk + 1)]:
             copy.wait()
         for mat in range(mats):
-            value = gbuf[mat, at].astype(F32) + ebuf[mat, at]
-            high = value.astype(BF16)
-            low = (value - high.astype(F32)).astype(BF16)
-            product = lax.dot_general(weights, high, dims, preferred_element_type=F32)
+            error = ebuf[mat, at]
+            high = error.astype(BF16)
+            low = (error - high.astype(F32)).astype(BF16)
+            product = lax.dot_general(weights, gbuf[mat, at], dims, preferred_element_type=F32)
+            product = product + lax.dot_general(weights, high, dims, preferred_element_type=F32)
             product = product + lax.dot_general(weights, low, dims, preferred_element_type=F32)
             left = fold(mat, left, product)
         left_ref[:, at] = left

time: 33.7 us -> 34 us (level)
  no operation moved by 1% of the time
where the time goes in v12:
time: 34 us; the launch traced here: 33.8 us
  starting transfers between devices  13.2 us (39%)
  waiting for transfers between devices  10.9 us (32%)
  Pallas kernels  8.99 us (26%)
  between operations  0.68 us (2%)
    ppermute x10, starting transfers between devices, swap(): lax.ppermute(value, axes, pairs + [(target, source) for source, target in...  13.2 us
    ppermute x10, waiting for transfers between devices, swap(): lax.ppermute(value, axes, pairs + [(target, source) for source, target in...  10.9 us
    pallas_call x1, Pallas kernels, project(): pl.pallas_call(project_body, out_shape=(jax.ShapeDtypeStruct((mats * RANK...  3.63 us
    pallas_call x1, Pallas kernels, finish(): pl.pallas_call(functools.partial(finish_body, scale), out_shape=(jax.Shap...  3 us
    pallas_call x1, Pallas kernels, reflect(): pl.pallas_call(functools.partial(reflect_body, scale), out_shape=(jax.Sha...  1.36 us
    pallas_call x1, Pallas kernels, merge(): pl.pallas_call(merge_body, out_shape=(pltpu.VMEM(shape, F32), pltpu.VMEM(...  0.86 us
  transfers between devices with their start and end apart: 10, of which 9 were waited for; matrix products, arithmetic and copies ran while one was open for 0% of the time, Pallas kernels for 3%

profile of v12, /device:TPU:0, one launch (start us, length us, event | category | flops | bytes accessed | tf_op | source)
XLA Modules:
  0.0 33.8 jit_solution(3762897329835942868)
XLA Ops:
  0.6 3.6 %project.1 = (f32[8,1024]{1,0:T(8,128)S(1)}, bf16[2,1024,512]{2,1,0:T(8,128)(2,1)S(1)}, f32[2,1024,512]{2,1,0:T(8,128)S(1)}) custom-call(s32[2]{0:T(128)} %seeds_ref.1, bf16[1,2,1024,512]{3,2,1,0:T(8,128)(2,1)} %grads_ref.1, f32[1,2,1024,512]{3,2,1,0:T(8,128)} %errors_ref.1), custom_call_target="tpu_custom_call" | custom-call | tf_op jit(solution)/shard_map/project/pallas_call | solution.py:80
  4.3 3.0 %collective-permute-start = (f32[8,1024]{1,0:T(8,128)S(1)}, f32[8,1024]{1,0:T(8,128)S(1)}, u32[]{:S(2)}, u32[]{:S(2)}) collective-permute-start(f32[8,1024]{1,0:T(8,128)S(1)} %get-tuple-element.11), channel_id=1, source_target_pairs={{0,2},{1,3},{4,6},{5,7},{8,10},{9,11},{12,14},{13,15},{2,0},{3,1},... | collective-permute-start | bytes 98312 | tf_op jit(solution)/shard_map/ppermute | solution.py:256
  7.3 0.9 %merge.1 = (f32[2,1024,512]{2,1,0:T(8,128)S(1)}, bf16[2,1024,512]{2,1,0:T(8,128)(2,1)S(1)}, bf16[2,1024,512]{2,1,0:T(8,128)(2,1)S(1)}, f32[8,1024]{1,0:T(8,128)S(1)}) custom-call(bf16[2,1024,512]{2,1,0:T(8,128)(2,1)S(1)} %get-tuple-element.12.grads_ref, f32[2,1024,512]{2,1,0:T(8,128)S(1)} %get-tuple-element.13.errors_ref), custom_call_target="tpu_custom_call" | custom-call | flops 3145728 | bytes 14680064 | tf_op jit(solution)/shard_map/merge/pallas_call | solution.py:117
  8.2 1.0 %collective-permute-done = f32[8,1024]{1,0:T(8,128)S(1)} collective-permute-done((f32[8,1024]{1,0:T(8,128)S(1)}, f32[8,1024]{1,0:T(8,128)S(1)}, u32[]{:S(2)}, u32[]{:S(2)}) %collective-permute-start) | collective-permute-done | bytes 32800 | tf_op jit(solution)/shard_map/ppermute | solution.py:256
  9.2 4.2 %collective-permute-start.1 = (f32[8,1024]{1,0:T(8,128)S(1)}, f32[8,1024]{1,0:T(8,128)S(1)}, u32[]{:S(2)}, u32[]{:S(2)}) collective-permute-start(f32[8,1024]{1,0:T(8,128)S(1)} %add_add_fusion.1), channel_id=1, source_target_pairs={{0,12},{1,13},{2,14},{3,15},{4,8},{5,9},{6,10},{7,11},{12,0},{13,1... | collective-permute-start | bytes 98312 | tf_op jit(solution)/shard_map/ppermute | solution.py:256
  13.4 0.0 collective-permute-start.2
  13.4 0.6 %collective-permute-start.3 = (f32[8,1024]{1,0:T(8,128)S(1)}, f32[8,1024]{1,0:T(8,128)S(1)}, u32[]{:S(2)}, u32[]{:S(2)}) collective-permute-start(f32[8,1024]{1,0:T(8,128)S(1)} %add_add_fusion.1), channel_id=1, source_target_pairs={{0,4},{1,5},{2,6},{3,7},{8,12},{9,13},{10,14},{11,15},{4,0},{5,1},... | collective-permute-start | bytes 98312 | tf_op jit(solution)/shard_map/ppermute | solution.py:256
  14.0 1.3 %collective-permute-done.1 = f32[8,1024]{1,0:T(8,128)S(1)} collective-permute-done((f32[8,1024]{1,0:T(8,128)S(1)}, f32[8,1024]{1,0:T(8,128)S(1)}, u32[]{:S(2)}, u32[]{:S(2)}) %collective-permute-start.1) | collective-permute-done | bytes 32800 | tf_op jit(solution)/shard_map/ppermute | solution.py:256
  15.3 2.9 %collective-permute-done.2 = f32[8,1024]{1,0:T(8,128)S(1)} collective-permute-done((f32[8,1024]{1,0:T(8,128)S(1)}, f32[8,1024]{1,0:T(8,128)S(1)}, u32[]{:S(2)}, u32[]{:S(2)}) %collective-permute-start.2) | collective-permute-done | bytes 32800 | tf_op jit(solution)/shard_map/ppermute | solution.py:256
  18.2 0.0 collective-permute-done.3
  18.2 0.1 collective-permute-start.4
  18.3 1.2 %collective-permute-done.4.other_ref = f32[8,1024]{1,0:T(8,128)S(1)} collective-permute-done((f32[8,1024]{1,0:T(8,128)S(1)}, f32[8,1024]{1,0:T(8,128)S(1)}, u32[]{:S(2)}, u32[]{:S(2)}) %collective-permute-start.4) | collective-permute-done | bytes 32800 | tf_op jit(solution)/shard_map/ppermute | solution.py:256
  19.5 1.4 %reflect.1 = (f32[8,1024]{1,0:T(8,128)S(1)}, f32[8,512]{1,0:T(8,128)S(1)}) custom-call(f32[8,1024]{1,0:T(8,128)S(1)} %add_add_fusion.mine_ref, f32[8,1024]{1,0:T(8,128)S(1)} %collective-permute-done.4.other_ref, bf16[2,1024,512]{2,1,0:T(8,128)(2,1)S(1)} %get-tuple-element.15.high_ref, bf16[2,1024,512]{2,1,0:T(8,128)(2,1)S(1)} %get-tuple-element.16.low_ref), custom_call_target="tpu_custom_call" | custom-call | tf_op jit(solution)/shard_map/reflect/pallas_call | solution.py:175
  20.8 0.2 collective-permute-start.5
  21.0 1.0 %collective-permute-done.5 = f32[8,512]{1,0:T(8,128)S(1)} collective-permute-done((f32[8,512]{1,0:T(8,128)S(1)}, f32[8,512]{1,0:T(8,128)S(1)}, u32[]{:S(2)}, u32[]{:S(2)}) %collective-permute-start.5) | collective-permute-done | bytes 16416 | tf_op jit(solution)/shard_map/ppermute | solution.py:256
  22.0 1.3 %collective-permute-start.6 = (f32[8,512]{1,0:T(8,128)S(1)}, f32[8,512]{1,0:T(8,128)S(1)}, u32[]{:S(2)}, u32[]{:S(2)}) collective-permute-start(f32[8,512]{1,0:T(8,128)S(1)} %add.35), channel_id=1, source_target_pairs={{0,3},{1,2},{4,7},{5,6},{8,11},{9,10},{12,15},{13,14},{3,0},{2,1},... | collective-permute-start | bytes 49160 | tf_op jit(solution)/shard_map/ppermute | solution.py:256
  23.3 1.9 %collective-permute-done.6 = f32[8,512]{1,0:T(8,128)S(1)} collective-permute-done((f32[8,512]{1,0:T(8,128)S(1)}, f32[8,512]{1,0:T(8,128)S(1)}, u32[]{:S(2)}, u32[]{:S(2)}) %collective-permute-start.6) | collective-permute-done | bytes 16416 | tf_op jit(solution)/shard_map/ppermute | solution.py:256
  25.2 1.2 %collective-permute-start.7 = (f32[8,512]{1,0:T(8,128)S(1)}, f32[8,512]{1,0:T(8,128)S(1)}, u32[]{:S(2)}, u32[]{:S(2)}) collective-permute-start(f32[8,512]{1,0:T(8,128)S(1)} %add.36), channel_id=1, source_target_pairs={{0,13},{1,12},{2,15},{3,14},{4,9},{5,8},{6,11},{7,10},{13,0},{12,1... | collective-permute-start | bytes 49160 | tf_op jit(solution)/shard_map/ppermute | solution.py:256
  26.4 0.6 %collective-permute-start.8 = (f32[8,512]{1,0:T(8,128)S(1)}, f32[8,512]{1,0:T(8,128)S(1)}, u32[]{:S(2)}, u32[]{:S(2)}) collective-permute-start(f32[8,512]{1,0:T(8,128)S(1)} %add.36), channel_id=1, source_target_pairs={{0,9},{1,8},{2,11},{3,10},{4,13},{5,12},{6,15},{7,14},{9,0},{8,1},... | collective-permute-start | bytes 49160 | tf_op jit(solution)/shard_map/ppermute | solution.py:256
  27.1 2.0 %collective-permute-start.9 = (f32[8,512]{1,0:T(8,128)S(1)}, f32[8,512]{1,0:T(8,128)S(1)}, u32[]{:S(2)}, u32[]{:S(2)}) collective-permute-start(f32[8,512]{1,0:T(8,128)S(1)} %add.36), channel_id=1, source_target_pairs={{0,5},{1,4},{2,7},{3,6},{8,13},{9,12},{10,15},{11,14},{5,0},{4,1},... | collective-permute-start | bytes 49160 | tf_op jit(solution)/shard_map/ppermute | solution.py:256
  29.1 0.1 turn.1.left_ref
  29.2 0.9 %collective-permute-done.7 = f32[8,512]{1,0:T(8,128)S(1)} collective-permute-done((f32[8,512]{1,0:T(8,128)S(1)}, f32[8,512]{1,0:T(8,128)S(1)}, u32[]{:S(2)}, u32[]{:S(2)}) %collective-permute-start.7) | collective-permute-done | bytes 16416 | tf_op jit(solution)/shard_map/ppermute | solution.py:256
  30.2 0.5 %collective-permute-done.8 = f32[8,512]{1,0:T(8,128)S(1)} collective-permute-done((f32[8,512]{1,0:T(8,128)S(1)}, f32[8,512]{1,0:T(8,128)S(1)}, u32[]{:S(2)}, u32[]{:S(2)}) %collective-permute-start.8) | collective-permute-done | bytes 16416 | tf_op jit(solution)/shard_map/ppermute | solution.py:256
  30.7 0.1 collective-permute-done.9
  30.9 3.0 %finish.1 = (bf16[2,1024,512]{2,1,0:T(8,128)(2,1)}, f32[1,2,1024,512]{3,2,1,0:T(8,128)}) custom-call(bf16[1024,32]{1,0:T(8,128)(2,1)S(1)} %turn.1.left_ref, f32[8,512]{1,0:T(8,128)S(1)} %add_add_fusion.2.right_ref, f32[2,1024,512]{2,1,0:T(8,128)S(1)} %get-tuple-element.19.merged_ref), custom_call_target="tpu_custom_call" | custom-call | tf_op jit(solution)/shard_map/finish/pallas_call | solution.py:233
  (5 shorter events, 0.0 us)
Async XLA Ops:
  4.3 4.9 %collective-permute-start = (f32[8,1024]{1,0:T(8,128)S(1)}, f32[8,1024]{1,0:T(8,128)S(1)}, u32[]{:S(2)}, u32[]{:S(2)}) collective-permute-start(f32[8,1024]{1,0:T(8,128)S(1)} %get-tuple-element.11), channel_id=1, source_target_pairs={{0,2},{1,3},{4,6},{5,7},{8,10},{9,11},{12,14},{13,15},{2,0},{3,1},... | collective-permute-start | bytes 98312 | tf_op jit(solution)/shard_map/ppermute | solution.py:256
  9.2 6.1 %collective-permute-start.1 = (f32[8,1024]{1,0:T(8,128)S(1)}, f32[8,1024]{1,0:T(8,128)S(1)}, u32[]{:S(2)}, u32[]{:S(2)}) collective-permute-start(f32[8,1024]{1,0:T(8,128)S(1)} %add_add_fusion.1), channel_id=1, source_target_pairs={{0,12},{1,13},{2,14},{3,15},{4,8},{5,9},{6,10},{7,11},{12,0},{13,1... | collective-permute-start | bytes 98312 | tf_op jit(solution)/shard_map/ppermute | solution.py:256
  13.4 4.8 %collective-permute-start.2 = (f32[8,1024]{1,0:T(8,128)S(1)}, f32[8,1024]{1,0:T(8,128)S(1)}, u32[]{:S(2)}, u32[]{:S(2)}) collective-permute-start(f32[8,1024]{1,0:T(8,128)S(1)} %add_add_fusion.1), channel_id=1, source_target_pairs={{0,8},{1,9},{2,10},{3,11},{4,12},{5,13},{6,14},{7,15},{8,0},{9,1},... | collective-permute-start | bytes 98312 | tf_op jit(solution)/shard_map/ppermute | solution.py:256
  13.4 4.8 %collective-permute-start.3 = (f32[8,1024]{1,0:T(8,128)S(1)}, f32[8,1024]{1,0:T(8,128)S(1)}, u32[]{:S(2)}, u32[]{:S(2)}) collective-permute-start(f32[8,1024]{1,0:T(8,128)S(1)} %add_add_fusion.1), channel_id=1, source_target_pairs={{0,4},{1,5},{2,6},{3,7},{8,12},{9,13},{10,14},{11,15},{4,0},{5,1},... | collective-permute-start | bytes 98312 | tf_op jit(solution)/shard_map/ppermute | solution.py:256
  18.2 1.3 %collective-permute-start.4 = (f32[8,1024]{1,0:T(8,128)S(1)}, f32[8,1024]{1,0:T(8,128)S(1)}, u32[]{:S(2)}, u32[]{:S(2)}) collective-permute-start(f32[8,1024]{1,0:T(8,128)S(1)} %add_add_fusion.mine_ref), channel_id=1, source_target_pairs={{0,1},{1,0},{2,3},{3,2},{4,5},{5,4},{6,7},{7,6},{8,9},{9,8},{10,11... | collective-permute-start | bytes 98312 | tf_op jit(solution)/shard_map/ppermute | solution.py:256
  20.8 1.2 %collective-permute-start.5 = (f32[8,512]{1,0:T(8,128)S(1)}, f32[8,512]{1,0:T(8,128)S(1)}, u32[]{:S(2)}, u32[]{:S(2)}) collective-permute-start(f32[8,512]{1,0:T(8,128)S(1)} %get-tuple-element.18), channel_id=1, source_target_pairs={{0,1},{1,0},{2,3},{3,2},{4,5},{5,4},{6,7},{7,6},{8,9},{9,8},{10,11... | collective-permute-start | bytes 49160 | tf_op jit(solution)/shard_map/ppermute | solution.py:256
  22.0 3.2 %collective-permute-start.6 = (f32[8,512]{1,0:T(8,128)S(1)}, f32[8,512]{1,0:T(8,128)S(1)}, u32[]{:S(2)}, u32[]{:S(2)}) collective-permute-start(f32[8,512]{1,0:T(8,128)S(1)} %add.35), channel_id=1, source_target_pairs={{0,3},{1,2},{4,7},{5,6},{8,11},{9,10},{12,15},{13,14},{3,0},{2,1},... | collective-permute-start | bytes 49160 | tf_op jit(solution)/shard_map/ppermute | solution.py:256
  25.2 5.0 %collective-permute-start.7 = (f32[8,512]{1,0:T(8,128)S(1)}, f32[8,512]{1,0:T(8,128)S(1)}, u32[]{:S(2)}, u32[]{:S(2)}) collective-permute-start(f32[8,512]{1,0:T(8,128)S(1)} %add.36), channel_id=1, source_target_pairs={{0,13},{1,12},{2,15},{3,14},{4,9},{5,8},{6,11},{7,10},{13,0},{12,1... | collective-permute-start | bytes 49160 | tf_op jit(solution)/shard_map/ppermute | solution.py:256
  26.4 4.3 %collective-permute-start.8 = (f32[8,512]{1,0:T(8,128)S(1)}, f32[8,512]{1,0:T(8,128)S(1)}, u32[]{:S(2)}, u32[]{:S(2)}) collective-permute-start(f32[8,512]{1,0:T(8,128)S(1)} %add.36), channel_id=1, source_target_pairs={{0,9},{1,8},{2,11},{3,10},{4,13},{5,12},{6,15},{7,14},{9,0},{8,1},... | collective-permute-start | bytes 49160 | tf_op jit(solution)/shard_map/ppermute | solution.py:256
  27.1 3.8 %collective-permute-start.9 = (f32[8,512]{1,0:T(8,128)S(1)}, f32[8,512]{1,0:T(8,128)S(1)}, u32[]{:S(2)}, u32[]{:S(2)}) collective-permute-start(f32[8,512]{1,0:T(8,128)S(1)} %add.36), channel_id=1, source_target_pairs={{0,5},{1,4},{2,7},{3,6},{8,13},{9,12},{10,15},{11,14},{5,0},{4,1},... | collective-permute-start | bytes 49160 | tf_op jit(solution)/shard_map/ppermute | solution.py:256

commit v13 on v11

--- a/solution.py
+++ b/solution.py
@@ -270,13 +270,13 @@
     last = max(count // 4, 1)
     step = 1
     while step < last:
-        value = value + (swap_chips(value, step, cross) + zero)
+        value = value + (zero + swap_chips(value, step, cross))
         zero = 0.0
         step *= 2
     terms = [swap_chips(value, offset, cross) for offset in range(count - last, 0, -last)]
     terms = [value] + terms[::-1]
     while len(terms) > 1:
-        terms = [terms[at + 1] + terms[at] for at in range(0, len(terms), 2)]
+        terms = [terms[at] + terms[at + 1] for at in range(0, len(terms), 2)]
     return terms[0]
 
 

time: 33.7 us -> 33.9 us (level)
  waiting for transfers between devices: 10.9 us -> 12.1 us
  starting transfers between devices: 13.2 us -> 12.3 us
    ppermute x10, waiting for transfers between devices: 10.9 us -> 12.1 us  [swap(): lax.ppermute(value, axes, pairs + [(target, source) for source, target in...]
    ppermute x10, starting transfers between devices: 13.2 us -> 12.3 us  [swap(): lax.ppermute(value, axes, pairs + [(target, source) for source, target in...]
  transfers between devices with their start and end apart: 10 -> 10, of which waited for: 9 -> 8; matrix products, arithmetic and copies ran while one was open for 0% -> 0% of each run, Pallas kernels for 3% -> 3%
where the time goes in v13:
time: 33.9 us; the launch traced here: 33.8 us
  starting transfers between devices  12.3 us (36%)
  waiting for transfers between devices  12.1 us (36%)
  Pallas kernels  8.71 us (26%)
  between operations  0.68 us (2%)
    ppermute x10, starting transfers between devices, swap(): lax.ppermute(value, axes, pairs + [(target, source) for source, target in...  12.3 us
    ppermute x10, waiting for transfers between devices, swap(): lax.ppermute(value, axes, pairs + [(target, source) for source, target in...  12.1 us
    pallas_call x1, Pallas kernels, project(): pl.pallas_call(project_body, out_shape=(jax.ShapeDtypeStruct((mats * RANK...  3.35 us
    pallas_call x1, Pallas kernels, finish(): pl.pallas_call(functools.partial(finish_body, scale), out_shape=(jax.Shap...  3 us
    pallas_call x1, Pallas kernels, reflect(): pl.pallas_call(functools.partial(reflect_body, scale), out_shape=(jax.Sha...  1.36 us
    pallas_call x1, Pallas kernels, merge(): pl.pallas_call(merge_body, out_shape=(pltpu.VMEM(shape, F32), pltpu.VMEM(...  0.86 us
  transfers between devices with their start and end apart: 10, of which 8 were waited for; matrix products, arithmetic and copies ran while one was open for 0% of the time, Pallas kernels for 3%

profile of v13, /device:TPU:0, one launch (start us, length us, event | category | flops | bytes accessed | tf_op | source)
XLA Modules:
  0.0 33.8 jit_solution(14334794562251807917)
XLA Ops:
  0.6 3.4 %project.1 = (f32[8,1024]{1,0:T(8,128)S(1)}, bf16[2,1024,512]{2,1,0:T(8,128)(2,1)S(1)}, f32[2,1024,512]{2,1,0:T(8,128)S(1)}) custom-call(s32[2]{0:T(128)} %seeds_ref.1, bf16[1,2,1024,512]{3,2,1,0:T(8,128)(2,1)} %grads_ref.1, f32[1,2,1024,512]{3,2,1,0:T(8,128)} %errors_ref.1), custom_call_target="tpu_custom_call" | custom-call | tf_op jit(solution)/shard_map/project/pallas_call | solution.py:79
  4.0 3.0 %collective-permute-start = (f32[8,1024]{1,0:T(8,128)S(1)}, f32[8,1024]{1,0:T(8,128)S(1)}, u32[]{:S(2)}, u32[]{:S(2)}) collective-permute-start(f32[8,1024]{1,0:T(8,128)S(1)} %get-tuple-element.11), channel_id=1, source_target_pairs={{0,2},{1,3},{4,6},{5,7},{8,10},{9,11},{12,14},{13,15},{2,0},{3,1},... | collective-permute-start | bytes 98312 | tf_op jit(solution)/shard_map/ppermute | solution.py:255
  7.0 0.9 %merge.1 = (f32[2,1024,512]{2,1,0:T(8,128)S(1)}, bf16[2,1024,512]{2,1,0:T(8,128)(2,1)S(1)}, bf16[2,1024,512]{2,1,0:T(8,128)(2,1)S(1)}, f32[8,1024]{1,0:T(8,128)S(1)}) custom-call(bf16[2,1024,512]{2,1,0:T(8,128)(2,1)S(1)} %get-tuple-element.12.grads_ref, f32[2,1024,512]{2,1,0:T(8,128)S(1)} %get-tuple-element.13.errors_ref), custom_call_target="tpu_custom_call" | custom-call | flops 3145728 | bytes 14680064 | tf_op jit(solution)/shard_map/merge/pallas_call | solution.py:116
  7.9 1.0 %collective-permute-done = f32[8,1024]{1,0:T(8,128)S(1)} collective-permute-done((f32[8,1024]{1,0:T(8,128)S(1)}, f32[8,1024]{1,0:T(8,128)S(1)}, u32[]{:S(2)}, u32[]{:S(2)}) %collective-permute-start) | collective-permute-done | bytes 32800 | tf_op jit(solution)/shard_map/ppermute | solution.py:255
  8.9 3.1 %collective-permute-start.2 = (f32[8,1024]{1,0:T(8,128)S(1)}, f32[8,1024]{1,0:T(8,128)S(1)}, u32[]{:S(2)}, u32[]{:S(2)}) collective-permute-start(f32[8,1024]{1,0:T(8,128)S(1)} %add_add_fusion.1), channel_id=1, source_target_pairs={{0,8},{1,9},{2,10},{3,11},{4,12},{5,13},{6,14},{7,15},{8,0},{9,1},... | collective-permute-start | bytes 98312 | tf_op jit(solution)/shard_map/ppermute | solution.py:255
  12.1 1.3 %collective-permute-start.3 = (f32[8,1024]{1,0:T(8,128)S(1)}, f32[8,1024]{1,0:T(8,128)S(1)}, u32[]{:S(2)}, u32[]{:S(2)}) collective-permute-start(f32[8,1024]{1,0:T(8,128)S(1)} %add_add_fusion.1), channel_id=1, source_target_pairs={{0,12},{1,13},{2,14},{3,15},{4,8},{5,9},{6,10},{7,11},{12,0},{13,1... | collective-permute-start | bytes 98312 | tf_op jit(solution)/shard_map/ppermute | solution.py:255
  13.4 0.2 collective-permute-start.1
  13.7 0.3 collective-permute-done.2
  14.0 3.8 %collective-permute-done.3 = f32[8,1024]{1,0:T(8,128)S(1)} collective-permute-done((f32[8,1024]{1,0:T(8,128)S(1)}, f32[8,1024]{1,0:T(8,128)S(1)}, u32[]{:S(2)}, u32[]{:S(2)}) %collective-permute-start.3) | collective-permute-done | bytes 32800 | tf_op jit(solution)/shard_map/ppermute | solution.py:255
  17.8 0.0 collective-permute-done.1
  17.8 0.1 collective-permute-start.4
  17.9 1.2 %collective-permute-done.4.other_ref = f32[8,1024]{1,0:T(8,128)S(1)} collective-permute-done((f32[8,1024]{1,0:T(8,128)S(1)}, f32[8,1024]{1,0:T(8,128)S(1)}, u32[]{:S(2)}, u32[]{:S(2)}) %collective-permute-start.4) | collective-permute-done | bytes 32800 | tf_op jit(solution)/shard_map/ppermute | solution.py:255
  19.1 1.4 %reflect.1 = (f32[8,1024]{1,0:T(8,128)S(1)}, f32[8,512]{1,0:T(8,128)S(1)}) custom-call(f32[8,1024]{1,0:T(8,128)S(1)} %add_add_fusion.mine_ref, f32[8,1024]{1,0:T(8,128)S(1)} %collective-permute-done.4.other_ref, bf16[2,1024,512]{2,1,0:T(8,128)(2,1)S(1)} %get-tuple-element.15.high_ref, bf16[2,1024,512]{2,1,0:T(8,128)(2,1)S(1)} %get-tuple-element.16.low_ref), custom_call_target="tpu_custom_call" | custom-call | tf_op jit(solution)/shard_map/reflect/pallas_call | solution.py:174
  20.4 0.2 collective-permute-start.5
  20.6 1.0 %collective-permute-done.5 = f32[8,512]{1,0:T(8,128)S(1)} collective-permute-done((f32[8,512]{1,0:T(8,128)S(1)}, f32[8,512]{1,0:T(8,128)S(1)}, u32[]{:S(2)}, u32[]{:S(2)}) %collective-permute-start.5) | collective-permute-done | bytes 16416 | tf_op jit(solution)/shard_map/ppermute | solution.py:255
  21.6 1.3 %collective-permute-start.6 = (f32[8,512]{1,0:T(8,128)S(1)}, f32[8,512]{1,0:T(8,128)S(1)}, u32[]{:S(2)}, u32[]{:S(2)}) collective-permute-start(f32[8,512]{1,0:T(8,128)S(1)} %add.35), channel_id=1, source_target_pairs={{0,3},{1,2},{4,7},{5,6},{8,11},{9,10},{12,15},{13,14},{3,0},{2,1},... | collective-permute-start | bytes 49160 | tf_op jit(solution)/shard_map/ppermute | solution.py:255
  22.9 1.9 %collective-permute-done.6 = f32[8,512]{1,0:T(8,128)S(1)} collective-permute-done((f32[8,512]{1,0:T(8,128)S(1)}, f32[8,512]{1,0:T(8,128)S(1)}, u32[]{:S(2)}, u32[]{:S(2)}) %collective-permute-start.6) | collective-permute-done | bytes 16416 | tf_op jit(solution)/shard_map/ppermute | solution.py:255
  24.8 1.0 %collective-permute-start.8 = (f32[8,512]{1,0:T(8,128)S(1)}, f32[8,512]{1,0:T(8,128)S(1)}, u32[]{:S(2)}, u32[]{:S(2)}) collective-permute-start(f32[8,512]{1,0:T(8,128)S(1)} %add.36), channel_id=1, source_target_pairs={{0,9},{1,8},{2,11},{3,10},{4,13},{5,12},{6,15},{7,14},{9,0},{8,1},... | collective-permute-start | bytes 49160 | tf_op jit(solution)/shard_map/ppermute | solution.py:255
  25.8 1.0 %collective-permute-start.9 = (f32[8,512]{1,0:T(8,128)S(1)}, f32[8,512]{1,0:T(8,128)S(1)}, u32[]{:S(2)}, u32[]{:S(2)}) collective-permute-start(f32[8,512]{1,0:T(8,128)S(1)} %add.36), channel_id=1, source_target_pairs={{0,13},{1,12},{2,15},{3,14},{4,9},{5,8},{6,11},{7,10},{13,0},{12,1... | collective-permute-start | bytes 49160 | tf_op jit(solution)/shard_map/ppermute | solution.py:255
  26.8 1.0 %collective-permute-start.7 = (f32[8,512]{1,0:T(8,128)S(1)}, f32[8,512]{1,0:T(8,128)S(1)}, u32[]{:S(2)}, u32[]{:S(2)}) collective-permute-start(f32[8,512]{1,0:T(8,128)S(1)} %add.36), channel_id=1, source_target_pairs={{0,5},{1,4},{2,7},{3,6},{8,13},{9,12},{10,15},{11,14},{5,0},{4,1},... | collective-permute-start | bytes 49160 | tf_op jit(solution)/shard_map/ppermute | solution.py:255
  27.8 0.1 turn.1.left_ref
  27.9 0.9 %collective-permute-done.8 = f32[8,512]{1,0:T(8,128)S(1)} collective-permute-done((f32[8,512]{1,0:T(8,128)S(1)}, f32[8,512]{1,0:T(8,128)S(1)}, u32[]{:S(2)}, u32[]{:S(2)}) %collective-permute-start.8) | collective-permute-done | bytes 16416 | tf_op jit(solution)/shard_map/ppermute | solution.py:255
  28.9 1.9 %collective-permute-done.9 = f32[8,512]{1,0:T(8,128)S(1)} collective-permute-done((f32[8,512]{1,0:T(8,128)S(1)}, f32[8,512]{1,0:T(8,128)S(1)}, u32[]{:S(2)}, u32[]{:S(2)}) %collective-permute-start.9) | collective-permute-done | bytes 16416 | tf_op jit(solution)/shard_map/ppermute | solution.py:255
  30.8 0.0 collective-permute-done.7
  30.8 3.0 %finish.1 = (bf16[2,1024,512]{2,1,0:T(8,128)(2,1)}, f32[1,2,1024,512]{3,2,1,0:T(8,128)}) custom-call(bf16[1024,32]{1,0:T(8,128)(2,1)S(1)} %turn.1.left_ref, f32[8,512]{1,0:T(8,128)S(1)} %add_add_fusion.2.right_ref, f32[2,1024,512]{2,1,0:T(8,128)S(1)} %get-tuple-element.19.merged_ref), custom_call_target="tpu_custom_call" | custom-call | tf_op jit(solution)/shard_map/finish/pallas_call | solution.py:232
  (5 shorter events, 0.0 us)
Async XLA Ops:
  4.0 4.9 %collective-permute-start = (f32[8,1024]{1,0:T(8,128)S(1)}, f32[8,1024]{1,0:T(8,128)S(1)}, u32[]{:S(2)}, u32[]{:S(2)}) collective-permute-start(f32[8,1024]{1,0:T(8,128)S(1)} %get-tuple-element.11), channel_id=1, source_target_pairs={{0,2},{1,3},{4,6},{5,7},{8,10},{9,11},{12,14},{13,15},{2,0},{3,1},... | collective-permute-start | bytes 98312 | tf_op jit(solution)/shard_map/ppermute | solution.py:255
  8.9 5.0 %collective-permute-start.2 = (f32[8,1024]{1,0:T(8,128)S(1)}, f32[8,1024]{1,0:T(8,128)S(1)}, u32[]{:S(2)}, u32[]{:S(2)}) collective-permute-start(f32[8,1024]{1,0:T(8,128)S(1)} %add_add_fusion.1), channel_id=1, source_target_pairs={{0,8},{1,9},{2,10},{3,11},{4,12},{5,13},{6,14},{7,15},{8,0},{9,1},... | collective-permute-start | bytes 98312 | tf_op jit(solution)/shard_map/ppermute | solution.py:255
  12.1 5.7 %collective-permute-start.3 = (f32[8,1024]{1,0:T(8,128)S(1)}, f32[8,1024]{1,0:T(8,128)S(1)}, u32[]{:S(2)}, u32[]{:S(2)}) collective-permute-start(f32[8,1024]{1,0:T(8,128)S(1)} %add_add_fusion.1), channel_id=1, source_target_pairs={{0,12},{1,13},{2,14},{3,15},{4,8},{5,9},{6,10},{7,11},{12,0},{13,1... | collective-permute-start | bytes 98312 | tf_op jit(solution)/shard_map/ppermute | solution.py:255
  13.4 4.4 %collective-permute-start.1 = (f32[8,1024]{1,0:T(8,128)S(1)}, f32[8,1024]{1,0:T(8,128)S(1)}, u32[]{:S(2)}, u32[]{:S(2)}) collective-permute-start(f32[8,1024]{1,0:T(8,128)S(1)} %add_add_fusion.1), channel_id=1, source_target_pairs={{0,4},{1,5},{2,6},{3,7},{8,12},{9,13},{10,14},{11,15},{4,0},{5,1},... | collective-permute-start | bytes 98312 | tf_op jit(solution)/shard_map/ppermute | solution.py:255
  17.8 1.3 %collective-permute-start.4 = (f32[8,1024]{1,0:T(8,128)S(1)}, f32[8,1024]{1,0:T(8,128)S(1)}, u32[]{:S(2)}, u32[]{:S(2)}) collective-permute-start(f32[8,1024]{1,0:T(8,128)S(1)} %add_add_fusion.mine_ref), channel_id=1, source_target_pairs={{0,1},{1,0},{2,3},{3,2},{4,5},{5,4},{6,7},{7,6},{8,9},{9,8},{10,11... | collective-permute-start | bytes 98312 | tf_op jit(solution)/shard_map/ppermute | solution.py:255
  20.4 1.2 %collective-permute-start.5 = (f32[8,512]{1,0:T(8,128)S(1)}, f32[8,512]{1,0:T(8,128)S(1)}, u32[]{:S(2)}, u32[]{:S(2)}) collective-permute-start(f32[8,512]{1,0:T(8,128)S(1)} %get-tuple-element.18), channel_id=1, source_target_pairs={{0,1},{1,0},{2,3},{3,2},{4,5},{5,4},{6,7},{7,6},{8,9},{9,8},{10,11... | collective-permute-start | bytes 49160 | tf_op jit(solution)/shard_map/ppermute | solution.py:255
  21.6 3.2 %collective-permute-start.6 = (f32[8,512]{1,0:T(8,128)S(1)}, f32[8,512]{1,0:T(8,128)S(1)}, u32[]{:S(2)}, u32[]{:S(2)}) collective-permute-start(f32[8,512]{1,0:T(8,128)S(1)} %add.35), channel_id=1, source_target_pairs={{0,3},{1,2},{4,7},{5,6},{8,11},{9,10},{12,15},{13,14},{3,0},{2,1},... | collective-permute-start | bytes 49160 | tf_op jit(solution)/shard_map/ppermute | solution.py:255
  24.8 4.1 %collective-permute-start.8 = (f32[8,512]{1,0:T(8,128)S(1)}, f32[8,512]{1,0:T(8,128)S(1)}, u32[]{:S(2)}, u32[]{:S(2)}) collective-permute-start(f32[8,512]{1,0:T(8,128)S(1)} %add.36), channel_id=1, source_target_pairs={{0,9},{1,8},{2,11},{3,10},{4,13},{5,12},{6,15},{7,14},{9,0},{8,1},... | collective-permute-start | bytes 49160 | tf_op jit(solution)/shard_map/ppermute | solution.py:255
  25.8 5.0 %collective-permute-start.9 = (f32[8,512]{1,0:T(8,128)S(1)}, f32[8,512]{1,0:T(8,128)S(1)}, u32[]{:S(2)}, u32[]{:S(2)}) collective-permute-start(f32[8,512]{1,0:T(8,128)S(1)} %add.36), channel_id=1, source_target_pairs={{0,13},{1,12},{2,15},{3,14},{4,9},{5,8},{6,11},{7,10},{13,0},{12,1... | collective-permute-start | bytes 49160 | tf_op jit(solution)/shard_map/ppermute | solution.py:255
  26.8 4.0 %collective-permute-start.7 = (f32[8,512]{1,0:T(8,128)S(1)}, f32[8,512]{1,0:T(8,128)S(1)}, u32[]{:S(2)}, u32[]{:S(2)}) collective-permute-start(f32[8,512]{1,0:T(8,128)S(1)} %add.36), channel_id=1, source_target_pairs={{0,5},{1,4},{2,7},{3,6},{8,13},{9,12},{10,15},{11,14},{5,0},{4,1},... | collective-permute-start | bytes 49160 | tf_op jit(solution)/shard_map/ppermute | solution.py:255

commit v14 on v9

--- a/solution.py
+++ b/solution.py
@@ -10,8 +10,8 @@
 RANK = 4
 EPSILON = 1e-08
 CHUNKS = 4
-SPLIT = ((3, 6), (5, 4), (1, 7))
-SHARED = 2
+SPLIT = ((1, 7), (5, 4), (2, 6))
+SHARED = 3
 BF16 = jnp.bfloat16
 F32 = jnp.float32
 
@@ -59,7 +59,8 @@
         copy.start()
     seed_copy.wait()
     start = start_rows(seed, mats, cols)
-    weights = jnp.concatenate(halves(start), axis=0).T.astype(BF16)
+    weights = jnp.concatenate(halves(start), axis=0).astype(BF16)
+    dims = (((1,), (1,)), ((), ()))
     for chunk in range(CHUNKS):
         at = pl.ds(chunk * size, size)
         left = jnp.zeros((mats * RANK, size), F32)
@@ -69,9 +70,9 @@
             value = gbuf[mat, at].astype(F32) + ebuf[mat, at]
             high = value.astype(BF16)
             low = (value - high.astype(F32)).astype(BF16)
-            product = jnp.dot(high, weights, preferred_element_type=F32)
-            product = product + jnp.dot(low, weights, preferred_element_type=F32)
-            left = fold(mat, left, product.T)
+            product = lax.dot_general(weights, high, dims, preferred_element_type=F32)
+            product = product + lax.dot_general(weights, low, dims, preferred_element_type=F32)
+            left = fold(mat, left, product)
         left_ref[:, at] = left
 
 
@@ -96,9 +97,10 @@
     )(*[pltpu.with_memory_space_constraint(value, pltpu.HBM) for value in (seeds, grads, errors)])
 
 
-def merge_body(grads_ref, errors_ref, merged_ref, high_ref, low_ref):
+def merge_body(grads_ref, errors_ref, merged_ref, high_ref, low_ref, zero_ref):
     mats, rows, cols = grads_ref.shape
     size = 64
+    zero_ref[...] = jnp.zeros_like(zero_ref)
 
     @pl.loop(0, rows // size)
     def _(step):
@@ -115,9 +117,14 @@
     shape = grads.shape
     return pl.pallas_call(
         merge_body,
-        out_shape=(pltpu.VMEM(shape, F32), pltpu.VMEM(shape, BF16), pltpu.VMEM(shape, BF16)),
+        out_shape=(
+            pltpu.VMEM(shape, F32),
+            pltpu.VMEM(shape, BF16),
+            pltpu.VMEM(shape, BF16),
+            jax.ShapeDtypeStruct((shape[0] * RANK, shape[1]), F32),
+        ),
         in_specs=[pl.BlockSpec(memory_space=pltpu.VMEM)] * 2,
-        out_specs=[pl.BlockSpec(memory_space=pltpu.VMEM)] * 3,
+        out_specs=[pl.BlockSpec(memory_space=pltpu.VMEM)] * 4,
         compiler_params=pltpu.CompilerParams(vmem_limit_bytes=16 * 2**20),
         cost_estimate=pl.CostEstimate(flops=3 * grads.size, bytes_accessed=14 * grads.size, transcendentals=0),
         name="merge",
@@ -287,12 +294,13 @@
     return swap(value, ("dp", "tensor"), pairs)
 
 
-def chips_sum(value):
+def chips_sum(value, zero):
     count = lax.axis_size("dp")
     last = max(count // 4, 1)
     step = 1
     while step < last:
-        value = value + swap_chips(value, (step, step))
+        value = value + (zero + swap_chips(value, (step, step)))
+        zero = 0.0
         step *= 2
     terms = [value] + [swap_chips(value, (offset, offset)) for offset in range(last, count, last)]
     while len(terms) > 1:
@@ -315,8 +323,8 @@
 def body(grads, errors, seeds):
     replicas = lax.axis_size("dp")
     left_part, grads, errors = project(seeds, grads, errors)
-    merged, high, low = merge(grads, errors)
-    mine = chips_sum(left_part)
+    merged, high, low, zero = merge(grads, errors)
+    mine = chips_sum(left_part, zero)
     left, right_part = reflect(mine, swap_cores(mine), high, low, 1.0 / replicas)
     terms = chips_terms(right_part + swap_cores(right_part))
     return finish(turn(left), merged, *terms, 1.0 / replicas)

time: 34.2 us -> 33.3 us (0.974)
  waiting for transfers between devices: 9.93 us -> 9.46 us
    ppermute x13, waiting for transfers between devices: 9.93 us -> 9.46 us  [swap(): lax.ppermute(value, axes, pairs + [(target, source) for source, target in...]
where the time goes in v14:
time: 33.3 us; the launch traced here: 33.2 us
  starting transfers between devices  14.3 us (43%)
  waiting for transfers between devices  9.46 us (28%)
  Pallas kernels  8.72 us (26%)
  between operations  0.68 us (2%)
    ppermute x13, starting transfers between devices, swap(): lax.ppermute(value, axes, pairs + [(target, source) for source, target in...  14.3 us
    ppermute x13, waiting for transfers between devices, swap(): lax.ppermute(value, axes, pairs + [(target, source) for source, target in...  9.46 us
    pallas_call x1, Pallas kernels, project(): pl.pallas_call(project_body, out_shape=(jax.ShapeDtypeStruct((mats * RANK...  3.35 us
    pallas_call x1, Pallas kernels, finish(): pl.pallas_call(functools.partial(finish_body, scale, len(taken)), out_sha...  3 us
    pallas_call x1, Pallas kernels, reflect(): pl.pallas_call(functools.partial(reflect_body, scale), out_shape=(jax.Sha...  1.36 us
    pallas_call x1, Pallas kernels, merge(): pl.pallas_call(merge_body, out_shape=(pltpu.VMEM(shape, F32), pltpu.VMEM(...  0.86 us
  transfers between devices with their start and end apart: 13, of which 9 were waited for; matrix products, arithmetic and copies ran while one was open for 0% of the time, Pallas kernels for 3%

profile of v14, /device:TPU:0, one launch (start us, length us, event | category | flops | bytes accessed | tf_op | source)
XLA Modules:
  0.0 33.2 jit_solution(12711531907767353432)
XLA Ops:
  0.6 3.4 %project.1 = (f32[8,1024]{1,0:T(8,128)S(1)}, bf16[2,1024,512]{2,1,0:T(8,128)(2,1)S(1)}, f32[2,1024,512]{2,1,0:T(8,128)S(1)}) custom-call(s32[2]{0:T(128)} %seeds_ref.1, bf16[1,2,1024,512]{3,2,1,0:T(8,128)(2,1)} %grads_ref.1, f32[1,2,1024,512]{3,2,1,0:T(8,128)} %errors_ref.1), custom_call_target="tpu_custom_call" | custom-call | tf_op jit(solution)/shard_map/project/pallas_call | solution.py:81
  4.0 3.0 %collective-permute-start = (f32[8,1024]{1,0:T(8,128)S(1)}, f32[8,1024]{1,0:T(8,128)S(1)}, u32[]{:S(2)}, u32[]{:S(2)}) collective-permute-start(f32[8,1024]{1,0:T(8,128)S(1)} %get-tuple-element.11), channel_id=1, source_target_pairs={{0,2},{4,6},{8,10},{12,14},{1,3},{5,7},{9,11},{13,15},{2,0},{6,4},... | collective-permute-start | bytes 98312 | tf_op jit(solution)/shard_map/ppermute | solution.py:280
  7.0 0.9 %merge.1 = (f32[2,1024,512]{2,1,0:T(8,128)S(1)}, bf16[2,1024,512]{2,1,0:T(8,128)(2,1)S(1)}, bf16[2,1024,512]{2,1,0:T(8,128)(2,1)S(1)}, f32[8,1024]{1,0:T(8,128)S(1)}) custom-call(bf16[2,1024,512]{2,1,0:T(8,128)(2,1)S(1)} %get-tuple-element.12.grads_ref, f32[2,1024,512]{2,1,0:T(8,128)S(1)} %get-tuple-element.13.errors_ref), custom_call_target="tpu_custom_call" | custom-call | flops 3145728 | bytes 14680064 | tf_op jit(solution)/shard_map/merge/pallas_call | solution.py:118
  7.9 1.0 %collective-permute-done = f32[8,1024]{1,0:T(8,128)S(1)} collective-permute-done((f32[8,1024]{1,0:T(8,128)S(1)}, f32[8,1024]{1,0:T(8,128)S(1)}, u32[]{:S(2)}, u32[]{:S(2)}) %collective-permute-start) | collective-permute-done | bytes 32800 | tf_op jit(solution)/shard_map/ppermute | solution.py:280
  8.9 3.1 %collective-permute-start.2 = (f32[8,1024]{1,0:T(8,128)S(1)}, f32[8,1024]{1,0:T(8,128)S(1)}, u32[]{:S(2)}, u32[]{:S(2)}) collective-permute-start(f32[8,1024]{1,0:T(8,128)S(1)} %add_add_fusion.1), channel_id=1, source_target_pairs={{0,8},{2,10},{4,12},{6,14},{1,9},{3,11},{5,13},{7,15},{8,0},{10,2}... | collective-permute-start | bytes 98312 | tf_op jit(solution)/shard_map/ppermute | solution.py:280
  12.1 1.3 %collective-permute-start.3 = (f32[8,1024]{1,0:T(8,128)S(1)}, f32[8,1024]{1,0:T(8,128)S(1)}, u32[]{:S(2)}, u32[]{:S(2)}) collective-permute-start(f32[8,1024]{1,0:T(8,128)S(1)} %add_add_fusion.1), channel_id=1, source_target_pairs={{0,12},{2,14},{4,8},{6,10},{1,13},{3,15},{5,9},{7,11},{12,0},{14,2... | collective-permute-start | bytes 98312 | tf_op jit(solution)/shard_map/ppermute | solution.py:280
  13.4 0.2 collective-permute-start.1
  13.7 0.3 collective-permute-done.2
  14.0 3.8 %collective-permute-done.3 = f32[8,1024]{1,0:T(8,128)S(1)} collective-permute-done((f32[8,1024]{1,0:T(8,128)S(1)}, f32[8,1024]{1,0:T(8,128)S(1)}, u32[]{:S(2)}, u32[]{:S(2)}) %collective-permute-start.3) | collective-permute-done | bytes 32800 | tf_op jit(solution)/shard_map/ppermute | solution.py:280
  17.8 0.0 collective-permute-done.1
  17.8 0.1 collective-permute-start.4
  17.9 1.2 %collective-permute-done.4.other_ref = f32[8,1024]{1,0:T(8,128)S(1)} collective-permute-done((f32[8,1024]{1,0:T(8,128)S(1)}, f32[8,1024]{1,0:T(8,128)S(1)}, u32[]{:S(2)}, u32[]{:S(2)}) %collective-permute-start.4) | collective-permute-done | bytes 32800 | tf_op jit(solution)/shard_map/ppermute | solution.py:280
  19.1 1.4 %reflect.1 = (f32[8,1024]{1,0:T(8,128)S(1)}, f32[8,512]{1,0:T(8,128)S(1)}) custom-call(f32[8,1024]{1,0:T(8,128)S(1)} %add_add_fusion.mine_ref, f32[8,1024]{1,0:T(8,128)S(1)} %collective-permute-done.4.other_ref, bf16[2,1024,512]{2,1,0:T(8,128)(2,1)S(1)} %get-tuple-element.15.high_ref, bf16[2,1024,512]{2,1,0:T(8,128)(2,1)S(1)} %get-tuple-element.16.low_ref), custom_call_target="tpu_custom_call" | custom-call | tf_op jit(solution)/shard_map/reflect/pallas_call | solution.py:176
  20.4 0.2 collective-permute-start.5
  20.6 1.0 %collective-permute-done.5 = f32[8,512]{1,0:T(8,128)S(1)} collective-permute-done((f32[8,512]{1,0:T(8,128)S(1)}, f32[8,512]{1,0:T(8,128)S(1)}, u32[]{:S(2)}, u32[]{:S(2)}) %collective-permute-start.5) | collective-permute-done | bytes 16416 | tf_op jit(solution)/shard_map/ppermute | solution.py:280
  21.6 1.5 %collective-permute-start.7 = (f32[8,512]{1,0:T(8,128)S(1)}, f32[8,512]{1,0:T(8,128)S(1)}, u32[]{:S(2)}, u32[]{:S(2)}) collective-permute-start(f32[8,512]{1,0:T(8,128)S(1)} %add.23.own_ref), channel_id=1, source_target_pairs={{0,2},{4,6},{8,10},{12,14},{1,15},{3,13},{5,11},{7,9},{2,0},{6,4},... | collective-permute-start | bytes 49160 | tf_op jit(solution)/shard_map/ppermute | solution.py:280
  23.2 1.2 %collective-permute-start.8 = (f32[8,512]{1,0:T(8,128)S(1)}, f32[8,512]{1,0:T(8,128)S(1)}, u32[]{:S(2)}, u32[]{:S(2)}) collective-permute-start(f32[8,512]{1,0:T(8,128)S(1)} %add.23.own_ref), channel_id=1, source_target_pairs={{0,10},{2,8},{4,14},{6,12},{1,9},{3,11},{5,13},{7,15},{10,0},{8,2}... | collective-permute-start | bytes 49160 | tf_op jit(solution)/shard_map/ppermute | solution.py:280
  24.3 1.3 %collective-permute-start.9 = (f32[8,512]{1,0:T(8,128)S(1)}, f32[8,512]{1,0:T(8,128)S(1)}, u32[]{:S(2)}, u32[]{:S(2)}) collective-permute-start(f32[8,512]{1,0:T(8,128)S(1)} %add.23.own_ref), channel_id=1, source_target_pairs={{0,4},{2,6},{8,12},{10,14},{1,13},{3,15},{5,9},{7,11},{4,0},{6,2},... | collective-permute-start | bytes 49160 | tf_op jit(solution)/shard_map/ppermute | solution.py:280
  25.7 1.3 %collective-permute-start.6 = (f32[8,512]{1,0:T(8,128)S(1)}, f32[8,512]{1,0:T(8,128)S(1)}, u32[]{:S(2)}, u32[]{:S(2)}) collective-permute-start(f32[8,512]{1,0:T(8,128)S(1)} %add.23.own_ref), channel_id=1, source_target_pairs={{0,7},{2,5},{8,15},{10,13},{1,6},{3,4},{9,14},{11,12},{7,0},{5,2},... | collective-permute-start | bytes 49160 | tf_op jit(solution)/shard_map/ppermute | solution.py:280
  27.0 0.0 collective-permute-done.7.refs_0_
  27.0 0.5 %collective-permute-start.10 = (f32[8,512]{1,0:T(8,128)S(1)}, f32[8,512]{1,0:T(8,128)S(1)}, u32[]{:S(2)}, u32[]{:S(2)}) collective-permute-start(f32[8,512]{1,0:T(8,128)S(1)} %collective-permute-done.7.refs_0_), channel_id=1, source_target_pairs={{0,1},{1,0},{2,3},{3,2},{4,5},{5,4},{6,7},{7,6},{8,9},{9,8},{10,11... | collective-permute-start | bytes 49160 | tf_op jit(solution)/shard_map/ppermute | solution.py:280
  27.4 1.4 %collective-permute-done.8.refs_1_ = f32[8,512]{1,0:T(8,128)S(1)} collective-permute-done((f32[8,512]{1,0:T(8,128)S(1)}, f32[8,512]{1,0:T(8,128)S(1)}, u32[]{:S(2)}, u32[]{:S(2)}) %collective-permute-start.8) | collective-permute-done | bytes 16416 | tf_op jit(solution)/shard_map/ppermute | solution.py:280
  28.8 0.0 collective-permute-start.11
  28.8 0.0 collective-permute-done.9.refs_2_
  28.8 0.5 %collective-permute-start.12 = (f32[8,512]{1,0:T(8,128)S(1)}, f32[8,512]{1,0:T(8,128)S(1)}, u32[]{:S(2)}, u32[]{:S(2)}) collective-permute-start(f32[8,512]{1,0:T(8,128)S(1)} %collective-permute-done.9.refs_2_), channel_id=1, source_target_pairs={{0,1},{1,0},{2,3},{3,2},{4,5},{5,4},{6,7},{7,6},{8,9},{9,8},{10,11... | collective-permute-start | bytes 49160 | tf_op jit(solution)/shard_map/ppermute | solution.py:280
  29.3 0.1 turn.1.left_ref
  29.5 0.3 collective-permute-done.6.both_ref
  29.8 0.0 collective-permute-done.10.refs_3_
  29.8 0.2 collective-permute-done.11.refs_4_
  30.0 0.2 collective-permute-done.12.refs_5_
  30.2 3.0 %finish.1 = (bf16[2,1024,512]{2,1,0:T(8,128)(2,1)}, f32[1,2,1024,512]{3,2,1,0:T(8,128)}) custom-call(bf16[1024,32]{1,0:T(8,128)(2,1)S(1)} %turn.1.left_ref, f32[2,1024,512]{2,1,0:T(8,128)S(1)} %get-tuple-element.18.merged_ref, f32[8,512]{1,0:T(8,128)S(1)} %add.23.own_ref, f32[8,512]{1,0:T(8,128)S(1)} %collective-permute-done.6.both_ref, ...), custom_call_target="tpu_custom_call" | custom-call | tf_op jit(solution)/shard_map/finish/pallas_call | solution.py:254
  (3 shorter events, 0.0 us)
Async XLA Ops:
  4.0 4.9 %collective-permute-start = (f32[8,1024]{1,0:T(8,128)S(1)}, f32[8,1024]{1,0:T(8,128)S(1)}, u32[]{:S(2)}, u32[]{:S(2)}) collective-permute-start(f32[8,1024]{1,0:T(8,128)S(1)} %get-tuple-element.11), channel_id=1, source_target_pairs={{0,2},{4,6},{8,10},{12,14},{1,3},{5,7},{9,11},{13,15},{2,0},{6,4},... | collective-permute-start | bytes 98312 | tf_op jit(solution)/shard_map/ppermute | solution.py:280
  8.9 5.0 %collective-permute-start.2 = (f32[8,1024]{1,0:T(8,128)S(1)}, f32[8,1024]{1,0:T(8,128)S(1)}, u32[]{:S(2)}, u32[]{:S(2)}) collective-permute-start(f32[8,1024]{1,0:T(8,128)S(1)} %add_add_fusion.1), channel_id=1, source_target_pairs={{0,8},{2,10},{4,12},{6,14},{1,9},{3,11},{5,13},{7,15},{8,0},{10,2}... | collective-permute-start | bytes 98312 | tf_op jit(solution)/shard_map/ppermute | solution.py:280
  12.1 5.7 %collective-permute-start.3 = (f32[8,1024]{1,0:T(8,128)S(1)}, f32[8,1024]{1,0:T(8,128)S(1)}, u32[]{:S(2)}, u32[]{:S(2)}) collective-permute-start(f32[8,1024]{1,0:T(8,128)S(1)} %add_add_fusion.1), channel_id=1, source_target_pairs={{0,12},{2,14},{4,8},{6,10},{1,13},{3,15},{5,9},{7,11},{12,0},{14,2... | collective-permute-start | bytes 98312 | tf_op jit(solution)/shard_map/ppermute | solution.py:280
  13.4 4.4 %collective-permute-start.1 = (f32[8,1024]{1,0:T(8,128)S(1)}, f32[8,1024]{1,0:T(8,128)S(1)}, u32[]{:S(2)}, u32[]{:S(2)}) collective-permute-start(f32[8,1024]{1,0:T(8,128)S(1)} %add_add_fusion.1), channel_id=1, source_target_pairs={{0,4},{2,6},{8,12},{10,14},{1,5},{3,7},{9,13},{11,15},{4,0},{6,2},... | collective-permute-start | bytes 98312 | tf_op jit(solution)/shard_map/ppermute | solution.py:280
  17.8 1.3 %collective-permute-start.4 = (f32[8,1024]{1,0:T(8,128)S(1)}, f32[8,1024]{1,0:T(8,128)S(1)}, u32[]{:S(2)}, u32[]{:S(2)}) collective-permute-start(f32[8,1024]{1,0:T(8,128)S(1)} %add_add_fusion.mine_ref), channel_id=1, source_target_pairs={{0,1},{1,0},{2,3},{3,2},{4,5},{5,4},{6,7},{7,6},{8,9},{9,8},{10,11... | collective-permute-start | bytes 98312 | tf_op jit(solution)/shard_map/ppermute | solution.py:280
  20.4 1.2 %collective-permute-start.5 = (f32[8,512]{1,0:T(8,128)S(1)}, f32[8,512]{1,0:T(8,128)S(1)}, u32[]{:S(2)}, u32[]{:S(2)}) collective-permute-start(f32[8,512]{1,0:T(8,128)S(1)} %get-tuple-element.19), channel_id=1, source_target_pairs={{0,1},{1,0},{2,3},{3,2},{4,5},{5,4},{6,7},{7,6},{8,9},{9,8},{10,11... | collective-permute-start | bytes 49160 | tf_op jit(solution)/shard_map/ppermute | solution.py:280
  21.6 5.3 %collective-permute-start.7 = (f32[8,512]{1,0:T(8,128)S(1)}, f32[8,512]{1,0:T(8,128)S(1)}, u32[]{:S(2)}, u32[]{:S(2)}) collective-permute-start(f32[8,512]{1,0:T(8,128)S(1)} %add.23.own_ref), channel_id=1, source_target_pairs={{0,2},{4,6},{8,10},{12,14},{1,15},{3,13},{5,11},{7,9},{2,0},{6,4},... | collective-permute-start | bytes 49160 | tf_op jit(solution)/shard_map/ppermute | solution.py:280
  23.2 5.7 %collective-permute-start.8 = (f32[8,512]{1,0:T(8,128)S(1)}, f32[8,512]{1,0:T(8,128)S(1)}, u32[]{:S(2)}, u32[]{:S(2)}) collective-permute-start(f32[8,512]{1,0:T(8,128)S(1)} %add.23.own_ref), channel_id=1, source_target_pairs={{0,10},{2,8},{4,14},{6,12},{1,9},{3,11},{5,13},{7,15},{10,0},{8,2}... | collective-permute-start | bytes 49160 | tf_op jit(solution)/shard_map/ppermute | solution.py:280
  24.3 4.5 %collective-permute-start.9 = (f32[8,512]{1,0:T(8,128)S(1)}, f32[8,512]{1,0:T(8,128)S(1)}, u32[]{:S(2)}, u32[]{:S(2)}) collective-permute-start(f32[8,512]{1,0:T(8,128)S(1)} %add.23.own_ref), channel_id=1, source_target_pairs={{0,4},{2,6},{8,12},{10,14},{1,13},{3,15},{5,9},{7,11},{4,0},{6,2},... | collective-permute-start | bytes 49160 | tf_op jit(solution)/shard_map/ppermute | solution.py:280
  25.7 4.1 %collective-permute-start.6 = (f32[8,512]{1,0:T(8,128)S(1)}, f32[8,512]{1,0:T(8,128)S(1)}, u32[]{:S(2)}, u32[]{:S(2)}) collective-permute-start(f32[8,512]{1,0:T(8,128)S(1)} %add.23.own_ref), channel_id=1, source_target_pairs={{0,7},{2,5},{8,15},{10,13},{1,6},{3,4},{9,14},{11,12},{7,0},{5,2},... | collective-permute-start | bytes 49160 | tf_op jit(solution)/shard_map/ppermute | solution.py:280
  27.0 2.8 %collective-permute-start.10 = (f32[8,512]{1,0:T(8,128)S(1)}, f32[8,512]{1,0:T(8,128)S(1)}, u32[]{:S(2)}, u32[]{:S(2)}) collective-permute-start(f32[8,512]{1,0:T(8,128)S(1)} %collective-permute-done.7.refs_0_), channel_id=1, source_target_pairs={{0,1},{1,0},{2,3},{3,2},{4,5},{5,4},{6,7},{7,6},{8,9},{9,8},{10,11... | collective-permute-start | bytes 49160 | tf_op jit(solution)/shard_map/ppermute | solution.py:280
  28.8 1.2 %collective-permute-start.11 = (f32[8,512]{1,0:T(8,128)S(1)}, f32[8,512]{1,0:T(8,128)S(1)}, u32[]{:S(2)}, u32[]{:S(2)}) collective-permute-start(f32[8,512]{1,0:T(8,128)S(1)} %collective-permute-done.8.refs_1_), channel_id=1, source_target_pairs={{0,1},{1,0},{2,3},{3,2},{4,5},{5,4},{6,7},{7,6},{8,9},{9,8},{10,11... | collective-permute-start | bytes 49160 | tf_op jit(solution)/shard_map/ppermute | solution.py:280
  28.8 1.3 %collective-permute-start.12 = (f32[8,512]{1,0:T(8,128)S(1)}, f32[8,512]{1,0:T(8,128)S(1)}, u32[]{:S(2)}, u32[]{:S(2)}) collective-permute-start(f32[8,512]{1,0:T(8,128)S(1)} %collective-permute-done.9.refs_2_), channel_id=1, source_target_pairs={{0,1},{1,0},{2,3},{3,2},{4,5},{5,4},{6,7},{7,6},{8,9},{9,8},{10,11... | collective-permute-start | bytes 49160 | tf_op jit(solution)/shard_map/ppermute | solution.py:280

commit v15 on v14

--- a/solution.py
+++ b/solution.py
@@ -158,9 +158,20 @@
     return mine
 
 
-def reflect_body(scale, mine_ref, other_ref, high_ref, low_ref, left_ref, right_ref):
+def reflect_body(scale, count, high_ref, low_ref, own_ref, both_ref, *refs):
     mats, rows, cols = high_ref.shape
-    left = orthogonal(mine_ref[...] * scale, other_ref[...] * scale)
+    left_ref, right_ref = refs[2 * count :]
+    mine, other = [
+        total(
+            own_ref[at],
+            both_ref[1 - at],
+            [ref[at] for ref in refs[:count]],
+            [ref[1 - at] for ref in refs[count : 2 * count]],
+        )
+        * scale
+        for at in range(2)
+    ]
+    left = orthogonal(mine, other)
     left_ref[...] = left
     weights = jnp.concatenate(halves(left), axis=0).astype(BF16)
     right = jnp.zeros((mats * RANK, cols), F32)
@@ -171,19 +182,26 @@
     right_ref[...] = right
 
 
-def reflect(mine, other, high, low, scale):
+def reflect(high, low, own, both, taken, given, scale):
     mats, rows, cols = high.shape
     return pl.pallas_call(
-        functools.partial(reflect_body, scale),
+        functools.partial(reflect_body, scale, len(taken)),
         out_shape=(
             jax.ShapeDtypeStruct((mats * RANK, rows), F32),
             jax.ShapeDtypeStruct((mats * RANK, cols), F32),
         ),
-        in_specs=[pl.BlockSpec(memory_space=pltpu.VMEM)] * 4,
+        in_specs=[pl.BlockSpec(memory_space=pltpu.VMEM)] * (4 + 2 * len(taken)),
         out_specs=[pl.BlockSpec(memory_space=pltpu.VMEM)] * 2,
-        compiler_params=pltpu.CompilerParams(vmem_limit_bytes=24 * 2**20),
+        compiler_params=pltpu.CompilerParams(vmem_limit_bytes=16 * 2**20),
         name="reflect",
-    )(mine, other, pltpu.with_memory_space_constraint(high, pltpu.VMEM), pltpu.with_memory_space_constraint(low, pltpu.VMEM))
+    )(
+        pltpu.with_memory_space_constraint(high, pltpu.VMEM),
+        pltpu.with_memory_space_constraint(low, pltpu.VMEM),
+        own,
+        both,
+        *taken,
+        *given,
+    )
 
 
 def turn_body(left_ref, turned_ref):
@@ -204,13 +222,12 @@
     )(left)
 
 
-def total(own_ref, both_ref, taken_refs, given_refs):
+def total(own, both, taken, given):
     first = lax.axis_index("tensor") == 0
-    terms = {0: own_ref[...], SHARED: both_ref[...]}
-    for masks, taken_ref, given_ref in zip(SPLIT, taken_refs, given_refs):
-        taken, given = taken_ref[...], given_ref[...]
-        terms[masks[0]] = jnp.where(first, taken, given)
-        terms[masks[1]] = jnp.where(first, given, taken)
+    terms = {0: own, SHARED: both}
+    for masks, near, far in zip(SPLIT, taken, given):
+        terms[masks[0]] = jnp.where(first, near, far)
+        terms[masks[1]] = jnp.where(first, far, near)
     sums = [terms[index] for index in range(len(terms))]
     while len(sums) > 1:
         sums = [sums[at] + sums[at + 1] for at in range(0, len(sums), 2)]
@@ -218,9 +235,9 @@
 
 
 def finish_body(scale, count, left_ref, merged_ref, own_ref, both_ref, *refs):
-    taken_refs, given_refs = refs[:count], refs[count : 2 * count]
+    taken, given = [ref[...] for ref in refs[:count]], [ref[...] for ref in refs[count : 2 * count]]
     update_ref, errors_ref, ubuf, ebuf, sems = refs[2 * count :]
-    right = total(own_ref, both_ref, taken_refs, given_refs) * scale
+    right = total(own_ref[...], both_ref[...], taken, given) * scale
     finish_rows(right, left_ref, merged_ref, update_ref, errors_ref, ubuf, ebuf, sems)
 
 
@@ -294,26 +311,12 @@
     return swap(value, ("dp", "tensor"), pairs)
 
 
-def chips_sum(value, zero):
-    count = lax.axis_size("dp")
-    last = max(count // 4, 1)
-    step = 1
-    while step < last:
-        value = value + (zero + swap_chips(value, (step, step)))
-        zero = 0.0
-        step *= 2
-    terms = [value] + [swap_chips(value, (offset, offset)) for offset in range(last, count, last)]
-    while len(terms) > 1:
-        terms = [terms[at] + terms[at + 1] for at in range(0, len(terms), 2)]
-    return terms[0]
-
-
-def chips_terms(value):
+def chips_terms(value, turned):
     count = lax.axis_size("dp")
     last = count // 8
     step = 1
     while step < last:
-        value = value + swap_chips(value, (step, step), 1)
+        value = value + turned(swap_chips(value, (step, step), 1))
         step *= 2
     both = swap_chips(value, (SHARED * last, SHARED * last), 1)
     taken = [swap_chips(value, (lower * last, upper * last)) for lower, upper in SPLIT[::-1]][::-1]
@@ -324,9 +327,10 @@
     replicas = lax.axis_size("dp")
     left_part, grads, errors = project(seeds, grads, errors)
     merged, high, low, zero = merge(grads, errors)
-    mine = chips_sum(left_part, zero)
-    left, right_part = reflect(mine, swap_cores(mine), high, low, 1.0 / replicas)
-    terms = chips_terms(right_part + swap_cores(right_part))
+    both = jnp.stack([left_part, swap_cores(left_part) + zero], axis=0)
+    terms = chips_terms(both, lambda taken: lax.rev(taken, (0,)))
+    left, right_part = reflect(high, low, *terms, 1.0 / replicas)
+    terms = chips_terms(right_part + swap_cores(right_part), lambda taken: taken)
     return finish(turn(left), merged, *terms, 1.0 / replicas)
 
 

time: 33.3 us -> 33.4 us (level)
  starting transfers between devices: 14.3 us -> 17.3 us
  waiting for transfers between devices: 9.46 us -> 6.55 us
    ppermute x13 -> x16, starting transfers between devices: 14.3 us -> 17.3 us  [swap(): lax.ppermute(value, axes, pairs + [(target, source) for source, target in...]
    ppermute x13 -> x16, waiting for transfers between devices: 9.46 us -> 6.55 us  [swap(): lax.ppermute(value, axes, pairs + [(target, source) for source, target in...]
  transfers between devices with their start and end apart: 13 -> 16, of which waited for: 9 -> 6; matrix products, arithmetic and copies ran while one was open for 0% -> 0% of each run, Pallas kernels for 3% -> 3%
where the time goes in v15:
time: 33.4 us; the launch traced here: 33.3 us
  starting transfers between devices  17.3 us (52%)
  Pallas kernels  8.76 us (26%)
  waiting for transfers between devices  6.55 us (20%)
  between operations  0.7 us (2%)
    ppermute x16, starting transfers between devices, swap(): lax.ppermute(value, axes, pairs + [(target, source) for source, target in...  17.3 us
    ppermute x16, waiting for transfers between devices, swap(): lax.ppermute(value, axes, pairs + [(target, source) for source, target in...  6.55 us
    pallas_call x1, Pallas kernels, project(): pl.pallas_call(project_body, out_shape=(jax.ShapeDtypeStruct((mats * RANK...  3.35 us
    pallas_call x1, Pallas kernels, finish(): pl.pallas_call(functools.partial(finish_body, scale, len(taken)), out_sha...  3 us
    pallas_call x1, Pallas kernels, reflect(): pl.pallas_call(functools.partial(reflect_body, scale, len(taken)), out_sh...  1.41 us
    pallas_call x1, Pallas kernels, merge(): pl.pallas_call(merge_body, out_shape=(pltpu.VMEM(shape, F32), pltpu.VMEM(...  0.86 us
  transfers between devices with their start and end apart: 16, of which 6 were waited for; matrix products, arithmetic and copies ran while one was open for 0% of the time, Pallas kernels for 3%

profile of v15, /device:TPU:0, one launch (start us, length us, event | category | flops | bytes accessed | tf_op | source)
XLA Modules:
  0.0 33.3 jit_solution(530666867377312297)
XLA Ops:
  0.6 3.4 %project.1 = (f32[8,1024]{1,0:T(8,128)S(1)}, bf16[2,1024,512]{2,1,0:T(8,128)(2,1)S(1)}, f32[2,1024,512]{2,1,0:T(8,128)S(1)}) custom-call(s32[2]{0:T(128)} %seeds_ref.1, bf16[1,2,1024,512]{3,2,1,0:T(8,128)(2,1)} %grads_ref.1, f32[1,2,1024,512]{3,2,1,0:T(8,128)} %errors_ref.1), custom_call_target="tpu_custom_call" | custom-call | tf_op jit(solution)/shard_map/project/pallas_call | solution.py:81
  4.0 0.5 %collective-permute-start = (f32[8,1024]{1,0:T(8,128)S(1)}, f32[8,1024]{1,0:T(8,128)S(1)}, u32[]{:S(2)}, u32[]{:S(2)}) collective-permute-start(f32[8,1024]{1,0:T(8,128)S(1)} %get-tuple-element.15), channel_id=1, source_target_pairs={{0,1},{1,0},{2,3},{3,2},{4,5},{5,4},{6,7},{7,6},{8,9},{9,8},{10,11... | collective-permute-start | bytes 98312 | tf_op jit(solution)/shard_map/ppermute | solution.py:297
  4.5 0.9 %merge.1 = (f32[2,1024,512]{2,1,0:T(8,128)S(1)}, bf16[2,1024,512]{2,1,0:T(8,128)(2,1)S(1)}, bf16[2,1024,512]{2,1,0:T(8,128)(2,1)S(1)}, f32[8,1024]{1,0:T(8,128)S(1)}) custom-call(bf16[2,1024,512]{2,1,0:T(8,128)(2,1)S(1)} %get-tuple-element.11.grads_ref, f32[2,1024,512]{2,1,0:T(8,128)S(1)} %get-tuple-element.12.errors_ref), custom_call_target="tpu_custom_call" | custom-call | flops 3145728 | bytes 14680064 | tf_op jit(solution)/shard_map/merge/pallas_call | solution.py:118
  5.4 0.0 collective-permute-done
  5.4 2.9 %collective-permute-start.2 = (f32[2,8,1024]{2,1,0:T(8,128)S(1)}, f32[2,8,1024]{2,1,0:T(8,128)S(1)}, u32[]{:S(2)}, u32[]{:S(2)}) collective-permute-start(f32[2,8,1024]{2,1,0:T(8,128)S(1)} %pad_maximum_fusion.own_ref), channel_id=1, source_target_pairs={{0,2},{4,6},{8,10},{12,14},{1,15},{3,13},{5,11},{7,9},{2,0},{6,4},... | collective-permute-start | bytes 196616 | tf_op jit(solution)/shard_map/ppermute | solution.py:297
  8.3 2.5 %collective-permute-start.3 = (f32[2,8,1024]{2,1,0:T(8,128)S(1)}, f32[2,8,1024]{2,1,0:T(8,128)S(1)}, u32[]{:S(2)}, u32[]{:S(2)}) collective-permute-start(f32[2,8,1024]{2,1,0:T(8,128)S(1)} %pad_maximum_fusion.own_ref), channel_id=1, source_target_pairs={{0,10},{2,8},{4,14},{6,12},{1,9},{3,11},{5,13},{7,15},{10,0},{8,2}... | collective-permute-start | bytes 196616 | tf_op jit(solution)/shard_map/ppermute | solution.py:297
  10.8 1.6 %collective-permute-start.4 = (f32[2,8,1024]{2,1,0:T(8,128)S(1)}, f32[2,8,1024]{2,1,0:T(8,128)S(1)}, u32[]{:S(2)}, u32[]{:S(2)}) collective-permute-start(f32[2,8,1024]{2,1,0:T(8,128)S(1)} %pad_maximum_fusion.own_ref), channel_id=1, source_target_pairs={{0,4},{2,6},{8,12},{10,14},{1,13},{3,15},{5,9},{7,11},{4,0},{6,2},... | collective-permute-start | bytes 196616 | tf_op jit(solution)/shard_map/ppermute | solution.py:297
  12.4 1.3 %collective-permute-start.1 = (f32[2,8,1024]{2,1,0:T(8,128)S(1)}, f32[2,8,1024]{2,1,0:T(8,128)S(1)}, u32[]{:S(2)}, u32[]{:S(2)}) collective-permute-start(f32[2,8,1024]{2,1,0:T(8,128)S(1)} %pad_maximum_fusion.own_ref), channel_id=1, source_target_pairs={{0,7},{2,5},{8,15},{10,13},{1,6},{3,4},{9,14},{11,12},{7,0},{5,2},... | collective-permute-start | bytes 196616 | tf_op jit(solution)/shard_map/ppermute | solution.py:297
  13.8 0.2 collective-permute-start.5
  13.9 3.0 %collective-permute-done.3.refs_1_ = f32[2,8,1024]{2,1,0:T(8,128)S(1)} collective-permute-done((f32[2,8,1024]{2,1,0:T(8,128)S(1)}, f32[2,8,1024]{2,1,0:T(8,128)S(1)}, u32[]{:S(2)}, u32[]{:S(2)}) %collective-permute-start.3) | collective-permute-done | bytes 65568 | tf_op jit(solution)/shard_map/ppermute | solution.py:297
  17.0 0.0 collective-permute-start.6
  17.0 0.0 collective-permute-done.4.refs_2_
  17.0 0.5 %collective-permute-start.7 = (f32[2,8,1024]{2,1,0:T(8,128)S(1)}, f32[2,8,1024]{2,1,0:T(8,128)S(1)}, u32[]{:S(2)}, u32[]{:S(2)}) collective-permute-start(f32[2,8,1024]{2,1,0:T(8,128)S(1)} %collective-permute-done.4.refs_2_), channel_id=1, source_target_pairs={{0,1},{1,0},{2,3},{3,2},{4,5},{5,4},{6,7},{7,6},{8,9},{9,8},{10,11... | collective-permute-start | bytes 196616 | tf_op jit(solution)/shard_map/ppermute | solution.py:297
  17.5 1.2 %collective-permute-done.1.both_ref = f32[2,8,1024]{2,1,0:T(8,128)S(1)} collective-permute-done((f32[2,8,1024]{2,1,0:T(8,128)S(1)}, f32[2,8,1024]{2,1,0:T(8,128)S(1)}, u32[]{:S(2)}, u32[]{:S(2)}) %collective-permute-start.1) | collective-permute-done | bytes 65568 | tf_op jit(solution)/shard_map/ppermute | solution.py:297
  18.7 0.0 collective-permute-done.5.refs_3_
  18.7 0.0 collective-permute-done.6.refs_4_
  18.7 0.0 collective-permute-done.7.refs_5_
  18.7 1.4 %reflect.1 = (f32[8,1024]{1,0:T(8,128)S(1)}, f32[8,512]{1,0:T(8,128)S(1)}) custom-call(bf16[2,1024,512]{2,1,0:T(8,128)(2,1)S(1)} %get-tuple-element.13.high_ref, bf16[2,1024,512]{2,1,0:T(8,128)(2,1)S(1)} %get-tuple-element.14.low_ref, f32[2,8,1024]{2,1,0:T(8,128)S(1)} %pad_maximum_fusion.own_ref, f32[2,8,1024]{2,1,0:T(8,128)S(1)} %collective-permute-done.1.both_ref, ...), custom_call_target="tpu_custom_call" | custom-call | tf_op jit(solution)/shard_map/reflect/pallas_call | solution.py:187
  20.1 0.4 %collective-permute-start.8 = (f32[8,512]{1,0:T(8,128)S(1)}, f32[8,512]{1,0:T(8,128)S(1)}, u32[]{:S(2)}, u32[]{:S(2)}) collective-permute-start(f32[8,512]{1,0:T(8,128)S(1)} %get-tuple-element.19), channel_id=1, source_target_pairs={{0,1},{1,0},{2,3},{3,2},{4,5},{5,4},{6,7},{7,6},{8,9},{9,8},{10,11... | collective-permute-start | bytes 49160 | tf_op jit(solution)/shard_map/ppermute | solution.py:297
  20.5 0.8 %collective-permute-done.8 = f32[8,512]{1,0:T(8,128)S(1)} collective-permute-done((f32[8,512]{1,0:T(8,128)S(1)}, f32[8,512]{1,0:T(8,128)S(1)}, u32[]{:S(2)}, u32[]{:S(2)}) %collective-permute-start.8) | collective-permute-done | bytes 16416 | tf_op jit(solution)/shard_map/ppermute | solution.py:297
  21.4 1.5 %collective-permute-start.10 = (f32[8,512]{1,0:T(8,128)S(1)}, f32[8,512]{1,0:T(8,128)S(1)}, u32[]{:S(2)}, u32[]{:S(2)}) collective-permute-start(f32[8,512]{1,0:T(8,128)S(1)} %add.7.own_ref), channel_id=1, source_target_pairs={{0,2},{4,6},{8,10},{12,14},{1,15},{3,13},{5,11},{7,9},{2,0},{6,4},... | collective-permute-start | bytes 49160 | tf_op jit(solution)/shard_map/ppermute | solution.py:297
  22.9 1.2 %collective-permute-start.11 = (f32[8,512]{1,0:T(8,128)S(1)}, f32[8,512]{1,0:T(8,128)S(1)}, u32[]{:S(2)}, u32[]{:S(2)}) collective-permute-start(f32[8,512]{1,0:T(8,128)S(1)} %add.7.own_ref), channel_id=1, source_target_pairs={{0,10},{2,8},{4,14},{6,12},{1,9},{3,11},{5,13},{7,15},{10,0},{8,2}... | collective-permute-start | bytes 49160 | tf_op jit(solution)/shard_map/ppermute | solution.py:297
  24.1 2.1 %collective-permute-start.12 = (f32[8,512]{1,0:T(8,128)S(1)}, f32[8,512]{1,0:T(8,128)S(1)}, u32[]{:S(2)}, u32[]{:S(2)}) collective-permute-start(f32[8,512]{1,0:T(8,128)S(1)} %add.7.own_ref), channel_id=1, source_target_pairs={{0,4},{2,6},{8,12},{10,14},{1,13},{3,15},{5,9},{7,11},{4,0},{6,2},... | collective-permute-start | bytes 49160 | tf_op jit(solution)/shard_map/ppermute | solution.py:297
  26.1 1.5 %collective-permute-start.9 = (f32[8,512]{1,0:T(8,128)S(1)}, f32[8,512]{1,0:T(8,128)S(1)}, u32[]{:S(2)}, u32[]{:S(2)}) collective-permute-start(f32[8,512]{1,0:T(8,128)S(1)} %add.7.own_ref), channel_id=1, source_target_pairs={{0,7},{2,5},{8,15},{10,13},{1,6},{3,4},{9,14},{11,12},{7,0},{5,2},... | collective-permute-start | bytes 49160 | tf_op jit(solution)/shard_map/ppermute | solution.py:297
  27.6 0.8 %collective-permute-done.11.refs_1_ = f32[8,512]{1,0:T(8,128)S(1)} collective-permute-done((f32[8,512]{1,0:T(8,128)S(1)}, f32[8,512]{1,0:T(8,128)S(1)}, u32[]{:S(2)}, u32[]{:S(2)}) %collective-permute-start.11) | collective-permute-done | bytes 16416 | tf_op jit(solution)/shard_map/ppermute | solution.py:297
  28.4 0.1 collective-permute-start.14
  28.5 0.9 %collective-permute-start.15 = (f32[8,512]{1,0:T(8,128)S(1)}, f32[8,512]{1,0:T(8,128)S(1)}, u32[]{:S(2)}, u32[]{:S(2)}) collective-permute-start(f32[8,512]{1,0:T(8,128)S(1)} %collective-permute-done.12.refs_2_), channel_id=1, source_target_pairs={{0,1},{1,0},{2,3},{3,2},{4,5},{5,4},{6,7},{7,6},{8,9},{9,8},{10,11... | collective-permute-start | bytes 49160 | tf_op jit(solution)/shard_map/ppermute | solution.py:297
  29.4 0.1 turn.1.left_ref
  29.6 0.6 %collective-permute-done.9.both_ref = f32[8,512]{1,0:T(8,128)S(1)} collective-permute-done((f32[8,512]{1,0:T(8,128)S(1)}, f32[8,512]{1,0:T(8,128)S(1)}, u32[]{:S(2)}, u32[]{:S(2)}) %collective-permute-start.9) | collective-permute-done | bytes 16416 | tf_op jit(solution)/shard_map/ppermute | solution.py:297
  30.2 0.0 collective-permute-done.13.refs_3_
  30.2 0.1 collective-permute-done.15.refs_5_
  30.3 3.0 %finish.1 = (bf16[2,1024,512]{2,1,0:T(8,128)(2,1)}, f32[1,2,1024,512]{3,2,1,0:T(8,128)}) custom-call(bf16[1024,32]{1,0:T(8,128)(2,1)S(1)} %turn.1.left_ref, f32[2,1024,512]{2,1,0:T(8,128)S(1)} %get-tuple-element.18.merged_ref, f32[8,512]{1,0:T(8,128)S(1)} %add.7.own_ref, f32[8,512]{1,0:T(8,128)S(1)} %collective-permute-done.9.both_ref, ...), custom_call_target="tpu_custom_call" | custom-call | tf_op jit(solution)/shard_map/finish/pallas_call | solution.py:271
  (8 shorter events, 0.0 us)
Async XLA Ops:
  4.0 1.4 %collective-permute-start = (f32[8,1024]{1,0:T(8,128)S(1)}, f32[8,1024]{1,0:T(8,128)S(1)}, u32[]{:S(2)}, u32[]{:S(2)}) collective-permute-start(f32[8,1024]{1,0:T(8,128)S(1)} %get-tuple-element.15), channel_id=1, source_target_pairs={{0,1},{1,0},{2,3},{3,2},{4,5},{5,4},{6,7},{7,6},{8,9},{9,8},{10,11... | collective-permute-start | bytes 98312 | tf_op jit(solution)/shard_map/ppermute | solution.py:297
  5.4 8.3 %collective-permute-start.2 = (f32[2,8,1024]{2,1,0:T(8,128)S(1)}, f32[2,8,1024]{2,1,0:T(8,128)S(1)}, u32[]{:S(2)}, u32[]{:S(2)}) collective-permute-start(f32[2,8,1024]{2,1,0:T(8,128)S(1)} %pad_maximum_fusion.own_ref), channel_id=1, source_target_pairs={{0,2},{4,6},{8,10},{12,14},{1,15},{3,13},{5,11},{7,9},{2,0},{6,4},... | collective-permute-start | bytes 196616 | tf_op jit(solution)/shard_map/ppermute | solution.py:297
  8.3 8.7 %collective-permute-start.3 = (f32[2,8,1024]{2,1,0:T(8,128)S(1)}, f32[2,8,1024]{2,1,0:T(8,128)S(1)}, u32[]{:S(2)}, u32[]{:S(2)}) collective-permute-start(f32[2,8,1024]{2,1,0:T(8,128)S(1)} %pad_maximum_fusion.own_ref), channel_id=1, source_target_pairs={{0,10},{2,8},{4,14},{6,12},{1,9},{3,11},{5,13},{7,15},{10,0},{8,2}... | collective-permute-start | bytes 196616 | tf_op jit(solution)/shard_map/ppermute | solution.py:297
  10.8 6.1 %collective-permute-start.4 = (f32[2,8,1024]{2,1,0:T(8,128)S(1)}, f32[2,8,1024]{2,1,0:T(8,128)S(1)}, u32[]{:S(2)}, u32[]{:S(2)}) collective-permute-start(f32[2,8,1024]{2,1,0:T(8,128)S(1)} %pad_maximum_fusion.own_ref), channel_id=1, source_target_pairs={{0,4},{2,6},{8,12},{10,14},{1,13},{3,15},{5,9},{7,11},{4,0},{6,2},... | collective-permute-start | bytes 196616 | tf_op jit(solution)/shard_map/ppermute | solution.py:297
  12.4 6.3 %collective-permute-start.1 = (f32[2,8,1024]{2,1,0:T(8,128)S(1)}, f32[2,8,1024]{2,1,0:T(8,128)S(1)}, u32[]{:S(2)}, u32[]{:S(2)}) collective-permute-start(f32[2,8,1024]{2,1,0:T(8,128)S(1)} %pad_maximum_fusion.own_ref), channel_id=1, source_target_pairs={{0,7},{2,5},{8,15},{10,13},{1,6},{3,4},{9,14},{11,12},{7,0},{5,2},... | collective-permute-start | bytes 196616 | tf_op jit(solution)/shard_map/ppermute | solution.py:297
  13.8 4.9 %collective-permute-start.5 = (f32[2,8,1024]{2,1,0:T(8,128)S(1)}, f32[2,8,1024]{2,1,0:T(8,128)S(1)}, u32[]{:S(2)}, u32[]{:S(2)}) collective-permute-start(f32[2,8,1024]{2,1,0:T(8,128)S(1)} %collective-permute-done.2.refs_0_), channel_id=1, source_target_pairs={{0,1},{1,0},{2,3},{3,2},{4,5},{5,4},{6,7},{7,6},{8,9},{9,8},{10,11... | collective-permute-start | bytes 196616 | tf_op jit(solution)/shard_map/ppermute | solution.py:297
  17.0 1.7 %collective-permute-start.6 = (f32[2,8,1024]{2,1,0:T(8,128)S(1)}, f32[2,8,1024]{2,1,0:T(8,128)S(1)}, u32[]{:S(2)}, u32[]{:S(2)}) collective-permute-start(f32[2,8,1024]{2,1,0:T(8,128)S(1)} %collective-permute-done.3.refs_1_), channel_id=1, source_target_pairs={{0,1},{1,0},{2,3},{3,2},{4,5},{5,4},{6,7},{7,6},{8,9},{9,8},{10,11... | collective-permute-start | bytes 196616 | tf_op jit(solution)/shard_map/ppermute | solution.py:297
  17.0 1.7 %collective-permute-start.7 = (f32[2,8,1024]{2,1,0:T(8,128)S(1)}, f32[2,8,1024]{2,1,0:T(8,128)S(1)}, u32[]{:S(2)}, u32[]{:S(2)}) collective-permute-start(f32[2,8,1024]{2,1,0:T(8,128)S(1)} %collective-permute-done.4.refs_2_), channel_id=1, source_target_pairs={{0,1},{1,0},{2,3},{3,2},{4,5},{5,4},{6,7},{7,6},{8,9},{9,8},{10,11... | collective-permute-start | bytes 196616 | tf_op jit(solution)/shard_map/ppermute | solution.py:297
  20.1 1.3 %collective-permute-start.8 = (f32[8,512]{1,0:T(8,128)S(1)}, f32[8,512]{1,0:T(8,128)S(1)}, u32[]{:S(2)}, u32[]{:S(2)}) collective-permute-start(f32[8,512]{1,0:T(8,128)S(1)} %get-tuple-element.19), channel_id=1, source_target_pairs={{0,1},{1,0},{2,3},{3,2},{4,5},{5,4},{6,7},{7,6},{8,9},{9,8},{10,11... | collective-permute-start | bytes 49160 | tf_op jit(solution)/shard_map/ppermute | solution.py:297
  21.4 6.3 %collective-permute-start.10 = (f32[8,512]{1,0:T(8,128)S(1)}, f32[8,512]{1,0:T(8,128)S(1)}, u32[]{:S(2)}, u32[]{:S(2)}) collective-permute-start(f32[8,512]{1,0:T(8,128)S(1)} %add.7.own_ref), channel_id=1, source_target_pairs={{0,2},{4,6},{8,10},{12,14},{1,15},{3,13},{5,11},{7,9},{2,0},{6,4},... | collective-permute-start | bytes 49160 | tf_op jit(solution)/shard_map/ppermute | solution.py:297
  22.9 5.5 %collective-permute-start.11 = (f32[8,512]{1,0:T(8,128)S(1)}, f32[8,512]{1,0:T(8,128)S(1)}, u32[]{:S(2)}, u32[]{:S(2)}) collective-permute-start(f32[8,512]{1,0:T(8,128)S(1)} %add.7.own_ref), channel_id=1, source_target_pairs={{0,10},{2,8},{4,14},{6,12},{1,9},{3,11},{5,13},{7,15},{10,0},{8,2}... | collective-permute-start | bytes 49160 | tf_op jit(solution)/shard_map/ppermute | solution.py:297
  24.1 4.5 %collective-permute-start.12 = (f32[8,512]{1,0:T(8,128)S(1)}, f32[8,512]{1,0:T(8,128)S(1)}, u32[]{:S(2)}, u32[]{:S(2)}) collective-permute-start(f32[8,512]{1,0:T(8,128)S(1)} %add.7.own_ref), channel_id=1, source_target_pairs={{0,4},{2,6},{8,12},{10,14},{1,13},{3,15},{5,9},{7,11},{4,0},{6,2},... | collective-permute-start | bytes 49160 | tf_op jit(solution)/shard_map/ppermute | solution.py:297
  26.1 4.1 %collective-permute-start.9 = (f32[8,512]{1,0:T(8,128)S(1)}, f32[8,512]{1,0:T(8,128)S(1)}, u32[]{:S(2)}, u32[]{:S(2)}) collective-permute-start(f32[8,512]{1,0:T(8,128)S(1)} %add.7.own_ref), channel_id=1, source_target_pairs={{0,7},{2,5},{8,15},{10,13},{1,6},{3,4},{9,14},{11,12},{7,0},{5,2},... | collective-permute-start | bytes 49160 | tf_op jit(solution)/shard_map/ppermute | solution.py:297
  27.6 2.6 %collective-permute-start.13 = (f32[8,512]{1,0:T(8,128)S(1)}, f32[8,512]{1,0:T(8,128)S(1)}, u32[]{:S(2)}, u32[]{:S(2)}) collective-permute-start(f32[8,512]{1,0:T(8,128)S(1)} %collective-permute-done.10.refs_0_), channel_id=1, source_target_pairs={{0,1},{1,0},{2,3},{3,2},{4,5},{5,4},{6,7},{7,6},{8,9},{9,8},{10,11... | collective-permute-start | bytes 49160 | tf_op jit(solution)/shard_map/ppermute | solution.py:297
  28.4 1.8 %collective-permute-start.14 = (f32[8,512]{1,0:T(8,128)S(1)}, f32[8,512]{1,0:T(8,128)S(1)}, u32[]{:S(2)}, u32[]{:S(2)}) collective-permute-start(f32[8,512]{1,0:T(8,128)S(1)} %collective-permute-done.11.refs_1_), channel_id=1, source_target_pairs={{0,1},{1,0},{2,3},{3,2},{4,5},{5,4},{6,7},{7,6},{8,9},{9,8},{10,11... | collective-permute-start | bytes 49160 | tf_op jit(solution)/shard_map/ppermute | solution.py:297
  28.5 1.7 %collective-permute-start.15 = (f32[8,512]{1,0:T(8,128)S(1)}, f32[8,512]{1,0:T(8,128)S(1)}, u32[]{:S(2)}, u32[]{:S(2)}) collective-permute-start(f32[8,512]{1,0:T(8,128)S(1)} %collective-permute-done.12.refs_2_), channel_id=1, source_target_pairs={{0,1},{1,0},{2,3},{3,2},{4,5},{5,4},{6,7},{7,6},{8,9},{9,8},{10,11... | collective-permute-start | bytes 49160 | tf_op jit(solution)/shard_map/ppermute | solution.py:297

commit v16 on v15

--- a/solution.py
+++ b/solution.py
@@ -10,7 +10,8 @@
 RANK = 4
 EPSILON = 1e-08
 CHUNKS = 4
-SPLIT = ((1, 7), (5, 4), (2, 6))
+LEFT_SPLIT = ((6, 4), (1, 7), (2, 5))
+RIGHT_SPLIT = ((1, 7), (5, 4), (2, 6))
 SHARED = 3
 BF16 = jnp.bfloat16
 F32 = jnp.float32
@@ -163,6 +164,7 @@
     left_ref, right_ref = refs[2 * count :]
     mine, other = [
         total(
+            LEFT_SPLIT,
             own_ref[at],
             both_ref[1 - at],
             [ref[at] for ref in refs[:count]],
@@ -222,10 +224,10 @@
     )(left)
 
 
-def total(own, both, taken, given):
+def total(split, own, both, taken, given):
     first = lax.axis_index("tensor") == 0
     terms = {0: own, SHARED: both}
-    for masks, near, far in zip(SPLIT, taken, given):
+    for masks, near, far in zip(split, taken, given):
         terms[masks[0]] = jnp.where(first, near, far)
         terms[masks[1]] = jnp.where(first, far, near)
     sums = [terms[index] for index in range(len(terms))]
@@ -237,7 +239,7 @@
 def finish_body(scale, count, left_ref, merged_ref, own_ref, both_ref, *refs):
     taken, given = [ref[...] for ref in refs[:count]], [ref[...] for ref in refs[count : 2 * count]]
     update_ref, errors_ref, ubuf, ebuf, sems = refs[2 * count :]
-    right = total(own_ref[...], both_ref[...], taken, given) * scale
+    right = total(RIGHT_SPLIT, own_ref[...], both_ref[...], taken, given) * scale
     finish_rows(right, left_ref, merged_ref, update_ref, errors_ref, ubuf, ebuf, sems)
 
 
@@ -311,7 +313,7 @@
     return swap(value, ("dp", "tensor"), pairs)
 
 
-def chips_terms(value, turned):
+def chips_terms(value, split, turned):
     count = lax.axis_size("dp")
     last = count // 8
     step = 1
@@ -319,7 +321,7 @@
         value = value + turned(swap_chips(value, (step, step), 1))
         step *= 2
     both = swap_chips(value, (SHARED * last, SHARED * last), 1)
-    taken = [swap_chips(value, (lower * last, upper * last)) for lower, upper in SPLIT[::-1]][::-1]
+    taken = [swap_chips(value, (lower * last, upper * last)) for lower, upper in split[::-1]][::-1]
     return value, both, taken, [swap_cores(term) for term in taken]
 
 
@@ -328,9 +330,9 @@
     left_part, grads, errors = project(seeds, grads, errors)
     merged, high, low, zero = merge(grads, errors)
     both = jnp.stack([left_part, swap_cores(left_part) + zero], axis=0)
-    terms = chips_terms(both, lambda taken: lax.rev(taken, (0,)))
+    terms = chips_terms(both, LEFT_SPLIT, lambda taken: lax.rev(taken, (0,)))
     left, right_part = reflect(high, low, *terms, 1.0 / replicas)
-    terms = chips_terms(right_part + swap_cores(right_part), lambda taken: taken)
+    terms = chips_terms(right_part + swap_cores(right_part), RIGHT_SPLIT, lambda taken: taken)
     return finish(turn(left), merged, *terms, 1.0 / replicas)
 
 

time: 33.4 us -> 33.2 us (level)
  transfers between devices with their start and end apart: 16 -> 16, of which waited for: 6 -> 8; matrix products, arithmetic and copies ran while one was open for 0% -> 0% of each run, Pallas kernels for 3% -> 3%
where the time goes in v16:
time: 33.2 us; the launch traced here: 33.1 us
  starting transfers between devices  17.4 us (52%)
  Pallas kernels  8.77 us (26%)
  waiting for transfers between devices  6.24 us (19%)
  between operations  0.7 us (2%)
    ppermute x16, starting transfers between devices, swap(): lax.ppermute(value, axes, pairs + [(target, source) for source, target in...  17.4 us
    ppermute x16, waiting for transfers between devices, swap(): lax.ppermute(value, axes, pairs + [(target, source) for source, target in...  6.24 us
    pallas_call x1, Pallas kernels, project(): pl.pallas_call(project_body, out_shape=(jax.ShapeDtypeStruct((mats * RANK...  3.35 us
    pallas_call x1, Pallas kernels, finish(): pl.pallas_call(functools.partial(finish_body, scale, len(taken)), out_sha...  3.01 us
    pallas_call x1, Pallas kernels, reflect(): pl.pallas_call(functools.partial(reflect_body, scale, len(taken)), out_sh...  1.4 us
    pallas_call x1, Pallas kernels, merge(): pl.pallas_call(merge_body, out_shape=(pltpu.VMEM(shape, F32), pltpu.VMEM(...  0.86 us
  transfers between devices with their start and end apart: 16, of which 8 were waited for; matrix products, arithmetic and copies ran while one was open for 0% of the time, Pallas kernels for 3%

profile of v16, /device:TPU:0, one launch (start us, length us, event | category | flops | bytes accessed | tf_op | source)
XLA Modules:
  0.0 33.1 jit_solution(12704499984959265561)
XLA Ops:
  0.6 3.4 %project.1 = (f32[8,1024]{1,0:T(8,128)S(1)}, bf16[2,1024,512]{2,1,0:T(8,128)(2,1)S(1)}, f32[2,1024,512]{2,1,0:T(8,128)S(1)}) custom-call(s32[2]{0:T(128)} %seeds_ref.1, bf16[1,2,1024,512]{3,2,1,0:T(8,128)(2,1)} %grads_ref.1, f32[1,2,1024,512]{3,2,1,0:T(8,128)} %errors_ref.1), custom_call_target="tpu_custom_call" | custom-call | tf_op jit(solution)/shard_map/project/pallas_call | solution.py:82
  4.0 0.5 %collective-permute-start = (f32[8,1024]{1,0:T(8,128)S(1)}, f32[8,1024]{1,0:T(8,128)S(1)}, u32[]{:S(2)}, u32[]{:S(2)}) collective-permute-start(f32[8,1024]{1,0:T(8,128)S(1)} %get-tuple-element.15), channel_id=1, source_target_pairs={{0,1},{1,0},{2,3},{3,2},{4,5},{5,4},{6,7},{7,6},{8,9},{9,8},{10,11... | collective-permute-start | bytes 98312 | tf_op jit(solution)/shard_map/ppermute | solution.py:299
  4.5 0.9 %merge.1 = (f32[2,1024,512]{2,1,0:T(8,128)S(1)}, bf16[2,1024,512]{2,1,0:T(8,128)(2,1)S(1)}, bf16[2,1024,512]{2,1,0:T(8,128)(2,1)S(1)}, f32[8,1024]{1,0:T(8,128)S(1)}) custom-call(bf16[2,1024,512]{2,1,0:T(8,128)(2,1)S(1)} %get-tuple-element.11.grads_ref, f32[2,1024,512]{2,1,0:T(8,128)S(1)} %get-tuple-element.12.errors_ref), custom_call_target="tpu_custom_call" | custom-call | flops 3145728 | bytes 14680064 | tf_op jit(solution)/shard_map/merge/pallas_call | solution.py:119
  5.4 0.0 collective-permute-done
  5.4 5.0 %collective-permute-start.2 = (f32[2,8,1024]{2,1,0:T(8,128)S(1)}, f32[2,8,1024]{2,1,0:T(8,128)S(1)}, u32[]{:S(2)}, u32[]{:S(2)}) collective-permute-start(f32[2,8,1024]{2,1,0:T(8,128)S(1)} %pad_maximum_fusion.own_ref), channel_id=1, source_target_pairs={{0,12},{2,14},{4,8},{6,10},{1,9},{3,11},{5,13},{7,15},{12,0},{14,2... | collective-permute-start | bytes 196616 | tf_op jit(solution)/shard_map/ppermute | solution.py:299
  10.4 1.5 %collective-permute-start.3 = (f32[2,8,1024]{2,1,0:T(8,128)S(1)}, f32[2,8,1024]{2,1,0:T(8,128)S(1)}, u32[]{:S(2)}, u32[]{:S(2)}) collective-permute-start(f32[2,8,1024]{2,1,0:T(8,128)S(1)} %pad_maximum_fusion.own_ref), channel_id=1, source_target_pairs={{0,2},{4,6},{8,10},{12,14},{1,15},{3,13},{5,11},{7,9},{2,0},{6,4},... | collective-permute-start | bytes 196616 | tf_op jit(solution)/shard_map/ppermute | solution.py:299
  11.9 0.0 collective-permute-start.4
  11.9 2.7 %collective-permute-start.1 = (f32[2,8,1024]{2,1,0:T(8,128)S(1)}, f32[2,8,1024]{2,1,0:T(8,128)S(1)}, u32[]{:S(2)}, u32[]{:S(2)}) collective-permute-start(f32[2,8,1024]{2,1,0:T(8,128)S(1)} %pad_maximum_fusion.own_ref), channel_id=1, source_target_pairs={{0,7},{2,5},{8,15},{10,13},{1,6},{3,4},{9,14},{11,12},{7,0},{5,2},... | collective-permute-start | bytes 196616 | tf_op jit(solution)/shard_map/ppermute | solution.py:299
  14.6 0.0 collective-permute-done.2.refs_0_
  14.6 0.0 collective-permute-start.5
  14.6 0.1 collective-permute-done.3.refs_1_
  14.7 1.0 %collective-permute-start.6 = (f32[2,8,1024]{2,1,0:T(8,128)S(1)}, f32[2,8,1024]{2,1,0:T(8,128)S(1)}, u32[]{:S(2)}, u32[]{:S(2)}) collective-permute-start(f32[2,8,1024]{2,1,0:T(8,128)S(1)} %collective-permute-done.3.refs_1_), channel_id=1, source_target_pairs={{0,1},{1,0},{2,3},{3,2},{4,5},{5,4},{6,7},{7,6},{8,9},{9,8},{10,11... | collective-permute-start | bytes 196616 | tf_op jit(solution)/shard_map/ppermute | solution.py:299
  15.7 1.8 %collective-permute-done.4.refs_2_ = f32[2,8,1024]{2,1,0:T(8,128)S(1)} collective-permute-done((f32[2,8,1024]{2,1,0:T(8,128)S(1)}, f32[2,8,1024]{2,1,0:T(8,128)S(1)}, u32[]{:S(2)}, u32[]{:S(2)}) %collective-permute-start.4) | collective-permute-done | bytes 65568 | tf_op jit(solution)/shard_map/ppermute | solution.py:299
  17.5 0.0 collective-permute-start.7
  17.5 0.5 %collective-permute-done.1.both_ref = f32[2,8,1024]{2,1,0:T(8,128)S(1)} collective-permute-done((f32[2,8,1024]{2,1,0:T(8,128)S(1)}, f32[2,8,1024]{2,1,0:T(8,128)S(1)}, u32[]{:S(2)}, u32[]{:S(2)}) %collective-permute-start.1) | collective-permute-done | bytes 65568 | tf_op jit(solution)/shard_map/ppermute | solution.py:299
  18.0 0.8 %collective-permute-done.7.refs_5_ = f32[2,8,1024]{2,1,0:T(8,128)S(1)} collective-permute-done((f32[2,8,1024]{2,1,0:T(8,128)S(1)}, f32[2,8,1024]{2,1,0:T(8,128)S(1)}, u32[]{:S(2)}, u32[]{:S(2)}) %collective-permute-start.7) | collective-permute-done | bytes 65568 | tf_op jit(solution)/shard_map/ppermute | solution.py:299
  18.8 1.4 %reflect.1 = (f32[8,1024]{1,0:T(8,128)S(1)}, f32[8,512]{1,0:T(8,128)S(1)}) custom-call(bf16[2,1024,512]{2,1,0:T(8,128)(2,1)S(1)} %get-tuple-element.13.high_ref, bf16[2,1024,512]{2,1,0:T(8,128)(2,1)S(1)} %get-tuple-element.14.low_ref, f32[2,8,1024]{2,1,0:T(8,128)S(1)} %pad_maximum_fusion.own_ref, f32[2,8,1024]{2,1,0:T(8,128)S(1)} %collective-permute-done.1.both_ref, ...), custom_call_target="tpu_custom_call" | custom-call | tf_op jit(solution)/shard_map/reflect/pallas_call | solution.py:189
  20.2 0.2 collective-permute-start.8
  20.4 1.0 %collective-permute-done.8 = f32[8,512]{1,0:T(8,128)S(1)} collective-permute-done((f32[8,512]{1,0:T(8,128)S(1)}, f32[8,512]{1,0:T(8,128)S(1)}, u32[]{:S(2)}, u32[]{:S(2)}) %collective-permute-start.8) | collective-permute-done | bytes 16416 | tf_op jit(solution)/shard_map/ppermute | solution.py:299
  21.4 0.7 %collective-permute-start.10 = (f32[8,512]{1,0:T(8,128)S(1)}, f32[8,512]{1,0:T(8,128)S(1)}, u32[]{:S(2)}, u32[]{:S(2)}) collective-permute-start(f32[8,512]{1,0:T(8,128)S(1)} %add.7.own_ref), channel_id=1, source_target_pairs={{0,2},{4,6},{8,10},{12,14},{1,15},{3,13},{5,11},{7,9},{2,0},{6,4},... | collective-permute-start | bytes 49160 | tf_op jit(solution)/shard_map/ppermute | solution.py:299
  22.1 2.9 %collective-permute-start.11 = (f32[8,512]{1,0:T(8,128)S(1)}, f32[8,512]{1,0:T(8,128)S(1)}, u32[]{:S(2)}, u32[]{:S(2)}) collective-permute-start(f32[8,512]{1,0:T(8,128)S(1)} %add.7.own_ref), channel_id=1, source_target_pairs={{0,10},{2,8},{4,14},{6,12},{1,9},{3,11},{5,13},{7,15},{10,0},{8,2}... | collective-permute-start | bytes 49160 | tf_op jit(solution)/shard_map/ppermute | solution.py:299
  25.0 1.1 %collective-permute-start.12 = (f32[8,512]{1,0:T(8,128)S(1)}, f32[8,512]{1,0:T(8,128)S(1)}, u32[]{:S(2)}, u32[]{:S(2)}) collective-permute-start(f32[8,512]{1,0:T(8,128)S(1)} %add.7.own_ref), channel_id=1, source_target_pairs={{0,4},{2,6},{8,12},{10,14},{1,13},{3,15},{5,9},{7,11},{4,0},{6,2},... | collective-permute-start | bytes 49160 | tf_op jit(solution)/shard_map/ppermute | solution.py:299
  26.0 1.5 %collective-permute-start.9 = (f32[8,512]{1,0:T(8,128)S(1)}, f32[8,512]{1,0:T(8,128)S(1)}, u32[]{:S(2)}, u32[]{:S(2)}) collective-permute-start(f32[8,512]{1,0:T(8,128)S(1)} %add.7.own_ref), channel_id=1, source_target_pairs={{0,7},{2,5},{8,15},{10,13},{1,6},{3,4},{9,14},{11,12},{7,0},{5,2},... | collective-permute-start | bytes 49160 | tf_op jit(solution)/shard_map/ppermute | solution.py:299
  27.5 0.1 collective-permute-done.11.refs_1_
  27.6 0.4 %collective-permute-start.14 = (f32[8,512]{1,0:T(8,128)S(1)}, f32[8,512]{1,0:T(8,128)S(1)}, u32[]{:S(2)}, u32[]{:S(2)}) collective-permute-start(f32[8,512]{1,0:T(8,128)S(1)} %collective-permute-done.11.refs_1_), channel_id=1, source_target_pairs={{0,1},{1,0},{2,3},{3,2},{4,5},{5,4},{6,7},{7,6},{8,9},{9,8},{10,11... | collective-permute-start | bytes 49160 | tf_op jit(solution)/shard_map/ppermute | solution.py:299
  28.0 0.7 %collective-permute-done.12.refs_2_ = f32[8,512]{1,0:T(8,128)S(1)} collective-permute-done((f32[8,512]{1,0:T(8,128)S(1)}, f32[8,512]{1,0:T(8,128)S(1)}, u32[]{:S(2)}, u32[]{:S(2)}) %collective-permute-start.12) | collective-permute-done | bytes 16416 | tf_op jit(solution)/shard_map/ppermute | solution.py:299
  28.7 0.1 turn.1.left_ref
  28.8 1.2 %collective-permute-done.9.both_ref = f32[8,512]{1,0:T(8,128)S(1)} collective-permute-done((f32[8,512]{1,0:T(8,128)S(1)}, f32[8,512]{1,0:T(8,128)S(1)}, u32[]{:S(2)}, u32[]{:S(2)}) %collective-permute-start.9) | collective-permute-done | bytes 16416 | tf_op jit(solution)/shard_map/ppermute | solution.py:299
  30.1 0.0 collective-permute-done.13.refs_3_
  30.1 0.0 collective-permute-done.14.refs_4_
  30.1 0.0 collective-permute-done.15.refs_5_
  30.1 3.0 %finish.1 = (bf16[2,1024,512]{2,1,0:T(8,128)(2,1)}, f32[1,2,1024,512]{3,2,1,0:T(8,128)}) custom-call(bf16[1024,32]{1,0:T(8,128)(2,1)S(1)} %turn.1.left_ref, f32[2,1024,512]{2,1,0:T(8,128)S(1)} %get-tuple-element.18.merged_ref, f32[8,512]{1,0:T(8,128)S(1)} %add.7.own_ref, f32[8,512]{1,0:T(8,128)S(1)} %collective-permute-done.9.both_ref, ...), custom_call_target="tpu_custom_call" | custom-call | tf_op jit(solution)/shard_map/finish/pallas_call | solution.py:273
  (8 shorter events, 0.0 us)
Async XLA Ops:
  4.0 1.4 %collective-permute-start = (f32[8,1024]{1,0:T(8,128)S(1)}, f32[8,1024]{1,0:T(8,128)S(1)}, u32[]{:S(2)}, u32[]{:S(2)}) collective-permute-start(f32[8,1024]{1,0:T(8,128)S(1)} %get-tuple-element.15), channel_id=1, source_target_pairs={{0,1},{1,0},{2,3},{3,2},{4,5},{5,4},{6,7},{7,6},{8,9},{9,8},{10,11... | collective-permute-start | bytes 98312 | tf_op jit(solution)/shard_map/ppermute | solution.py:299
  5.4 9.2 %collective-permute-start.2 = (f32[2,8,1024]{2,1,0:T(8,128)S(1)}, f32[2,8,1024]{2,1,0:T(8,128)S(1)}, u32[]{:S(2)}, u32[]{:S(2)}) collective-permute-start(f32[2,8,1024]{2,1,0:T(8,128)S(1)} %pad_maximum_fusion.own_ref), channel_id=1, source_target_pairs={{0,12},{2,14},{4,8},{6,10},{1,9},{3,11},{5,13},{7,15},{12,0},{14,2... | collective-permute-start | bytes 196616 | tf_op jit(solution)/shard_map/ppermute | solution.py:299
  10.4 4.3 %collective-permute-start.3 = (f32[2,8,1024]{2,1,0:T(8,128)S(1)}, f32[2,8,1024]{2,1,0:T(8,128)S(1)}, u32[]{:S(2)}, u32[]{:S(2)}) collective-permute-start(f32[2,8,1024]{2,1,0:T(8,128)S(1)} %pad_maximum_fusion.own_ref), channel_id=1, source_target_pairs={{0,2},{4,6},{8,10},{12,14},{1,15},{3,13},{5,11},{7,9},{2,0},{6,4},... | collective-permute-start | bytes 196616 | tf_op jit(solution)/shard_map/ppermute | solution.py:299
  11.9 5.6 %collective-permute-start.4 = (f32[2,8,1024]{2,1,0:T(8,128)S(1)}, f32[2,8,1024]{2,1,0:T(8,128)S(1)}, u32[]{:S(2)}, u32[]{:S(2)}) collective-permute-start(f32[2,8,1024]{2,1,0:T(8,128)S(1)} %pad_maximum_fusion.own_ref), channel_id=1, source_target_pairs={{0,4},{2,6},{8,12},{10,14},{1,11},{3,9},{5,15},{7,13},{4,0},{6,2},... | collective-permute-start | bytes 196616 | tf_op jit(solution)/shard_map/ppermute | solution.py:299
  11.9 6.1 %collective-permute-start.1 = (f32[2,8,1024]{2,1,0:T(8,128)S(1)}, f32[2,8,1024]{2,1,0:T(8,128)S(1)}, u32[]{:S(2)}, u32[]{:S(2)}) collective-permute-start(f32[2,8,1024]{2,1,0:T(8,128)S(1)} %pad_maximum_fusion.own_ref), channel_id=1, source_target_pairs={{0,7},{2,5},{8,15},{10,13},{1,6},{3,4},{9,14},{11,12},{7,0},{5,2},... | collective-permute-start | bytes 196616 | tf_op jit(solution)/shard_map/ppermute | solution.py:299
  14.6 3.4 %collective-permute-start.5 = (f32[2,8,1024]{2,1,0:T(8,128)S(1)}, f32[2,8,1024]{2,1,0:T(8,128)S(1)}, u32[]{:S(2)}, u32[]{:S(2)}) collective-permute-start(f32[2,8,1024]{2,1,0:T(8,128)S(1)} %collective-permute-done.2.refs_0_), channel_id=1, source_target_pairs={{0,1},{1,0},{2,3},{3,2},{4,5},{5,4},{6,7},{7,6},{8,9},{9,8},{10,11... | collective-permute-start | bytes 196616 | tf_op jit(solution)/shard_map/ppermute | solution.py:299
  14.7 3.3 %collective-permute-start.6 = (f32[2,8,1024]{2,1,0:T(8,128)S(1)}, f32[2,8,1024]{2,1,0:T(8,128)S(1)}, u32[]{:S(2)}, u32[]{:S(2)}) collective-permute-start(f32[2,8,1024]{2,1,0:T(8,128)S(1)} %collective-permute-done.3.refs_1_), channel_id=1, source_target_pairs={{0,1},{1,0},{2,3},{3,2},{4,5},{5,4},{6,7},{7,6},{8,9},{9,8},{10,11... | collective-permute-start | bytes 196616 | tf_op jit(solution)/shard_map/ppermute | solution.py:299
  17.5 1.3 %collective-permute-start.7 = (f32[2,8,1024]{2,1,0:T(8,128)S(1)}, f32[2,8,1024]{2,1,0:T(8,128)S(1)}, u32[]{:S(2)}, u32[]{:S(2)}) collective-permute-start(f32[2,8,1024]{2,1,0:T(8,128)S(1)} %collective-permute-done.4.refs_2_), channel_id=1, source_target_pairs={{0,1},{1,0},{2,3},{3,2},{4,5},{5,4},{6,7},{7,6},{8,9},{9,8},{10,11... | collective-permute-start | bytes 196616 | tf_op jit(solution)/shard_map/ppermute | solution.py:299
  20.2 1.2 %collective-permute-start.8 = (f32[8,512]{1,0:T(8,128)S(1)}, f32[8,512]{1,0:T(8,128)S(1)}, u32[]{:S(2)}, u32[]{:S(2)}) collective-permute-start(f32[8,512]{1,0:T(8,128)S(1)} %get-tuple-element.19), channel_id=1, source_target_pairs={{0,1},{1,0},{2,3},{3,2},{4,5},{5,4},{6,7},{7,6},{8,9},{9,8},{10,11... | collective-permute-start | bytes 49160 | tf_op jit(solution)/shard_map/ppermute | solution.py:299
  21.4 6.1 %collective-permute-start.10 = (f32[8,512]{1,0:T(8,128)S(1)}, f32[8,512]{1,0:T(8,128)S(1)}, u32[]{:S(2)}, u32[]{:S(2)}) collective-permute-start(f32[8,512]{1,0:T(8,128)S(1)} %add.7.own_ref), channel_id=1, source_target_pairs={{0,2},{4,6},{8,10},{12,14},{1,15},{3,13},{5,11},{7,9},{2,0},{6,4},... | collective-permute-start | bytes 49160 | tf_op jit(solution)/shard_map/ppermute | solution.py:299
  22.1 5.5 %collective-permute-start.11 = (f32[8,512]{1,0:T(8,128)S(1)}, f32[8,512]{1,0:T(8,128)S(1)}, u32[]{:S(2)}, u32[]{:S(2)}) collective-permute-start(f32[8,512]{1,0:T(8,128)S(1)} %add.7.own_ref), channel_id=1, source_target_pairs={{0,10},{2,8},{4,14},{6,12},{1,9},{3,11},{5,13},{7,15},{10,0},{8,2}... | collective-permute-start | bytes 49160 | tf_op jit(solution)/shard_map/ppermute | solution.py:299
  25.0 3.7 %collective-permute-start.12 = (f32[8,512]{1,0:T(8,128)S(1)}, f32[8,512]{1,0:T(8,128)S(1)}, u32[]{:S(2)}, u32[]{:S(2)}) collective-permute-start(f32[8,512]{1,0:T(8,128)S(1)} %add.7.own_ref), channel_id=1, source_target_pairs={{0,4},{2,6},{8,12},{10,14},{1,13},{3,15},{5,9},{7,11},{4,0},{6,2},... | collective-permute-start | bytes 49160 | tf_op jit(solution)/shard_map/ppermute | solution.py:299
  26.0 4.1 %collective-permute-start.9 = (f32[8,512]{1,0:T(8,128)S(1)}, f32[8,512]{1,0:T(8,128)S(1)}, u32[]{:S(2)}, u32[]{:S(2)}) collective-permute-start(f32[8,512]{1,0:T(8,128)S(1)} %add.7.own_ref), channel_id=1, source_target_pairs={{0,7},{2,5},{8,15},{10,13},{1,6},{3,4},{9,14},{11,12},{7,0},{5,2},... | collective-permute-start | bytes 49160 | tf_op jit(solution)/shard_map/ppermute | solution.py:299
  27.5 2.6 %collective-permute-start.13 = (f32[8,512]{1,0:T(8,128)S(1)}, f32[8,512]{1,0:T(8,128)S(1)}, u32[]{:S(2)}, u32[]{:S(2)}) collective-permute-start(f32[8,512]{1,0:T(8,128)S(1)} %collective-permute-done.10.refs_0_), channel_id=1, source_target_pairs={{0,1},{1,0},{2,3},{3,2},{4,5},{5,4},{6,7},{7,6},{8,9},{9,8},{10,11... | collective-permute-start | bytes 49160 | tf_op jit(solution)/shard_map/ppermute | solution.py:299
  27.6 2.5 %collective-permute-start.14 = (f32[8,512]{1,0:T(8,128)S(1)}, f32[8,512]{1,0:T(8,128)S(1)}, u32[]{:S(2)}, u32[]{:S(2)}) collective-permute-start(f32[8,512]{1,0:T(8,128)S(1)} %collective-permute-done.11.refs_1_), channel_id=1, source_target_pairs={{0,1},{1,0},{2,3},{3,2},{4,5},{5,4},{6,7},{7,6},{8,9},{9,8},{10,11... | collective-permute-start | bytes 49160 | tf_op jit(solution)/shard_map/ppermute | solution.py:299
  28.7 1.4 %collective-permute-start.15 = (f32[8,512]{1,0:T(8,128)S(1)}, f32[8,512]{1,0:T(8,128)S(1)}, u32[]{:S(2)}, u32[]{:S(2)}) collective-permute-start(f32[8,512]{1,0:T(8,128)S(1)} %collective-permute-done.12.refs_2_), channel_id=1, source_target_pairs={{0,1},{1,0},{2,3},{3,2},{4,5},{5,4},{6,7},{7,6},{8,9},{9,8},{10,11... | collective-permute-start | bytes 49160 | tf_op jit(solution)/shard_map/ppermute | solution.py:299

commit v17 on v14

--- a/solution.py
+++ b/solution.py
@@ -158,9 +158,12 @@
     return mine
 
 
-def reflect_body(scale, mine_ref, other_ref, high_ref, low_ref, left_ref, right_ref):
+def reflect_body(scale, kept_ref, given_ref, high_ref, low_ref, left_ref, right_ref):
     mats, rows, cols = high_ref.shape
-    left = orthogonal(mine_ref[...] * scale, other_ref[...] * scale)
+    idle = lax.axis_index("tensor") == 0
+    mine = jnp.where(idle, given_ref[1], kept_ref[0]) * scale
+    other = jnp.where(idle, given_ref[0], kept_ref[1]) * scale
+    left = orthogonal(mine, other)
     left_ref[...] = left
     weights = jnp.concatenate(halves(left), axis=0).astype(BF16)
     right = jnp.zeros((mats * RANK, cols), F32)
@@ -171,7 +174,7 @@
     right_ref[...] = right
 
 
-def reflect(mine, other, high, low, scale):
+def reflect(kept, given, high, low, scale):
     mats, rows, cols = high.shape
     return pl.pallas_call(
         functools.partial(reflect_body, scale),
@@ -183,7 +186,7 @@
         out_specs=[pl.BlockSpec(memory_space=pltpu.VMEM)] * 2,
         compiler_params=pltpu.CompilerParams(vmem_limit_bytes=24 * 2**20),
         name="reflect",
-    )(mine, other, pltpu.with_memory_space_constraint(high, pltpu.VMEM), pltpu.with_memory_space_constraint(low, pltpu.VMEM))
+    )(kept, given, pltpu.with_memory_space_constraint(high, pltpu.VMEM), pltpu.with_memory_space_constraint(low, pltpu.VMEM))
 
 
 def turn_body(left_ref, turned_ref):
@@ -294,17 +297,31 @@
     return swap(value, ("dp", "tensor"), pairs)
 
 
-def chips_sum(value, zero):
+def swap_fast(value, mask):
+    groups, count = lax.axis_size("groups"), lax.axis_size("dp")
+    pairs = []
+    for group in range(groups):
+        for at in range(count):
+            place = 2 * (group * count + at)
+            partner = 2 * (group * count + (at ^ mask))
+            idle = 2 * ((group ^ 1) * count + at) if groups % 2 == 0 else partner
+            if place < partner:
+                pairs.append((place + 1, partner + 1))
+            if place < idle:
+                pairs.append((place, idle))
+    return swap(value, ("groups", "dp", "tensor"), pairs)
+
+
+def fast_sum(value):
     count = lax.axis_size("dp")
     last = max(count // 4, 1)
     step = 1
     while step < last:
-        value = value + (zero + swap_chips(value, (step, step)))
-        zero = 0.0
+        value = value + swap_fast(value, step)
         step *= 2
-    terms = [value] + [swap_chips(value, (offset, offset)) for offset in range(last, count, last)]
+    terms = [value] + [swap_fast(value, offset) for offset in range(last, count, last)]
     while len(terms) > 1:
-        terms = [terms[at] + terms[at + 1] for at in range(0, len(terms), 2)]
+        terms = [terms[at + 1] + terms[at] for at in range(0, len(terms), 2)]
     return terms[0]
 
 
@@ -324,8 +341,8 @@
     replicas = lax.axis_size("dp")
     left_part, grads, errors = project(seeds, grads, errors)
     merged, high, low, zero = merge(grads, errors)
-    mine = chips_sum(left_part, zero)
-    left, right_part = reflect(mine, swap_cores(mine), high, low, 1.0 / replicas)
+    kept = fast_sum(jnp.stack([left_part, swap_cores(left_part) + zero], axis=0))
+    left, right_part = reflect(kept, swap_cores(kept), high, low, 1.0 / replicas)
     terms = chips_terms(right_part + swap_cores(right_part))
     return finish(turn(left), merged, *terms, 1.0 / replicas)
 

time: 33.3 us -> 34.4 us (1.033)
  starting transfers between devices: 14.3 us -> 16.5 us
  waiting for transfers between devices: 9.46 us -> 8.24 us
    ppermute x13 -> x14, starting transfers between devices: 14.3 us -> 16.5 us  [swap(): lax.ppermute(value, axes, pairs + [(target, source) for source, target in...]
    ppermute x13 -> x14, waiting for transfers between devices: 9.46 us -> 8.24 us  [swap(): lax.ppermute(value, axes, pairs + [(target, source) for source, target in...]
  transfers between devices with their start and end apart: 13 -> 14, of which waited for: 9 -> 8; matrix products, arithmetic and copies ran while one was open for 0% -> 0% of each run, Pallas kernels for 3% -> 3%
where the time goes in v17:
time: 34.4 us; the launch traced here: 34.2 us
  starting transfers between devices  16.5 us (48%)
  Pallas kernels  8.73 us (25%)
  waiting for transfers between devices  8.24 us (24%)
  between operations  0.71 us (2%)
    ppermute x14, starting transfers between devices, swap(): lax.ppermute(value, axes, pairs + [(target, source) for source, target in...  16.5 us
    ppermute x14, waiting for transfers between devices, swap(): lax.ppermute(value, axes, pairs + [(target, source) for source, target in...  8.24 us
    pallas_call x1, Pallas kernels, project(): pl.pallas_call(project_body, out_shape=(jax.ShapeDtypeStruct((mats * RANK...  3.35 us
    pallas_call x1, Pallas kernels, finish(): pl.pallas_call(functools.partial(finish_body, scale, len(taken)), out_sha...  3.01 us
    pallas_call x1, Pallas kernels, reflect(): pl.pallas_call(functools.partial(reflect_body, scale), out_shape=(jax.Sha...  1.37 us
    pallas_call x1, Pallas kernels, merge(): pl.pallas_call(merge_body, out_shape=(pltpu.VMEM(shape, F32), pltpu.VMEM(...  0.86 us
  transfers between devices with their start and end apart: 14, of which 8 were waited for; matrix products, arithmetic and copies ran while one was open for 0% of the time, Pallas kernels for 3%

profile of v17, /device:TPU:0, one launch (start us, length us, event | category | flops | bytes accessed | tf_op | source)
XLA Modules:
  0.0 34.2 jit_solution(8929871458394853218)
XLA Ops:
  0.6 3.4 %project.1 = (f32[8,1024]{1,0:T(8,128)S(1)}, bf16[2,1024,512]{2,1,0:T(8,128)(2,1)S(1)}, f32[2,1024,512]{2,1,0:T(8,128)S(1)}) custom-call(s32[2]{0:T(128)} %seeds_ref.1, bf16[1,2,1024,512]{3,2,1,0:T(8,128)(2,1)} %grads_ref.1, f32[1,2,1024,512]{3,2,1,0:T(8,128)} %errors_ref.1), custom_call_target="tpu_custom_call" | custom-call | tf_op jit(solution)/shard_map/project/pallas_call | solution.py:81
  4.0 0.5 %collective-permute-start = (f32[8,1024]{1,0:T(8,128)S(1)}, f32[8,1024]{1,0:T(8,128)S(1)}, u32[]{:S(2)}, u32[]{:S(2)}) collective-permute-start(f32[8,1024]{1,0:T(8,128)S(1)} %get-tuple-element.11), channel_id=1, source_target_pairs={{0,1},{1,0},{2,3},{3,2},{4,5},{5,4},{6,7},{7,6},{8,9},{9,8},{10,11... | collective-permute-start | bytes 98312 | tf_op jit(solution)/shard_map/ppermute | solution.py:283
  4.5 0.9 %merge.1 = (f32[2,1024,512]{2,1,0:T(8,128)S(1)}, bf16[2,1024,512]{2,1,0:T(8,128)(2,1)S(1)}, bf16[2,1024,512]{2,1,0:T(8,128)(2,1)S(1)}, f32[8,1024]{1,0:T(8,128)S(1)}) custom-call(bf16[2,1024,512]{2,1,0:T(8,128)(2,1)S(1)} %get-tuple-element.12.grads_ref, f32[2,1024,512]{2,1,0:T(8,128)S(1)} %get-tuple-element.13.errors_ref), custom_call_target="tpu_custom_call" | custom-call | flops 3145728 | bytes 14680064 | tf_op jit(solution)/shard_map/merge/pallas_call | solution.py:118
  5.4 0.0 collective-permute-done
  5.4 2.9 %collective-permute-start.1 = (f32[2,8,1024]{2,1,0:T(8,128)S(1)}, f32[2,8,1024]{2,1,0:T(8,128)S(1)}, u32[]{:S(2)}, u32[]{:S(2)}) collective-permute-start(f32[2,8,1024]{2,1,0:T(8,128)S(1)} %pad_maximum_fusion), channel_id=1, source_target_pairs={{1,3},{0,16},{2,18},{5,7},{4,20},{6,22},{9,11},{8,24},{10,26},{13,... | collective-permute-start | bytes 196616 | tf_op jit(solution)/shard_map/ppermute | solution.py:283
  8.3 2.2 %collective-permute-done.1 = f32[2,8,1024]{2,1,0:T(8,128)S(1)} collective-permute-done((f32[2,8,1024]{2,1,0:T(8,128)S(1)}, f32[2,8,1024]{2,1,0:T(8,128)S(1)}, u32[]{:S(2)}, u32[]{:S(2)}) %collective-permute-start.1) | collective-permute-done | bytes 65568 | tf_op jit(solution)/shard_map/ppermute | solution.py:283
  10.5 2.1 %collective-permute-start.2 = (f32[2,8,1024]{2,1,0:T(8,128)S(1)}, f32[2,8,1024]{2,1,0:T(8,128)S(1)}, u32[]{:S(2)}, u32[]{:S(2)}) collective-permute-start(f32[2,8,1024]{2,1,0:T(8,128)S(1)} %fusion), channel_id=1, source_target_pairs={{1,13},{0,16},{3,15},{2,18},{5,9},{4,20},{7,11},{6,22},{8,24},{10,... | collective-permute-start | bytes 196616 | tf_op jit(solution)/shard_map/ppermute | solution.py:283
  12.6 0.1 collective-permute-start.3
  12.7 1.9 %collective-permute-start.4 = (f32[2,8,1024]{2,1,0:T(8,128)S(1)}, f32[2,8,1024]{2,1,0:T(8,128)S(1)}, u32[]{:S(2)}, u32[]{:S(2)}) collective-permute-start(f32[2,8,1024]{2,1,0:T(8,128)S(1)} %fusion), channel_id=1, source_target_pairs={{1,5},{0,16},{3,7},{2,18},{4,20},{6,22},{9,13},{8,24},{11,15},{10,... | collective-permute-start | bytes 196616 | tf_op jit(solution)/shard_map/ppermute | solution.py:283
  14.7 0.2 collective-permute-done.2
  14.9 2.0 %collective-permute-done.3 = f32[2,8,1024]{2,1,0:T(8,128)S(1)} collective-permute-done((f32[2,8,1024]{2,1,0:T(8,128)S(1)}, f32[2,8,1024]{2,1,0:T(8,128)S(1)}, u32[]{:S(2)}, u32[]{:S(2)}) %collective-permute-start.3) | collective-permute-done | bytes 65568 | tf_op jit(solution)/shard_map/ppermute | solution.py:283
  16.9 0.7 %collective-permute-done.4 = f32[2,8,1024]{2,1,0:T(8,128)S(1)} collective-permute-done((f32[2,8,1024]{2,1,0:T(8,128)S(1)}, f32[2,8,1024]{2,1,0:T(8,128)S(1)}, u32[]{:S(2)}, u32[]{:S(2)}) %collective-permute-start.4) | collective-permute-done | bytes 65568 | tf_op jit(solution)/shard_map/ppermute | solution.py:283
  17.6 0.1 collective-permute-start.5
  17.7 1.2 %collective-permute-done.5.given_ref = f32[2,8,1024]{2,1,0:T(8,128)S(1)} collective-permute-done((f32[2,8,1024]{2,1,0:T(8,128)S(1)}, f32[2,8,1024]{2,1,0:T(8,128)S(1)}, u32[]{:S(2)}, u32[]{:S(2)}) %collective-permute-start.5) | collective-permute-done | bytes 65568 | tf_op jit(solution)/shard_map/ppermute | solution.py:283
  18.9 1.4 %reflect.1 = (f32[8,1024]{1,0:T(8,128)S(1)}, f32[8,512]{1,0:T(8,128)S(1)}) custom-call(f32[2,8,1024]{2,1,0:T(8,128)S(1)} %add_add_fusion.kept_ref, f32[2,8,1024]{2,1,0:T(8,128)S(1)} %collective-permute-done.5.given_ref, bf16[2,1024,512]{2,1,0:T(8,128)(2,1)S(1)} %get-tuple-element.15.high_ref, bf16[2,1024,512]{2,1,0:T(8,128)(2,1)S(1)} %get-tuple-element.16.low_ref), custom_call_target="tpu_custom_call" | custom-call | tf_op jit(solution)/shard_map/reflect/pallas_call | solution.py:179
  20.3 0.2 collective-permute-start.6
  20.5 1.0 %collective-permute-done.6 = f32[8,512]{1,0:T(8,128)S(1)} collective-permute-done((f32[8,512]{1,0:T(8,128)S(1)}, f32[8,512]{1,0:T(8,128)S(1)}, u32[]{:S(2)}, u32[]{:S(2)}) %collective-permute-start.6) | collective-permute-done | bytes 16416 | tf_op jit(solution)/shard_map/ppermute | solution.py:283
  21.5 1.5 %collective-permute-start.8 = (f32[8,512]{1,0:T(8,128)S(1)}, f32[8,512]{1,0:T(8,128)S(1)}, u32[]{:S(2)}, u32[]{:S(2)}) collective-permute-start(f32[8,512]{1,0:T(8,128)S(1)} %add.23.own_ref), channel_id=1, source_target_pairs={{0,2},{4,6},{8,10},{12,14},{1,15},{3,13},{5,11},{7,9},{2,0},{6,4},... | collective-permute-start | bytes 49160 | tf_op jit(solution)/shard_map/ppermute | solution.py:283
  23.0 2.5 %collective-permute-start.9 = (f32[8,512]{1,0:T(8,128)S(1)}, f32[8,512]{1,0:T(8,128)S(1)}, u32[]{:S(2)}, u32[]{:S(2)}) collective-permute-start(f32[8,512]{1,0:T(8,128)S(1)} %add.23.own_ref), channel_id=1, source_target_pairs={{0,10},{2,8},{4,14},{6,12},{1,9},{3,11},{5,13},{7,15},{10,0},{8,2}... | collective-permute-start | bytes 49160 | tf_op jit(solution)/shard_map/ppermute | solution.py:283
  25.6 1.6 %collective-permute-start.10 = (f32[8,512]{1,0:T(8,128)S(1)}, f32[8,512]{1,0:T(8,128)S(1)}, u32[]{:S(2)}, u32[]{:S(2)}) collective-permute-start(f32[8,512]{1,0:T(8,128)S(1)} %add.23.own_ref), channel_id=1, source_target_pairs={{0,4},{2,6},{8,12},{10,14},{1,13},{3,15},{5,9},{7,11},{4,0},{6,2},... | collective-permute-start | bytes 49160 | tf_op jit(solution)/shard_map/ppermute | solution.py:283
  27.1 1.3 %collective-permute-start.7 = (f32[8,512]{1,0:T(8,128)S(1)}, f32[8,512]{1,0:T(8,128)S(1)}, u32[]{:S(2)}, u32[]{:S(2)}) collective-permute-start(f32[8,512]{1,0:T(8,128)S(1)} %add.23.own_ref), channel_id=1, source_target_pairs={{0,7},{2,5},{8,15},{10,13},{1,6},{3,4},{9,14},{11,12},{7,0},{5,2},... | collective-permute-start | bytes 49160 | tf_op jit(solution)/shard_map/ppermute | solution.py:283
  28.4 0.0 collective-permute-done.8.refs_0_
  28.4 0.2 collective-permute-start.11
  28.7 0.1 collective-permute-done.9.refs_1_
  28.7 0.7 %collective-permute-start.12 = (f32[8,512]{1,0:T(8,128)S(1)}, f32[8,512]{1,0:T(8,128)S(1)}, u32[]{:S(2)}, u32[]{:S(2)}) collective-permute-start(f32[8,512]{1,0:T(8,128)S(1)} %collective-permute-done.9.refs_1_), channel_id=1, source_target_pairs={{0,1},{1,0},{2,3},{3,2},{4,5},{5,4},{6,7},{7,6},{8,9},{9,8},{10,11... | collective-permute-start | bytes 49160 | tf_op jit(solution)/shard_map/ppermute | solution.py:283
  29.4 0.0 collective-permute-done.10.refs_2_
  29.4 0.9 %collective-permute-start.13 = (f32[8,512]{1,0:T(8,128)S(1)}, f32[8,512]{1,0:T(8,128)S(1)}, u32[]{:S(2)}, u32[]{:S(2)}) collective-permute-start(f32[8,512]{1,0:T(8,128)S(1)} %collective-permute-done.10.refs_2_), channel_id=1, source_target_pairs={{0,1},{1,0},{2,3},{3,2},{4,5},{5,4},{6,7},{7,6},{8,9},{9,8},{10,11... | collective-permute-start | bytes 49160 | tf_op jit(solution)/shard_map/ppermute | solution.py:283
  30.3 0.1 turn.1.left_ref
  30.5 0.7 %collective-permute-done.7.both_ref = f32[8,512]{1,0:T(8,128)S(1)} collective-permute-done((f32[8,512]{1,0:T(8,128)S(1)}, f32[8,512]{1,0:T(8,128)S(1)}, u32[]{:S(2)}, u32[]{:S(2)}) %collective-permute-start.7) | collective-permute-done | bytes 16416 | tf_op jit(solution)/shard_map/ppermute | solution.py:283
  31.2 0.0 collective-permute-done.11.refs_3_
  31.2 0.0 collective-permute-done.12.refs_4_
  31.2 3.0 %finish.1 = (bf16[2,1024,512]{2,1,0:T(8,128)(2,1)}, f32[1,2,1024,512]{3,2,1,0:T(8,128)}) custom-call(bf16[1024,32]{1,0:T(8,128)(2,1)S(1)} %turn.1.left_ref, f32[2,1024,512]{2,1,0:T(8,128)S(1)} %get-tuple-element.18.merged_ref, f32[8,512]{1,0:T(8,128)S(1)} %add.23.own_ref, f32[8,512]{1,0:T(8,128)S(1)} %collective-permute-done.7.both_ref, ...), custom_call_target="tpu_custom_call" | custom-call | tf_op jit(solution)/shard_map/finish/pallas_call | solution.py:257
  (6 shorter events, 0.1 us)
Async XLA Ops:
  4.0 1.4 %collective-permute-start = (f32[8,1024]{1,0:T(8,128)S(1)}, f32[8,1024]{1,0:T(8,128)S(1)}, u32[]{:S(2)}, u32[]{:S(2)}) collective-permute-start(f32[8,1024]{1,0:T(8,128)S(1)} %get-tuple-element.11), channel_id=1, source_target_pairs={{0,1},{1,0},{2,3},{3,2},{4,5},{5,4},{6,7},{7,6},{8,9},{9,8},{10,11... | collective-permute-start | bytes 98312 | tf_op jit(solution)/shard_map/ppermute | solution.py:283
  5.4 5.1 %collective-permute-start.1 = (f32[2,8,1024]{2,1,0:T(8,128)S(1)}, f32[2,8,1024]{2,1,0:T(8,128)S(1)}, u32[]{:S(2)}, u32[]{:S(2)}) collective-permute-start(f32[2,8,1024]{2,1,0:T(8,128)S(1)} %pad_maximum_fusion), channel_id=1, source_target_pairs={{1,3},{0,16},{2,18},{5,7},{4,20},{6,22},{9,11},{8,24},{10,26},{13,... | collective-permute-start | bytes 196616 | tf_op jit(solution)/shard_map/ppermute | solution.py:283
  10.5 4.3 %collective-permute-start.2 = (f32[2,8,1024]{2,1,0:T(8,128)S(1)}, f32[2,8,1024]{2,1,0:T(8,128)S(1)}, u32[]{:S(2)}, u32[]{:S(2)}) collective-permute-start(f32[2,8,1024]{2,1,0:T(8,128)S(1)} %fusion), channel_id=1, source_target_pairs={{1,13},{0,16},{3,15},{2,18},{5,9},{4,20},{7,11},{6,22},{8,24},{10,... | collective-permute-start | bytes 196616 | tf_op jit(solution)/shard_map/ppermute | solution.py:283
  12.6 4.3 %collective-permute-start.3 = (f32[2,8,1024]{2,1,0:T(8,128)S(1)}, f32[2,8,1024]{2,1,0:T(8,128)S(1)}, u32[]{:S(2)}, u32[]{:S(2)}) collective-permute-start(f32[2,8,1024]{2,1,0:T(8,128)S(1)} %fusion), channel_id=1, source_target_pairs={{1,9},{0,16},{3,11},{2,18},{5,13},{4,20},{7,15},{6,22},{8,24},{10,... | collective-permute-start | bytes 196616 | tf_op jit(solution)/shard_map/ppermute | solution.py:283
  12.7 4.9 %collective-permute-start.4 = (f32[2,8,1024]{2,1,0:T(8,128)S(1)}, f32[2,8,1024]{2,1,0:T(8,128)S(1)}, u32[]{:S(2)}, u32[]{:S(2)}) collective-permute-start(f32[2,8,1024]{2,1,0:T(8,128)S(1)} %fusion), channel_id=1, source_target_pairs={{1,5},{0,16},{3,7},{2,18},{4,20},{6,22},{9,13},{8,24},{11,15},{10,... | collective-permute-start | bytes 196616 | tf_op jit(solution)/shard_map/ppermute | solution.py:283
  17.6 1.3 %collective-permute-start.5 = (f32[2,8,1024]{2,1,0:T(8,128)S(1)}, f32[2,8,1024]{2,1,0:T(8,128)S(1)}, u32[]{:S(2)}, u32[]{:S(2)}) collective-permute-start(f32[2,8,1024]{2,1,0:T(8,128)S(1)} %add_add_fusion.kept_ref), channel_id=1, source_target_pairs={{0,1},{1,0},{2,3},{3,2},{4,5},{5,4},{6,7},{7,6},{8,9},{9,8},{10,11... | collective-permute-start | bytes 196616 | tf_op jit(solution)/shard_map/ppermute | solution.py:283
  20.3 1.2 %collective-permute-start.6 = (f32[8,512]{1,0:T(8,128)S(1)}, f32[8,512]{1,0:T(8,128)S(1)}, u32[]{:S(2)}, u32[]{:S(2)}) collective-permute-start(f32[8,512]{1,0:T(8,128)S(1)} %get-tuple-element.19), channel_id=1, source_target_pairs={{0,1},{1,0},{2,3},{3,2},{4,5},{5,4},{6,7},{7,6},{8,9},{9,8},{10,11... | collective-permute-start | bytes 49160 | tf_op jit(solution)/shard_map/ppermute | solution.py:283
  21.5 6.9 %collective-permute-start.8 = (f32[8,512]{1,0:T(8,128)S(1)}, f32[8,512]{1,0:T(8,128)S(1)}, u32[]{:S(2)}, u32[]{:S(2)}) collective-permute-start(f32[8,512]{1,0:T(8,128)S(1)} %add.23.own_ref), channel_id=1, source_target_pairs={{0,2},{4,6},{8,10},{12,14},{1,15},{3,13},{5,11},{7,9},{2,0},{6,4},... | collective-permute-start | bytes 49160 | tf_op jit(solution)/shard_map/ppermute | solution.py:283
  23.0 5.7 %collective-permute-start.9 = (f32[8,512]{1,0:T(8,128)S(1)}, f32[8,512]{1,0:T(8,128)S(1)}, u32[]{:S(2)}, u32[]{:S(2)}) collective-permute-start(f32[8,512]{1,0:T(8,128)S(1)} %add.23.own_ref), channel_id=1, source_target_pairs={{0,10},{2,8},{4,14},{6,12},{1,9},{3,11},{5,13},{7,15},{10,0},{8,2}... | collective-permute-start | bytes 49160 | tf_op jit(solution)/shard_map/ppermute | solution.py:283
  25.6 3.9 %collective-permute-start.10 = (f32[8,512]{1,0:T(8,128)S(1)}, f32[8,512]{1,0:T(8,128)S(1)}, u32[]{:S(2)}, u32[]{:S(2)}) collective-permute-start(f32[8,512]{1,0:T(8,128)S(1)} %add.23.own_ref), channel_id=1, source_target_pairs={{0,4},{2,6},{8,12},{10,14},{1,13},{3,15},{5,9},{7,11},{4,0},{6,2},... | collective-permute-start | bytes 49160 | tf_op jit(solution)/shard_map/ppermute | solution.py:283
  27.1 4.1 %collective-permute-start.7 = (f32[8,512]{1,0:T(8,128)S(1)}, f32[8,512]{1,0:T(8,128)S(1)}, u32[]{:S(2)}, u32[]{:S(2)}) collective-permute-start(f32[8,512]{1,0:T(8,128)S(1)} %add.23.own_ref), channel_id=1, source_target_pairs={{0,7},{2,5},{8,15},{10,13},{1,6},{3,4},{9,14},{11,12},{7,0},{5,2},... | collective-permute-start | bytes 49160 | tf_op jit(solution)/shard_map/ppermute | solution.py:283
  28.4 2.8 %collective-permute-start.11 = (f32[8,512]{1,0:T(8,128)S(1)}, f32[8,512]{1,0:T(8,128)S(1)}, u32[]{:S(2)}, u32[]{:S(2)}) collective-permute-start(f32[8,512]{1,0:T(8,128)S(1)} %collective-permute-done.8.refs_0_), channel_id=1, source_target_pairs={{0,1},{1,0},{2,3},{3,2},{4,5},{5,4},{6,7},{7,6},{8,9},{9,8},{10,11... | collective-permute-start | bytes 49160 | tf_op jit(solution)/shard_map/ppermute | solution.py:283
  28.7 2.5 %collective-permute-start.12 = (f32[8,512]{1,0:T(8,128)S(1)}, f32[8,512]{1,0:T(8,128)S(1)}, u32[]{:S(2)}, u32[]{:S(2)}) collective-permute-start(f32[8,512]{1,0:T(8,128)S(1)} %collective-permute-done.9.refs_1_), channel_id=1, source_target_pairs={{0,1},{1,0},{2,3},{3,2},{4,5},{5,4},{6,7},{7,6},{8,9},{9,8},{10,11... | collective-permute-start | bytes 49160 | tf_op jit(solution)/shard_map/ppermute | solution.py:283
  29.4 1.8 %collective-permute-start.13 = (f32[8,512]{1,0:T(8,128)S(1)}, f32[8,512]{1,0:T(8,128)S(1)}, u32[]{:S(2)}, u32[]{:S(2)}) collective-permute-start(f32[8,512]{1,0:T(8,128)S(1)} %collective-permute-done.10.refs_2_), channel_id=1, source_target_pairs={{0,1},{1,0},{2,3},{3,2},{4,5},{5,4},{6,7},{7,6},{8,9},{9,8},{10,11... | collective-permute-start | bytes 49160 | tf_op jit(solution)/shard_map/ppermute | solution.py:283

commit v18 on v14

--- a/solution.py
+++ b/solution.py
@@ -19,6 +19,12 @@
 def halves(value):
     high = value.astype(BF16).astype(F32)
     return high, value - high
+
+
+def thirds(value):
+    high, rest = halves(value)
+    middle, low = halves(rest)
+    return high, middle, low
 
 
 def start_rows(seeds_ref, mats, cols):
@@ -187,15 +193,15 @@
 
 
 def turn_body(left_ref, turned_ref):
-    high, low = halves(left_ref[...])
-    turned_ref[...] = jnp.concatenate([high, low, high, low], axis=0).T.astype(BF16)
+    high, middle, low = thirds(left_ref[...])
+    turned_ref[...] = jnp.concatenate([high, high, high, middle, middle, low], axis=0).T.astype(BF16)
 
 
 def turn(left):
     count, rows = left.shape
     return pl.pallas_call(
         turn_body,
-        out_shape=pltpu.VMEM((rows, 4 * count), BF16),
+        out_shape=pltpu.VMEM((rows, 6 * count), BF16),
         in_specs=[pl.BlockSpec(memory_space=pltpu.VMEM)],
         out_specs=pl.BlockSpec(memory_space=pltpu.VMEM),
         compiler_params=pltpu.CompilerParams(vmem_limit_bytes=16 * 2**20),
@@ -227,8 +233,8 @@
 def finish_rows(right, left_ref, merged_ref, update_ref, errors_ref, ubuf, ebuf, sems):
     mats, rows, cols = merged_ref.shape
     size = rows // CHUNKS
-    high, low = halves(right)
-    right = jnp.concatenate([high, high, low, low], axis=0)
+    high, middle, low = thirds(right)
+    right = jnp.concatenate([high, middle, low, high, middle, high], axis=0)
     row = lax.broadcasted_iota(jnp.int32, right.shape, 0) % (mats * RANK)
     copies = []
     for mat in range(mats):

time: 33.3 us -> 33.3 us (level)
  no operation moved by 1% of the time
where the time goes in v18:
time: 33.3 us; the launch traced here: 33.2 us
  starting transfers between devices  14.3 us (43%)
  waiting for transfers between devices  9.46 us (28%)
  Pallas kernels  8.72 us (26%)
  between operations  0.68 us (2%)
    ppermute x13, starting transfers between devices, swap(): lax.ppermute(value, axes, pairs + [(target, source) for source, target in...  14.3 us
    ppermute x13, waiting for transfers between devices, swap(): lax.ppermute(value, axes, pairs + [(target, source) for source, target in...  9.46 us
    pallas_call x1, Pallas kernels, project(): pl.pallas_call(project_body, out_shape=(jax.ShapeDtypeStruct((mats * RANK...  3.35 us
    pallas_call x1, Pallas kernels, finish(): pl.pallas_call(functools.partial(finish_body, scale, len(taken)), out_sha...  3.01 us
    pallas_call x1, Pallas kernels, reflect(): pl.pallas_call(functools.partial(reflect_body, scale), out_shape=(jax.Sha...  1.36 us
    pallas_call x1, Pallas kernels, merge(): pl.pallas_call(merge_body, out_shape=(pltpu.VMEM(shape, F32), pltpu.VMEM(...  0.86 us
  transfers between devices with their start and end apart: 13, of which 9 were waited for; matrix products, arithmetic and copies ran while one was open for 0% of the time, Pallas kernels for 3%

profile of v18, /device:TPU:0, one launch (start us, length us, event | category | flops | bytes accessed | tf_op | source)
XLA Modules:
  0.0 33.2 jit_solution(14315274434063223600)
XLA Ops:
  0.6 3.4 %project.1 = (f32[8,1024]{1,0:T(8,128)S(1)}, bf16[2,1024,512]{2,1,0:T(8,128)(2,1)S(1)}, f32[2,1024,512]{2,1,0:T(8,128)S(1)}) custom-call(s32[2]{0:T(128)} %seeds_ref.1, bf16[1,2,1024,512]{3,2,1,0:T(8,128)(2,1)} %grads_ref.1, f32[1,2,1024,512]{3,2,1,0:T(8,128)} %errors_ref.1), custom_call_target="tpu_custom_call" | custom-call | tf_op jit(solution)/shard_map/project/pallas_call | solution.py:87
  4.0 3.0 %collective-permute-start = (f32[8,1024]{1,0:T(8,128)S(1)}, f32[8,1024]{1,0:T(8,128)S(1)}, u32[]{:S(2)}, u32[]{:S(2)}) collective-permute-start(f32[8,1024]{1,0:T(8,128)S(1)} %get-tuple-element.11), channel_id=1, source_target_pairs={{0,2},{4,6},{8,10},{12,14},{1,3},{5,7},{9,11},{13,15},{2,0},{6,4},... | collective-permute-start | bytes 98312 | tf_op jit(solution)/shard_map/ppermute | solution.py:286
  7.0 0.9 %merge.1 = (f32[2,1024,512]{2,1,0:T(8,128)S(1)}, bf16[2,1024,512]{2,1,0:T(8,128)(2,1)S(1)}, bf16[2,1024,512]{2,1,0:T(8,128)(2,1)S(1)}, f32[8,1024]{1,0:T(8,128)S(1)}) custom-call(bf16[2,1024,512]{2,1,0:T(8,128)(2,1)S(1)} %get-tuple-element.12.grads_ref, f32[2,1024,512]{2,1,0:T(8,128)S(1)} %get-tuple-element.13.errors_ref), custom_call_target="tpu_custom_call" | custom-call | flops 3145728 | bytes 14680064 | tf_op jit(solution)/shard_map/merge/pallas_call | solution.py:124
  7.9 1.0 %collective-permute-done = f32[8,1024]{1,0:T(8,128)S(1)} collective-permute-done((f32[8,1024]{1,0:T(8,128)S(1)}, f32[8,1024]{1,0:T(8,128)S(1)}, u32[]{:S(2)}, u32[]{:S(2)}) %collective-permute-start) | collective-permute-done | bytes 32800 | tf_op jit(solution)/shard_map/ppermute | solution.py:286
  8.9 3.1 %collective-permute-start.2 = (f32[8,1024]{1,0:T(8,128)S(1)}, f32[8,1024]{1,0:T(8,128)S(1)}, u32[]{:S(2)}, u32[]{:S(2)}) collective-permute-start(f32[8,1024]{1,0:T(8,128)S(1)} %add_add_fusion.1), channel_id=1, source_target_pairs={{0,8},{2,10},{4,12},{6,14},{1,9},{3,11},{5,13},{7,15},{8,0},{10,2}... | collective-permute-start | bytes 98312 | tf_op jit(solution)/shard_map/ppermute | solution.py:286
  12.1 1.3 %collective-permute-start.3 = (f32[8,1024]{1,0:T(8,128)S(1)}, f32[8,1024]{1,0:T(8,128)S(1)}, u32[]{:S(2)}, u32[]{:S(2)}) collective-permute-start(f32[8,1024]{1,0:T(8,128)S(1)} %add_add_fusion.1), channel_id=1, source_target_pairs={{0,12},{2,14},{4,8},{6,10},{1,13},{3,15},{5,9},{7,11},{12,0},{14,2... | collective-permute-start | bytes 98312 | tf_op jit(solution)/shard_map/ppermute | solution.py:286
  13.4 0.2 collective-permute-start.1
  13.7 0.3 collective-permute-done.2
  14.0 3.8 %collective-permute-done.3 = f32[8,1024]{1,0:T(8,128)S(1)} collective-permute-done((f32[8,1024]{1,0:T(8,128)S(1)}, f32[8,1024]{1,0:T(8,128)S(1)}, u32[]{:S(2)}, u32[]{:S(2)}) %collective-permute-start.3) | collective-permute-done | bytes 32800 | tf_op jit(solution)/shard_map/ppermute | solution.py:286
  17.8 0.0 collective-permute-done.1
  17.8 0.1 collective-permute-start.4
  17.9 1.2 %collective-permute-done.4.other_ref = f32[8,1024]{1,0:T(8,128)S(1)} collective-permute-done((f32[8,1024]{1,0:T(8,128)S(1)}, f32[8,1024]{1,0:T(8,128)S(1)}, u32[]{:S(2)}, u32[]{:S(2)}) %collective-permute-start.4) | collective-permute-done | bytes 32800 | tf_op jit(solution)/shard_map/ppermute | solution.py:286
  19.1 1.4 %reflect.1 = (f32[8,1024]{1,0:T(8,128)S(1)}, f32[8,512]{1,0:T(8,128)S(1)}) custom-call(f32[8,1024]{1,0:T(8,128)S(1)} %add_add_fusion.mine_ref, f32[8,1024]{1,0:T(8,128)S(1)} %collective-permute-done.4.other_ref, bf16[2,1024,512]{2,1,0:T(8,128)(2,1)S(1)} %get-tuple-element.15.high_ref, bf16[2,1024,512]{2,1,0:T(8,128)(2,1)S(1)} %get-tuple-element.16.low_ref), custom_call_target="tpu_custom_call" | custom-call | tf_op jit(solution)/shard_map/reflect/pallas_call | solution.py:182
  20.4 0.2 collective-permute-start.5
  20.6 1.0 %collective-permute-done.5 = f32[8,512]{1,0:T(8,128)S(1)} collective-permute-done((f32[8,512]{1,0:T(8,128)S(1)}, f32[8,512]{1,0:T(8,128)S(1)}, u32[]{:S(2)}, u32[]{:S(2)}) %collective-permute-start.5) | collective-permute-done | bytes 16416 | tf_op jit(solution)/shard_map/ppermute | solution.py:286
  21.6 1.5 %collective-permute-start.7 = (f32[8,512]{1,0:T(8,128)S(1)}, f32[8,512]{1,0:T(8,128)S(1)}, u32[]{:S(2)}, u32[]{:S(2)}) collective-permute-start(f32[8,512]{1,0:T(8,128)S(1)} %add.23.own_ref), channel_id=1, source_target_pairs={{0,2},{4,6},{8,10},{12,14},{1,15},{3,13},{5,11},{7,9},{2,0},{6,4},... | collective-permute-start | bytes 49160 | tf_op jit(solution)/shard_map/ppermute | solution.py:286
  23.2 1.2 %collective-permute-start.8 = (f32[8,512]{1,0:T(8,128)S(1)}, f32[8,512]{1,0:T(8,128)S(1)}, u32[]{:S(2)}, u32[]{:S(2)}) collective-permute-start(f32[8,512]{1,0:T(8,128)S(1)} %add.23.own_ref), channel_id=1, source_target_pairs={{0,10},{2,8},{4,14},{6,12},{1,9},{3,11},{5,13},{7,15},{10,0},{8,2}... | collective-permute-start | bytes 49160 | tf_op jit(solution)/shard_map/ppermute | solution.py:286
  24.3 1.3 %collective-permute-start.9 = (f32[8,512]{1,0:T(8,128)S(1)}, f32[8,512]{1,0:T(8,128)S(1)}, u32[]{:S(2)}, u32[]{:S(2)}) collective-permute-start(f32[8,512]{1,0:T(8,128)S(1)} %add.23.own_ref), channel_id=1, source_target_pairs={{0,4},{2,6},{8,12},{10,14},{1,13},{3,15},{5,9},{7,11},{4,0},{6,2},... | collective-permute-start | bytes 49160 | tf_op jit(solution)/shard_map/ppermute | solution.py:286
  25.7 1.3 %collective-permute-start.6 = (f32[8,512]{1,0:T(8,128)S(1)}, f32[8,512]{1,0:T(8,128)S(1)}, u32[]{:S(2)}, u32[]{:S(2)}) collective-permute-start(f32[8,512]{1,0:T(8,128)S(1)} %add.23.own_ref), channel_id=1, source_target_pairs={{0,7},{2,5},{8,15},{10,13},{1,6},{3,4},{9,14},{11,12},{7,0},{5,2},... | collective-permute-start | bytes 49160 | tf_op jit(solution)/shard_map/ppermute | solution.py:286
  27.0 0.0 collective-permute-done.7.refs_0_
  27.0 0.5 %collective-permute-start.10 = (f32[8,512]{1,0:T(8,128)S(1)}, f32[8,512]{1,0:T(8,128)S(1)}, u32[]{:S(2)}, u32[]{:S(2)}) collective-permute-start(f32[8,512]{1,0:T(8,128)S(1)} %collective-permute-done.7.refs_0_), channel_id=1, source_target_pairs={{0,1},{1,0},{2,3},{3,2},{4,5},{5,4},{6,7},{7,6},{8,9},{9,8},{10,11... | collective-permute-start | bytes 49160 | tf_op jit(solution)/shard_map/ppermute | solution.py:286
  27.4 1.4 %collective-permute-done.8.refs_1_ = f32[8,512]{1,0:T(8,128)S(1)} collective-permute-done((f32[8,512]{1,0:T(8,128)S(1)}, f32[8,512]{1,0:T(8,128)S(1)}, u32[]{:S(2)}, u32[]{:S(2)}) %collective-permute-start.8) | collective-permute-done | bytes 16416 | tf_op jit(solution)/shard_map/ppermute | solution.py:286
  28.8 0.0 collective-permute-start.11
  28.8 0.0 collective-permute-done.9.refs_2_
  28.8 0.5 %collective-permute-start.12 = (f32[8,512]{1,0:T(8,128)S(1)}, f32[8,512]{1,0:T(8,128)S(1)}, u32[]{:S(2)}, u32[]{:S(2)}) collective-permute-start(f32[8,512]{1,0:T(8,128)S(1)} %collective-permute-done.9.refs_2_), channel_id=1, source_target_pairs={{0,1},{1,0},{2,3},{3,2},{4,5},{5,4},{6,7},{7,6},{8,9},{9,8},{10,11... | collective-permute-start | bytes 49160 | tf_op jit(solution)/shard_map/ppermute | solution.py:286
  29.3 0.1 turn.1.left_ref
  29.5 0.3 collective-permute-done.6.both_ref
  29.8 0.0 collective-permute-done.10.refs_3_
  29.8 0.2 collective-permute-done.11.refs_4_
  30.0 0.2 collective-permute-done.12.refs_5_
  30.2 3.0 %finish.1 = (bf16[2,1024,512]{2,1,0:T(8,128)(2,1)}, f32[1,2,1024,512]{3,2,1,0:T(8,128)}) custom-call(bf16[1024,48]{1,0:T(8,128)(2,1)S(1)} %turn.1.left_ref, f32[2,1024,512]{2,1,0:T(8,128)S(1)} %get-tuple-element.18.merged_ref, f32[8,512]{1,0:T(8,128)S(1)} %add.23.own_ref, f32[8,512]{1,0:T(8,128)S(1)} %collective-permute-done.6.both_ref, ...), custom_call_target="tpu_custom_call" | custom-call | tf_op jit(solution)/shard_map/finish/pallas_call | solution.py:260
  (3 shorter events, 0.0 us)
Async XLA Ops:
  4.0 4.9 %collective-permute-start = (f32[8,1024]{1,0:T(8,128)S(1)}, f32[8,1024]{1,0:T(8,128)S(1)}, u32[]{:S(2)}, u32[]{:S(2)}) collective-permute-start(f32[8,1024]{1,0:T(8,128)S(1)} %get-tuple-element.11), channel_id=1, source_target_pairs={{0,2},{4,6},{8,10},{12,14},{1,3},{5,7},{9,11},{13,15},{2,0},{6,4},... | collective-permute-start | bytes 98312 | tf_op jit(solution)/shard_map/ppermute | solution.py:286
  8.9 5.0 %collective-permute-start.2 = (f32[8,1024]{1,0:T(8,128)S(1)}, f32[8,1024]{1,0:T(8,128)S(1)}, u32[]{:S(2)}, u32[]{:S(2)}) collective-permute-start(f32[8,1024]{1,0:T(8,128)S(1)} %add_add_fusion.1), channel_id=1, source_target_pairs={{0,8},{2,10},{4,12},{6,14},{1,9},{3,11},{5,13},{7,15},{8,0},{10,2}... | collective-permute-start | bytes 98312 | tf_op jit(solution)/shard_map/ppermute | solution.py:286
  12.1 5.7 %collective-permute-start.3 = (f32[8,1024]{1,0:T(8,128)S(1)}, f32[8,1024]{1,0:T(8,128)S(1)}, u32[]{:S(2)}, u32[]{:S(2)}) collective-permute-start(f32[8,1024]{1,0:T(8,128)S(1)} %add_add_fusion.1), channel_id=1, source_target_pairs={{0,12},{2,14},{4,8},{6,10},{1,13},{3,15},{5,9},{7,11},{12,0},{14,2... | collective-permute-start | bytes 98312 | tf_op jit(solution)/shard_map/ppermute | solution.py:286
  13.4 4.4 %collective-permute-start.1 = (f32[8,1024]{1,0:T(8,128)S(1)}, f32[8,1024]{1,0:T(8,128)S(1)}, u32[]{:S(2)}, u32[]{:S(2)}) collective-permute-start(f32[8,1024]{1,0:T(8,128)S(1)} %add_add_fusion.1), channel_id=1, source_target_pairs={{0,4},{2,6},{8,12},{10,14},{1,5},{3,7},{9,13},{11,15},{4,0},{6,2},... | collective-permute-start | bytes 98312 | tf_op jit(solution)/shard_map/ppermute | solution.py:286
  17.8 1.3 %collective-permute-start.4 = (f32[8,1024]{1,0:T(8,128)S(1)}, f32[8,1024]{1,0:T(8,128)S(1)}, u32[]{:S(2)}, u32[]{:S(2)}) collective-permute-start(f32[8,1024]{1,0:T(8,128)S(1)} %add_add_fusion.mine_ref), channel_id=1, source_target_pairs={{0,1},{1,0},{2,3},{3,2},{4,5},{5,4},{6,7},{7,6},{8,9},{9,8},{10,11... | collective-permute-start | bytes 98312 | tf_op jit(solution)/shard_map/ppermute | solution.py:286
  20.4 1.2 %collective-permute-start.5 = (f32[8,512]{1,0:T(8,128)S(1)}, f32[8,512]{1,0:T(8,128)S(1)}, u32[]{:S(2)}, u32[]{:S(2)}) collective-permute-start(f32[8,512]{1,0:T(8,128)S(1)} %get-tuple-element.19), channel_id=1, source_target_pairs={{0,1},{1,0},{2,3},{3,2},{4,5},{5,4},{6,7},{7,6},{8,9},{9,8},{10,11... | collective-permute-start | bytes 49160 | tf_op jit(solution)/shard_map/ppermute | solution.py:286
  21.6 5.3 %collective-permute-start.7 = (f32[8,512]{1,0:T(8,128)S(1)}, f32[8,512]{1,0:T(8,128)S(1)}, u32[]{:S(2)}, u32[]{:S(2)}) collective-permute-start(f32[8,512]{1,0:T(8,128)S(1)} %add.23.own_ref), channel_id=1, source_target_pairs={{0,2},{4,6},{8,10},{12,14},{1,15},{3,13},{5,11},{7,9},{2,0},{6,4},... | collective-permute-start | bytes 49160 | tf_op jit(solution)/shard_map/ppermute | solution.py:286
  23.2 5.7 %collective-permute-start.8 = (f32[8,512]{1,0:T(8,128)S(1)}, f32[8,512]{1,0:T(8,128)S(1)}, u32[]{:S(2)}, u32[]{:S(2)}) collective-permute-start(f32[8,512]{1,0:T(8,128)S(1)} %add.23.own_ref), channel_id=1, source_target_pairs={{0,10},{2,8},{4,14},{6,12},{1,9},{3,11},{5,13},{7,15},{10,0},{8,2}... | collective-permute-start | bytes 49160 | tf_op jit(solution)/shard_map/ppermute | solution.py:286
  24.3 4.5 %collective-permute-start.9 = (f32[8,512]{1,0:T(8,128)S(1)}, f32[8,512]{1,0:T(8,128)S(1)}, u32[]{:S(2)}, u32[]{:S(2)}) collective-permute-start(f32[8,512]{1,0:T(8,128)S(1)} %add.23.own_ref), channel_id=1, source_target_pairs={{0,4},{2,6},{8,12},{10,14},{1,13},{3,15},{5,9},{7,11},{4,0},{6,2},... | collective-permute-start | bytes 49160 | tf_op jit(solution)/shard_map/ppermute | solution.py:286
  25.7 4.1 %collective-permute-start.6 = (f32[8,512]{1,0:T(8,128)S(1)}, f32[8,512]{1,0:T(8,128)S(1)}, u32[]{:S(2)}, u32[]{:S(2)}) collective-permute-start(f32[8,512]{1,0:T(8,128)S(1)} %add.23.own_ref), channel_id=1, source_target_pairs={{0,7},{2,5},{8,15},{10,13},{1,6},{3,4},{9,14},{11,12},{7,0},{5,2},... | collective-permute-start | bytes 49160 | tf_op jit(solution)/shard_map/ppermute | solution.py:286
  27.0 2.8 %collective-permute-start.10 = (f32[8,512]{1,0:T(8,128)S(1)}, f32[8,512]{1,0:T(8,128)S(1)}, u32[]{:S(2)}, u32[]{:S(2)}) collective-permute-start(f32[8,512]{1,0:T(8,128)S(1)} %collective-permute-done.7.refs_0_), channel_id=1, source_target_pairs={{0,1},{1,0},{2,3},{3,2},{4,5},{5,4},{6,7},{7,6},{8,9},{9,8},{10,11... | collective-permute-start | bytes 49160 | tf_op jit(solution)/shard_map/ppermute | solution.py:286
  28.8 1.2 %collective-permute-start.11 = (f32[8,512]{1,0:T(8,128)S(1)}, f32[8,512]{1,0:T(8,128)S(1)}, u32[]{:S(2)}, u32[]{:S(2)}) collective-permute-start(f32[8,512]{1,0:T(8,128)S(1)} %collective-permute-done.8.refs_1_), channel_id=1, source_target_pairs={{0,1},{1,0},{2,3},{3,2},{4,5},{5,4},{6,7},{7,6},{8,9},{9,8},{10,11... | collective-permute-start | bytes 49160 | tf_op jit(solution)/shard_map/ppermute | solution.py:286
  28.8 1.3 %collective-permute-start.12 = (f32[8,512]{1,0:T(8,128)S(1)}, f32[8,512]{1,0:T(8,128)S(1)}, u32[]{:S(2)}, u32[]{:S(2)}) collective-permute-start(f32[8,512]{1,0:T(8,128)S(1)} %collective-permute-done.9.refs_2_), channel_id=1, source_target_pairs={{0,1},{1,0},{2,3},{3,2},{4,5},{5,4},{6,7},{7,6},{8,9},{9,8},{10,11... | collective-permute-start | bytes 49160 | tf_op jit(solution)/shard_map/ppermute | solution.py:286

commit v19 on v18

--- a/solution.py
+++ b/solution.py
@@ -150,25 +150,28 @@
 def orthogonal(mine, other):
     count = mine.shape[0]
     rank = lax.broadcasted_iota(jnp.int32, (count, 1), 0) % RANK
+    steps = []
     for index in range(RANK):
         current = pick(mine, index, count)
         partner = pick(other, index, count)
         products = jnp.sum(mine * current + other * partner, axis=1, keepdims=True)
         inverse = 1.0 / (jnp.sqrt(pick(products, index, count)) + EPSILON)
-        inner = products * inverse
-        weight = jnp.where(rank > index, inner * inverse, 0.0)
-        here = rank == index
-        mine = jnp.where(here, mine * inverse, mine - weight * current)
+        weight = jnp.where(rank > index, products * inverse * inverse, 0.0)
+        steps.append(jnp.where(rank == index, inverse, weight))
+        mine = row_step(mine, current, steps[-1], index)
         if index < RANK - 1:
-            other = jnp.where(here, other * inverse, other - weight * partner)
-    return mine
-
-
-def reflect_body(scale, mine_ref, other_ref, high_ref, low_ref, left_ref, right_ref):
+            other = row_step(other, partner, steps[-1], index)
+    return mine, steps
+
+
+def row_step(rows, current, step, index):
+    rank = lax.broadcasted_iota(jnp.int32, (rows.shape[0], 1), 0) % RANK
+    return jnp.where(rank == index, rows * step, rows - step * current)
+
+
+def reflect_body(scale, mine_ref, high_ref, low_ref, right_ref):
     mats, rows, cols = high_ref.shape
-    left = orthogonal(mine_ref[...] * scale, other_ref[...] * scale)
-    left_ref[...] = left
-    weights = jnp.concatenate(halves(left), axis=0).astype(BF16)
+    weights = jnp.concatenate(halves(mine_ref[...] * scale), axis=0).astype(BF16)
     right = jnp.zeros((mats * RANK, cols), F32)
     for mat in range(mats):
         product = jnp.dot(weights, high_ref[mat], preferred_element_type=F32)
@@ -177,37 +180,43 @@
     right_ref[...] = right
 
 
-def reflect(mine, other, high, low, scale):
+def reflect(mine, high, low, scale):
     mats, rows, cols = high.shape
     return pl.pallas_call(
         functools.partial(reflect_body, scale),
+        out_shape=jax.ShapeDtypeStruct((mats * RANK, cols), F32),
+        in_specs=[pl.BlockSpec(memory_space=pltpu.VMEM)] * 3,
+        out_specs=pl.BlockSpec(memory_space=pltpu.VMEM),
+        compiler_params=pltpu.CompilerParams(vmem_limit_bytes=16 * 2**20),
+        cost_estimate=pl.CostEstimate(flops=64 * high.size, bytes_accessed=4 * high.size, transcendentals=0),
+        name="reflect",
+    )(mine, pltpu.with_memory_space_constraint(high, pltpu.VMEM), pltpu.with_memory_space_constraint(low, pltpu.VMEM))
+
+
+def turn_body(scale, mine_ref, other_ref, turned_ref, steps_ref, zero_ref):
+    zero_ref[...] = jnp.zeros_like(zero_ref)
+    left, steps = orthogonal(mine_ref[...] * scale, other_ref[...] * scale)
+    for index in range(RANK):
+        steps_ref[index] = jnp.broadcast_to(steps[index], steps_ref.shape[1:])
+    high, middle, low = thirds(left)
+    turned_ref[...] = jnp.concatenate([high, high, high, middle, middle, low], axis=0).T.astype(BF16)
+
+
+def turn(mine, other, cols, scale):
+    count, rows = mine.shape
+    return pl.pallas_call(
+        functools.partial(turn_body, scale),
         out_shape=(
-            jax.ShapeDtypeStruct((mats * RANK, rows), F32),
-            jax.ShapeDtypeStruct((mats * RANK, cols), F32),
+            pltpu.VMEM((rows, 6 * count), BF16),
+            jax.ShapeDtypeStruct((RANK, count, cols), F32),
+            jax.ShapeDtypeStruct((count, cols), F32),
         ),
-        in_specs=[pl.BlockSpec(memory_space=pltpu.VMEM)] * 4,
-        out_specs=[pl.BlockSpec(memory_space=pltpu.VMEM)] * 2,
-        compiler_params=pltpu.CompilerParams(vmem_limit_bytes=24 * 2**20),
-        name="reflect",
-    )(mine, other, pltpu.with_memory_space_constraint(high, pltpu.VMEM), pltpu.with_memory_space_constraint(low, pltpu.VMEM))
-
-
-def turn_body(left_ref, turned_ref):
-    high, middle, low = thirds(left_ref[...])
-    turned_ref[...] = jnp.concatenate([high, high, high, middle, middle, low], axis=0).T.astype(BF16)
-
-
-def turn(left):
-    count, rows = left.shape
-    return pl.pallas_call(
-        turn_body,
-        out_shape=pltpu.VMEM((rows, 6 * count), BF16),
-        in_specs=[pl.BlockSpec(memory_space=pltpu.VMEM)],
-        out_specs=pl.BlockSpec(memory_space=pltpu.VMEM),
-        compiler_params=pltpu.CompilerParams(vmem_limit_bytes=16 * 2**20),
-        cost_estimate=pl.CostEstimate(flops=16 * left.size, bytes_accessed=64 * left.size, transcendentals=0),
+        in_specs=[pl.BlockSpec(memory_space=pltpu.VMEM)] * 2,
+        out_specs=[pl.BlockSpec(memory_space=pltpu.VMEM)] * 3,
+        compiler_params=pltpu.CompilerParams(vmem_limit_bytes=16 * 2**20),
+        cost_estimate=pl.CostEstimate(flops=64 * mine.size, bytes_accessed=128 * mine.size, transcendentals=0),
         name="turn",
-    )(left)
+    )(mine, other)
 
 
 def total(own_ref, both_ref, taken_refs, given_refs):
@@ -223,10 +232,12 @@
     return sums[0]
 
 
-def finish_body(scale, count, left_ref, merged_ref, own_ref, both_ref, *refs):
+def finish_body(scale, count, left_ref, steps_ref, merged_ref, own_ref, both_ref, *refs):
     taken_refs, given_refs = refs[:count], refs[count : 2 * count]
     update_ref, errors_ref, ubuf, ebuf, sems = refs[2 * count :]
     right = total(own_ref, both_ref, taken_refs, given_refs) * scale
+    for index in range(RANK):
+        right = row_step(right, pick(right, index, right.shape[0]), steps_ref[index], index)
     finish_rows(right, left_ref, merged_ref, update_ref, errors_ref, ubuf, ebuf, sems)
 
 
@@ -255,7 +266,7 @@
         copy.wait()
 
 
-def finish(left, merged, own, both, taken, given, scale):
+def finish(left, steps, merged, own, both, taken, given, scale):
     mats, rows, cols = merged.shape
     return pl.pallas_call(
         functools.partial(finish_body, scale, len(taken)),
@@ -263,7 +274,7 @@
             jax.ShapeDtypeStruct((mats, rows, cols), BF16),
             jax.ShapeDtypeStruct((1, mats, rows, cols), F32),
         ),
-        in_specs=[pl.BlockSpec(memory_space=pltpu.VMEM)] * (4 + 2 * len(taken)),
+        in_specs=[pl.BlockSpec(memory_space=pltpu.VMEM)] * (5 + 2 * len(taken)),
         out_specs=[pl.BlockSpec(memory_space=pltpu.HBM)] * 2,
         scratch_shapes=[
             pltpu.VMEM((mats, rows, cols), BF16),
@@ -274,6 +285,7 @@
         name="finish",
     )(
         pltpu.with_memory_space_constraint(left, pltpu.VMEM),
+        steps,
         pltpu.with_memory_space_constraint(merged, pltpu.VMEM),
         own,
         both,
@@ -331,9 +343,11 @@
     left_part, grads, errors = project(seeds, grads, errors)
     merged, high, low, zero = merge(grads, errors)
     mine = chips_sum(left_part, zero)
-    left, right_part = reflect(mine, swap_cores(mine), high, low, 1.0 / replicas)
-    terms = chips_terms(right_part + swap_cores(right_part))
-    return finish(turn(left), merged, *terms, 1.0 / replicas)
+    other = swap_cores(mine)
+    right_part = reflect(mine, high, low, 1.0 / replicas)
+    left, steps, zero = turn(mine, other, right_part.shape[1], 1.0 / replicas)
+    terms = chips_terms(right_part + (zero + swap_cores(right_part)))
+    return finish(left, steps, merged, *terms, 1.0 / replicas)
 
 
 def solution(mesh):

time: 33.3 us -> 31.8 us (0.955)
  waiting for transfers between devices: 9.46 us -> 7.42 us
  starting transfers between devices: 14.3 us -> 14.7 us
    ppermute x13, waiting for transfers between devices: 9.46 us -> 7.42 us  [swap(): lax.ppermute(value, axes, pairs + [(target, source) for source, target in...]
    ppermute x13, starting transfers between devices: 14.3 us -> 14.7 us  [swap(): lax.ppermute(value, axes, pairs + [(target, source) for source, target in...]
  transfers between devices with their start and end apart: 13 -> 13, of which waited for: 9 -> 7; matrix products, arithmetic and copies ran while one was open for 0% -> 0% of each run, Pallas kernels for 3% -> 8%
where the time goes in v19:
time: 31.8 us; the launch traced here: 31.6 us
  starting transfers between devices  14.7 us (46%)
  Pallas kernels  8.77 us (28%)
  waiting for transfers between devices  7.42 us (23%)
  between operations  0.69 us (2%)
    ppermute x13, starting transfers between devices, swap(): lax.ppermute(value, axes, pairs + [(target, source) for source, target in...  14.7 us
    ppermute x13, waiting for transfers between devices, swap(): lax.ppermute(value, axes, pairs + [(target, source) for source, target in...  7.42 us
    pallas_call x1, Pallas kernels, project(): pl.pallas_call(project_body, out_shape=(jax.ShapeDtypeStruct((mats * RANK...  3.35 us
    pallas_call x1, Pallas kernels, finish(): pl.pallas_call(functools.partial(finish_body, scale, len(taken)), out_sha...  3.03 us
    pallas_call x1, Pallas kernels, turn(): pl.pallas_call(functools.partial(turn_body, scale), out_shape=(pltpu.VMEM...  0.88 us
    pallas_call x1, Pallas kernels, merge(): pl.pallas_call(merge_body, out_shape=(pltpu.VMEM(shape, F32), pltpu.VMEM(...  0.86 us
    pallas_call x1, Pallas kernels, reflect(): pl.pallas_call(functools.partial(reflect_body, scale), out_shape=jax.Shap...  0.64 us
  transfers between devices with their start and end apart: 13, of which 7 were waited for; matrix products, arithmetic and copies ran while one was open for 0% of the time, Pallas kernels for 8%

profile of v19, /device:TPU:0, one launch (start us, length us, event | category | flops | bytes accessed | tf_op | source)
XLA Modules:
  0.0 31.6 jit_solution(3595952074105128842)
XLA Ops:
  0.6 3.4 %project.1 = (f32[8,1024]{1,0:T(8,128)S(1)}, bf16[2,1024,512]{2,1,0:T(8,128)(2,1)S(1)}, f32[2,1024,512]{2,1,0:T(8,128)S(1)}) custom-call(s32[2]{0:T(128)} %seeds_ref.1, bf16[1,2,1024,512]{3,2,1,0:T(8,128)(2,1)} %grads_ref.1, f32[1,2,1024,512]{3,2,1,0:T(8,128)} %errors_ref.1), custom_call_target="tpu_custom_call" | custom-call | tf_op jit(solution)/shard_map/project/pallas_call | solution.py:87
  4.0 3.0 %collective-permute-start = (f32[8,1024]{1,0:T(8,128)S(1)}, f32[8,1024]{1,0:T(8,128)S(1)}, u32[]{:S(2)}, u32[]{:S(2)}) collective-permute-start(f32[8,1024]{1,0:T(8,128)S(1)} %get-tuple-element.12), channel_id=1, source_target_pairs={{0,2},{4,6},{8,10},{12,14},{1,3},{5,7},{9,11},{13,15},{2,0},{6,4},... | collective-permute-start | bytes 98312 | tf_op jit(solution)/shard_map/ppermute | solution.py:298
  7.0 0.9 %merge.1 = (f32[2,1024,512]{2,1,0:T(8,128)S(1)}, bf16[2,1024,512]{2,1,0:T(8,128)(2,1)S(1)}, bf16[2,1024,512]{2,1,0:T(8,128)(2,1)S(1)}, f32[8,1024]{1,0:T(8,128)S(1)}) custom-call(bf16[2,1024,512]{2,1,0:T(8,128)(2,1)S(1)} %get-tuple-element.13.grads_ref, f32[2,1024,512]{2,1,0:T(8,128)S(1)} %get-tuple-element.14.errors_ref), custom_call_target="tpu_custom_call" | custom-call | flops 3145728 | bytes 14680064 | tf_op jit(solution)/shard_map/merge/pallas_call | solution.py:124
  7.9 1.0 %collective-permute-done = f32[8,1024]{1,0:T(8,128)S(1)} collective-permute-done((f32[8,1024]{1,0:T(8,128)S(1)}, f32[8,1024]{1,0:T(8,128)S(1)}, u32[]{:S(2)}, u32[]{:S(2)}) %collective-permute-start) | collective-permute-done | bytes 32800 | tf_op jit(solution)/shard_map/ppermute | solution.py:298
  8.9 3.1 %collective-permute-start.2 = (f32[8,1024]{1,0:T(8,128)S(1)}, f32[8,1024]{1,0:T(8,128)S(1)}, u32[]{:S(2)}, u32[]{:S(2)}) collective-permute-start(f32[8,1024]{1,0:T(8,128)S(1)} %add_add_fusion.1), channel_id=1, source_target_pairs={{0,8},{2,10},{4,12},{6,14},{1,9},{3,11},{5,13},{7,15},{8,0},{10,2}... | collective-permute-start | bytes 98312 | tf_op jit(solution)/shard_map/ppermute | solution.py:298
  12.1 1.3 %collective-permute-start.3 = (f32[8,1024]{1,0:T(8,128)S(1)}, f32[8,1024]{1,0:T(8,128)S(1)}, u32[]{:S(2)}, u32[]{:S(2)}) collective-permute-start(f32[8,1024]{1,0:T(8,128)S(1)} %add_add_fusion.1), channel_id=1, source_target_pairs={{0,12},{2,14},{4,8},{6,10},{1,13},{3,15},{5,9},{7,11},{12,0},{14,2... | collective-permute-start | bytes 98312 | tf_op jit(solution)/shard_map/ppermute | solution.py:298
  13.4 0.2 collective-permute-start.1
  13.7 0.3 collective-permute-done.2
  14.0 3.8 %collective-permute-done.3 = f32[8,1024]{1,0:T(8,128)S(1)} collective-permute-done((f32[8,1024]{1,0:T(8,128)S(1)}, f32[8,1024]{1,0:T(8,128)S(1)}, u32[]{:S(2)}, u32[]{:S(2)}) %collective-permute-start.3) | collective-permute-done | bytes 32800 | tf_op jit(solution)/shard_map/ppermute | solution.py:298
  17.8 0.0 collective-permute-done.1
  17.8 0.1 collective-permute-start.4
  17.9 0.6 %reflect.1 = f32[8,512]{1,0:T(8,128)S(1)} custom-call(f32[8,1024]{1,0:T(8,128)S(1)} %add_add_fusion.mine_ref, bf16[2,1024,512]{2,1,0:T(8,128)(2,1)S(1)} %get-tuple-element.19.high_ref, bf16[2,1024,512]{2,1,0:T(8,128)(2,1)S(1)} %get-tuple-element.20.low_ref), custom_call_target="tpu_custom_call" | custom-call | flops 67108864 | bytes 4194304 | tf_op jit(solution)/shard_map/reflect/pallas_call | solution.py:185
  18.5 0.5 %collective-permute-start.5 = (f32[8,512]{1,0:T(8,128)S(1)}, f32[8,512]{1,0:T(8,128)S(1)}, u32[]{:S(2)}, u32[]{:S(2)}) collective-permute-start(f32[8,512]{1,0:T(8,128)S(1)} %reflect.1), channel_id=1, source_target_pairs={{0,1},{1,0},{2,3},{3,2},{4,5},{5,4},{6,7},{7,6},{8,9},{9,8},{10,11... | collective-permute-start | bytes 49160 | tf_op jit(solution)/shard_map/ppermute | solution.py:298
  19.0 0.0 collective-permute-done.4.other_ref
  19.1 0.9 %turn.1 = (bf16[1024,48]{1,0:T(8,128)(2,1)S(1)}, f32[4,8,512]{2,1,0:T(8,128)S(1)}, f32[8,512]{1,0:T(8,128)S(1)}) custom-call(f32[8,1024]{1,0:T(8,128)S(1)} %add_add_fusion.mine_ref, f32[8,1024]{1,0:T(8,128)S(1)} %collective-permute-done.4.other_ref), custom_call_target="tpu_custom_call" | custom-call | flops 524288 | bytes 1048576 | tf_op jit(solution)/shard_map/turn/pallas_call | solution.py:207
  20.0 0.0 collective-permute-done.5
  20.0 1.6 %collective-permute-start.7 = (f32[8,512]{1,0:T(8,128)S(1)}, f32[8,512]{1,0:T(8,128)S(1)}, u32[]{:S(2)}, u32[]{:S(2)}) collective-permute-start(f32[8,512]{1,0:T(8,128)S(1)} %add_add_fusion.2.own_ref), channel_id=1, source_target_pairs={{0,2},{4,6},{8,10},{12,14},{1,15},{3,13},{5,11},{7,9},{2,0},{6,4},... | collective-permute-start | bytes 49160 | tf_op jit(solution)/shard_map/ppermute | solution.py:298
  21.6 1.2 %collective-permute-start.8 = (f32[8,512]{1,0:T(8,128)S(1)}, f32[8,512]{1,0:T(8,128)S(1)}, u32[]{:S(2)}, u32[]{:S(2)}) collective-permute-start(f32[8,512]{1,0:T(8,128)S(1)} %add_add_fusion.2.own_ref), channel_id=1, source_target_pairs={{0,10},{2,8},{4,14},{6,12},{1,9},{3,11},{5,13},{7,15},{10,0},{8,2}... | collective-permute-start | bytes 49160 | tf_op jit(solution)/shard_map/ppermute | solution.py:298
  22.8 1.3 %collective-permute-start.9 = (f32[8,512]{1,0:T(8,128)S(1)}, f32[8,512]{1,0:T(8,128)S(1)}, u32[]{:S(2)}, u32[]{:S(2)}) collective-permute-start(f32[8,512]{1,0:T(8,128)S(1)} %add_add_fusion.2.own_ref), channel_id=1, source_target_pairs={{0,4},{2,6},{8,12},{10,14},{1,13},{3,15},{5,9},{7,11},{4,0},{6,2},... | collective-permute-start | bytes 49160 | tf_op jit(solution)/shard_map/ppermute | solution.py:298
  24.1 1.3 %collective-permute-start.6 = (f32[8,512]{1,0:T(8,128)S(1)}, f32[8,512]{1,0:T(8,128)S(1)}, u32[]{:S(2)}, u32[]{:S(2)}) collective-permute-start(f32[8,512]{1,0:T(8,128)S(1)} %add_add_fusion.2.own_ref), channel_id=1, source_target_pairs={{0,7},{2,5},{8,15},{10,13},{1,6},{3,4},{9,14},{11,12},{7,0},{5,2},... | collective-permute-start | bytes 49160 | tf_op jit(solution)/shard_map/ppermute | solution.py:298
  25.4 0.0 collective-permute-done.7.refs_0_
  25.4 0.4 %collective-permute-start.10 = (f32[8,512]{1,0:T(8,128)S(1)}, f32[8,512]{1,0:T(8,128)S(1)}, u32[]{:S(2)}, u32[]{:S(2)}) collective-permute-start(f32[8,512]{1,0:T(8,128)S(1)} %collective-permute-done.7.refs_0_), channel_id=1, source_target_pairs={{0,1},{1,0},{2,3},{3,2},{4,5},{5,4},{6,7},{7,6},{8,9},{9,8},{10,11... | collective-permute-start | bytes 49160 | tf_op jit(solution)/shard_map/ppermute | solution.py:298
  25.9 1.4 %collective-permute-done.8.refs_1_ = f32[8,512]{1,0:T(8,128)S(1)} collective-permute-done((f32[8,512]{1,0:T(8,128)S(1)}, f32[8,512]{1,0:T(8,128)S(1)}, u32[]{:S(2)}, u32[]{:S(2)}) %collective-permute-start.8) | collective-permute-done | bytes 16416 | tf_op jit(solution)/shard_map/ppermute | solution.py:298
  27.2 0.0 collective-permute-start.11
  27.2 0.0 collective-permute-done.9.refs_2_
  27.2 0.5 %collective-permute-start.12 = (f32[8,512]{1,0:T(8,128)S(1)}, f32[8,512]{1,0:T(8,128)S(1)}, u32[]{:S(2)}, u32[]{:S(2)}) collective-permute-start(f32[8,512]{1,0:T(8,128)S(1)} %collective-permute-done.9.refs_2_), channel_id=1, source_target_pairs={{0,1},{1,0},{2,3},{3,2},{4,5},{5,4},{6,7},{7,6},{8,9},{9,8},{10,11... | collective-permute-start | bytes 49160 | tf_op jit(solution)/shard_map/ppermute | solution.py:298
  27.8 0.4 %collective-permute-done.6.both_ref = f32[8,512]{1,0:T(8,128)S(1)} collective-permute-done((f32[8,512]{1,0:T(8,128)S(1)}, f32[8,512]{1,0:T(8,128)S(1)}, u32[]{:S(2)}, u32[]{:S(2)}) %collective-permute-start.6) | collective-permute-done | bytes 16416 | tf_op jit(solution)/shard_map/ppermute | solution.py:298
  28.2 0.0 collective-permute-done.10.refs_3_
  28.2 0.2 collective-permute-done.11.refs_4_
  28.4 0.2 collective-permute-done.12.refs_5_
  28.6 3.0 %finish.1 = (bf16[2,1024,512]{2,1,0:T(8,128)(2,1)}, f32[1,2,1024,512]{3,2,1,0:T(8,128)}) custom-call(bf16[1024,48]{1,0:T(8,128)(2,1)S(1)} %get-tuple-element.16.left_ref, f32[4,8,512]{2,1,0:T(8,128)S(1)} %get-tuple-element.17.steps_ref, f32[2,1024,512]{2,1,0:T(8,128)S(1)} %get-tuple-element.18.merged_ref, f32[8,512]{1,0:T(8,128)S(1)} %add_add_fusion.2.own_ref, ...), custom_call_target="tpu_custom_call" | custom-call | tf_op jit(solution)/shard_map/finish/pallas_call | solution.py:271
  (3 shorter events, 0.0 us)
Async XLA Ops:
  4.0 4.9 %collective-permute-start = (f32[8,1024]{1,0:T(8,128)S(1)}, f32[8,1024]{1,0:T(8,128)S(1)}, u32[]{:S(2)}, u32[]{:S(2)}) collective-permute-start(f32[8,1024]{1,0:T(8,128)S(1)} %get-tuple-element.12), channel_id=1, source_target_pairs={{0,2},{4,6},{8,10},{12,14},{1,3},{5,7},{9,11},{13,15},{2,0},{6,4},... | collective-permute-start | bytes 98312 | tf_op jit(solution)/shard_map/ppermute | solution.py:298
  8.9 5.0 %collective-permute-start.2 = (f32[8,1024]{1,0:T(8,128)S(1)}, f32[8,1024]{1,0:T(8,128)S(1)}, u32[]{:S(2)}, u32[]{:S(2)}) collective-permute-start(f32[8,1024]{1,0:T(8,128)S(1)} %add_add_fusion.1), channel_id=1, source_target_pairs={{0,8},{2,10},{4,12},{6,14},{1,9},{3,11},{5,13},{7,15},{8,0},{10,2}... | collective-permute-start | bytes 98312 | tf_op jit(solution)/shard_map/ppermute | solution.py:298
  12.1 5.7 %collective-permute-start.3 = (f32[8,1024]{1,0:T(8,128)S(1)}, f32[8,1024]{1,0:T(8,128)S(1)}, u32[]{:S(2)}, u32[]{:S(2)}) collective-permute-start(f32[8,1024]{1,0:T(8,128)S(1)} %add_add_fusion.1), channel_id=1, source_target_pairs={{0,12},{2,14},{4,8},{6,10},{1,13},{3,15},{5,9},{7,11},{12,0},{14,2... | collective-permute-start | bytes 98312 | tf_op jit(solution)/shard_map/ppermute | solution.py:298
  13.4 4.4 %collective-permute-start.1 = (f32[8,1024]{1,0:T(8,128)S(1)}, f32[8,1024]{1,0:T(8,128)S(1)}, u32[]{:S(2)}, u32[]{:S(2)}) collective-permute-start(f32[8,1024]{1,0:T(8,128)S(1)} %add_add_fusion.1), channel_id=1, source_target_pairs={{0,4},{2,6},{8,12},{10,14},{1,5},{3,7},{9,13},{11,15},{4,0},{6,2},... | collective-permute-start | bytes 98312 | tf_op jit(solution)/shard_map/ppermute | solution.py:298
  17.8 1.3 %collective-permute-start.4 = (f32[8,1024]{1,0:T(8,128)S(1)}, f32[8,1024]{1,0:T(8,128)S(1)}, u32[]{:S(2)}, u32[]{:S(2)}) collective-permute-start(f32[8,1024]{1,0:T(8,128)S(1)} %add_add_fusion.mine_ref), channel_id=1, source_target_pairs={{0,1},{1,0},{2,3},{3,2},{4,5},{5,4},{6,7},{7,6},{8,9},{9,8},{10,11... | collective-permute-start | bytes 98312 | tf_op jit(solution)/shard_map/ppermute | solution.py:298
  18.5 1.4 %collective-permute-start.5 = (f32[8,512]{1,0:T(8,128)S(1)}, f32[8,512]{1,0:T(8,128)S(1)}, u32[]{:S(2)}, u32[]{:S(2)}) collective-permute-start(f32[8,512]{1,0:T(8,128)S(1)} %reflect.1), channel_id=1, source_target_pairs={{0,1},{1,0},{2,3},{3,2},{4,5},{5,4},{6,7},{7,6},{8,9},{9,8},{10,11... | collective-permute-start | bytes 49160 | tf_op jit(solution)/shard_map/ppermute | solution.py:298
  20.0 5.4 %collective-permute-start.7 = (f32[8,512]{1,0:T(8,128)S(1)}, f32[8,512]{1,0:T(8,128)S(1)}, u32[]{:S(2)}, u32[]{:S(2)}) collective-permute-start(f32[8,512]{1,0:T(8,128)S(1)} %add_add_fusion.2.own_ref), channel_id=1, source_target_pairs={{0,2},{4,6},{8,10},{12,14},{1,15},{3,13},{5,11},{7,9},{2,0},{6,4},... | collective-permute-start | bytes 49160 | tf_op jit(solution)/shard_map/ppermute | solution.py:298
  21.6 5.7 %collective-permute-start.8 = (f32[8,512]{1,0:T(8,128)S(1)}, f32[8,512]{1,0:T(8,128)S(1)}, u32[]{:S(2)}, u32[]{:S(2)}) collective-permute-start(f32[8,512]{1,0:T(8,128)S(1)} %add_add_fusion.2.own_ref), channel_id=1, source_target_pairs={{0,10},{2,8},{4,14},{6,12},{1,9},{3,11},{5,13},{7,15},{10,0},{8,2}... | collective-permute-start | bytes 49160 | tf_op jit(solution)/shard_map/ppermute | solution.py:298
  22.8 4.5 %collective-permute-start.9 = (f32[8,512]{1,0:T(8,128)S(1)}, f32[8,512]{1,0:T(8,128)S(1)}, u32[]{:S(2)}, u32[]{:S(2)}) collective-permute-start(f32[8,512]{1,0:T(8,128)S(1)} %add_add_fusion.2.own_ref), channel_id=1, source_target_pairs={{0,4},{2,6},{8,12},{10,14},{1,13},{3,15},{5,9},{7,11},{4,0},{6,2},... | collective-permute-start | bytes 49160 | tf_op jit(solution)/shard_map/ppermute | solution.py:298
  24.1 4.1 %collective-permute-start.6 = (f32[8,512]{1,0:T(8,128)S(1)}, f32[8,512]{1,0:T(8,128)S(1)}, u32[]{:S(2)}, u32[]{:S(2)}) collective-permute-start(f32[8,512]{1,0:T(8,128)S(1)} %add_add_fusion.2.own_ref), channel_id=1, source_target_pairs={{0,7},{2,5},{8,15},{10,13},{1,6},{3,4},{9,14},{11,12},{7,0},{5,2},... | collective-permute-start | bytes 49160 | tf_op jit(solution)/shard_map/ppermute | solution.py:298
  25.4 2.8 %collective-permute-start.10 = (f32[8,512]{1,0:T(8,128)S(1)}, f32[8,512]{1,0:T(8,128)S(1)}, u32[]{:S(2)}, u32[]{:S(2)}) collective-permute-start(f32[8,512]{1,0:T(8,128)S(1)} %collective-permute-done.7.refs_0_), channel_id=1, source_target_pairs={{0,1},{1,0},{2,3},{3,2},{4,5},{5,4},{6,7},{7,6},{8,9},{9,8},{10,11... | collective-permute-start | bytes 49160 | tf_op jit(solution)/shard_map/ppermute | solution.py:298
  27.2 1.2 %collective-permute-start.11 = (f32[8,512]{1,0:T(8,128)S(1)}, f32[8,512]{1,0:T(8,128)S(1)}, u32[]{:S(2)}, u32[]{:S(2)}) collective-permute-start(f32[8,512]{1,0:T(8,128)S(1)} %collective-permute-done.8.refs_1_), channel_id=1, source_target_pairs={{0,1},{1,0},{2,3},{3,2},{4,5},{5,4},{6,7},{7,6},{8,9},{9,8},{10,11... | collective-permute-start | bytes 49160 | tf_op jit(solution)/shard_map/ppermute | solution.py:298
  27.2 1.3 %collective-permute-start.12 = (f32[8,512]{1,0:T(8,128)S(1)}, f32[8,512]{1,0:T(8,128)S(1)}, u32[]{:S(2)}, u32[]{:S(2)}) collective-permute-start(f32[8,512]{1,0:T(8,128)S(1)} %collective-permute-done.9.refs_2_), channel_id=1, source_target_pairs={{0,1},{1,0},{2,3},{3,2},{4,5},{5,4},{6,7},{7,6},{8,9},{9,8},{10,11... | collective-permute-start | bytes 49160 | tf_op jit(solution)/shard_map/ppermute | solution.py:298

commit v20 on v19

--- a/solution.py
+++ b/solution.py
@@ -243,15 +243,17 @@
 
 def finish_rows(right, left_ref, merged_ref, update_ref, errors_ref, ubuf, ebuf, sems):
     mats, rows, cols = merged_ref.shape
-    size = rows // CHUNKS
     high, middle, low = thirds(right)
     right = jnp.concatenate([high, middle, low, high, middle, high], axis=0)
     row = lax.broadcasted_iota(jnp.int32, right.shape, 0) % (mats * RANK)
     copies = []
     for mat in range(mats):
         weights = jnp.where(row // RANK == mat, right, 0.0).astype(BF16)
-        for chunk in range(CHUNKS):
-            at = pl.ds(chunk * size, size)
+        parts = (8, 8, 4, 2) if mat == 0 else (2, 2)
+        start = 0
+        for chunk, part in enumerate(parts):
+            at = pl.ds(start, rows // part)
+            start += rows // part
             slot = mat * CHUNKS + chunk
             approx = jnp.dot(left_ref[at], weights, preferred_element_type=F32)
             ubuf[mat, at] = approx.astype(BF16)

time: 31.8 us -> 31.8 us (level)
  no operation moved by 1% of the time
where the time goes in v20:
time: 31.8 us; the launch traced here: 31.6 us
  starting transfers between devices  14.7 us (46%)
  Pallas kernels  8.78 us (28%)
  waiting for transfers between devices  7.42 us (23%)
  between operations  0.69 us (2%)
    ppermute x13, starting transfers between devices, swap(): lax.ppermute(value, axes, pairs + [(target, source) for source, target in...  14.7 us
    ppermute x13, waiting for transfers between devices, swap(): lax.ppermute(value, axes, pairs + [(target, source) for source, target in...  7.42 us
    pallas_call x1, Pallas kernels, project(): pl.pallas_call(project_body, out_shape=(jax.ShapeDtypeStruct((mats * RANK...  3.35 us
    pallas_call x1, Pallas kernels, finish(): pl.pallas_call(functools.partial(finish_body, scale, len(taken)), out_sha...  3.03 us
    pallas_call x1, Pallas kernels, turn(): pl.pallas_call(functools.partial(turn_body, scale), out_shape=(pltpu.VMEM...  0.88 us
    pallas_call x1, Pallas kernels, merge(): pl.pallas_call(merge_body, out_shape=(pltpu.VMEM(shape, F32), pltpu.VMEM(...  0.86 us
    pallas_call x1, Pallas kernels, reflect(): pl.pallas_call(functools.partial(reflect_body, scale), out_shape=jax.Shap...  0.64 us
  transfers between devices with their start and end apart: 13, of which 7 were waited for; matrix products, arithmetic and copies ran while one was open for 0% of the time, Pallas kernels for 8%

profile of v20, /device:TPU:0, one launch (start us, length us, event | category | flops | bytes accessed | tf_op | source)
XLA Modules:
  0.0 31.6 jit_solution(17755415766917709363)
XLA Ops:
  0.6 3.4 %project.1 = (f32[8,1024]{1,0:T(8,128)S(1)}, bf16[2,1024,512]{2,1,0:T(8,128)(2,1)S(1)}, f32[2,1024,512]{2,1,0:T(8,128)S(1)}) custom-call(s32[2]{0:T(128)} %seeds_ref.1, bf16[1,2,1024,512]{3,2,1,0:T(8,128)(2,1)} %grads_ref.1, f32[1,2,1024,512]{3,2,1,0:T(8,128)} %errors_ref.1), custom_call_target="tpu_custom_call" | custom-call | tf_op jit(solution)/shard_map/project/pallas_call | solution.py:87
  4.0 3.0 %collective-permute-start = (f32[8,1024]{1,0:T(8,128)S(1)}, f32[8,1024]{1,0:T(8,128)S(1)}, u32[]{:S(2)}, u32[]{:S(2)}) collective-permute-start(f32[8,1024]{1,0:T(8,128)S(1)} %get-tuple-element.12), channel_id=1, source_target_pairs={{0,2},{4,6},{8,10},{12,14},{1,3},{5,7},{9,11},{13,15},{2,0},{6,4},... | collective-permute-start | bytes 98312 | tf_op jit(solution)/shard_map/ppermute | solution.py:300
  7.0 0.9 %merge.1 = (f32[2,1024,512]{2,1,0:T(8,128)S(1)}, bf16[2,1024,512]{2,1,0:T(8,128)(2,1)S(1)}, bf16[2,1024,512]{2,1,0:T(8,128)(2,1)S(1)}, f32[8,1024]{1,0:T(8,128)S(1)}) custom-call(bf16[2,1024,512]{2,1,0:T(8,128)(2,1)S(1)} %get-tuple-element.13.grads_ref, f32[2,1024,512]{2,1,0:T(8,128)S(1)} %get-tuple-element.14.errors_ref), custom_call_target="tpu_custom_call" | custom-call | flops 3145728 | bytes 14680064 | tf_op jit(solution)/shard_map/merge/pallas_call | solution.py:124
  7.9 1.0 %collective-permute-done = f32[8,1024]{1,0:T(8,128)S(1)} collective-permute-done((f32[8,1024]{1,0:T(8,128)S(1)}, f32[8,1024]{1,0:T(8,128)S(1)}, u32[]{:S(2)}, u32[]{:S(2)}) %collective-permute-start) | collective-permute-done | bytes 32800 | tf_op jit(solution)/shard_map/ppermute | solution.py:300
  8.9 3.1 %collective-permute-start.2 = (f32[8,1024]{1,0:T(8,128)S(1)}, f32[8,1024]{1,0:T(8,128)S(1)}, u32[]{:S(2)}, u32[]{:S(2)}) collective-permute-start(f32[8,1024]{1,0:T(8,128)S(1)} %add_add_fusion.1), channel_id=1, source_target_pairs={{0,8},{2,10},{4,12},{6,14},{1,9},{3,11},{5,13},{7,15},{8,0},{10,2}... | collective-permute-start | bytes 98312 | tf_op jit(solution)/shard_map/ppermute | solution.py:300
  12.1 1.3 %collective-permute-start.3 = (f32[8,1024]{1,0:T(8,128)S(1)}, f32[8,1024]{1,0:T(8,128)S(1)}, u32[]{:S(2)}, u32[]{:S(2)}) collective-permute-start(f32[8,1024]{1,0:T(8,128)S(1)} %add_add_fusion.1), channel_id=1, source_target_pairs={{0,12},{2,14},{4,8},{6,10},{1,13},{3,15},{5,9},{7,11},{12,0},{14,2... | collective-permute-start | bytes 98312 | tf_op jit(solution)/shard_map/ppermute | solution.py:300
  13.4 0.2 collective-permute-start.1
  13.7 0.3 collective-permute-done.2
  14.0 3.8 %collective-permute-done.3 = f32[8,1024]{1,0:T(8,128)S(1)} collective-permute-done((f32[8,1024]{1,0:T(8,128)S(1)}, f32[8,1024]{1,0:T(8,128)S(1)}, u32[]{:S(2)}, u32[]{:S(2)}) %collective-permute-start.3) | collective-permute-done | bytes 32800 | tf_op jit(solution)/shard_map/ppermute | solution.py:300
  17.8 0.0 collective-permute-done.1
  17.8 0.1 collective-permute-start.4
  17.9 0.6 %reflect.1 = f32[8,512]{1,0:T(8,128)S(1)} custom-call(f32[8,1024]{1,0:T(8,128)S(1)} %add_add_fusion.mine_ref, bf16[2,1024,512]{2,1,0:T(8,128)(2,1)S(1)} %get-tuple-element.19.high_ref, bf16[2,1024,512]{2,1,0:T(8,128)(2,1)S(1)} %get-tuple-element.20.low_ref), custom_call_target="tpu_custom_call" | custom-call | flops 67108864 | bytes 4194304 | tf_op jit(solution)/shard_map/reflect/pallas_call | solution.py:185
  18.5 0.5 %collective-permute-start.5 = (f32[8,512]{1,0:T(8,128)S(1)}, f32[8,512]{1,0:T(8,128)S(1)}, u32[]{:S(2)}, u32[]{:S(2)}) collective-permute-start(f32[8,512]{1,0:T(8,128)S(1)} %reflect.1), channel_id=1, source_target_pairs={{0,1},{1,0},{2,3},{3,2},{4,5},{5,4},{6,7},{7,6},{8,9},{9,8},{10,11... | collective-permute-start | bytes 49160 | tf_op jit(solution)/shard_map/ppermute | solution.py:300
  19.0 0.0 collective-permute-done.4.other_ref
  19.1 0.9 %turn.1 = (bf16[1024,48]{1,0:T(8,128)(2,1)S(1)}, f32[4,8,512]{2,1,0:T(8,128)S(1)}, f32[8,512]{1,0:T(8,128)S(1)}) custom-call(f32[8,1024]{1,0:T(8,128)S(1)} %add_add_fusion.mine_ref, f32[8,1024]{1,0:T(8,128)S(1)} %collective-permute-done.4.other_ref), custom_call_target="tpu_custom_call" | custom-call | flops 524288 | bytes 1048576 | tf_op jit(solution)/shard_map/turn/pallas_call | solution.py:207
  20.0 0.0 collective-permute-done.5
  20.0 1.6 %collective-permute-start.7 = (f32[8,512]{1,0:T(8,128)S(1)}, f32[8,512]{1,0:T(8,128)S(1)}, u32[]{:S(2)}, u32[]{:S(2)}) collective-permute-start(f32[8,512]{1,0:T(8,128)S(1)} %add_add_fusion.2.own_ref), channel_id=1, source_target_pairs={{0,2},{4,6},{8,10},{12,14},{1,15},{3,13},{5,11},{7,9},{2,0},{6,4},... | collective-permute-start | bytes 49160 | tf_op jit(solution)/shard_map/ppermute | solution.py:300
  21.6 1.2 %collective-permute-start.8 = (f32[8,512]{1,0:T(8,128)S(1)}, f32[8,512]{1,0:T(8,128)S(1)}, u32[]{:S(2)}, u32[]{:S(2)}) collective-permute-start(f32[8,512]{1,0:T(8,128)S(1)} %add_add_fusion.2.own_ref), channel_id=1, source_target_pairs={{0,10},{2,8},{4,14},{6,12},{1,9},{3,11},{5,13},{7,15},{10,0},{8,2}... | collective-permute-start | bytes 49160 | tf_op jit(solution)/shard_map/ppermute | solution.py:300
  22.8 1.3 %collective-permute-start.9 = (f32[8,512]{1,0:T(8,128)S(1)}, f32[8,512]{1,0:T(8,128)S(1)}, u32[]{:S(2)}, u32[]{:S(2)}) collective-permute-start(f32[8,512]{1,0:T(8,128)S(1)} %add_add_fusion.2.own_ref), channel_id=1, source_target_pairs={{0,4},{2,6},{8,12},{10,14},{1,13},{3,15},{5,9},{7,11},{4,0},{6,2},... | collective-permute-start | bytes 49160 | tf_op jit(solution)/shard_map/ppermute | solution.py:300
  24.1 1.3 %collective-permute-start.6 = (f32[8,512]{1,0:T(8,128)S(1)}, f32[8,512]{1,0:T(8,128)S(1)}, u32[]{:S(2)}, u32[]{:S(2)}) collective-permute-start(f32[8,512]{1,0:T(8,128)S(1)} %add_add_fusion.2.own_ref), channel_id=1, source_target_pairs={{0,7},{2,5},{8,15},{10,13},{1,6},{3,4},{9,14},{11,12},{7,0},{5,2},... | collective-permute-start | bytes 49160 | tf_op jit(solution)/shard_map/ppermute | solution.py:300
  25.4 0.0 collective-permute-done.7.refs_0_
  25.4 0.4 %collective-permute-start.10 = (f32[8,512]{1,0:T(8,128)S(1)}, f32[8,512]{1,0:T(8,128)S(1)}, u32[]{:S(2)}, u32[]{:S(2)}) collective-permute-start(f32[8,512]{1,0:T(8,128)S(1)} %collective-permute-done.7.refs_0_), channel_id=1, source_target_pairs={{0,1},{1,0},{2,3},{3,2},{4,5},{5,4},{6,7},{7,6},{8,9},{9,8},{10,11... | collective-permute-start | bytes 49160 | tf_op jit(solution)/shard_map/ppermute | solution.py:300
  25.9 1.4 %collective-permute-done.8.refs_1_ = f32[8,512]{1,0:T(8,128)S(1)} collective-permute-done((f32[8,512]{1,0:T(8,128)S(1)}, f32[8,512]{1,0:T(8,128)S(1)}, u32[]{:S(2)}, u32[]{:S(2)}) %collective-permute-start.8) | collective-permute-done | bytes 16416 | tf_op jit(solution)/shard_map/ppermute | solution.py:300
  27.2 0.0 collective-permute-start.11
  27.2 0.0 collective-permute-done.9.refs_2_
  27.2 0.5 %collective-permute-start.12 = (f32[8,512]{1,0:T(8,128)S(1)}, f32[8,512]{1,0:T(8,128)S(1)}, u32[]{:S(2)}, u32[]{:S(2)}) collective-permute-start(f32[8,512]{1,0:T(8,128)S(1)} %collective-permute-done.9.refs_2_), channel_id=1, source_target_pairs={{0,1},{1,0},{2,3},{3,2},{4,5},{5,4},{6,7},{7,6},{8,9},{9,8},{10,11... | collective-permute-start | bytes 49160 | tf_op jit(solution)/shard_map/ppermute | solution.py:300
  27.8 0.4 %collective-permute-done.6.both_ref = f32[8,512]{1,0:T(8,128)S(1)} collective-permute-done((f32[8,512]{1,0:T(8,128)S(1)}, f32[8,512]{1,0:T(8,128)S(1)}, u32[]{:S(2)}, u32[]{:S(2)}) %collective-permute-start.6) | collective-permute-done | bytes 16416 | tf_op jit(solution)/shard_map/ppermute | solution.py:300
  28.2 0.0 collective-permute-done.10.refs_3_
  28.2 0.2 collective-permute-done.11.refs_4_
  28.4 0.2 collective-permute-done.12.refs_5_
  28.6 3.0 %finish.1 = (bf16[2,1024,512]{2,1,0:T(8,128)(2,1)}, f32[1,2,1024,512]{3,2,1,0:T(8,128)}) custom-call(bf16[1024,48]{1,0:T(8,128)(2,1)S(1)} %get-tuple-element.16.left_ref, f32[4,8,512]{2,1,0:T(8,128)S(1)} %get-tuple-element.17.steps_ref, f32[2,1024,512]{2,1,0:T(8,128)S(1)} %get-tuple-element.18.merged_ref, f32[8,512]{1,0:T(8,128)S(1)} %add_add_fusion.2.own_ref, ...), custom_call_target="tpu_custom_call" | custom-call | tf_op jit(solution)/shard_map/finish/pallas_call | solution.py:273
  (3 shorter events, 0.0 us)
Async XLA Ops:
  4.0 4.9 %collective-permute-start = (f32[8,1024]{1,0:T(8,128)S(1)}, f32[8,1024]{1,0:T(8,128)S(1)}, u32[]{:S(2)}, u32[]{:S(2)}) collective-permute-start(f32[8,1024]{1,0:T(8,128)S(1)} %get-tuple-element.12), channel_id=1, source_target_pairs={{0,2},{4,6},{8,10},{12,14},{1,3},{5,7},{9,11},{13,15},{2,0},{6,4},... | collective-permute-start | bytes 98312 | tf_op jit(solution)/shard_map/ppermute | solution.py:300
  8.9 5.0 %collective-permute-start.2 = (f32[8,1024]{1,0:T(8,128)S(1)}, f32[8,1024]{1,0:T(8,128)S(1)}, u32[]{:S(2)}, u32[]{:S(2)}) collective-permute-start(f32[8,1024]{1,0:T(8,128)S(1)} %add_add_fusion.1), channel_id=1, source_target_pairs={{0,8},{2,10},{4,12},{6,14},{1,9},{3,11},{5,13},{7,15},{8,0},{10,2}... | collective-permute-start | bytes 98312 | tf_op jit(solution)/shard_map/ppermute | solution.py:300
  12.1 5.7 %collective-permute-start.3 = (f32[8,1024]{1,0:T(8,128)S(1)}, f32[8,1024]{1,0:T(8,128)S(1)}, u32[]{:S(2)}, u32[]{:S(2)}) collective-permute-start(f32[8,1024]{1,0:T(8,128)S(1)} %add_add_fusion.1), channel_id=1, source_target_pairs={{0,12},{2,14},{4,8},{6,10},{1,13},{3,15},{5,9},{7,11},{12,0},{14,2... | collective-permute-start | bytes 98312 | tf_op jit(solution)/shard_map/ppermute | solution.py:300
  13.4 4.4 %collective-permute-start.1 = (f32[8,1024]{1,0:T(8,128)S(1)}, f32[8,1024]{1,0:T(8,128)S(1)}, u32[]{:S(2)}, u32[]{:S(2)}) collective-permute-start(f32[8,1024]{1,0:T(8,128)S(1)} %add_add_fusion.1), channel_id=1, source_target_pairs={{0,4},{2,6},{8,12},{10,14},{1,5},{3,7},{9,13},{11,15},{4,0},{6,2},... | collective-permute-start | bytes 98312 | tf_op jit(solution)/shard_map/ppermute | solution.py:300
  17.8 1.3 %collective-permute-start.4 = (f32[8,1024]{1,0:T(8,128)S(1)}, f32[8,1024]{1,0:T(8,128)S(1)}, u32[]{:S(2)}, u32[]{:S(2)}) collective-permute-start(f32[8,1024]{1,0:T(8,128)S(1)} %add_add_fusion.mine_ref), channel_id=1, source_target_pairs={{0,1},{1,0},{2,3},{3,2},{4,5},{5,4},{6,7},{7,6},{8,9},{9,8},{10,11... | collective-permute-start | bytes 98312 | tf_op jit(solution)/shard_map/ppermute | solution.py:300
  18.5 1.4 %collective-permute-start.5 = (f32[8,512]{1,0:T(8,128)S(1)}, f32[8,512]{1,0:T(8,128)S(1)}, u32[]{:S(2)}, u32[]{:S(2)}) collective-permute-start(f32[8,512]{1,0:T(8,128)S(1)} %reflect.1), channel_id=1, source_target_pairs={{0,1},{1,0},{2,3},{3,2},{4,5},{5,4},{6,7},{7,6},{8,9},{9,8},{10,11... | collective-permute-start | bytes 49160 | tf_op jit(solution)/shard_map/ppermute | solution.py:300
  20.0 5.4 %collective-permute-start.7 = (f32[8,512]{1,0:T(8,128)S(1)}, f32[8,512]{1,0:T(8,128)S(1)}, u32[]{:S(2)}, u32[]{:S(2)}) collective-permute-start(f32[8,512]{1,0:T(8,128)S(1)} %add_add_fusion.2.own_ref), channel_id=1, source_target_pairs={{0,2},{4,6},{8,10},{12,14},{1,15},{3,13},{5,11},{7,9},{2,0},{6,4},... | collective-permute-start | bytes 49160 | tf_op jit(solution)/shard_map/ppermute | solution.py:300
  21.6 5.7 %collective-permute-start.8 = (f32[8,512]{1,0:T(8,128)S(1)}, f32[8,512]{1,0:T(8,128)S(1)}, u32[]{:S(2)}, u32[]{:S(2)}) collective-permute-start(f32[8,512]{1,0:T(8,128)S(1)} %add_add_fusion.2.own_ref), channel_id=1, source_target_pairs={{0,10},{2,8},{4,14},{6,12},{1,9},{3,11},{5,13},{7,15},{10,0},{8,2}... | collective-permute-start | bytes 49160 | tf_op jit(solution)/shard_map/ppermute | solution.py:300
  22.8 4.5 %collective-permute-start.9 = (f32[8,512]{1,0:T(8,128)S(1)}, f32[8,512]{1,0:T(8,128)S(1)}, u32[]{:S(2)}, u32[]{:S(2)}) collective-permute-start(f32[8,512]{1,0:T(8,128)S(1)} %add_add_fusion.2.own_ref), channel_id=1, source_target_pairs={{0,4},{2,6},{8,12},{10,14},{1,13},{3,15},{5,9},{7,11},{4,0},{6,2},... | collective-permute-start | bytes 49160 | tf_op jit(solution)/shard_map/ppermute | solution.py:300
  24.1 4.1 %collective-permute-start.6 = (f32[8,512]{1,0:T(8,128)S(1)}, f32[8,512]{1,0:T(8,128)S(1)}, u32[]{:S(2)}, u32[]{:S(2)}) collective-permute-start(f32[8,512]{1,0:T(8,128)S(1)} %add_add_fusion.2.own_ref), channel_id=1, source_target_pairs={{0,7},{2,5},{8,15},{10,13},{1,6},{3,4},{9,14},{11,12},{7,0},{5,2},... | collective-permute-start | bytes 49160 | tf_op jit(solution)/shard_map/ppermute | solution.py:300
  25.4 2.8 %collective-permute-start.10 = (f32[8,512]{1,0:T(8,128)S(1)}, f32[8,512]{1,0:T(8,128)S(1)}, u32[]{:S(2)}, u32[]{:S(2)}) collective-permute-start(f32[8,512]{1,0:T(8,128)S(1)} %collective-permute-done.7.refs_0_), channel_id=1, source_target_pairs={{0,1},{1,0},{2,3},{3,2},{4,5},{5,4},{6,7},{7,6},{8,9},{9,8},{10,11... | collective-permute-start | bytes 49160 | tf_op jit(solution)/shard_map/ppermute | solution.py:300
  27.2 1.2 %collective-permute-start.11 = (f32[8,512]{1,0:T(8,128)S(1)}, f32[8,512]{1,0:T(8,128)S(1)}, u32[]{:S(2)}, u32[]{:S(2)}) collective-permute-start(f32[8,512]{1,0:T(8,128)S(1)} %collective-permute-done.8.refs_1_), channel_id=1, source_target_pairs={{0,1},{1,0},{2,3},{3,2},{4,5},{5,4},{6,7},{7,6},{8,9},{9,8},{10,11... | collective-permute-start | bytes 49160 | tf_op jit(solution)/shard_map/ppermute | solution.py:300
  27.2 1.3 %collective-permute-start.12 = (f32[8,512]{1,0:T(8,128)S(1)}, f32[8,512]{1,0:T(8,128)S(1)}, u32[]{:S(2)}, u32[]{:S(2)}) collective-permute-start(f32[8,512]{1,0:T(8,128)S(1)} %collective-permute-done.9.refs_2_), channel_id=1, source_target_pairs={{0,1},{1,0},{2,3},{3,2},{4,5},{5,4},{6,7},{7,6},{8,9},{9,8},{10,11... | collective-permute-start | bytes 49160 | tf_op jit(solution)/shard_map/ppermute | solution.py:300

commit v21 on v20

--- a/solution.py
+++ b/solution.py
@@ -319,12 +319,12 @@
     last = max(count // 4, 1)
     step = 1
     while step < last:
-        value = value + (zero + swap_chips(value, (step, step)))
+        value = value + (swap_chips(value, (step, step)) + zero)
         zero = 0.0
         step *= 2
     terms = [value] + [swap_chips(value, (offset, offset)) for offset in range(last, count, last)]
     while len(terms) > 1:
-        terms = [terms[at] + terms[at + 1] for at in range(0, len(terms), 2)]
+        terms = [terms[at + 1] + terms[at] for at in range(0, len(terms), 2)]
     return terms[0]
 
 

time: 31.8 us -> 32.2 us (1.013)
  starting transfers between devices: 14.7 us -> 15.5 us
  waiting for transfers between devices: 7.42 us -> 6.71 us
    ppermute x13, starting transfers between devices: 14.7 us -> 15.5 us  [swap(): lax.ppermute(value, axes, pairs + [(target, source) for source, target in...]
    ppermute x13, waiting for transfers between devices: 7.42 us -> 6.71 us  [swap(): lax.ppermute(value, axes, pairs + [(target, source) for source, target in...]
  transfers between devices with their start and end apart: 13 -> 13, of which waited for: 7 -> 6; matrix products, arithmetic and copies ran while one was open for 0% -> 0% of each run, Pallas kernels for 8% -> 8%
where the time goes in v21:
time: 32.2 us; the launch traced here: 31.7 us
  starting transfers between devices  15.5 us (48%)
  Pallas kernels  8.77 us (27%)
  waiting for transfers between devices  6.71 us (21%)
  between operations  0.69 us (2%)
    ppermute x13, starting transfers between devices, swap(): lax.ppermute(value, axes, pairs + [(target, source) for source, target in...  15.5 us
    ppermute x13, waiting for transfers between devices, swap(): lax.ppermute(value, axes, pairs + [(target, source) for source, target in...  6.71 us
    pallas_call x1, Pallas kernels, project(): pl.pallas_call(project_body, out_shape=(jax.ShapeDtypeStruct((mats * RANK...  3.35 us
    pallas_call x1, Pallas kernels, finish(): pl.pallas_call(functools.partial(finish_body, scale, len(taken)), out_sha...  3.03 us
    pallas_call x1, Pallas kernels, turn(): pl.pallas_call(functools.partial(turn_body, scale), out_shape=(pltpu.VMEM...  0.88 us
    pallas_call x1, Pallas kernels, merge(): pl.pallas_call(merge_body, out_shape=(pltpu.VMEM(shape, F32), pltpu.VMEM(...  0.86 us
  transfers between devices with their start and end apart: 13, of which 6 were waited for; matrix products, arithmetic and copies ran while one was open for 0% of the time, Pallas kernels for 8%

profile of v21, /device:TPU:0, one launch (start us, length us, event | category | flops | bytes accessed | tf_op | source)
XLA Modules:
  0.0 31.7 jit_solution(11530090134124929491)
XLA Ops:
  0.6 3.4 %project.1 = (f32[8,1024]{1,0:T(8,128)S(1)}, bf16[2,1024,512]{2,1,0:T(8,128)(2,1)S(1)}, f32[2,1024,512]{2,1,0:T(8,128)S(1)}) custom-call(s32[2]{0:T(128)} %seeds_ref.1, bf16[1,2,1024,512]{3,2,1,0:T(8,128)(2,1)} %grads_ref.1, f32[1,2,1024,512]{3,2,1,0:T(8,128)} %errors_ref.1), custom_call_target="tpu_custom_call" | custom-call | tf_op jit(solution)/shard_map/project/pallas_call | solution.py:87
  4.0 3.0 %collective-permute-start = (f32[8,1024]{1,0:T(8,128)S(1)}, f32[8,1024]{1,0:T(8,128)S(1)}, u32[]{:S(2)}, u32[]{:S(2)}) collective-permute-start(f32[8,1024]{1,0:T(8,128)S(1)} %get-tuple-element.12), channel_id=1, source_target_pairs={{0,2},{4,6},{8,10},{12,14},{1,3},{5,7},{9,11},{13,15},{2,0},{6,4},... | collective-permute-start | bytes 98312 | tf_op jit(solution)/shard_map/ppermute | solution.py:300
  7.0 0.9 %merge.1 = (f32[2,1024,512]{2,1,0:T(8,128)S(1)}, bf16[2,1024,512]{2,1,0:T(8,128)(2,1)S(1)}, bf16[2,1024,512]{2,1,0:T(8,128)(2,1)S(1)}, f32[8,1024]{1,0:T(8,128)S(1)}) custom-call(bf16[2,1024,512]{2,1,0:T(8,128)(2,1)S(1)} %get-tuple-element.13.grads_ref, f32[2,1024,512]{2,1,0:T(8,128)S(1)} %get-tuple-element.14.errors_ref), custom_call_target="tpu_custom_call" | custom-call | flops 3145728 | bytes 14680064 | tf_op jit(solution)/shard_map/merge/pallas_call | solution.py:124
  7.9 1.0 %collective-permute-done = f32[8,1024]{1,0:T(8,128)S(1)} collective-permute-done((f32[8,1024]{1,0:T(8,128)S(1)}, f32[8,1024]{1,0:T(8,128)S(1)}, u32[]{:S(2)}, u32[]{:S(2)}) %collective-permute-start) | collective-permute-done | bytes 32800 | tf_op jit(solution)/shard_map/ppermute | solution.py:300
  8.9 4.2 %collective-permute-start.1 = (f32[8,1024]{1,0:T(8,128)S(1)}, f32[8,1024]{1,0:T(8,128)S(1)}, u32[]{:S(2)}, u32[]{:S(2)}) collective-permute-start(f32[8,1024]{1,0:T(8,128)S(1)} %add_add_fusion.1), channel_id=1, source_target_pairs={{0,12},{2,14},{4,8},{6,10},{1,13},{3,15},{5,9},{7,11},{12,0},{14,2... | collective-permute-start | bytes 98312 | tf_op jit(solution)/shard_map/ppermute | solution.py:300
  13.1 0.0 collective-permute-start.2
  13.1 0.6 %collective-permute-start.3 = (f32[8,1024]{1,0:T(8,128)S(1)}, f32[8,1024]{1,0:T(8,128)S(1)}, u32[]{:S(2)}, u32[]{:S(2)}) collective-permute-start(f32[8,1024]{1,0:T(8,128)S(1)} %add_add_fusion.1), channel_id=1, source_target_pairs={{0,4},{2,6},{8,12},{10,14},{1,5},{3,7},{9,13},{11,15},{4,0},{6,2},... | collective-permute-start | bytes 98312 | tf_op jit(solution)/shard_map/ppermute | solution.py:300
  13.7 1.3 %collective-permute-done.1 = f32[8,1024]{1,0:T(8,128)S(1)} collective-permute-done((f32[8,1024]{1,0:T(8,128)S(1)}, f32[8,1024]{1,0:T(8,128)S(1)}, u32[]{:S(2)}, u32[]{:S(2)}) %collective-permute-start.1) | collective-permute-done | bytes 32800 | tf_op jit(solution)/shard_map/ppermute | solution.py:300
  15.0 2.9 %collective-permute-done.2 = f32[8,1024]{1,0:T(8,128)S(1)} collective-permute-done((f32[8,1024]{1,0:T(8,128)S(1)}, f32[8,1024]{1,0:T(8,128)S(1)}, u32[]{:S(2)}, u32[]{:S(2)}) %collective-permute-start.2) | collective-permute-done | bytes 32800 | tf_op jit(solution)/shard_map/ppermute | solution.py:300
  17.9 0.0 collective-permute-done.3
  17.9 0.1 collective-permute-start.4
  18.0 0.6 %reflect.1 = f32[8,512]{1,0:T(8,128)S(1)} custom-call(f32[8,1024]{1,0:T(8,128)S(1)} %add_add_fusion.mine_ref, bf16[2,1024,512]{2,1,0:T(8,128)(2,1)S(1)} %get-tuple-element.19.high_ref, bf16[2,1024,512]{2,1,0:T(8,128)(2,1)S(1)} %get-tuple-element.20.low_ref), custom_call_target="tpu_custom_call" | custom-call | flops 67108864 | bytes 4194304 | tf_op jit(solution)/shard_map/reflect/pallas_call | solution.py:185
  18.6 0.5 %collective-permute-start.5 = (f32[8,512]{1,0:T(8,128)S(1)}, f32[8,512]{1,0:T(8,128)S(1)}, u32[]{:S(2)}, u32[]{:S(2)}) collective-permute-start(f32[8,512]{1,0:T(8,128)S(1)} %reflect.1), channel_id=1, source_target_pairs={{0,1},{1,0},{2,3},{3,2},{4,5},{5,4},{6,7},{7,6},{8,9},{9,8},{10,11... | collective-permute-start | bytes 49160 | tf_op jit(solution)/shard_map/ppermute | solution.py:300
  19.2 0.0 collective-permute-done.4.other_ref
  19.2 0.9 %turn.1 = (bf16[1024,48]{1,0:T(8,128)(2,1)S(1)}, f32[4,8,512]{2,1,0:T(8,128)S(1)}, f32[8,512]{1,0:T(8,128)S(1)}) custom-call(f32[8,1024]{1,0:T(8,128)S(1)} %add_add_fusion.mine_ref, f32[8,1024]{1,0:T(8,128)S(1)} %collective-permute-done.4.other_ref), custom_call_target="tpu_custom_call" | custom-call | flops 524288 | bytes 1048576 | tf_op jit(solution)/shard_map/turn/pallas_call | solution.py:207
  20.1 0.0 collective-permute-done.5
  20.1 1.6 %collective-permute-start.7 = (f32[8,512]{1,0:T(8,128)S(1)}, f32[8,512]{1,0:T(8,128)S(1)}, u32[]{:S(2)}, u32[]{:S(2)}) collective-permute-start(f32[8,512]{1,0:T(8,128)S(1)} %add_add_fusion.2.own_ref), channel_id=1, source_target_pairs={{0,2},{4,6},{8,10},{12,14},{1,15},{3,13},{5,11},{7,9},{2,0},{6,4},... | collective-permute-start | bytes 49160 | tf_op jit(solution)/shard_map/ppermute | solution.py:300
  21.7 2.0 %collective-permute-start.8 = (f32[8,512]{1,0:T(8,128)S(1)}, f32[8,512]{1,0:T(8,128)S(1)}, u32[]{:S(2)}, u32[]{:S(2)}) collective-permute-start(f32[8,512]{1,0:T(8,128)S(1)} %add_add_fusion.2.own_ref), channel_id=1, source_target_pairs={{0,10},{2,8},{4,14},{6,12},{1,9},{3,11},{5,13},{7,15},{10,0},{8,2}... | collective-permute-start | bytes 49160 | tf_op jit(solution)/shard_map/ppermute | solution.py:300
  23.7 0.0 collective-permute-start.9
  23.7 1.3 %collective-permute-start.6 = (f32[8,512]{1,0:T(8,128)S(1)}, f32[8,512]{1,0:T(8,128)S(1)}, u32[]{:S(2)}, u32[]{:S(2)}) collective-permute-start(f32[8,512]{1,0:T(8,128)S(1)} %add_add_fusion.2.own_ref), channel_id=1, source_target_pairs={{0,7},{2,5},{8,15},{10,13},{1,6},{3,4},{9,14},{11,12},{7,0},{5,2},... | collective-permute-start | bytes 49160 | tf_op jit(solution)/shard_map/ppermute | solution.py:300
  25.0 0.0 collective-permute-done.7.refs_0_
  25.0 1.8 %collective-permute-start.10 = (f32[8,512]{1,0:T(8,128)S(1)}, f32[8,512]{1,0:T(8,128)S(1)}, u32[]{:S(2)}, u32[]{:S(2)}) collective-permute-start(f32[8,512]{1,0:T(8,128)S(1)} %collective-permute-done.7.refs_0_), channel_id=1, source_target_pairs={{0,1},{1,0},{2,3},{3,2},{4,5},{5,4},{6,7},{7,6},{8,9},{9,8},{10,11... | collective-permute-start | bytes 49160 | tf_op jit(solution)/shard_map/ppermute | solution.py:300
  26.8 0.6 %collective-permute-done.8.refs_1_ = f32[8,512]{1,0:T(8,128)S(1)} collective-permute-done((f32[8,512]{1,0:T(8,128)S(1)}, f32[8,512]{1,0:T(8,128)S(1)}, u32[]{:S(2)}, u32[]{:S(2)}) %collective-permute-start.8) | collective-permute-done | bytes 16416 | tf_op jit(solution)/shard_map/ppermute | solution.py:300
  27.4 0.0 collective-permute-start.11
  27.4 0.0 collective-permute-done.9.refs_2_
  27.4 0.5 %collective-permute-start.12 = (f32[8,512]{1,0:T(8,128)S(1)}, f32[8,512]{1,0:T(8,128)S(1)}, u32[]{:S(2)}, u32[]{:S(2)}) collective-permute-start(f32[8,512]{1,0:T(8,128)S(1)} %collective-permute-done.9.refs_2_), channel_id=1, source_target_pairs={{0,1},{1,0},{2,3},{3,2},{4,5},{5,4},{6,7},{7,6},{8,9},{9,8},{10,11... | collective-permute-start | bytes 49160 | tf_op jit(solution)/shard_map/ppermute | solution.py:300
  27.9 0.0 collective-permute-done.6.both_ref
  27.9 0.0 collective-permute-done.10.refs_3_
  27.9 0.7 %collective-permute-done.11.refs_4_ = f32[8,512]{1,0:T(8,128)S(1)} collective-permute-done((f32[8,512]{1,0:T(8,128)S(1)}, f32[8,512]{1,0:T(8,128)S(1)}, u32[]{:S(2)}, u32[]{:S(2)}) %collective-permute-start.11) | collective-permute-done | bytes 16416 | tf_op jit(solution)/shard_map/ppermute | solution.py:300
  28.5 0.2 collective-permute-done.12.refs_5_
  28.7 3.0 %finish.1 = (bf16[2,1024,512]{2,1,0:T(8,128)(2,1)}, f32[1,2,1024,512]{3,2,1,0:T(8,128)}) custom-call(bf16[1024,48]{1,0:T(8,128)(2,1)S(1)} %get-tuple-element.16.left_ref, f32[4,8,512]{2,1,0:T(8,128)S(1)} %get-tuple-element.17.steps_ref, f32[2,1024,512]{2,1,0:T(8,128)S(1)} %get-tuple-element.18.merged_ref, f32[8,512]{1,0:T(8,128)S(1)} %add_add_fusion.2.own_ref, ...), custom_call_target="tpu_custom_call" | custom-call | tf_op jit(solution)/shard_map/finish/pallas_call | solution.py:273
  (3 shorter events, 0.0 us)
Async XLA Ops:
  4.0 4.9 %collective-permute-start = (f32[8,1024]{1,0:T(8,128)S(1)}, f32[8,1024]{1,0:T(8,128)S(1)}, u32[]{:S(2)}, u32[]{:S(2)}) collective-permute-start(f32[8,1024]{1,0:T(8,128)S(1)} %get-tuple-element.12), channel_id=1, source_target_pairs={{0,2},{4,6},{8,10},{12,14},{1,3},{5,7},{9,11},{13,15},{2,0},{6,4},... | collective-permute-start | bytes 98312 | tf_op jit(solution)/shard_map/ppermute | solution.py:300
  8.9 6.1 %collective-permute-start.1 = (f32[8,1024]{1,0:T(8,128)S(1)}, f32[8,1024]{1,0:T(8,128)S(1)}, u32[]{:S(2)}, u32[]{:S(2)}) collective-permute-start(f32[8,1024]{1,0:T(8,128)S(1)} %add_add_fusion.1), channel_id=1, source_target_pairs={{0,12},{2,14},{4,8},{6,10},{1,13},{3,15},{5,9},{7,11},{12,0},{14,2... | collective-permute-start | bytes 98312 | tf_op jit(solution)/shard_map/ppermute | solution.py:300
  13.1 4.8 %collective-permute-start.2 = (f32[8,1024]{1,0:T(8,128)S(1)}, f32[8,1024]{1,0:T(8,128)S(1)}, u32[]{:S(2)}, u32[]{:S(2)}) collective-permute-start(f32[8,1024]{1,0:T(8,128)S(1)} %add_add_fusion.1), channel_id=1, source_target_pairs={{0,8},{2,10},{4,12},{6,14},{1,9},{3,11},{5,13},{7,15},{8,0},{10,2}... | collective-permute-start | bytes 98312 | tf_op jit(solution)/shard_map/ppermute | solution.py:300
  13.1 4.8 %collective-permute-start.3 = (f32[8,1024]{1,0:T(8,128)S(1)}, f32[8,1024]{1,0:T(8,128)S(1)}, u32[]{:S(2)}, u32[]{:S(2)}) collective-permute-start(f32[8,1024]{1,0:T(8,128)S(1)} %add_add_fusion.1), channel_id=1, source_target_pairs={{0,4},{2,6},{8,12},{10,14},{1,5},{3,7},{9,13},{11,15},{4,0},{6,2},... | collective-permute-start | bytes 98312 | tf_op jit(solution)/shard_map/ppermute | solution.py:300
  17.9 1.3 %collective-permute-start.4 = (f32[8,1024]{1,0:T(8,128)S(1)}, f32[8,1024]{1,0:T(8,128)S(1)}, u32[]{:S(2)}, u32[]{:S(2)}) collective-permute-start(f32[8,1024]{1,0:T(8,128)S(1)} %add_add_fusion.mine_ref), channel_id=1, source_target_pairs={{0,1},{1,0},{2,3},{3,2},{4,5},{5,4},{6,7},{7,6},{8,9},{9,8},{10,11... | collective-permute-start | bytes 98312 | tf_op jit(solution)/shard_map/ppermute | solution.py:300
  18.6 1.4 %collective-permute-start.5 = (f32[8,512]{1,0:T(8,128)S(1)}, f32[8,512]{1,0:T(8,128)S(1)}, u32[]{:S(2)}, u32[]{:S(2)}) collective-permute-start(f32[8,512]{1,0:T(8,128)S(1)} %reflect.1), channel_id=1, source_target_pairs={{0,1},{1,0},{2,3},{3,2},{4,5},{5,4},{6,7},{7,6},{8,9},{9,8},{10,11... | collective-permute-start | bytes 49160 | tf_op jit(solution)/shard_map/ppermute | solution.py:300
  20.1 4.9 %collective-permute-start.7 = (f32[8,512]{1,0:T(8,128)S(1)}, f32[8,512]{1,0:T(8,128)S(1)}, u32[]{:S(2)}, u32[]{:S(2)}) collective-permute-start(f32[8,512]{1,0:T(8,128)S(1)} %add_add_fusion.2.own_ref), channel_id=1, source_target_pairs={{0,2},{4,6},{8,10},{12,14},{1,15},{3,13},{5,11},{7,9},{2,0},{6,4},... | collective-permute-start | bytes 49160 | tf_op jit(solution)/shard_map/ppermute | solution.py:300
  21.7 5.7 %collective-permute-start.8 = (f32[8,512]{1,0:T(8,128)S(1)}, f32[8,512]{1,0:T(8,128)S(1)}, u32[]{:S(2)}, u32[]{:S(2)}) collective-permute-start(f32[8,512]{1,0:T(8,128)S(1)} %add_add_fusion.2.own_ref), channel_id=1, source_target_pairs={{0,10},{2,8},{4,14},{6,12},{1,9},{3,11},{5,13},{7,15},{10,0},{8,2}... | collective-permute-start | bytes 49160 | tf_op jit(solution)/shard_map/ppermute | solution.py:300
  23.7 3.7 %collective-permute-start.9 = (f32[8,512]{1,0:T(8,128)S(1)}, f32[8,512]{1,0:T(8,128)S(1)}, u32[]{:S(2)}, u32[]{:S(2)}) collective-permute-start(f32[8,512]{1,0:T(8,128)S(1)} %add_add_fusion.2.own_ref), channel_id=1, source_target_pairs={{0,4},{2,6},{8,12},{10,14},{1,13},{3,15},{5,9},{7,11},{4,0},{6,2},... | collective-permute-start | bytes 49160 | tf_op jit(solution)/shard_map/ppermute | solution.py:300
  23.7 4.2 %collective-permute-start.6 = (f32[8,512]{1,0:T(8,128)S(1)}, f32[8,512]{1,0:T(8,128)S(1)}, u32[]{:S(2)}, u32[]{:S(2)}) collective-permute-start(f32[8,512]{1,0:T(8,128)S(1)} %add_add_fusion.2.own_ref), channel_id=1, source_target_pairs={{0,7},{2,5},{8,15},{10,13},{1,6},{3,4},{9,14},{11,12},{7,0},{5,2},... | collective-permute-start | bytes 49160 | tf_op jit(solution)/shard_map/ppermute | solution.py:300
  25.0 2.9 %collective-permute-start.10 = (f32[8,512]{1,0:T(8,128)S(1)}, f32[8,512]{1,0:T(8,128)S(1)}, u32[]{:S(2)}, u32[]{:S(2)}) collective-permute-start(f32[8,512]{1,0:T(8,128)S(1)} %collective-permute-done.7.refs_0_), channel_id=1, source_target_pairs={{0,1},{1,0},{2,3},{3,2},{4,5},{5,4},{6,7},{7,6},{8,9},{9,8},{10,11... | collective-permute-start | bytes 49160 | tf_op jit(solution)/shard_map/ppermute | solution.py:300
  27.4 1.2 %collective-permute-start.11 = (f32[8,512]{1,0:T(8,128)S(1)}, f32[8,512]{1,0:T(8,128)S(1)}, u32[]{:S(2)}, u32[]{:S(2)}) collective-permute-start(f32[8,512]{1,0:T(8,128)S(1)} %collective-permute-done.8.refs_1_), channel_id=1, source_target_pairs={{0,1},{1,0},{2,3},{3,2},{4,5},{5,4},{6,7},{7,6},{8,9},{9,8},{10,11... | collective-permute-start | bytes 49160 | tf_op jit(solution)/shard_map/ppermute | solution.py:300
  27.4 1.3 %collective-permute-start.12 = (f32[8,512]{1,0:T(8,128)S(1)}, f32[8,512]{1,0:T(8,128)S(1)}, u32[]{:S(2)}, u32[]{:S(2)}) collective-permute-start(f32[8,512]{1,0:T(8,128)S(1)} %collective-permute-done.9.refs_2_), channel_id=1, source_target_pairs={{0,1},{1,0},{2,3},{3,2},{4,5},{5,4},{6,7},{7,6},{8,9},{9,8},{10,11... | collective-permute-start | bytes 49160 | tf_op jit(solution)/shard_map/ppermute | solution.py:300
